TPU v7x, 32 devices: a whole 2x2x4 slice. The times are simulated.
32 devices in a mesh: batch: 8 (over z, x), chan: 4 (over y, core).
Axes of the slice: x: 2, y: 2, z: 4, core: 2. Of those that a mesh axis runs over, the one named last changes fastest.
Arguments:
- features: bfloat16 [192, 9, 9, 2048], P('batch', None, None, 'chan'), may hold values from -6 to 6
- w_reduce: bfloat16 [2048, 1024], P(None, 'chan'), may hold values from -0.125 to 0.125
- gain_one: float32 [1024], P('chan'), may hold values from 0.25 to 1.75
- shift_one: float32 [1024], P('chan'), may hold values from -1.5 to 1.5
- w_group: bfloat16 [3, 3, 32, 1024], P(None, None, None, 'chan'), may hold values from -0.375 to 0.375
- gain_two: float32 [1024], P('chan'), may hold values from 0.25 to 1.75
- shift_two: float32 [1024], P('chan'), may hold values from -1.5 to 1.5
- w_expand: bfloat16 [1024, 2048], P('chan'), may hold values from -0.1875 to 0.1875
- gain_three: float32 [2048], replicated, may hold values from 0.25 to 1.75
- shift_three: float32 [2048], replicated, may hold values from -1.5 to 1.5
- cotangent: bfloat16 [192, 9, 9, 2048], P('batch'), may hold values from -6 to 6
- resolution: int32 [8], P('batch'), may hold values from 5 to 9, as said below
- crop_count: int32 [8], P('batch'), may hold values from 18 to 24, as said below
Outputs:
- block_out: bfloat16 [192, 9, 9, 2048], P('batch', None, None, 'chan')
- features_grad: float32 [192, 9, 9, 2048], P('batch', None, None, 'chan')
- reduce_grad: float32 [2048, 1024], P(None, 'chan')
- gain_one_grad: float32 [1024], P('chan')
- shift_one_grad: float32 [1024], P('chan')
- group_grad: float32 [3, 3, 32, 1024], P(None, None, None, 'chan')
- gain_two_grad: float32 [1024], P('chan')
- shift_two_grad: float32 [1024], P('chan')
- expand_grad: float32 [1024, 2048], P('chan')
- gain_three_grad: float32 [2048], P('chan')
- shift_three_grad: float32 [2048], P('chan')
Inputs may be any that keep to these rules, and one draw needn't show every extreme that they name: `resolution`: each entry is 5, 7 or 9, and some batch rank has 9 in every draw. `crop_count`: some batch rank uses all 24 slots in every draw.
All inputs are finite; a program needn't handle non-finite values.
Results may differ from a plain program's by a relative error of at most 0.018.
Values may be sent and summed in bfloat16 or wider, within the bound.
No kernel may reach another device: no remote copies, remote signals or barrier semaphores. Data moves between devices by JAX's collectives and lax.ppermute only.
A program may use at most 192 MiB of HBM per device.

v0:
```python
import functools

import jax
import jax.numpy as jnp
from jax import lax
from jax.experimental import pallas as pl
from jax.experimental.pallas import tpu as pltpu
from jax.sharding import PartitionSpec as P

EPSILON = 1e-05
ROOT = 0.7978845608028654
CUBE = 0.044715
F32 = jnp.float32
BF16 = jnp.bfloat16
STEP = 256
LANES = 128
TN = (((0,), (0,)), ((), ()))
NT = (((1,), (1,)), ((), ()))
VM = pl.BlockSpec(memory_space=pltpu.VMEM)
SM = pl.BlockSpec(memory_space=pltpu.SMEM)


def dot(a, b):
    return jnp.dot(a, b, preferred_element_type=F32)


def dot_tn(a, b):
    return lax.dot_general(a, b, TN, preferred_element_type=F32)


def dot_nt(a, b):
    return lax.dot_general(a, b, NT, preferred_element_type=F32)


def bend(v):
    return jnp.tanh(v * (ROOT + (ROOT * CUBE) * (v * v)))


def act(v):
    half = 0.5 * v
    return half + half * bend(v)


def act_slope(v):
    t = bend(v)
    inner = v * (0.5 * ROOT + (1.5 * ROOT * CUBE) * (v * v))
    return 0.5 + 0.5 * t + inner * (1.0 - t * t)


def chunks(total, body, step=STEP):
    full = total // step

    def go(c, carry):
        body(pl.multiple_of(c * step, step), step)
        return carry

    if full:
        lax.fori_loop(0, full, go, 0)
    if total % step:
        body(full * step, total % step)


def fold(v):
    return jnp.sum(v.reshape(v.shape[0] // 8, 8, v.shape[1]), axis=0)


def widen(live, width):
    return jnp.concatenate([live] * (width // LANES), axis=1) if width > LANES else live


def norm_of(got, counts):
    s = jnp.sum(got[...], axis=0)
    share_of = 1.0 / jnp.sum(counts[...], axis=0)[2:3, 0:1]
    mu = s[0:1] * share_of
    return mu, lax.rsqrt(s[1:2] * share_of - mu * mu + EPSILON), share_of


def send_sums(out, acc):
    out[...] = jnp.broadcast_to(jnp.sum(acc[...], axis=1)[None], out.shape)


def near_kernel(dims, *refs):
    *feats, w, out = refs
    share = feats[0].shape[1]
    me = dims[2]
    ws = [w[pl.ds(pl.multiple_of((me ^ k) * share, share), share), :] for k in range(len(feats))]

    def body(o, n):
        out[pl.ds(o, n), :] = sum(dot(f[pl.ds(o, n), :], wk) for f, wk in zip(feats, ws))

    chunks(out.shape[0], body)


def far_kernel(halves, dims, live, part, *refs):
    *feats, w, out, spread, acc = refs
    share = feats[0].shape[1]
    half = part.shape[0] // halves
    me = dims[2]
    acc[...] = jnp.zeros_like(acc)
    ks = range(len(feats) // halves)
    ws = [w[pl.ds(pl.multiple_of((me ^ (k + 2)) * share, share), share), :] for k in ks]
    for h in range(halves):

        def body(o, n, h=h):
            rows = pl.ds(h * half + o, n)
            z = part[rows, :] + sum(dot(feats[k * halves + h][pl.ds(o, n), :], ws[k]) for k in ks)
            out[rows, :] = z
            m = widen(live[rows, :], z.shape[1])
            mz = m * z
            acc[0] += fold(mz)
            acc[1] += fold(mz * z)
            acc[2] += fold(m)

        chunks(half, body)
    send_sums(spread, acc)


def pad_edges(pad, side, line, wide, slots):
    width = pad.shape[1]
    pad[0:wide] = jnp.zeros((wide, width), F32)
    pad[(side + 1) * wide : (side + 2) * wide] = jnp.zeros((wide, width), F32)


def pad_line(pad, i, value, line, wide, slots):
    o = pl.multiple_of((i + 1) * wide, 8)
    edge = jnp.zeros((slots, pad.shape[1]), F32)
    pad[pl.ds(o, slots), :] = edge
    pad[pl.ds(o + slots, line), :] = value
    pad[pl.ds(o + slots + line, slots), :] = edge


def conv_line(pad, i, taps, line, wide, slots, flip):
    total = None
    for t in range(9):
        a, b = divmod(t, 3)
        o = pl.multiple_of((i + a) * wide + b * slots, 8)
        d = dot(pad[pl.ds(o, line), :].astype(BF16), taps[8 - t if flip else t])
        total = d if total is None else total + d
    return total


def conv_kernel(side, slots, live, z, got, gain, shift, taps, hid, out, spread, pad, acc):
    line, wide = side * slots, (side + 2) * slots
    rows, width = z.shape
    mu, r, _ = norm_of(got, got)
    a = r * gain[...]
    b = shift[...] - mu * a
    pad_edges(pad, side, line, wide, slots)
    acc[...] = jnp.zeros_like(acc)

    def fill(i, carry):
        here = pl.ds(pl.multiple_of(i * line, 8), line)
        h = widen(live[here, :], width) * act(z[here, :] * a + b)
        h = h.astype(BF16).astype(F32)
        hid[here, :] = h
        pad_line(pad, i, h, line, wide, slots)
        return carry

    lax.fori_loop(0, side, fill, 0)

    def conv(i, carry):
        here = pl.ds(pl.multiple_of(i * line, 8), line)
        total = conv_line(pad, i, taps, line, wide, slots, False)
        out[here, :] = total
        m = widen(live[here, :], width) * total
        acc[0] += fold(m)
        acc[1] += fold(m * total)
        return carry

    lax.fori_loop(0, side, conv, 0)
    used = side * line
    out[used:rows] = jnp.zeros((rows - used, width), F32)
    hid[used:rows] = jnp.zeros((rows - used, width), F32)
    send_sums(spread, acc)


def hidden_kernel(live, z, counts, got, gain, shift, out):
    mu, r, _ = norm_of(got, counts)
    a = r * gain[...]
    b = shift[...] - mu * a

    def body(o, n):
        rows = pl.ds(o, n)
        m = widen(live[rows, :], z.shape[1])
        out[rows, :] = (m * act(z[rows, :] * a + b)).astype(BF16)

    chunks(z.shape[0], body)


def slope_kernel(live, z, counts, got, gain, shift, out):
    mu, r, _ = norm_of(got, counts)
    a = r * gain[...]
    b = shift[...] - mu * a

    def body(o, n):
        rows = pl.ds(o, n)
        out[rows, :] = widen(live[rows, :], z.shape[1]) * act_slope(z[rows, :] * a + b)

    chunks(z.shape[0], body)


def expand_near_kernel(*refs):
    *ins, out = refs
    k = len(ins) // 2
    hs, ws = ins[:k], ins[k:]

    def body(o, n):
        out[pl.ds(o, n), :] = sum(dot(h[pl.ds(o, n), :], w[...]) for h, w in zip(hs, ws))

    chunks(out.shape[0], body)


def expand_far_kernel(live, part, *refs):
    *ins, out, spread, acc = refs
    k = len(ins) // 2
    hs, ws = ins[:k], ins[k:]
    acc[...] = jnp.zeros_like(acc)

    def body(o, n):
        rows = pl.ds(o, n)
        e = part[rows, :] + sum(dot(h[rows, :], w[...]) for h, w in zip(hs, ws))
        out[rows, :] = e
        m = widen(live[rows, :], e.shape[1]) * e
        acc[0] += fold(m)
        acc[1] += fold(m * e)

    chunks(out.shape[0], body)
    send_sums(spread, acc)


def third_kernel(live, e, counts, got, gain, shift, feats, cot, d_pre, spread, acc):
    mu, r, _ = norm_of(got, counts)
    acc[...] = jnp.zeros_like(acc)

    def body(o, n):
        rows = pl.ds(o, n)
        zhat = (e[rows, :] - mu) * r
        v = zhat * gain[...] + shift[...] + feats[rows, :].astype(F32)
        m = widen(live[rows, :], v.shape[1])
        d = m * cot[rows, :].astype(F32) * act_slope(v)
        d_pre[rows, :] = d
        acc[0] += fold(d)
        acc[1] += fold(d * zhat)

    chunks(e.shape[0], body, 128)
    send_sums(spread, acc)


def block_kernel(live, e, counts, got, gain, shift, feats, out):
    mu, r, _ = norm_of(got, counts)

    def body(o, n):
        rows = pl.ds(o, n)
        v = (e[rows, :] - mu) * r * gain[...] + shift[...] + feats[rows, :].astype(F32)
        out[rows, :] = (widen(live[rows, :], v.shape[1]) * act(v)).astype(BF16)

    chunks(out.shape[0], body)


def d_expanded_kernel(live, e, d_pre, counts, got, totals, gain, *refs):
    k = (len(refs) - 1) // 2
    ws, d_exp, outs = refs[:k], refs[k], refs[k + 1 :]
    mu, r, share_of = norm_of(got, counts)
    t = jnp.sum(totals[...], axis=0) * share_of
    scale = r * gain[...]

    def body(o, n):
        rows = pl.ds(o, n)
        zhat = (e[rows, :] - mu) * r
        m = widen(live[rows, :], zhat.shape[1])
        d = (m * scale * (d_pre[rows, :] - t[0:1] - zhat * t[1:2])).astype(BF16)
        d_exp[rows, :] = d
        for w, out in zip(ws, outs):
            out[rows, :] = dot_nt(d, w[...]).astype(out.dtype)

    chunks(e.shape[0], body)


def back_expand_kernel(d_exp, *refs):
    k = len(refs) // 2
    ws, outs = refs[:k], refs[k:]

    def body(o, n):
        rows = pl.ds(o, n)
        for w, out in zip(ws, outs):
            out[rows, :] = dot_nt(d_exp[rows, :], w[...]).astype(out.dtype)

    chunks(d_exp.shape[0], body)


def expand_grad_kernel(d_exp, *refs):
    *hs, out = refs
    for k, h in enumerate(hs):
        out[k] = dot_tn(h[...], d_exp[...]).astype(BF16)


def d_two_kernel(slope, z, counts, got, *refs):
    *terms, d_out, spread, acc = refs
    mu, r, _ = norm_of(got, counts)
    acc[...] = jnp.zeros_like(acc)

    def body(o, n):
        rows = pl.ds(o, n)
        d = sum(t[rows, :].astype(F32) for t in terms) * slope[rows, :]
        d_out[rows, :] = d
        acc[0] += fold(d)
        acc[1] += fold(d * ((z[rows, :] - mu) * r))

    chunks(z.shape[0], body)
    send_sums(spread, acc)


def conv_back_kernel(
    side, slots, live, d_two, grouped, got_two, totals, gain, slope, z, got, taps,
    d_grouped, d_one, spread, pad, acc,
):
    line, wide = side * slots, (side + 2) * slots
    rows, width = z.shape
    mu_two, r_two, share_of = norm_of(got_two, got)
    mu, r, _ = norm_of(got, got)
    t = jnp.sum(totals[...], axis=0) * share_of
    scale = r_two * gain[...]
    pad_edges(pad, side, line, wide, slots)
    acc[...] = jnp.zeros_like(acc)

    def fill(i, carry):
        here = pl.ds(pl.multiple_of(i * line, 8), line)
        zhat = (grouped[here, :] - mu_two) * r_two
        m = widen(live[here, :], width)
        d = m * scale * (d_two[here, :] - t[0:1] - zhat * t[1:2])
        d = d.astype(BF16).astype(F32)
        d_grouped[here, :] = d
        pad_line(pad, i, d, line, wide, slots)
        return carry

    lax.fori_loop(0, side, fill, 0)

    def conv(i, carry):
        here = pl.ds(pl.multiple_of(i * line, 8), line)
        d = conv_line(pad, i, taps, line, wide, slots, True) * slope[here, :]
        d_one[here, :] = d
        acc[0] += fold(d)
        acc[1] += fold(d * ((z[here, :] - mu) * r))
        return carry

    lax.fori_loop(0, side, conv, 0)
    used = side * line
    d_one[used:rows] = jnp.zeros((rows - used, width), F32)
    d_grouped[used:rows] = jnp.zeros((rows - used, width), F32)
    send_sums(spread, acc)


def d_reduced_kernel(live, d_one, z, got, totals, gain, out):
    mu, r, share_of = norm_of(got, got)
    t = jnp.sum(totals[...], axis=0) * share_of
    scale = r * gain[...]

    def body(o, n):
        rows = pl.ds(o, n)
        zhat = (z[rows, :] - mu) * r
        m = widen(live[rows, :], zhat.shape[1])
        out[rows, :] = (m * scale * (d_one[rows, :] - t[0:1] - zhat * t[1:2])).astype(BF16)

    chunks(z.shape[0], body)


def group_grad_kernel(side, slots, group_width, hid, d_grouped, out, pad):
    line, wide = side * slots, (side + 2) * slots
    width = hid.shape[1]
    pad_edges(pad, side, line, wide, slots)

    def fill(i, carry):
        here = pl.ds(pl.multiple_of(i * line, 8), line)
        pad_line(pad, i, hid[here, :], line, wide, slots)
        return carry

    lax.fori_loop(0, side, fill, 0)
    d = d_grouped[0 : side * line].astype(BF16)
    ids = [lax.broadcasted_iota(jnp.int32, (width, width), b) // group_width for b in range(2)]
    same = ids[0] == ids[1]
    for t in range(9):
        a, b = divmod(t, 3)
        starts = [(i + a) * wide + b * slots for i in range(side)]
        x = jnp.concatenate([pad[o : o + line].astype(BF16) for o in starts], axis=0)
        dense = jnp.where(same, dot_tn(x, d), 0.0)
        picked = jnp.sum(dense.reshape(width // group_width, group_width, width), axis=0)
        out[t * group_width : (t + 1) * group_width] = picked.astype(BF16)
    used = 9 * group_width
    out[used:] = jnp.zeros((out.shape[0] - used, width), BF16)


def reduce_grad_kernel(halves, dims, d_red, group_part, *refs):
    *feats, out = refs
    share = feats[0].shape[1]
    me = dims[2]
    half = d_red.shape[0] // halves
    for k in range(2):
        rows = pl.ds(pl.multiple_of((me ^ k) * share, share), share)
        out[rows, :] = dot_tn(feats[k][...], d_red[...]).astype(BF16)
    far = feats[2:]
    for k in range(len(far) // halves):
        rows = pl.ds(pl.multiple_of((me ^ (k + 2)) * share, share), share)
        out[rows, :] = sum(
            dot_tn(far[k * halves + h][...], d_red[h * half : (h + 1) * half])
            for h in range(halves)
        ).astype(BF16)
    base = out.shape[0] - group_part.shape[0]
    out[base:] = group_part[...]


def features_grad_kernel(part, *refs):
    *ins, out = refs
    k = len(ins) // 2
    ds, ws = ins[:k], ins[k:]

    def body(o, n):
        rows = pl.ds(o, n)
        out[rows, :] = part[rows, :] + sum(dot_nt(d[rows, :], w[...]) for d, w in zip(ds, ws))

    chunks(out.shape[0], body)


def call(kernel, outs, ins, scratch=(), flops=0, name=None, smem=False):
    moved = sum(x.size * x.dtype.itemsize for x in ins)
    moved += sum(int(o.size) * o.dtype.itemsize for o in outs)
    specs = [VM] * len(ins)
    if smem:
        specs[0] = SM
    got = pl.pallas_call(
        kernel,
        out_shape=list(outs),
        in_specs=specs,
        out_specs=[VM] * len(outs),
        scratch_shapes=list(scratch),
        compiler_params=pltpu.CompilerParams(vmem_limit_bytes=32 << 20),
        cost_estimate=pl.CostEstimate(flops=flops, bytes_accessed=moved, transcendentals=0),
        name=name,
    )(*ins)
    return got[0] if len(outs) == 1 else got


def swap(v, axis, size, k):
    return lax.ppermute(v, axis, [(i, i ^ k) for i in range(size)])


def batch_sum(spread):
    return lax.all_to_all(spread, "batch", 0, 0)


def gather_chan(v, size):
    held = {0: v}
    bit = size // 2
    while bit:
        held.update({k | bit: swap(b, "chan", size, bit) for k, b in list(held.items())})
        bit //= 2
    return [held[k] for k in range(size)]


def scatter_chan(parts, size):
    def terms(k, below):
        got, bit = [parts[k]], 1
        while bit < below:
            inner = terms(k | bit, bit)
            total = sum(t.astype(F32) for t in inner) if len(inner) > 1 else inner[0]
            got.append(swap(total.astype(BF16), "chan", size, bit))
            bit *= 2
        return got

    return terms(0, size)


def reduce_batch(v, size, axis):
    me = lax.axis_index("batch")
    bit = 1
    while bit < size:
        half = v.shape[axis] // 2
        mine = (me // bit) % 2
        keep = lax.dynamic_slice_in_dim(v, mine * half, half, axis)
        send = lax.dynamic_slice_in_dim(v, (1 - mine) * half, half, axis)
        v = (keep.astype(F32) + swap(send, "batch", size, bit).astype(F32)).astype(BF16)
        bit *= 2
    return v


def spread_batch(v, size, axis):
    me = lax.axis_index("batch")
    bit = size // 2
    while bit:
        other = swap(v, "batch", size, bit)
        mine = (me // bit) % 2
        v = jnp.where(
            mine == 0, jnp.concatenate([v, other], axis), jnp.concatenate([other, v], axis)
        )
        bit //= 2
    return v


def dense_taps(w_group, width, group_width):
    taps = w_group.reshape(9, group_width, width)
    tiled = jnp.tile(taps, (1, width // group_width, 1))
    rows = lax.broadcasted_iota(jnp.int32, (width, width), 0) // group_width
    cols = lax.broadcasted_iota(jnp.int32, (width, width), 1) // group_width
    return jnp.where((rows == cols)[None], tiled, jnp.zeros_like(tiled))


def shards(n_batch, n_chan, *args):
    (features, w_reduce, gain_one, shift_one, w_group, gain_two, shift_two, w_expand,
     gain_three, shift_three, cotangent, resolution, crop_count) = args
    slots, side, _, share = features.shape
    width = w_reduce.shape[1]
    group_width = w_group.shape[2]
    rows = slots * side * side
    padded = -(-rows // 32) * 32
    half = padded // 2
    halves = 2
    line, wide = side * slots, (side + 2) * slots
    me = lax.axis_index("chan")
    others = range(n_chan)
    shape = jax.ShapeDtypeStruct
    acc = lambda n, c: pltpu.VMEM((n, 8, c), F32)
    tall = pltpu.VMEM(((side + 2) * wide, width), F32)
    mm = 2 * padded * share * width

    feats = features.transpose(1, 2, 0, 3).reshape(rows, share)
    ends = ((0, padded - rows), (0, 0))
    pieces = [feats[:half], jnp.pad(feats[half:], ends)]
    moved = [gather_far(p, n_chan) for p in pieces]
    own = jnp.pad(feats, ends)
    beside = swap(own, "chan", n_chan, 1)
    far = [moved[h][k] for k in others if k > 1 for h in range(halves)]

    dims = jnp.stack([resolution[0], crop_count[0], me.astype(jnp.int32)])
    row = lax.broadcasted_iota(jnp.int32, (padded, LANES), 0)
    crop, j, i = row % slots, (row // slots) % side, row // line
    live = ((crop < crop_count[0]) & (i < resolution[0]) & (j < resolution[0])).astype(F32)
    cot = lax.dynamic_slice_in_dim(
        cotangent.transpose(1, 2, 0, 3).reshape(rows, -1), me * share, share, 1
    )
    cot = jnp.pad(cot, ends)
    taps = dense_taps(w_group, width, group_width)
    taps_back = taps.transpose(0, 2, 1)
    line_of = lambda v: v.reshape(1, -1)
    gain_one, shift_one, gain_two, shift_two = map(
        line_of, (gain_one, shift_one, gain_two, shift_two)
    )
    gain_c = line_of(lax.dynamic_slice_in_dim(gain_three, me * share, share))
    shift_c = line_of(lax.dynamic_slice_in_dim(shift_three, me * share, share))

    part = call(
        near_kernel, [shape((padded, width), F32)], [dims, own, beside, w_reduce],
        flops=2 * mm, name="near", smem=True,
    )
    z, spread = call(
        functools.partial(far_kernel, halves),
        [shape((padded, width), F32), shape((n_batch, 3, width), F32)],
        [dims, live, part, *far, w_reduce], [acc(3, width)],
        flops=(n_chan - 2) * mm, name="far", smem=True,
    )
    got_one = batch_sum(spread)

    w_red_blocks = w_reduce.reshape(n_chan, share, width)
    w_exp_blocks = w_expand.reshape(width, n_chan, share)
    pick_red = lambda k: lax.dynamic_index_in_dim(w_red_blocks, me ^ k, 0, keepdims=False)
    pick_exp = lambda k: lax.dynamic_index_in_dim(w_exp_blocks, me ^ k, 1, keepdims=False)
    w_cols = [pick_exp(0)] + [swap(pick_exp(k), "chan", n_chan, k) for k in others if k]
    w_rows = [pick_red(0)] + [swap(pick_red(k), "chan", n_chan, k) for k in others if k]

    hid, grouped, spread = call(
        functools.partial(conv_kernel, side, slots),
        [shape((padded, width), F32)] * 2 + [shape((n_batch, 2, width), F32)],
        [live, z, got_one, gain_one, shift_one, taps], [tall, acc(2, width)],
        flops=18 * padded * width * width, name="conv",
    )
    got_two = batch_sum(spread)
    hidden_two = call(
        hidden_kernel, [shape((padded, width), BF16)],
        [live, grouped, got_one, got_two, gain_two, shift_two], flops=mm, name="hidden",
    )
    hidden_all = gather_chan(hidden_two, n_chan)
    slope_two = call(
        slope_kernel, [shape((padded, width), F32)],
        [live, grouped, got_one, got_two, gain_two, shift_two], flops=mm, name="slope_two",
    )
    slope_one = call(
        slope_kernel, [shape((padded, width), F32)],
        [live, z, got_one, got_one, gain_one, shift_one], flops=mm, name="slope_one",
    )
    part = call(
        expand_near_kernel, [shape((padded, share), F32)], [*hidden_all[:2], *w_cols[:2]],
        flops=2 * mm, name="expand_near",
    )
    expanded, spread = call(
        expand_far_kernel, [shape((padded, share), F32), shape((n_batch, 2, share), F32)],
        [live, part, *hidden_all[2:], *w_cols[2:]], [acc(2, share)],
        flops=(n_chan - 2) * mm, name="expand_far",
    )
    got_three = batch_sum(spread)
    d_pre, spread = call(
        third_kernel, [shape((padded, share), F32), shape((n_batch, 2, share), F32)],
        [live, expanded, got_one, got_three, gain_c, shift_c, own, cot], [acc(2, share)],
        flops=4 * mm, name="third",
    )
    totals_three = batch_sum(spread)
    block_out = call(
        block_kernel, [shape((rows, share), BF16)],
        [live, expanded, got_one, got_three, gain_c, shift_c, own], flops=2 * mm, name="block",
    )

    odd = [k for k in reversed(others) if k % 2]
    even = [k for k in reversed(others) if k % 2 == 0]
    d_expanded, *sent = call(
        d_expanded_kernel,
        [shape((padded, share), BF16)] + [shape((padded, width), BF16)] * len(odd),
        [live, expanded, d_pre, got_one, got_three, totals_three, gain_c]
        + [w_cols[k] for k in odd],
        flops=(1 + len(odd)) * mm, name="d_expanded",
    )
    kept = call(
        back_expand_kernel, [shape((padded, width), F32)] * len(even),
        [d_expanded] + [w_cols[k] for k in even], flops=len(even) * mm, name="back_expand",
    )
    parts = dict(zip(odd, sent)) | dict(zip(even, kept))
    terms = scatter_chan(parts, n_chan)
    expand_part = call(
        expand_grad_kernel, [shape((n_chan, width, share), BF16)], [d_expanded, *hidden_all],
        flops=n_chan * mm, name="expand_grad",
    )
    d_two, spread = call(
        d_two_kernel, [shape((padded, width), F32), shape((n_batch, 2, width), F32)],
        [slope_two, grouped, got_one, got_two, *terms], [acc(2, width)], flops=mm, name="d_two",
    )
    totals_two = batch_sum(spread)
    d_grouped, d_one, spread = call(
        functools.partial(conv_back_kernel, side, slots),
        [shape((padded, width), F32)] * 2 + [shape((n_batch, 2, width), F32)],
        [live, d_two, grouped, got_two, totals_two, gain_two, slope_one, z, got_one, taps_back],
        [tall, acc(2, width)], flops=18 * padded * width * width, name="conv_back",
    )
    totals_one = batch_sum(spread)
    group_rows = -(-9 * group_width // 128) * 128
    group_part = call(
        functools.partial(group_grad_kernel, side, slots, group_width),
        [shape((group_rows, width), BF16)], [hid, d_grouped], [tall],
        flops=18 * padded * width * width, name="group_grad",
    )
    d_reduced = call(
        d_reduced_kernel, [shape((padded, width), BF16)],
        [live, d_one, z, got_one, totals_one, gain_one], flops=mm, name="d_reduced",
    )
    d_red_all = gather_chan(d_reduced, n_chan)
    tail = call(
        functools.partial(reduce_grad_kernel, halves),
        [shape((n_chan * share + group_rows, width), BF16)],
        [dims, d_reduced, group_part, own, beside, *far],
        flops=n_chan * mm, name="reduce_grad", smem=True,
    )
    part = call(
        features_grad_kernel, [shape((padded, share), F32)],
        [d_pre, *d_red_all[:2], *w_rows[:2]], flops=2 * mm, name="input_near",
    )
    features_grad = call(
        features_grad_kernel, [shape((rows, share), F32)],
        [part, *d_red_all[2:], *w_rows[2:]], flops=(n_chan - 2) * mm, name="input_far",
    )

    mine = reduce_batch(expand_part, n_batch, 1)
    cols = [mine[0]] + [swap(mine[k], "chan", n_chan, k) for k in others if k]
    stacked = jnp.stack(cols)
    cols = [lax.dynamic_index_in_dim(stacked, me ^ k, 0, keepdims=False) for k in others]
    expand_grad = spread_batch(jnp.concatenate(cols, axis=1), n_batch, 0).astype(F32)

    tail = spread_batch(reduce_batch(tail, n_batch, 0), n_batch, 0)
    reduce_grad = tail[: n_chan * share].astype(F32)
    group_grad = tail[n_chan * share : n_chan * share + 9 * group_width].astype(F32)

    total = lambda v: jnp.sum(v, axis=0)
    totals_one, totals_two, totals_three = map(total, (totals_one, totals_two, totals_three))
    shaped = lambda v: v.reshape(side, side, slots, share).transpose(2, 0, 1, 3)
    return (
        shaped(block_out),
        shaped(features_grad),
        reduce_grad,
        totals_one[1],
        totals_one[0],
        group_grad.reshape(3, 3, group_width, width),
        totals_two[1],
        totals_two[0],
        expand_grad,
        totals_three[1],
        totals_three[0],
    )


def gather_far(v, size):
    held = {0: v}
    bit = size // 2
    while bit > 1:
        held.update({k | bit: swap(b, "chan", size, bit) for k, b in list(held.items())})
        bit //= 2
    far = {k: b for k, b in held.items() if k}
    far.update({k | 1: swap(b, "chan", size, 1) for k, b in list(far.items())})
    return far


def solution(mesh):
    in_specs = (
        P("batch", None, None, "chan"),
        P(None, "chan"),
        P("chan"),
        P("chan"),
        P(None, None, None, "chan"),
        P("chan"),
        P("chan"),
        P("chan", None),
        P(),
        P(),
        P("batch", None, None, None),
        P("batch"),
        P("batch"),
    )
    out_specs = (
        P("batch", None, None, "chan"),
        P("batch", None, None, "chan"),
        P(None, "chan"),
        P("chan"),
        P("chan"),
        P(None, None, None, "chan"),
        P("chan"),
        P("chan"),
        P("chan", None),
        P("chan"),
        P("chan"),
    )
    n_batch, n_chan = mesh.shape["batch"], mesh.shape["chan"]

    def run(*args):
        return shards(n_batch, n_chan, *args)

    return jax.shard_map(run, mesh=mesh, in_specs=in_specs, out_specs=out_specs, check_vma=False)
```

profile of v0, /device:TPU:0, one launch (start us, length us, event | category | flops | bytes accessed | tf_op | source)
XLA Modules:
  0.0 359.5 jit_solution(6228831054408207395)
XLA Ops:
  11.9 18.1 %collective-permute-done.2.refs_1_.refs_3_ = bf16[976,512]{1,0:T(8,128)(2,1)} collective-permute-done((bf16[976,512]{1,0:T(8,128)(2,1)}, bf16[976,512]{1,0:T(8,128)(2,1)}, u32[]{:S(2)}, u32[]{:S(2)}) %collective-permute-start.2) | collective-permute-done | bytes 999456 | tf_op jit(solution)/shard_map/ppermute | solution.py:443
  30.1 21.1 %collective-permute-done.1.refs_0_.refs_2_ = bf16[976,512]{1,0:T(8,128)(2,1)} collective-permute-done((bf16[976,512]{1,0:T(8,128)(2,1)S(1)}, bf16[976,512]{1,0:T(8,128)(2,1)}, u32[]{:S(2)}, u32[]{:S(2)}) %collective-permute-start.1) | collective-permute-done | bytes 999456 | tf_op jit(solution)/shard_map/ppermute | solution.py:443
  55.0 4.1 %near.1.part = f32[1952,256]{1,0:T(8,128)S(1)} custom-call(s32[3]{0:T(128)S(1)} %pad_add_fusion.dims, bf16[1952,512]{1,0:T(8,128)(2,1)S(1)} %pad.11.refs_0_.feats, bf16[1952,512]{1,0:T(8,128)(2,1)} %collective-permute-done.refs_1_, bf16[2048,256]{1,0:T(8,128)(2,1)S(1)} %copy-done.14), custom_call_target="tpu_custom_call" | custom-call | flops 1023410176 | bytes 7045132 | tf_op jit(solution)/shard_map/near/pallas_call | solution.py:429
  59.2 5.3 %far.1 = (f32[1952,256]{1,0:T(8,128)S(1)}, f32[8,3,256]{2,1,0:T(4,128)}) custom-call(s32[3]{0:T(128)S(1)} %pad_add_fusion.dims, f32[1952,128]{1,0:T(8,128)S(1)} %fusion.6.live, f32[1952,256]{1,0:T(8,128)S(1)} %near.1.part, bf16[976,512]{1,0:T(8,128)(2,1)} %collective-permute-done.1.refs_0_.refs_2_, bf16[976,512]{1,0:T(8,128)(2,1)} %collective-permute-done.2.refs_1_.refs_3_, ...), custom_call_target="tpu_custom_call" | custom-call | flops 1023410176 | bytes 10067980 | tf_op jit(solution)/shard_map/far/pallas_call | solution.py:429
  65.8 6.0 %all-to-all-start = ((f32[8,3,256]{2,1,0:T(4,128)}), f32[8,3,256]{2,1,0:T(4,128)S(1)}, u32[]{:S(2)}, u32[]{:S(2)}) async-start(f32[8,3,256]{2,1,0:T(4,128)} %get-tuple-element.31), calls=%async_computation | async-start | bytes 65536 | tf_op jit(solution)/shard_map/all_to_all | solution.py:447
  81.3 5.4 %conv.1 = (f32[1952,256]{1,0:T(8,128)S(1)}, f32[1952,256]{1,0:T(8,128)S(1)}, f32[8,2,256]{2,1,0:T(2,128)S(1)}) custom-call(f32[1952,128]{1,0:T(8,128)S(1)} %fusion.6.live, f32[1952,256]{1,0:T(8,128)S(1)} %copy-done.8, f32[8,3,256]{2,1,0:T(4,128)S(1)} %all-to-all-done.got.counts, f32[1,256]{1,0:T(1,128)S(1)} %bitcast.86, f32[1,256]{1,0:T(1,128)S(1)} %bitcast.89, ...), custom_call_target="tpu_custom_call" | custom-call | flops 2302672896 | bytes 8218624 | tf_op jit(solution)/shard_map/conv/pallas_call | solution.py:429
  88.0 10.5 %all_to_all.30.got.got_two = f32[8,2,256]{2,1,0:T(2,128)S(1)} all-to-all(f32[8,2,256]{2,1,0:T(2,128)S(1)} %get-tuple-element.33), channel_id=1, replica_groups=mesh['batch'=8,'chan'=4] {'batch'}, dimensions={0} | all-to-all | bytes 32768 | tf_op jit(solution)/shard_map/all_to_all | solution.py:447
  101.9 21.3 %collective-permute-done.7.refs_0_.refs_2_ = bf16[1952,256]{1,0:T(8,128)(2,1)} collective-permute-done((bf16[1952,256]{1,0:T(8,128)(2,1)}, bf16[1952,256]{1,0:T(8,128)(2,1)}, u32[]{:S(2)}, u32[]{:S(2)}) %collective-permute-start.7) | collective-permute-done | bytes 999456 | tf_op jit(solution)/shard_map/ppermute | solution.py:443
  125.9 4.7 %constant_dynamic-slice_fusion.7 = (bf16[256,1,512]{2,1,0:T(2,128)(2,1)S(1)}, bf16[256,1,512]{2,1,0:T(2,128)(2,1)S(1)}, bf16[256,1,512]{2,1,0:T(2,128)(2,1)S(1)}, bf16[256,1,512]{2,1,0:T(2,128)(2,1)S(1)}) fusion(bf16[256,4,512]{2,1,0:T(4,128)(2,1)} %reshape.151, s32[]{:T(128)S(6)} %select_n.210, s32[]{:T(128)S(6)} %select_n.209, s32[]{:T(128)S(6)} %select_n.208, ...), kind=kLoop, calls=%fused_computation.65 | loop fusion | bytes 2097168 | tf_op jit(solution)/shard_map/jit(dynamic_index_in_dim)/dynamic_slice | solution.py:564
  135.0 3.8 %expand_near.1.part = f32[1952,512]{1,0:T(8,128)S(1)} custom-call(bf16[1952,256]{1,0:T(8,128)(2,1)} %hidden.1.refs_0_, bf16[1952,256]{1,0:T(8,128)(2,1)} %collective-permute-done.5.refs_1_, bf16[256,512]{1,0:T(8,128)(2,1)S(1)} %bitcast.74, bf16[256,512]{1,0:T(8,128)(2,1)S(1)} %collective-permute-done.6.refs_3_.refs_1_), custom_call_target="tpu_custom_call" | custom-call | flops 1023410176 | bytes 6520832 | tf_op jit(solution)/shard_map/expand_near/pallas_call | solution.py:429
  141.3 5.8 %collective-permute-done.9.refs_2_.refs_0_ = bf16[256,512]{1,0:T(8,128)(2,1)} collective-permute-done((bf16[256,512]{1,0:T(8,128)(2,1)}, bf16[256,512]{1,0:T(8,128)(2,1)}, u32[]{:S(2)}, u32[]{:S(2)}) %collective-permute-start.9) | collective-permute-done | bytes 262176 | tf_op jit(solution)/shard_map/ppermute | solution.py:443
  147.1 4.2 %expand_far.1 = (f32[1952,512]{1,0:T(8,128)S(1)}, f32[8,2,512]{2,1,0:T(2,128)S(1)}) custom-call(f32[1952,128]{1,0:T(8,128)S(1)} %fusion.6.live, f32[1952,512]{1,0:T(8,128)S(1)} %expand_near.1.part, bf16[1952,256]{1,0:T(8,128)(2,1)} %collective-permute-done.7.refs_0_.refs_2_, bf16[1952,256]{1,0:T(8,128)(2,1)} %collective-permute-done.8.refs_1_.refs_3_, ...), custom_call_target="tpu_custom_call" | custom-call | flops 1023410176 | bytes 11550720 | tf_op jit(solution)/shard_map/expand_far/pallas_call | solution.py:429
  153.9 4.0 %all-to-all-start.2 = ((f32[8,2,512]{2,1,0:T(2,128)}), f32[8,2,512]{2,1,0:T(2,128)}, u32[]{:S(2)}, u32[]{:S(2)}) async-start(f32[8,2,512]{2,1,0:T(2,128)} %copy-done.37), calls=%async_computation.2 | async-start | bytes 65536 | tf_op jit(solution)/shard_map/all_to_all | solution.py:447
  169.6 4.6 %third.1 = (f32[1952,512]{1,0:T(8,128)S(1)}, f32[8,2,512]{2,1,0:T(2,128)S(1)}) custom-call(f32[1952,128]{1,0:T(8,128)S(1)} %fusion.6.live, f32[1952,512]{1,0:T(8,128)S(1)} %copy-done.1, f32[8,3,256]{2,1,0:T(4,128)S(1)} %all-to-all-done.got.counts, f32[8,2,512]{2,1,0:T(2,128)} %all-to-all-done.2.got, f32[1,512]{1,0:T(1,128)S(1)} %bitcast.76, ...), custom_call_target="tpu_custom_call" | custom-call | flops 2046820352 | bytes 13086720 | tf_op jit(solution)/shard_map/third/pallas_call | solution.py:429
  174.2 11.5 %all_to_all.31.totals = f32[8,2,512]{2,1,0:T(2,128)S(1)} all-to-all(f32[8,2,512]{2,1,0:T(2,128)S(1)} %get-tuple-element.37), channel_id=1, replica_groups=mesh['batch'=8,'chan'=4] {'batch'}, dimensions={0} | all-to-all | bytes 65536 | tf_op jit(solution)/shard_map/all_to_all | solution.py:447
  185.7 4.8 %d_expanded.1 = (bf16[1952,512]{1,0:T(8,128)(2,1)S(1)}, bf16[1952,256]{1,0:T(8,128)(2,1)}, bf16[1952,256]{1,0:T(8,128)(2,1)S(1)}) custom-call(f32[1952,128]{1,0:T(8,128)S(1)} %fusion.6.live, f32[1952,512]{1,0:T(8,128)S(1)} %copy-done.2, f32[1952,512]{1,0:T(8,128)S(1)} %get-tuple-element.36.d_pre.part, f32[8,3,256]{2,1,0:T(4,128)S(1)} %all-to-all-done.got.counts, ...), custom_call_target="tpu_custom_call" | custom-call | flops 1535115264 | bytes 13608960 | tf_op jit(solution)/shard_map/d_expanded/pallas_call | solution.py:429
  194.3 4.6 %expand_grad.1 = bf16[4,256,512]{2,1,0:T(8,128)(2,1)S(1)} custom-call(bf16[1952,512]{1,0:T(8,128)(2,1)S(1)} %copy-done.53, bf16[1952,256]{1,0:T(8,128)(2,1)} %hidden.1.refs_0_, bf16[1952,256]{1,0:T(8,128)(2,1)} %collective-permute-done.5.refs_1_, bf16[1952,256]{1,0:T(8,128)(2,1)} %collective-permute-done.7.refs_0_.refs_2_, ...), custom_call_target="tpu_custom_call" | custom-call | flops 2046820352 | bytes 7045120 | tf_op jit(solution)/shard_map/expand_grad/pallas_call | solution.py:429
  199.8 3.6 back_expand.1
  206.4 7.0 %collective-permute-done.26 = bf16[4,128,512]{2,1,0:T(8,128)(2,1)S(1)} collective-permute-done((bf16[4,128,512]{2,1,0:T(8,128)(2,1)S(1)}, bf16[4,128,512]{2,1,0:T(8,128)(2,1)S(1)}, u32[]{:S(2)}, u32[]{:S(2)}) %collective-permute-start.26) | collective-permute-done | bytes 524320 | tf_op jit(solution)/shard_map/ppermute | solution.py:443
  215.2 6.4 %collective-permute-done.27 = bf16[4,64,512]{2,1,0:T(8,128)(2,1)S(1)} collective-permute-done((bf16[4,64,512]{2,1,0:T(8,128)(2,1)S(1)}, bf16[4,64,512]{2,1,0:T(8,128)(2,1)S(1)}, u32[]{:S(2)}, u32[]{:S(2)}) %collective-permute-start.27) | collective-permute-done | bytes 262176 | tf_op jit(solution)/shard_map/ppermute | solution.py:443
  231.9 3.3 all-to-all-start.4
  236.2 5.6 %all-to-all-done.4.totals = f32[8,2,256]{2,1,0:T(2,128)S(1)} async-done(((f32[8,2,256]{2,1,0:T(2,128)}), f32[8,2,256]{2,1,0:T(2,128)S(1)}, u32[]{:S(2)}, u32[]{:S(2)}) %all-to-all-start.4) | async-done | bytes 16416 | tf_op jit(solution)/shard_map/all_to_all | solution.py:447
  249.2 5.9 %conv_back.1 = (f32[1952,256]{1,0:T(8,128)S(1)}, f32[1952,256]{1,0:T(8,128)S(1)}, f32[8,2,256]{2,1,0:T(2,128)}) custom-call(f32[1952,128]{1,0:T(8,128)S(1)} %fusion.6.live, f32[1952,256]{1,0:T(8,128)S(1)} %copy-done.29, f32[1952,256]{1,0:T(8,128)S(1)} %copy-done.6, f32[8,2,256]{2,1,0:T(2,128)S(1)} %copy-done.34, f32[8,2,256]{2,1,0:T(2,128)S(1)} %all-to-all-done.4.totals, ...), custom_call_target="tpu_custom_call" | custom-call | flops 2302672896 | bytes 14246912 | tf_op jit(solution)/shard_map/conv_back/pallas_call | solution.py:429
  257.7 3.3 all-to-all-start.5
  272.2 4.9 %reduce_grad.1 = bf16[2432,256]{1,0:T(8,128)(2,1)S(1)} custom-call(s32[3]{0:T(128)S(1)} %copy-done.45, bf16[1952,256]{1,0:T(8,128)(2,1)S(1)} %d_reduced.1.refs_0_.d_red, bf16[384,256]{1,0:T(8,128)(2,1)S(1)} %group_grad.1.group_part, bf16[1952,512]{1,0:T(8,128)(2,1)S(1)} %pad.11.refs_0_.feats, bf16[1952,512]{1,0:T(8,128)(2,1)} %collective-permute-done.refs_1_, ...), custom_call_target="tpu_custom_call" | custom-call | flops 2046820352 | bytes 10436620 | tf_op jit(solution)/shard_map/reduce_grad/pallas_call | solution.py:429
  287.3 5.2 %collective-permute-done.20 = bf16[1216,256]{1,0:T(8,128)(2,1)} collective-permute-done((bf16[1216,256]{1,0:T(8,128)(2,1)}, bf16[1216,256]{1,0:T(8,128)(2,1)}, u32[]{:S(2)}, u32[]{:S(2)}) %collective-permute-start.20) | collective-permute-done | bytes 622624 | tf_op jit(solution)/shard_map/ppermute | solution.py:443
  300.3 6.5 %collective-permute-done.21 = bf16[608,256]{1,0:T(8,128)(2,1)} collective-permute-done((bf16[608,256]{1,0:T(8,128)(2,1)}, bf16[608,256]{1,0:T(8,128)(2,1)}, u32[]{:S(2)}, u32[]{:S(2)}) %collective-permute-start.21) | collective-permute-done | bytes 311328 | tf_op jit(solution)/shard_map/ppermute | solution.py:443
  312.3 6.2 %collective-permute-done.22 = bf16[304,256]{1,0:T(8,128)(2,1)S(1)} collective-permute-done((bf16[304,256]{1,0:T(8,128)(2,1)S(1)}, bf16[304,256]{1,0:T(8,128)(2,1)S(1)}, u32[]{:S(2)}, u32[]{:S(2)}) %collective-permute-start.22) | collective-permute-done | bytes 155680 | tf_op jit(solution)/shard_map/ppermute | solution.py:443
  321.7 4.2 %block.1 = bf16[1944,512]{1,0:T(8,128)(2,1)} custom-call(f32[1952,128]{1,0:T(8,128)S(1)} %fusion.6.live, f32[1952,512]{1,0:T(8,128)S(1)} %copy-done.3, f32[8,3,256]{2,1,0:T(4,128)S(1)} %all-to-all-done.got.counts, f32[8,2,512]{2,1,0:T(2,128)} %all-to-all-done.2.got, f32[1,512]{1,0:T(1,128)S(1)} %bitcast.78, f32[1,512]{1,0:T(1,128)S(1)} %bitcast.80, ...), custom_call_target="tpu_custom_call" | custom-call | flops 1023410176 | bytes 9048064 | tf_op jit(solution)/shard_map/block/pallas_call | solution.py:429
  332.8 3.2 fusion
  343.6 3.6 input_near.1.part
  349.3 6.1 %input_far.1 = f32[1944,512]{1,0:T(8,128)} custom-call(f32[1952,512]{1,0:T(8,128)S(1)} %input_near.1.part, bf16[1952,256]{1,0:T(8,128)(2,1)} %collective-permute-done.16.refs_0_, bf16[1952,256]{1,0:T(8,128)(2,1)} %collective-permute-done.17.refs_1_, bf16[512,256]{1,0:T(8,128)(2,1)S(1)} %collective-permute-done.18.refs_2_, ...), custom_call_target="tpu_custom_call" | custom-call | flops 1023410176 | bytes 10502144 | tf_op jit(solution)/shard_map/input_far/pallas_call | solution.py:429
  (264 shorter events, 142.2 us)
Async XLA Ops:
  2.5 51.3 %collective-permute-start = (bf16[1952,512]{1,0:T(8,128)(2,1)S(1)}, bf16[1952,512]{1,0:T(8,128)(2,1)}, u32[]{:S(2)}, u32[]{:S(2)}) collective-permute-start(bf16[1952,512]{1,0:T(8,128)(2,1)S(1)} %pad.11.refs_0_.feats), channel_id=1, source_target_pairs={{0,1},{1,0},{2,3},{3,2},{4,5},{5,4},{6,7},{7,6},{8,9},{9,8},{10,11... | collective-permute-start | bytes 5996552 | tf_op jit(solution)/shard_map/ppermute | solution.py:443
  4.1 25.9 %collective-permute-start.2 = (bf16[976,512]{1,0:T(8,128)(2,1)}, bf16[976,512]{1,0:T(8,128)(2,1)}, u32[]{:S(2)}, u32[]{:S(2)}) collective-permute-start(bf16[976,512]{1,0:T(8,128)(2,1)} %pad.12), channel_id=1, source_target_pairs={{0,2},{1,3},{2,0},{3,1},{4,6},{5,7},{6,4},{7,5},{8,10},{9,11},{10,... | collective-permute-start | bytes 2998280 | tf_op jit(solution)/shard_map/ppermute | solution.py:443
  6.9 44.2 %collective-permute-start.1 = (bf16[976,512]{1,0:T(8,128)(2,1)S(1)}, bf16[976,512]{1,0:T(8,128)(2,1)}, u32[]{:S(2)}, u32[]{:S(2)}) collective-permute-start(bf16[976,512]{1,0:T(8,128)(2,1)S(1)} %slice.56), channel_id=1, source_target_pairs={{0,2},{1,3},{2,0},{3,1},{4,6},{5,7},{6,4},{7,5},{8,10},{9,11},{10,... | collective-permute-start | bytes 2998280 | tf_op jit(solution)/shard_map/ppermute | solution.py:443
  30.0 29.1 %collective-permute-start.4 = (bf16[976,512]{1,0:T(8,128)(2,1)}, bf16[976,512]{1,0:T(8,128)(2,1)S(1)}, u32[]{:S(2)}, u32[]{:S(2)}) collective-permute-start(bf16[976,512]{1,0:T(8,128)(2,1)} %collective-permute-done.2.refs_1_.refs_3_), channel_id=1, source_target_pairs={{0,1},{1,0},{2,3},{3,2},{4,5},{5,4},{6,7},{7,6},{8,9},{9,8},{10,11... | collective-permute-start | bytes 2998280 | tf_op jit(solution)/shard_map/ppermute | solution.py:443
  65.8 12.7 %all-to-all-start = ((f32[8,3,256]{2,1,0:T(4,128)}), f32[8,3,256]{2,1,0:T(4,128)S(1)}, u32[]{:S(2)}, u32[]{:S(2)}) async-start(f32[8,3,256]{2,1,0:T(4,128)} %get-tuple-element.31), calls=%async_computation | async-start | bytes 65536 | tf_op jit(solution)/shard_map/all_to_all | solution.py:447
  100.4 22.8 %collective-permute-start.7 = (bf16[1952,256]{1,0:T(8,128)(2,1)}, bf16[1952,256]{1,0:T(8,128)(2,1)}, u32[]{:S(2)}, u32[]{:S(2)}) collective-permute-start(bf16[1952,256]{1,0:T(8,128)(2,1)} %hidden.1.refs_0_), channel_id=1, source_target_pairs={{0,2},{1,3},{2,0},{3,1},{4,6},{5,7},{6,4},{7,5},{8,10},{9,11},{10,... | collective-permute-start | bytes 2998280 | tf_op jit(solution)/shard_map/ppermute | solution.py:443
  101.9 33.0 %collective-permute-start.5 = (bf16[1952,256]{1,0:T(8,128)(2,1)}, bf16[1952,256]{1,0:T(8,128)(2,1)}, u32[]{:S(2)}, u32[]{:S(2)}) collective-permute-start(bf16[1952,256]{1,0:T(8,128)(2,1)} %hidden.1.refs_0_), channel_id=1, source_target_pairs={{0,1},{1,0},{2,3},{3,2},{4,5},{5,4},{6,7},{7,6},{8,9},{9,8},{10,11... | collective-permute-start | bytes 2998280 | tf_op jit(solution)/shard_map/ppermute | solution.py:443
  123.2 23.8 %collective-permute-start.8 = (bf16[1952,256]{1,0:T(8,128)(2,1)}, bf16[1952,256]{1,0:T(8,128)(2,1)}, u32[]{:S(2)}, u32[]{:S(2)}) collective-permute-start(bf16[1952,256]{1,0:T(8,128)(2,1)} %collective-permute-done.7.refs_0_.refs_2_), channel_id=1, source_target_pairs={{0,1},{1,0},{2,3},{3,2},{4,5},{5,4},{6,7},{7,6},{8,9},{9,8},{10,11... | collective-permute-start | bytes 2998280 | tf_op jit(solution)/shard_map/ppermute | solution.py:443
  132.5 8.7 %collective-permute-start.10 = (bf16[256,512]{1,0:T(8,128)(2,1)}, bf16[256,512]{1,0:T(8,128)(2,1)}, u32[]{:S(2)}, u32[]{:S(2)}) collective-permute-start(bf16[256,512]{1,0:T(8,128)(2,1)} %bitcast.67), channel_id=1, source_target_pairs={{0,3},{1,2},{2,1},{3,0},{4,7},{5,6},{6,5},{7,4},{8,11},{9,10},{10,... | collective-permute-start | bytes 786440 | tf_op jit(solution)/shard_map/ppermute | solution.py:443
  134.4 12.7 %collective-permute-start.9 = (bf16[256,512]{1,0:T(8,128)(2,1)}, bf16[256,512]{1,0:T(8,128)(2,1)}, u32[]{:S(2)}, u32[]{:S(2)}) collective-permute-start(bf16[256,512]{1,0:T(8,128)(2,1)} %bitcast.68), channel_id=1, source_target_pairs={{0,2},{1,3},{2,0},{3,1},{4,6},{5,7},{6,4},{7,5},{8,10},{9,11},{10,... | collective-permute-start | bytes 786440 | tf_op jit(solution)/shard_map/ppermute | solution.py:443
  153.9 10.7 %all-to-all-start.2 = ((f32[8,2,512]{2,1,0:T(2,128)}), f32[8,2,512]{2,1,0:T(2,128)}, u32[]{:S(2)}, u32[]{:S(2)}) async-start(f32[8,2,512]{2,1,0:T(2,128)} %copy-done.37), calls=%async_computation.2 | async-start | bytes 65536 | tf_op jit(solution)/shard_map/all_to_all | solution.py:447
  192.7 10.6 %collective-permute-start.12 = (bf16[1952,256]{1,0:T(8,128)(2,1)}, bf16[1952,256]{1,0:T(8,128)(2,1)}, u32[]{:S(2)}, u32[]{:S(2)}) collective-permute-start(bf16[1952,256]{1,0:T(8,128)(2,1)} %get-tuple-element.42), channel_id=1, source_target_pairs={{0,1},{1,0},{2,3},{3,2},{4,5},{5,4},{6,7},{7,6},{8,9},{9,8},{10,11... | collective-permute-start | bytes 2998280 | tf_op jit(solution)/shard_map/ppermute | solution.py:443
  199.0 14.4 %collective-permute-start.26 = (bf16[4,128,512]{2,1,0:T(8,128)(2,1)S(1)}, bf16[4,128,512]{2,1,0:T(8,128)(2,1)S(1)}, u32[]{:S(2)}, u32[]{:S(2)}) collective-permute-start(bf16[4,128,512]{2,1,0:T(8,128)(2,1)S(1)} %constant_dynamic-slice_fusion.2), channel_id=1, source_target_pairs={{0,4},{4,0},{8,12},{12,8},{16,20},{20,16},{24,28},{28,24},{1,5},{5... | collective-permute-start | bytes 1572872 | tf_op jit(solution)/shard_map/ppermute | solution.py:443
  199.5 26.7 %collective-permute-start.11 = (bf16[1952,256]{1,0:T(8,128)(2,1)S(1)}, bf16[1952,256]{1,0:T(8,128)(2,1)S(1)}, u32[]{:S(2)}, u32[]{:S(2)}) collective-permute-start(bf16[1952,256]{1,0:T(8,128)(2,1)S(1)} %copy-done.58), channel_id=1, source_target_pairs={{0,1},{1,0},{2,3},{3,2},{4,5},{5,4},{6,7},{7,6},{8,9},{9,8},{10,11... | collective-permute-start | bytes 2998280 | tf_op jit(solution)/shard_map/ppermute | solution.py:443
  204.8 24.4 %collective-permute-start.13 = (bf16[1952,256]{1,0:T(8,128)(2,1)S(1)}, bf16[1952,256]{1,0:T(8,128)(2,1)S(1)}, u32[]{:S(2)}, u32[]{:S(2)}) collective-permute-start(bf16[1952,256]{1,0:T(8,128)(2,1)S(1)} %add_convert_fusion), channel_id=1, source_target_pairs={{0,2},{1,3},{2,0},{3,1},{4,6},{5,7},{6,4},{7,5},{8,10},{9,11},{10,... | collective-permute-start | bytes 2998280 | tf_op jit(solution)/shard_map/ppermute | solution.py:443
  221.8 13.5 %collective-permute-start.28 = (bf16[4,32,512]{2,1,0:T(8,128)(2,1)S(1)}, bf16[4,32,512]{2,1,0:T(8,128)(2,1)}, u32[]{:S(2)}, u32[]{:S(2)}) collective-permute-start(bf16[4,32,512]{2,1,0:T(8,128)(2,1)S(1)} %constant_dynamic-slice_fusion), channel_id=1, source_target_pairs={{0,16},{4,20},{8,24},{12,28},{16,0},{20,4},{24,8},{28,12},{1,17},{... | collective-permute-start | bytes 393224 | tf_op jit(solution)/shard_map/ppermute | solution.py:443
  231.9 9.9 %all-to-all-start.4 = ((f32[8,2,256]{2,1,0:T(2,128)}), f32[8,2,256]{2,1,0:T(2,128)S(1)}, u32[]{:S(2)}, u32[]{:S(2)}) async-start(f32[8,2,256]{2,1,0:T(2,128)} %get-tuple-element.44), calls=%async_computation.4 | async-start | bytes 32768 | tf_op jit(solution)/shard_map/all_to_all | solution.py:447
  257.7 9.9 %all-to-all-start.5 = ((f32[8,2,256]{2,1,0:T(2,128)}), f32[8,2,256]{2,1,0:T(2,128)S(1)}, u32[]{:S(2)}, u32[]{:S(2)}) async-start(f32[8,2,256]{2,1,0:T(2,128)} %get-tuple-element.46), calls=%async_computation.5 | async-start | bytes 32768 | tf_op jit(solution)/shard_map/all_to_all | solution.py:447
  278.3 14.2 %collective-permute-start.20 = (bf16[1216,256]{1,0:T(8,128)(2,1)}, bf16[1216,256]{1,0:T(8,128)(2,1)}, u32[]{:S(2)}, u32[]{:S(2)}) collective-permute-start(bf16[1216,256]{1,0:T(8,128)(2,1)} %constant_dynamic-slice_fusion.5), channel_id=1, source_target_pairs={{0,4},{4,0},{8,12},{12,8},{16,20},{20,16},{24,28},{28,24},{1,5},{5... | collective-permute-start | bytes 1867784 | tf_op jit(solution)/shard_map/ppermute | solution.py:443
  284.9 12.3 %collective-permute-start.32 = (bf16[32,2048]{1,0:T(8,128)(2,1)S(1)}, bf16[32,2048]{1,0:T(8,128)(2,1)}, u32[]{:S(2)}, u32[]{:S(2)}) collective-permute-start(bf16[32,2048]{1,0:T(8,128)(2,1)S(1)} %pad_maximum_fusion.1), channel_id=1, source_target_pairs={{0,16},{4,20},{8,24},{12,28},{16,0},{20,4},{24,8},{28,12},{1,17},{... | collective-permute-start | bytes 393224 | tf_op jit(solution)/shard_map/ppermute | solution.py:443
  295.5 11.2 %collective-permute-start.21 = (bf16[608,256]{1,0:T(8,128)(2,1)}, bf16[608,256]{1,0:T(8,128)(2,1)}, u32[]{:S(2)}, u32[]{:S(2)}) collective-permute-start(bf16[608,256]{1,0:T(8,128)(2,1)} %constant_dynamic-slice_fusion.4), channel_id=1, source_target_pairs={{0,8},{4,12},{8,0},{12,4},{16,24},{20,28},{24,16},{28,20},{1,9},{5... | collective-permute-start | bytes 933896 | tf_op jit(solution)/shard_map/ppermute | solution.py:443
  298.3 11.7 %collective-permute-start.33 = (bf16[64,2048]{1,0:T(8,128)(2,1)S(1)}, bf16[64,2048]{1,0:T(8,128)(2,1)S(1)}, u32[]{:S(2)}, u32[]{:S(2)}) collective-permute-start(bf16[64,2048]{1,0:T(8,128)(2,1)S(1)} %maximum_select_fusion.5), channel_id=1, source_target_pairs={{0,8},{4,12},{8,0},{12,4},{16,24},{20,28},{24,16},{28,20},{1,9},{5... | collective-permute-start | bytes 786440 | tf_op jit(solution)/shard_map/ppermute | solution.py:443
  298.7 34.0 %collective-permute-start.16 = (bf16[1952,256]{1,0:T(8,128)(2,1)}, bf16[1952,256]{1,0:T(8,128)(2,1)}, u32[]{:S(2)}, u32[]{:S(2)}) collective-permute-start(bf16[1952,256]{1,0:T(8,128)(2,1)} %copy-done.17), channel_id=1, source_target_pairs={{0,2},{1,3},{2,0},{3,1},{4,6},{5,7},{6,4},{7,5},{8,10},{9,11},{10,... | collective-permute-start | bytes 2998280 | tf_op jit(solution)/shard_map/ppermute | solution.py:443
  307.9 10.6 %collective-permute-start.22 = (bf16[304,256]{1,0:T(8,128)(2,1)S(1)}, bf16[304,256]{1,0:T(8,128)(2,1)S(1)}, u32[]{:S(2)}, u32[]{:S(2)}) collective-permute-start(bf16[304,256]{1,0:T(8,128)(2,1)S(1)} %constant_dynamic-slice_fusion.3), channel_id=1, source_target_pairs={{0,16},{4,20},{8,24},{12,28},{16,0},{20,4},{24,8},{28,12},{1,17},{... | collective-permute-start | bytes 466952 | tf_op jit(solution)/shard_map/ppermute | solution.py:443
  310.9 20.4 %collective-permute-start.34 = (bf16[128,2048]{1,0:T(8,128)(2,1)}, bf16[128,2048]{1,0:T(8,128)(2,1)}, u32[]{:S(2)}, u32[]{:S(2)}) collective-permute-start(bf16[128,2048]{1,0:T(8,128)(2,1)} %maximum_select_fusion.3), channel_id=1, source_target_pairs={{0,4},{4,0},{8,12},{12,8},{16,20},{20,16},{24,28},{28,24},{1,5},{5... | collective-permute-start | bytes 1572872 | tf_op jit(solution)/shard_map/ppermute | solution.py:443
  319.6 20.9 %collective-permute-start.15 = (bf16[512,256]{1,0:T(8,128)(2,1)}, bf16[512,256]{1,0:T(8,128)(2,1)}, u32[]{:S(2)}, u32[]{:S(2)}) collective-permute-start(bf16[512,256]{1,0:T(8,128)(2,1)} %get-tuple-element.51), channel_id=1, source_target_pairs={{0,1},{1,0},{2,3},{3,2},{4,5},{5,4},{6,7},{7,6},{8,9},{9,8},{10,11... | collective-permute-start | bytes 786440 | tf_op jit(solution)/shard_map/ppermute | solution.py:443
  325.9 15.5 %collective-permute-start.14 = (bf16[1952,256]{1,0:T(8,128)(2,1)}, bf16[1952,256]{1,0:T(8,128)(2,1)S(1)}, u32[]{:S(2)}, u32[]{:S(2)}) collective-permute-start(bf16[1952,256]{1,0:T(8,128)(2,1)} %copy-done.17), channel_id=1, source_target_pairs={{0,1},{1,0},{2,3},{3,2},{4,5},{5,4},{6,7},{7,6},{8,9},{9,8},{10,11... | collective-permute-start | bytes 2998280 | tf_op jit(solution)/shard_map/ppermute | solution.py:443
  327.6 10.6 %collective-permute-start.24 = (bf16[608,256]{1,0:T(8,128)(2,1)S(1)}, bf16[608,256]{1,0:T(8,128)(2,1)S(1)}, u32[]{:S(2)}, u32[]{:S(2)}) collective-permute-start(bf16[608,256]{1,0:T(8,128)(2,1)S(1)} %maximum_select_fusion.4), channel_id=1, source_target_pairs={{0,8},{4,12},{8,0},{12,4},{16,24},{20,28},{24,16},{28,20},{1,9},{5... | collective-permute-start | bytes 933896 | tf_op jit(solution)/shard_map/ppermute | solution.py:443
  331.2 15.9 %collective-permute-start.18 = (bf16[512,256]{1,0:T(8,128)(2,1)}, bf16[512,256]{1,0:T(8,128)(2,1)S(1)}, u32[]{:S(2)}, u32[]{:S(2)}) collective-permute-start(bf16[512,256]{1,0:T(8,128)(2,1)} %get-tuple-element.50), channel_id=1, source_target_pairs={{0,2},{1,3},{2,0},{3,1},{4,6},{5,7},{6,4},{7,5},{8,10},{9,11},{10,... | collective-permute-start | bytes 786440 | tf_op jit(solution)/shard_map/ppermute | solution.py:443
  332.8 16.5 %collective-permute-start.17 = (bf16[1952,256]{1,0:T(8,128)(2,1)}, bf16[1952,256]{1,0:T(8,128)(2,1)}, u32[]{:S(2)}, u32[]{:S(2)}) collective-permute-start(bf16[1952,256]{1,0:T(8,128)(2,1)} %collective-permute-done.16.refs_0_), channel_id=1, source_target_pairs={{0,1},{1,0},{2,3},{3,2},{4,5},{5,4},{6,7},{7,6},{8,9},{9,8},{10,11... | collective-permute-start | bytes 2998280 | tf_op jit(solution)/shard_map/ppermute | solution.py:443
  339.2 16.1 %collective-permute-start.25 = (bf16[1216,256]{1,0:T(8,128)(2,1)}, bf16[1216,256]{1,0:T(8,128)(2,1)}, u32[]{:S(2)}, u32[]{:S(2)}) collective-permute-start(bf16[1216,256]{1,0:T(8,128)(2,1)} %maximum_select_fusion.2), channel_id=1, source_target_pairs={{0,4},{4,0},{8,12},{12,8},{16,20},{20,16},{24,28},{28,24},{1,5},{5... | collective-permute-start | bytes 1867784 | tf_op jit(solution)/shard_map/ppermute | solution.py:443
  340.5 8.8 %collective-permute-start.19 = (bf16[512,256]{1,0:T(8,128)(2,1)}, bf16[512,256]{1,0:T(8,128)(2,1)S(1)}, u32[]{:S(2)}, u32[]{:S(2)}) collective-permute-start(bf16[512,256]{1,0:T(8,128)(2,1)} %get-tuple-element.49), channel_id=1, source_target_pairs={{0,3},{1,2},{2,1},{3,0},{4,7},{5,6},{6,5},{7,4},{8,11},{9,10},{10,... | collective-permute-start | bytes 786440 | tf_op jit(solution)/shard_map/ppermute | solution.py:443
  (74 other events, 367.0 us)
where the time goes:
time: 361 us; the launch traced here: 360 us
  waiting for transfers between devices  119 us (33%)
  Pallas kernels  74.4 us (21%)
  local copies, waits for them, and re-layouts  72 us (20%)
  starting transfers between devices  46.3 us (13%)
  other arithmetic  23 us (6%)
  blocking collectives  21.9 us (6%)
    ppermute x35, waiting for transfers between devices, swap(): return lax.ppermute(v, axis, [(i, i ^ k) for i in range(size)])  110 us
    pallas_call x20, Pallas kernels, call(): pl.pallas_call(kernel, out_shape=list(outs), in_specs=specs, out_specs=[V...  74.4 us
    unnamed x138, local copies, waits for them, and re-layouts  45.6 us
    ppermute x35, starting transfers between devices, swap(): return lax.ppermute(v, axis, [(i, i ^ k) for i in range(size)])  29.6 us
    all_to_all x2, blocking collectives, batch_sum(): return lax.all_to_all(spread, 'batch', 0, 0)  21.9 us
    all_to_all x4, starting transfers between devices, batch_sum(): return lax.all_to_all(spread, 'batch', 0, 0)  16.7 us
    all_to_all x4, waiting for transfers between devices, batch_sum(): return lax.all_to_all(spread, 'batch', 0, 0)  8.85 us
  transfers between devices with their start and end apart: 39, of which 19 were waited for; matrix products, arithmetic and copies ran while one was open for 12% of the time, Pallas kernels for 10%

commit v1 on v0

v1 whole, which is shorter than its diff:
```python
import functools

import jax
import jax.numpy as jnp
from jax import lax
from jax.experimental import pallas as pl
from jax.experimental.pallas import tpu as pltpu
from jax.sharding import PartitionSpec as P

EPSILON = 1e-05
ROOT = 0.7978845608028654
CUBE = 0.044715
F32 = jnp.float32
BF16 = jnp.bfloat16
STEP = 256
LANES = 128
LINES = 3
STEPS = 4
TN = (((0,), (0,)), ((), ()))
NT = (((1,), (1,)), ((), ()))
VM = pl.BlockSpec(memory_space=pltpu.VMEM)
SM = pl.BlockSpec(memory_space=pltpu.SMEM)


def dot(a, b):
    return jnp.dot(a, b, preferred_element_type=F32)


def dot_tn(a, b):
    return lax.dot_general(a, b, TN, preferred_element_type=F32)


def dot_nt(a, b):
    return lax.dot_general(a, b, NT, preferred_element_type=F32)


def bend(v):
    return jnp.tanh(v * (ROOT + (ROOT * CUBE) * (v * v)))


def act(v):
    half = 0.5 * v
    return half + half * bend(v)


def act_slope(v):
    t = bend(v)
    inner = v * (0.5 * ROOT + (1.5 * ROOT * CUBE) * (v * v))
    return 0.5 + 0.5 * t + inner * (1.0 - t * t)


def chunks(total, body, step=STEP):
    full = total // step

    def go(c, carry):
        body(pl.multiple_of(c * step, step), step)
        return carry

    if full:
        lax.fori_loop(0, full, go, 0)
    if total % step:
        body(full * step, total % step)


def fold(v):
    return jnp.sum(v.reshape(v.shape[0] // 8, 8, v.shape[1]), axis=0)


def widen(live, width):
    return jnp.concatenate([live] * (width // LANES), axis=1) if width > LANES else live


def norm_of(got, counts):
    s = jnp.sum(got[...], axis=0)
    share_of = 1.0 / jnp.sum(counts[...], axis=0)[2:3, 0:1]
    mu = s[0:1] * share_of
    return mu, lax.rsqrt(s[1:2] * share_of - mu * mu + EPSILON), share_of


def send_sums(out, acc):
    out[...] = jnp.broadcast_to(jnp.sum(acc[...], axis=1)[None], out.shape)


def start_sums(acc):
    @pl.when(pl.program_id(0) == 0)
    def _():
        acc[...] = jnp.zeros_like(acc)


def end_sums(out, acc):
    @pl.when(pl.program_id(0) == pl.num_programs(0) - 1)
    def _():
        send_sums(out, acc)


def near_kernel(dims, *refs):
    *feats, w, out = refs
    share = feats[0].shape[1]
    me = dims[2]
    ws = [w[pl.ds(pl.multiple_of((me ^ k) * share, share), share), :] for k in range(len(feats))]
    out[...] = sum(dot(f[...], wk) for f, wk in zip(feats, ws))


def far_kernel(dims, live, part, *refs):
    *feats, w, out, spread, acc = refs
    share = feats[0].shape[1]
    me = dims[2]
    start_sums(acc)
    z = part[...]
    for k, f in enumerate(feats, 2):
        z += dot(f[...], w[pl.ds(pl.multiple_of((me ^ k) * share, share), share), :])
    m = widen(live[...], z.shape[1])
    z = jnp.where(m > 0.0, z, 0.0)
    out[...] = z
    acc[0] += fold(z)
    acc[1] += fold(z * z)
    acc[2] += fold(m)
    end_sums(spread, acc)


def pad_edges(pad, side, line, wide, slots):
    width = pad.shape[1]
    pad[0:wide] = jnp.zeros((wide, width), F32)
    pad[(side + 1) * wide : (side + 2) * wide] = jnp.zeros((wide, width), F32)


def pad_line(pad, i, value, line, wide, slots):
    o = pl.multiple_of((i + 1) * wide, 8)
    edge = jnp.zeros((slots, pad.shape[1]), F32)
    pad[pl.ds(o, slots), :] = edge
    pad[pl.ds(o + slots, line), :] = value
    pad[pl.ds(o + slots + line, slots), :] = edge


def conv_lines(pad, first, count, taps, line, wide, slots, flip):
    total = None
    for t in range(9):
        a, b = divmod(t, 3)
        starts = [(first + i + a) * wide + b * slots for i in range(count)]
        x = jnp.concatenate([pad[o : o + line].astype(BF16) for o in starts], axis=0)
        d = dot_nt(x, taps[8 - t]) if flip else dot(x, taps[t])
        total = d if total is None else total + d
    return total


def taps_kernel(w, out):
    width, group_width = w.shape[2], w.shape[1]
    ids = [lax.broadcasted_iota(jnp.int32, (width, width), b) // group_width for b in range(2)]
    same = ids[0] == ids[1]
    for t in range(9):
        tiled = jnp.concatenate([w[t].astype(F32)] * (width // group_width), axis=0)
        out[t] = jnp.where(same, tiled, 0.0).astype(BF16)


def conv_kernel(side, slots, live, z, got, gain, shift, taps, hid, out, spread, pad, acc):
    line, wide = side * slots, (side + 2) * slots
    rows, width = z.shape
    mu, r, _ = norm_of(got, got)
    a = r * gain[...]
    b = shift[...] - mu * a
    pad_edges(pad, side, line, wide, slots)
    acc[...] = jnp.zeros_like(acc)

    def fill(i, carry):
        here = pl.ds(pl.multiple_of(i * line, 8), line)
        h = widen(live[here, :], width) * act(z[here, :] * a + b)
        h = h.astype(BF16).astype(F32)
        hid[here, :] = h
        pad_line(pad, i, h, line, wide, slots)
        return carry

    lax.fori_loop(0, side, fill, 0)

    for first in range(0, side, LINES):
        count = min(LINES, side - first)
        here = slice(first * line, (first + count) * line)
        total = conv_lines(pad, first, count, taps, line, wide, slots, False)
        out[here] = total
        m = widen(live[here], width) * total
        acc[0] += fold(m)
        acc[1] += fold(m * total)
    used = side * line
    out[used:rows] = jnp.zeros((rows - used, width), F32)
    hid[used:rows] = jnp.zeros((rows - used, width), F32)
    send_sums(spread, acc)


def hidden_kernel(live, z, counts, got, gain, shift, out):
    mu, r, _ = norm_of(got, counts)
    a = r * gain[...]
    b = shift[...] - mu * a
    m = widen(live[...], z.shape[1])
    out[...] = (m * act(z[...] * a + b)).astype(BF16)


def slope_kernel(live, z, counts, got, gain, shift, out):
    mu, r, _ = norm_of(got, counts)
    a = r * gain[...]
    b = shift[...] - mu * a
    out[...] = widen(live[...], z.shape[1]) * act_slope(z[...] * a + b)


def expand_near_kernel(*refs):
    *ins, out = refs
    k = len(ins) // 2
    out[...] = sum(dot(h[...], w[...]) for h, w in zip(ins[:k], ins[k:]))


def expand_far_kernel(live, part, *refs):
    *ins, out, spread, acc = refs
    k = len(ins) // 2
    start_sums(acc)
    e = part[...] + sum(dot(h[...], w[...]) for h, w in zip(ins[:k], ins[k:]))
    out[...] = e
    m = widen(live[...], e.shape[1]) * e
    acc[0] += fold(m)
    acc[1] += fold(m * e)
    end_sums(spread, acc)


def third_kernel(live, e, counts, got, gain, shift, feats, cot, d_pre, spread, acc):
    mu, r, _ = norm_of(got, counts)
    start_sums(acc)
    zhat = (e[...] - mu) * r
    v = zhat * gain[...] + shift[...] + feats[...].astype(F32)
    m = widen(live[...], v.shape[1])
    d = m * cot[...].astype(F32) * act_slope(v)
    d_pre[...] = d
    acc[0] += fold(d)
    acc[1] += fold(d * zhat)
    end_sums(spread, acc)


def block_kernel(live, e, counts, got, gain, shift, feats, out):
    mu, r, _ = norm_of(got, counts)
    v = (e[...] - mu) * r * gain[...] + shift[...] + feats[...].astype(F32)
    out[...] = (widen(live[...], v.shape[1]) * act(v)).astype(BF16)


def d_expanded_kernel(live, e, d_pre, counts, got, totals, gain, w, d_exp, out, sums):
    mu, r, share_of = norm_of(got, counts)
    t = jnp.sum(totals[...], axis=0)
    sums[...] = t
    t = t * share_of
    scale = r * gain[...]
    zhat = (e[...] - mu) * r
    m = widen(live[...], zhat.shape[1])
    d = (m * scale * (d_pre[...] - t[0:1] - zhat * t[1:2])).astype(BF16)
    d_exp[...] = d
    out[...] = dot_nt(d, w[...]).astype(BF16)


def back_expand_kernel(d_exp, *refs):
    k = len(refs) // 2
    for w, out in zip(refs[:k], refs[k:]):
        out[...] = dot_nt(d_exp[...], w[...]).astype(out.dtype)


def merge_kernel(d_exp, w, *refs):
    *got, out = refs
    total = dot_nt(d_exp[...], w[...]) + sum(g[...].astype(F32) for g in got)
    out[...] = total.astype(BF16)


def expand_grad_kernel(d_exp, *refs):
    *hs, out = refs
    for k, h in enumerate(hs):
        out[k] = dot_tn(h[...], d_exp[...]).astype(BF16)


def d_two_kernel(slope, z, counts, got, *refs):
    *terms, d_out, spread, acc = refs
    mu, r, _ = norm_of(got, counts)
    start_sums(acc)
    d = sum(t[...].astype(F32) for t in terms) * slope[...]
    d_out[...] = d
    acc[0] += fold(d)
    acc[1] += fold(d * ((z[...] - mu) * r))
    end_sums(spread, acc)


def conv_back_kernel(
    side, slots, live, d_two, grouped, got_two, totals, gain, slope, z, got, taps,
    d_grouped, d_one, spread, sums, pad, acc,
):
    line, wide = side * slots, (side + 2) * slots
    rows, width = z.shape
    mu_two, r_two, share_of = norm_of(got_two, got)
    mu, r, _ = norm_of(got, got)
    t = jnp.sum(totals[...], axis=0)
    sums[...] = t
    t = t * share_of
    scale = r_two * gain[...]
    pad_edges(pad, side, line, wide, slots)
    acc[...] = jnp.zeros_like(acc)

    def fill(i, carry):
        here = pl.ds(pl.multiple_of(i * line, 8), line)
        zhat = (grouped[here, :] - mu_two) * r_two
        m = widen(live[here, :], width)
        d = m * scale * (d_two[here, :] - t[0:1] - zhat * t[1:2])
        d = d.astype(BF16).astype(F32)
        d_grouped[here, :] = d
        pad_line(pad, i, d, line, wide, slots)
        return carry

    lax.fori_loop(0, side, fill, 0)

    for first in range(0, side, LINES):
        count = min(LINES, side - first)
        here = slice(first * line, (first + count) * line)
        d = conv_lines(pad, first, count, taps, line, wide, slots, True) * slope[here]
        d_one[here] = d
        acc[0] += fold(d)
        acc[1] += fold(d * ((z[here] - mu) * r))
    used = side * line
    d_one[used:rows] = jnp.zeros((rows - used, width), F32)
    d_grouped[used:rows] = jnp.zeros((rows - used, width), F32)
    send_sums(spread, acc)


def d_reduced_kernel(live, d_one, z, got, totals, gain, out, sums):
    mu, r, share_of = norm_of(got, got)
    t = jnp.sum(totals[...], axis=0)
    sums[...] = t
    t = t * share_of
    zhat = (z[...] - mu) * r
    m = widen(live[...], zhat.shape[1])
    out[...] = (m * (r * gain[...]) * (d_one[...] - t[0:1] - zhat * t[1:2])).astype(BF16)


def group_grad_kernel(side, slots, group_width, hid, d_grouped, out, pad):
    line, wide = side * slots, (side + 2) * slots
    width = hid.shape[1]
    pad_edges(pad, side, line, wide, slots)

    def fill(i, carry):
        here = pl.ds(pl.multiple_of(i * line, 8), line)
        pad_line(pad, i, hid[here, :], line, wide, slots)
        return carry

    lax.fori_loop(0, side, fill, 0)
    d = d_grouped[0 : side * line].astype(BF16)
    ids = [lax.broadcasted_iota(jnp.int32, (width, width), b) // group_width for b in range(2)]
    same = ids[0] == ids[1]
    for t in range(9):
        a, b = divmod(t, 3)
        starts = [(i + a) * wide + b * slots for i in range(side)]
        x = jnp.concatenate([pad[o : o + line].astype(BF16) for o in starts], axis=0)
        dense = jnp.where(same, dot_tn(x, d), 0.0)
        picked = jnp.sum(dense.reshape(width // group_width, group_width, width), axis=0)
        out[t * group_width : (t + 1) * group_width] = picked.astype(BF16)


def reduce_grad_kernel(dims, d_red, *refs):
    *feats, out = refs
    share = feats[0].shape[1]
    me = dims[2]
    for k, f in enumerate(feats):
        rows = pl.ds(pl.multiple_of((me ^ k) * share, share), share)
        out[rows, :] = dot_tn(f[...], d_red[0 : f.shape[0]]).astype(BF16)


def features_grad_kernel(part, *refs):
    *ins, out = refs
    k = len(ins) // 2
    out[...] = part[...] + sum(dot_nt(d[...], w[...]) for d, w in zip(ins[:k], ins[k:]))


def pick_kernel(dims, w_expand, w_reduce, gain, shift, cot, *outs):
    me = dims[2]
    n = (len(outs) - 3) // 2
    cols, rows, rest = outs[:n], outs[n : 2 * n], outs[2 * n :]
    share = rows[0].shape[0]

    @pl.when(pl.program_id(0) == 0)
    def _():
        for k in range(n):
            at = pl.ds(pl.multiple_of((me ^ k) * share, share), share)
            cols[k][...] = w_expand[:, at]
            rows[k][...] = w_reduce[at, :]
        at = pl.ds(pl.multiple_of(me * share, share), share)
        rest[0][...] = gain[:, at]
        rest[1][...] = shift[:, at]

    at = pl.ds(pl.multiple_of(me * share, share), share)
    first = pl.program_id(0) * cot.shape[0]
    row = lax.broadcasted_iota(jnp.int32, (cot.shape[0], share), 0) + first
    rest[2][...] = jnp.where(row < dims[4], cot[:, at].astype(F32), 0.0).astype(BF16)


def bit_of(v, bit):
    return lax.bitwise_and(lax.shift_right_logical(v, bit), 1)


def send_kernel(step, last, dims, *refs):
    *terms, out = refs
    total = None
    for first, term in enumerate(terms):
        rows, at = term.shape[-2], 0
        for t in range(first, step + (not last)):
            rows //= 2
            side = bit_of(dims[3], t)
            at += rows * (side if t < step else 1 - side)
        here = pl.ds(at if isinstance(at, int) else pl.multiple_of(at, 16), rows)
        v = term[:, here, :] if len(term.shape) == 3 else term[here, :]
        total = v.astype(F32) if total is None else total + v.astype(F32)
    out[...] = total.astype(BF16)


def arrange_kernel(dims, *refs):
    *cols, out = refs
    share = cols[0].shape[1]
    for k, c in enumerate(cols):
        out[:, pl.ds(pl.multiple_of((dims[2] ^ k) * share, share), share)] = c[...]


def double_kernel(bit, dims, mine, *refs):
    *other, out = refs
    n = mine.shape[0]
    upper = bit_of(dims[3], bit)
    out[pl.ds(pl.multiple_of(upper * n, 16), n), :] = mine[...].astype(out.dtype)
    at = (1 - upper) * n
    for v in other:
        out[pl.ds(pl.multiple_of(at, 16), v.shape[0]), :] = v[...].astype(out.dtype)
        at += v.shape[0]


def split_kernel(a, b, *outs):
    for k, out in enumerate(outs):
        out[...] = (a[k].astype(F32) + b[k].astype(F32)).astype(BF16)


def add_kernel(a, b, out):
    out[...] = (a[...].astype(F32) + b[...].astype(F32)).astype(out.dtype)


def input_far_kernel(part, *refs):
    *ins, out = refs
    n = len(ins) // (STEPS + 1)
    ds, ws = ins[: n * STEPS], ins[n * STEPS :]
    for step in range(STEPS):

        @pl.when(pl.program_id(0) == step)
        def _(step=step):
            got = sum(dot_nt(ds[k * STEPS + step][...], w[...]) for k, w in enumerate(ws))
            out[...] = part[...] + got


def call(kernel, outs, ins, scratch=(), flops=0, name=None, smem=False, steps=0):
    moved = sum(x.size * x.dtype.itemsize for x in ins)
    moved += sum(int(o.size) * o.dtype.itemsize for o in outs)
    block = -(-max(o.shape[0] for o in outs) // (16 * steps)) * 16 if steps else 0

    most = max(o.shape[0] for o in outs)

    def spec(x):
        if not steps:
            return VM
        if len(x.shape) == 2 and most - block < x.shape[0] <= steps * block:
            return pl.BlockSpec((block, x.shape[1]), lambda s: (s, 0))
        return pl.BlockSpec(x.shape, lambda s: (0,) * len(x.shape))

    specs = [spec(x) for x in ins]
    if smem:
        specs[0] = SM
    got = pl.pallas_call(
        kernel,
        out_shape=list(outs),
        grid=(steps,) if steps else (),
        in_specs=specs,
        out_specs=[spec(o) for o in outs],
        scratch_shapes=list(scratch),
        compiler_params=pltpu.CompilerParams(vmem_limit_bytes=32 << 20),
        cost_estimate=pl.CostEstimate(flops=flops, bytes_accessed=moved, transcendentals=0),
        name=name,
    )(*ins)
    return got[0] if len(outs) == 1 else got


def after(v, *others):
    return lax.optimization_barrier((v, *others))[0]


def swap(v, axis, size, k):
    return lax.ppermute(v, axis, [(i, i ^ k) for i in range(size)])


def batch_sum(spread):
    return lax.all_to_all(spread, "batch", 0, 0)


def pair_kernel(a, b, out):
    out[0:1] = a[...]
    out[1:2] = b[...]


def sum_kernel(*refs):
    *terms, out = refs
    out[...] = sum(t[...] for t in terms)


def batch_sum_stepwise(v, size):
    shape = jax.ShapeDtypeStruct(v.shape, v.dtype)
    got = [swap(v, "batch", size, k) for k in range(2, size, 2)]
    v = call(sum_kernel, [shape], [v, *got], name="sum")
    both = jax.ShapeDtypeStruct((2, *v.shape[1:]), v.dtype)
    return call(pair_kernel, [both], [v, swap(v, "batch", size, 1)], name="pair")


def gather_chan(v, size):
    held = {0: v}
    bit = size // 2
    while bit:
        held.update({k | bit: swap(b, "chan", size, bit) for k, b in list(held.items())})
        bit //= 2
    return [held[k] for k in range(size)]


def send_of(dims, terms, step, last=False):
    shape = list(terms[0].shape)
    shape[-2] >>= step + (not last)
    return call(
        functools.partial(send_kernel, step, last), [jax.ShapeDtypeStruct(tuple(shape), BF16)],
        [dims, *terms], name="send", smem=True,
    )


def double(dims, mine, other, bit, dtype=BF16):
    other = other if isinstance(other, list) else [other]
    shape = (2 * mine.shape[0], mine.shape[1])
    return call(
        functools.partial(double_kernel, bit), [jax.ShapeDtypeStruct(shape, dtype)],
        [dims, mine, *other], name="double", smem=True,
    )


def add(a, b, dtype=BF16):
    return call(add_kernel, [jax.ShapeDtypeStruct(a.shape, dtype)], [a, b], name="add")


def shards(n_batch, n_chan, *args):
    (features, w_reduce, gain_one, shift_one, w_group, gain_two, shift_two, w_expand,
     gain_three, shift_three, cotangent, resolution, crop_count) = args
    slots, side, _, share = features.shape
    width = w_reduce.shape[1]
    group_width = w_group.shape[2]
    rows = slots * side * side
    unit = 16 * STEPS
    padded = -(-rows // unit) * unit
    line, wide = side * slots, (side + 2) * slots
    me = lax.axis_index("chan")
    others = range(n_chan)
    shape = jax.ShapeDtypeStruct
    acc = lambda n, c: pltpu.VMEM((n, 8, c), F32)
    tall = pltpu.VMEM(((side + 2) * wide, width), F32)
    mm = 2 * padded * share * width

    feats = features.transpose(1, 2, 0, 3).reshape(rows, share)
    ends = ((0, padded - rows), (0, 0))
    first = gather_y(feats, n_chan)
    own = jnp.pad(feats, ends)
    beside = swap(own, "chan", n_chan, 1)

    dims = jnp.stack(
        [resolution[0], crop_count[0], me, lax.axis_index("batch"), jnp.int32(rows)]
    )
    row = lax.broadcasted_iota(jnp.int32, (padded, LANES), 0)
    crop, j, i = row % slots, (row // slots) % side, row // line
    live = ((crop < crop_count[0]) & (i < resolution[0]) & (j < resolution[0])).astype(F32)
    taps = call(
        taps_kernel, [shape((9, width, width), BF16)], [w_group.reshape(9, group_width, width)],
        flops=mm, name="taps",
    )
    line_of = lambda v: v.reshape(1, -1)
    gain_one, shift_one, gain_two, shift_two = map(
        line_of, (gain_one, shift_one, gain_two, shift_two)
    )

    *picked, gain_c, shift_c, cot = call(
        pick_kernel,
        [shape((width, share), BF16)] * n_chan + [shape((share, width), BF16)] * n_chan
        + [shape((1, share), F32)] * 2 + [shape((padded, share), BF16)],
        [dims, w_expand, w_reduce, line_of(gain_three), line_of(shift_three),
         cotangent.transpose(1, 2, 0, 3).reshape(rows, -1)],
        flops=mm, name="pick", smem=True, steps=STEPS,
    )

    part = call(
        near_kernel, [shape((padded, width), F32)], [dims, own, beside, w_reduce],
        flops=2 * mm, name="near", steps=STEPS, smem=True,
    )
    w_cols = [picked[0], swap(after(picked[1], part), "chan", n_chan, 1)]
    w_rows = [picked[n_chan], swap(after(picked[n_chan + 1], part), "chan", n_chan, 1)]
    ready = (part, live, cot, taps, gain_c, shift_c, w_cols[1], w_rows[1], *picked)
    first = {k: after(v, *ready) for k, v in first.items()}
    w_cols += [swap(after(picked[k], *first.values()), "chan", n_chan, k) for k in others[2:]]
    first = gather_core(first, n_chan)
    far = [first[k] for k in others[2:]]
    z, spread = call(
        far_kernel,
        [shape((padded, width), F32), shape((1, 3, width), F32)],
        [dims, live, part, *far, w_reduce], [acc(3, width)],
        flops=(n_chan - 2) * mm, name="far", steps=STEPS, smem=True,
    )
    got_one = batch_sum_stepwise(spread, n_batch)

    hid, grouped, spread = call(
        functools.partial(conv_kernel, side, slots),
        [shape((padded, width), F32)] * 2 + [shape((n_batch, 2, width), F32)],
        [live, z, got_one, gain_one, shift_one, taps], [tall, acc(2, width)],
        flops=18 * padded * width * width, name="conv",
    )
    got_two = batch_sum(after(spread, *w_cols))
    hidden_two = call(
        hidden_kernel, [shape((padded, width), BF16)],
        [live, grouped, got_one, got_two, gain_two, shift_two], flops=mm, name="hidden", steps=STEPS,
    )
    first = gather_y(hidden_two, n_chan)
    beside_two = swap(hidden_two, "chan", n_chan, 1)
    slope_two = call(
        slope_kernel, [shape((padded, width), F32)],
        [live, grouped, got_one, got_two, gain_two, shift_two], flops=mm, name="slope_two", steps=STEPS,
    )
    slope_one = call(
        slope_kernel, [shape((padded, width), F32)],
        [live, z, got_one, got_one, gain_one, shift_one], flops=mm, name="slope_one", steps=STEPS,
    )
    part = call(
        expand_near_kernel, [shape((padded, share), F32)], [hidden_two, beside_two, *w_cols[:2]],
        flops=2 * mm, name="expand_near", steps=STEPS,
    )
    first = {k: after(v, part, slope_one, slope_two, *w_cols) for k, v in first.items()}
    w_rows += [
        swap(after(picked[n_chan + k], *first.values()), "chan", n_chan, k) for k in others[2:]
    ]
    first = gather_core(first, n_chan)
    hidden_all = [hidden_two, beside_two] + [first[k] for k in others if k > 1]
    expanded, spread = call(
        expand_far_kernel, [shape((padded, share), F32), shape((n_batch, 2, share), F32)],
        [live, part, *hidden_all[2:], *w_cols[2:]], [acc(2, share)],
        flops=(n_chan - 2) * mm, name="expand_far", steps=STEPS,
    )
    got_three = batch_sum(spread)
    d_pre, spread = call(
        third_kernel, [shape((padded, share), F32), shape((n_batch, 2, share), F32)],
        [live, expanded, got_one, got_three, gain_c, shift_c, own, cot], [acc(2, share)],
        flops=4 * mm, name="third", steps=STEPS,
    )
    totals_three = batch_sum(after(spread, *w_rows))
    top = n_chan - 1
    d_expanded, sent, sums_three = call(
        d_expanded_kernel,
        [shape((padded, share), BF16), shape((padded, width), BF16), shape((2, share), F32)],
        [live, expanded, d_pre, got_one, got_three, totals_three, gain_c]
        + [w_cols[top]],
        flops=2 * mm, name="d_expanded", steps=STEPS,
    )
    early = [0, 1]
    d_zero, d_near = call(
        back_expand_kernel, [shape((padded, width), F32), shape((padded, width), BF16)],
        [after(d_expanded, sent)] + [w_cols[k] for k in early], flops=2 * mm,
        name="back_expand", steps=STEPS,
    )

    def part_sum(k, below):
        if k == top:
            return sent
        if k == 1:
            return d_near
        got, bit = [], 1
        while bit < below:
            got.append(swap(part_sum(k | bit, bit), "chan", n_chan, bit))
            bit *= 2
        if k == 0:
            return [d_zero, *got]
        return call(
            merge_kernel, [shape((padded, width), BF16)],
            [after(d_expanded, d_near), w_cols[k], *got], flops=mm, name="merge", steps=STEPS,
        )

    far_sum = part_sum(n_chan // 2, n_chan // 2)
    terms = [d_zero]
    bit = 1
    while bit < n_chan:
        mine = far_sum if bit == n_chan // 2 else part_sum(bit, bit)
        terms.append(swap(mine, "chan", n_chan, bit))
        bit *= 2
    expand_part = call(
        expand_grad_kernel, [shape((n_chan, width, share), BF16)],
        [after(d_expanded, far_sum), *hidden_all], flops=n_chan * mm, name="expand_grad",
    )
    block_out = call(
        block_kernel, [shape((rows, share), BF16)],
        [live, after(expanded, expand_part), got_one, got_three, gain_c, shift_c, own],
        flops=2 * mm, name="block", steps=STEPS,
    )
    expand_terms = [expand_part]
    bits = n_batch.bit_length() - 1
    for s in range(2):
        send = send_of(dims, expand_terms, s)
        expand_terms.append(swap(send, "batch", n_batch, 1 << s))
    for t in range(2, bits - 1):
        expand_send = send_of(dims, expand_terms, t)
        expand_terms.append(swap(expand_send, "batch", n_batch, 1 << t))
    mine = send_of(dims, expand_terms, bits - 1, True)
    expand_other = swap(mine, "batch", n_batch, 1 << (bits - 1))
    terms[0] = after(d_zero, mine, block_out)
    d_two, spread = call(
        d_two_kernel, [shape((padded, width), F32), shape((n_batch, 2, width), F32)],
        [slope_two, grouped, got_one, got_two, *terms], [acc(2, width)], flops=mm, name="d_two", steps=STEPS,
    )
    totals_two = batch_sum(spread)
    d_grouped, d_one, spread, sums_two = call(
        functools.partial(conv_back_kernel, side, slots),
        [shape((padded, width), F32)] * 2 + [shape((n_batch, 2, width), F32), shape((2, width), F32)],
        [live, d_two, grouped, got_two, totals_two, gain_two, slope_one, z, got_one, taps],
        [tall, acc(2, width)], flops=18 * padded * width * width, name="conv_back",
    )
    parts = call(
        split_kernel, [shape(mine.shape[1:], BF16)] * n_chan,
        [mine, after(expand_other, d_one)], name="split",
    )
    totals_one = batch_sum(after(spread, *parts))
    d_reduced, sums_one = call(
        d_reduced_kernel, [shape((padded, width), BF16), shape((2, width), F32)],
        [live, d_one, z, got_one, totals_one, gain_one], flops=mm, name="d_reduced", steps=STEPS,
    )
    tail = call(
        reduce_grad_kernel,
        [shape((n_chan * share, width), BF16)], [dims, d_reduced, own, beside, *far],
        flops=n_chan * mm, name="reduce_grad", smem=True,
    )
    d_beside = swap(d_reduced, "chan", n_chan, 1)
    tail_terms = [after(tail, d_beside)]
    quarter = padded // STEPS
    d_far = []

    def next_far(*ready):
        at = len(d_far) * quarter
        if d_far and len(d_far[-1]) < n_chan - 2:
            last = {k: after(v, *ready) for k, v in d_far[-1].items()}
            d_far[-1] = gather_core(last, n_chan)
        if at < padded:
            piece = after(d_reduced, *ready)[at : at + quarter]
            d_far.append(gather_y(piece, n_chan))
        return [v for d in d_far for v in d.values()]

    top = bits - 1
    for s in range(top):
        send = send_of(dims, tail_terms, s)
        got = swap(send, "batch", n_batch, 1 << s)
        if s == 0:
            cols = [parts[0]]
            cols += [swap(after(parts[k], send), "chan", n_chan, k) for k in others if k]
            group_part = call(
                functools.partial(group_grad_kernel, side, slots, group_width),
                [shape((9 * group_width, width), BF16)], [hid, after(d_grouped, *parts)],
                [tall], flops=mm, name="group_grad",
            )
            group_other = swap(group_part, "batch", n_batch, 2)
            cols[1] = after(cols[1], group_part)
            cols = call(
                arrange_kernel, [shape((mine.shape[1], n_chan * share), BF16)], [dims, *cols],
                name="arrange", smem=True,
            )
            for t in reversed(range(1, top)):
                other = swap(cols, "batch", n_batch, 1 << t)
                if t == 1:
                    group_part = add(group_part, after(group_other, cols))
                    other = after(other, group_part)
                cols = double(dims, cols, other, t)
            got = after(got, cols)
        elif s == 1:
            split = cols.shape[0] // 2
            others_cols = [swap(after(cols, send)[:split], "batch", n_batch, 1)]
            got = after(got, *others_cols, *next_far(send))
        tail_terms.append(got)
    mine = send_of(dims, tail_terms, top, True)
    other = swap(mine, "batch", n_batch, 1 << top)
    part = call(
        features_grad_kernel, [shape((padded, share), F32)],
        [d_pre, after(d_reduced, mine), d_beside, *w_rows[:2]], flops=2 * mm,
        name="input_near", steps=STEPS,
    )
    others_cols.append(swap(after(cols, part)[split:], "batch", n_batch, 1))
    moved = next_far(part)
    others_cols[0] = after(others_cols[0], part)
    expand_grad = double(dims, cols, others_cols, 0, F32)
    group_other = swap(after(group_part, part), "batch", n_batch, 1)
    group_part = add(group_part, after(group_other, expand_grad))
    moved = next_far(part)
    tail = add(mine, after(other, group_part, *moved))
    for s in reversed(range(top)):
        got = swap(tail, "batch", n_batch, 1 << s)
        before = next_far(tail)
        if s == 0:
            for t in range(2, bits):
                group_part = after(group_part, tail)
                group_other = swap(group_part, "batch", n_batch, 1 << t)
                group_part = add(group_part, group_other, BF16 if t + 1 < bits else F32)
            features_grad = call(
                input_far_kernel, [shape((rows, share), F32)],
                [after(part, tail), *[d[k] for k in others[2:] for d in d_far], *w_rows[2:]],
                flops=(n_chan - 2) * mm, name="input_far", steps=STEPS,
            )
            before = (features_grad, group_part)
        tail = double(dims, tail, after(got, *before), s, BF16 if s else F32)
    reduce_grad, group_grad = tail, group_part

    shaped = lambda v: v.reshape(side, side, slots, share).transpose(2, 0, 1, 3)
    return (
        shaped(block_out),
        shaped(features_grad),
        reduce_grad,
        sums_one[1],
        sums_one[0],
        group_grad.reshape(3, 3, group_width, width),
        sums_two[1],
        sums_two[0],
        expand_grad,
        sums_three[1],
        sums_three[0],
    )


def gather_y(v, size):
    held = {0: v}
    bit = size // 2
    while bit > 1:
        held.update({k | bit: swap(b, "chan", size, bit) for k, b in list(held.items())})
        bit //= 2
    return {k: b for k, b in held.items() if k}


def gather_core(held, size):
    return held | {k | 1: swap(b, "chan", size, 1) for k, b in held.items()}


def solution(mesh):
    in_specs = (
        P("batch", None, None, "chan"),
        P(None, "chan"),
        P("chan"),
        P("chan"),
        P(None, None, None, "chan"),
        P("chan"),
        P("chan"),
        P("chan", None),
        P(),
        P(),
        P("batch", None, None, None),
        P("batch"),
        P("batch"),
    )
    out_specs = (
        P("batch", None, None, "chan"),
        P("batch", None, None, "chan"),
        P(None, "chan"),
        P("chan"),
        P("chan"),
        P(None, None, None, "chan"),
        P("chan"),
        P("chan"),
        P("chan", None),
        P("chan"),
        P("chan"),
    )
    n_batch, n_chan = mesh.shape["batch"], mesh.shape["chan"]

    def run(*args):
        return shards(n_batch, n_chan, *args)

    return jax.shard_map(run, mesh=mesh, in_specs=in_specs, out_specs=out_specs, check_vma=False)
```

time: 361 us -> 281 us (0.78)
  local copies, waits for them, and re-layouts: 72 us -> 14.4 us
  blocking collectives: 21.9 us -> 49.1 us
  other arithmetic: 23 us -> 2.58 us
  starting transfers between devices: 46.3 us -> 32.6 us
  waiting for transfers between devices: 119 us -> 110 us
  Pallas kernels: 74.4 us -> 69.2 us
    unnamed x138 -> x64, local copies, waits for them, and re-layouts: 45.6 us -> 10.7 us
    all_to_all x2 -> x5, blocking collectives: 21.9 us -> 49.1 us  [batch_sum(): return lax.all_to_all(spread, 'batch', 0, 0)]
    all_to_all x4 -> x0, starting transfers between devices: 16.7 us -> none  [batch_sum(): return lax.all_to_all(spread, 'batch', 0, 0)]
    dynamic_slice x10 -> x0, local copies, waits for them, and re-layouts: 10.8 us -> none  [the longest x1 4.67 us: shards(): lax.dynamic_index_in_dim(w_exp_blocks, me ^ k, 1, keepdims=False)]
    convert_element_type x9 -> x0, other arithmetic: 9.89 us -> none  [the longest x6 3.78 us: reduce_batch(): (keep.astype(F32) + swap(send, 'batch', size, bit).astype(F32)).astype(BF16)]
    all_to_all x4 -> x0, waiting for transfers between devices: 8.85 us -> none  [batch_sum(): return lax.all_to_all(spread, 'batch', 0, 0)]
    select_n x6 -> x0, other arithmetic: 8.45 us -> none  [the longest x5 6.06 us: spread_batch(): jnp.where(mine == 0, jnp.concatenate([v, other], axis), jnp.concatenate([...]
    pallas_call x20 -> x41, Pallas kernels: 74.4 us -> 69.2 us  [call(): pl.pallas_call(kernel, out_shape=list(outs), grid=(steps,) if steps else...]
  transfers between devices with their start and end apart: 39 -> 45, of which waited for: 19 -> 19; matrix products, arithmetic and copies ran while one was open for 12% -> 2% of each run, Pallas kernels for 10% -> 20%
where the time goes in v1:
time: 281 us; the launch traced here: 280 us
  waiting for transfers between devices  110 us (39%)
  Pallas kernels  69.2 us (25%)
  blocking collectives  49.1 us (17%)
  starting transfers between devices  32.6 us (12%)
  local copies, waits for them, and re-layouts  14.4 us (5%)
    ppermute x45, waiting for transfers between devices, swap(): return lax.ppermute(v, axis, [(i, i ^ k) for i in range(size)])  110 us
    pallas_call x41, Pallas kernels, call(): pl.pallas_call(kernel, out_shape=list(outs), grid=(steps,) if steps else...  69.2 us
    all_to_all x5, blocking collectives, batch_sum(): return lax.all_to_all(spread, 'batch', 0, 0)  49.1 us
    ppermute x45, starting transfers between devices, swap(): return lax.ppermute(v, axis, [(i, i ^ k) for i in range(size)])  32.6 us
    unnamed x64, local copies, waits for them, and re-layouts  10.7 us
  transfers between devices with their start and end apart: 45, of which 19 were waited for; matrix products, arithmetic and copies ran while one was open for 2% of the time, Pallas kernels for 20%

profile of v1, /device:TPU:0, one launch (start us, length us, event | category | flops | bytes accessed | tf_op | source)
XLA Modules:
  0.0 280.5 jit_solution(9724773525996612437)
XLA Ops:
  3.0 2.6 collective-permute-start.1
  7.0 3.3 %copy-done.5 = bf16[24,9,9,2048]{3,0,2,1:T(8,128)(2,1)S(1)} copy-done((bf16[24,9,9,2048]{3,0,2,1:T(8,128)(2,1)S(1)}, bf16[24,9,9,2048]{3,0,2,1:T(8,128)(2,1)}, u32[]{:S(2)}) %copy-start.5) | copy-done | bytes 7962648
  14.1 3.5 %near.1.part = f32[1984,256]{1,0:T(8,128)S(1)} custom-call(s32[5]{0:T(128)S(1)} %stack.11.dims, bf16[1984,512]{1,0:T(8,128)(2,1)S(1)} %pad.4.refs_0_.feats, bf16[1984,512]{1,0:T(8,128)(2,1)} %collective-permute-done.refs_1_, bf16[2048,256]{1,0:T(8,128)(2,1)S(1)} %copy-done), custom_call_target="tpu_custom_call" | custom-call | flops 1040187392 | bytes 7143444 | tf_op jit(solution)/shard_map/near/pallas_call | solution.py:467
  18.2 2.5 fusion.5.live
  20.9 28.9 %collective-permute-done.1.refs_0_.refs_2_ = bf16[1944,512]{1,0:T(8,128)(2,1)} collective-permute-done((bf16[1944,512]{1,0:T(8,128)(2,1)}, bf16[1944,512]{1,0:T(8,128)(2,1)}, u32[]{:S(2)}, u32[]{:S(2)}) %collective-permute-start.1) | collective-permute-done | bytes 1990688 | tf_op jit(solution)/shard_map/ppermute | solution.py:486
  51.8 2.3 collective-permute-done.4.refs_1_.refs_3_
  54.1 3.9 %far.1 = (f32[1984,256]{1,0:T(8,128)S(1)}, f32[1,3,256]{2,1,0:T(4,128)S(1)}) custom-call(s32[5]{0:T(128)S(1)} %stack.11.dims, f32[1984,128]{1,0:T(8,128)S(1)} %fusion.5.live, f32[1984,256]{1,0:T(8,128)S(1)} %near.1.part, bf16[1944,512]{1,0:T(8,128)(2,1)} %collective-permute-done.1.refs_0_.refs_2_, ...), custom_call_target="tpu_custom_call" | custom-call | flops 1040187392 | bytes 10112020 | tf_op jit(solution)/shard_map/far/pallas_call | solution.py:467
  58.1 3.9 %collective-permute-start.7 = (f32[1,3,256]{2,1,0:T(4,128)S(1)}, f32[1,3,256]{2,1,0:T(4,128)S(1)}, u32[]{:S(2)}, u32[]{:S(2)}) collective-permute-start(f32[1,3,256]{2,1,0:T(4,128)S(1)} %get-tuple-element.108.refs_0_), channel_id=1, source_target_pairs={{0,24},{4,28},{8,16},{12,20},{16,8},{20,12},{24,0},{28,4},{1,25},{... | collective-permute-start | bytes 9224 | tf_op jit(solution)/shard_map/ppermute | solution.py:486
  63.6 2.9 %collective-permute-done.6.refs_2_ = f32[1,3,256]{2,1,0:T(4,128)S(1)} collective-permute-done((f32[1,3,256]{2,1,0:T(4,128)S(1)}, f32[1,3,256]{2,1,0:T(4,128)S(1)}, u32[]{:S(2)}, u32[]{:S(2)}) %collective-permute-start.6) | collective-permute-done | bytes 3104 | tf_op jit(solution)/shard_map/ppermute | solution.py:486
  70.2 3.6 %conv.1 = (f32[1984,256]{1,0:T(8,128)S(1)}, f32[1984,256]{1,0:T(8,128)S(1)}, f32[8,2,256]{2,1,0:T(2,128)S(1)}) custom-call(f32[1984,128]{1,0:T(8,128)S(1)} %fusion.5.live, f32[1984,256]{1,0:T(8,128)S(1)} %get-tuple-element.107.z, f32[2,3,256]{2,1,0:T(4,128)S(1)} %pair.1.got.counts, f32[1,256]{1,0:T(1,128)S(1)} %bitcast.40, f32[1,256]{1,0:T(1,128)S(1)} %bitcast.43, ...), custom_call_target="tpu_custom_call" | custom-call | flops 2340421632 | bytes 8314880 | tf_op jit(solution)/shard_map/conv/pallas_call | solution.py:467
  75.1 10.5 %all_to_all.25.got.got_two = f32[8,2,256]{2,1,0:T(2,128)S(1)} all-to-all(f32[8,2,256]{2,1,0:T(2,128)S(1)} %get-tuple-element.113), channel_id=1, replica_groups=mesh['batch'=8,'chan'=4] {'batch'}, dimensions={0} | all-to-all | bytes 32768 | tf_op jit(solution)/shard_map/all_to_all | solution.py:490
  88.9 2.5 slope_one.1.slope
  92.7 2.5 slope_two.1.slope
  98.3 13.9 %collective-permute-done.12.refs_0_.refs_2_ = bf16[1984,256]{1,0:T(8,128)(2,1)S(1)} collective-permute-done((bf16[1984,256]{1,0:T(8,128)(2,1)S(1)}, bf16[1984,256]{1,0:T(8,128)(2,1)S(1)}, u32[]{:S(2)}, u32[]{:S(2)}) %collective-permute-start.12) | collective-permute-done | bytes 1015840 | tf_op jit(solution)/shard_map/ppermute | solution.py:486
  116.8 9.1 %all_to_all.26.got = f32[8,2,512]{2,1,0:T(2,128)S(1)} all-to-all(f32[8,2,512]{2,1,0:T(2,128)S(1)} %get-tuple-element.116), channel_id=1, replica_groups=mesh['batch'=8,'chan'=4] {'batch'}, dimensions={0} | all-to-all | bytes 65536 | tf_op jit(solution)/shard_map/all_to_all | solution.py:490
  125.8 3.9 %third.1 = (f32[1984,512]{1,0:T(8,128)S(1)}, f32[8,2,512]{2,1,0:T(2,128)S(1)}) custom-call(f32[1984,128]{1,0:T(8,128)S(1)} %fusion.5.live, f32[1984,512]{1,0:T(8,128)S(1)} %get-tuple-element.128.e, f32[2,3,256]{2,1,0:T(4,128)S(1)} %pair.1.got.counts, f32[8,2,512]{2,1,0:T(2,128)S(1)} %all_to_all.26.got, f32[1,512]{1,0:T(1,128)S(1)} %get-tuple-element.94.gain, ...), custom_call_target="tpu_custom_call" | custom-call | flops 2080374784 | bytes 13281280 | tf_op jit(solution)/shard_map/third/pallas_call | solution.py:467
  131.1 9.0 %all_to_all.27.totals = f32[8,2,512]{2,1,0:T(2,128)S(1)} all-to-all(f32[8,2,512]{2,1,0:T(2,128)S(1)} %get-tuple-element.121), channel_id=1, replica_groups=mesh['batch'=8,'chan'=4] {'batch'}, dimensions={0} | all-to-all | bytes 65536 | tf_op jit(solution)/shard_map/all_to_all | solution.py:490
  147.8 2.4 expand_grad.1.refs_0_
  151.2 13.2 %collective-permute-done.17.refs_1_ = bf16[4,128,512]{2,1,0:T(8,128)(2,1)S(1)} collective-permute-done((bf16[4,128,512]{2,1,0:T(8,128)(2,1)S(1)}, bf16[4,128,512]{2,1,0:T(8,128)(2,1)S(1)}, u32[]{:S(2)}, u32[]{:S(2)}) %collective-permute-start.17) | collective-permute-done | bytes 524320 | tf_op jit(solution)/shard_map/ppermute | solution.py:486
  165.5 5.1 %block.1 = bf16[1944,512]{1,0:T(8,128)(2,1)} custom-call(f32[1984,128]{1,0:T(8,128)S(1)} %fusion.5.live, f32[1984,512]{1,0:T(8,128)S(1)} %get-tuple-element.128.e, f32[2,3,256]{2,1,0:T(4,128)S(1)} %pair.1.got.counts, f32[8,2,512]{2,1,0:T(2,128)S(1)} %all_to_all.26.got, f32[1,512]{1,0:T(1,128)S(1)} %get-tuple-element.94.gain, ...), custom_call_target="tpu_custom_call" | custom-call | flops 1040187392 | bytes 9144320 | tf_op jit(solution)/shard_map/block/pallas_call | solution.py:467
  174.8 11.4 %all_to_all.28.totals = f32[8,2,256]{2,1,0:T(2,128)S(1)} all-to-all(f32[8,2,256]{2,1,0:T(2,128)S(1)} %get-tuple-element.132), channel_id=1, replica_groups=mesh['batch'=8,'chan'=4] {'batch'}, dimensions={0} | all-to-all | bytes 32768 | tf_op jit(solution)/shard_map/all_to_all | solution.py:490
  186.2 3.5 %conv_back.1 = (f32[1984,256]{1,0:T(8,128)S(1)}, f32[1984,256]{1,0:T(8,128)S(1)}, f32[8,2,256]{2,1,0:T(2,128)S(1)}, f32[2,256]{1,0:T(2,128)S(1)}) custom-call(f32[1984,128]{1,0:T(8,128)S(1)} %fusion.5.live, f32[1984,256]{1,0:T(8,128)S(1)} %get-tuple-element.131.d_two, f32[1984,256]{1,0:T(8,128)S(1)} %get-tuple-element.109.z.grouped, ...), custom_call_target="tpu_custom_call" | custom-call | flops 2340421632 | bytes 14443520 | tf_op jit(solution)/shard_map/conv_back/pallas_call | solution.py:467
  189.8 9.1 %all_to_all.29.totals = f32[8,2,256]{2,1,0:T(2,128)S(1)} all-to-all(f32[8,2,256]{2,1,0:T(2,128)S(1)} %get-tuple-element.140), channel_id=1, replica_groups=mesh['batch'=8,'chan'=4] {'batch'}, dimensions={0} | all-to-all | bytes 32768 | tf_op jit(solution)/shard_map/all_to_all | solution.py:490
  200.5 4.8 %reduce_grad.1.refs_0_ = bf16[2048,256]{1,0:T(8,128)(2,1)S(1)} custom-call(s32[5]{0:T(128)S(1)} %stack.11.dims, bf16[1984,256]{1,0:T(8,128)(2,1)S(1)} %get-tuple-element.166.d_red.refs_0_, bf16[1984,512]{1,0:T(8,128)(2,1)S(1)} %pad.4.refs_0_.feats, bf16[1984,512]{1,0:T(8,128)(2,1)} %collective-permute-done.refs_1_, ...), custom_call_target="tpu_custom_call" | custom-call | flops 2080374784 | bytes 10108948 | tf_op jit(solution)/shard_map/reduce_grad/pallas_call | solution.py:467
  208.3 2.9 %group_grad.1.a = bf16[288,256]{1,0:T(8,128)(2,1)S(1)} custom-call(f32[1984,256]{1,0:T(8,128)S(1)} %copy-done.9, f32[1984,256]{1,0:T(8,128)S(1)} %get-tuple-element.146.d_grouped), custom_call_target="tpu_custom_call" | custom-call | flops 520093696 | bytes 4210688 | tf_op jit(solution)/shard_map/group_grad/pallas_call | solution.py:467
  214.6 9.9 %collective-permute-done.28.b = bf16[288,256]{1,0:T(8,128)(2,1)S(1)} collective-permute-done((bf16[288,256]{1,0:T(8,128)(2,1)S(1)}, bf16[288,256]{1,0:T(8,128)(2,1)S(1)}, u32[]{:S(2)}, u32[]{:S(2)}) %collective-permute-start.28) | collective-permute-done | bytes 147488 | tf_op jit(solution)/shard_map/ppermute | solution.py:486
  228.5 6.7 %collective-permute-done.31.refs_0_ = bf16[496,256]{1,0:T(8,128)(2,1)S(1)} collective-permute-done((bf16[496,256]{1,0:T(8,128)(2,1)S(1)}, bf16[496,256]{1,0:T(8,128)(2,1)S(1)}, u32[]{:S(2)}, u32[]{:S(2)}) %collective-permute-start.31) | collective-permute-done | bytes 253984 | tf_op jit(solution)/shard_map/ppermute | solution.py:486
  241.2 4.7 %collective-permute-done.36.refs_1_ = bf16[496,256]{1,0:T(8,128)(2,1)S(1)} collective-permute-done((bf16[496,256]{1,0:T(8,128)(2,1)S(1)}, bf16[496,256]{1,0:T(8,128)(2,1)S(1)}, u32[]{:S(2)}, u32[]{:S(2)}) %collective-permute-start.36) | collective-permute-done | bytes 253984 | tf_op jit(solution)/shard_map/ppermute | solution.py:486
  248.0 4.2 %collective-permute-done.33.b = bf16[288,256]{1,0:T(8,128)(2,1)S(1)} collective-permute-done((bf16[288,256]{1,0:T(8,128)(2,1)S(1)}, bf16[288,256]{1,0:T(8,128)(2,1)S(1)}, u32[]{:S(2)}, u32[]{:S(2)}) %collective-permute-start.33) | collective-permute-done | bytes 147488 | tf_op jit(solution)/shard_map/ppermute | solution.py:486
  255.5 7.0 %collective-permute-done.41.refs_3_ = bf16[496,256]{1,0:T(8,128)(2,1)S(1)} collective-permute-done((bf16[496,256]{1,0:T(8,128)(2,1)S(1)}, bf16[496,256]{1,0:T(8,128)(2,1)S(1)}, u32[]{:S(2)}, u32[]{:S(2)}) %collective-permute-start.41) | collective-permute-done | bytes 253984 | tf_op jit(solution)/shard_map/ppermute | solution.py:486
  265.4 9.0 %collective-permute-done.44.b = bf16[288,256]{1,0:T(8,128)(2,1)S(1)} collective-permute-done((bf16[288,256]{1,0:T(8,128)(2,1)S(1)}, bf16[288,256]{1,0:T(8,128)(2,1)S(1)}, u32[]{:S(2)}, u32[]{:S(2)}) %collective-permute-start.44) | collective-permute-done | bytes 147488 | tf_op jit(solution)/shard_map/ppermute | solution.py:486
  275.1 3.4 %input_far.1 = f32[1944,512]{1,0:T(8,128)} custom-call(f32[1984,512]{1,0:T(8,128)S(1)} %input_near.1.part, bf16[496,256]{1,0:T(8,128)(2,1)S(1)} %collective-permute-done.31.refs_0_, bf16[496,256]{1,0:T(8,128)(2,1)S(1)} %collective-permute-done.36.refs_1_, bf16[496,256]{1,0:T(8,128)(2,1)S(1)} %collective-permute-done.38.refs_2_, ...), custom_call_target="tpu_custom_call" | custom-call | flops 1040187392 | bytes 10600448 | tf_op jit(solution)/shard_map/input_far/pallas_call | solution.py:467
  (184 shorter events, 71.6 us)
Async XLA Ops:
  2.4 11.6 %collective-permute-start = (bf16[1984,512]{1,0:T(8,128)(2,1)S(1)}, bf16[1984,512]{1,0:T(8,128)(2,1)}, u32[]{:S(2)}, u32[]{:S(2)}) collective-permute-start(bf16[1984,512]{1,0:T(8,128)(2,1)S(1)} %pad.4.refs_0_.feats), channel_id=1, source_target_pairs={{0,1},{1,0},{2,3},{3,2},{4,5},{5,4},{6,7},{7,6},{8,9},{9,8},{10,11... | collective-permute-start | bytes 6094856 | tf_op jit(solution)/shard_map/ppermute | solution.py:486
  3.0 46.8 %collective-permute-start.1 = (bf16[1944,512]{1,0:T(8,128)(2,1)}, bf16[1944,512]{1,0:T(8,128)(2,1)}, u32[]{:S(2)}, u32[]{:S(2)}) collective-permute-start(bf16[1944,512]{1,0:T(8,128)(2,1)} %bitcast.5), channel_id=1, source_target_pairs={{0,2},{1,3},{2,0},{3,1},{4,6},{5,7},{6,4},{7,5},{8,10},{9,11},{10,... | collective-permute-start | bytes 5971976 | tf_op jit(solution)/shard_map/ppermute | solution.py:486
  17.6 32.2 %collective-permute-start.3 = (bf16[512,256]{1,0:T(8,128)(2,1)S(1)}, bf16[512,256]{1,0:T(8,128)(2,1)S(1)}, u32[]{:S(2)}, u32[]{:S(2)}) collective-permute-start(bf16[512,256]{1,0:T(8,128)(2,1)S(1)} %get-tuple-element.99), channel_id=1, source_target_pairs={{0,1},{1,0},{2,3},{3,2},{4,5},{5,4},{6,7},{7,6},{8,9},{9,8},{10,11... | collective-permute-start | bytes 786440 | tf_op jit(solution)/shard_map/ppermute | solution.py:486
  17.8 32.0 %collective-permute-start.2 = (bf16[256,512]{1,0:T(8,128)(2,1)S(1)}, bf16[256,512]{1,0:T(8,128)(2,1)S(1)}, u32[]{:S(2)}, u32[]{:S(2)}) collective-permute-start(bf16[256,512]{1,0:T(8,128)(2,1)S(1)} %get-tuple-element.97), channel_id=1, source_target_pairs={{0,1},{1,0},{2,3},{3,2},{4,5},{5,4},{6,7},{7,6},{8,9},{9,8},{10,11... | collective-permute-start | bytes 786440 | tf_op jit(solution)/shard_map/ppermute | solution.py:486
  49.9 25.2 %collective-permute-start.9 = (bf16[256,512]{1,0:T(8,128)(2,1)S(1)}, bf16[256,512]{1,0:T(8,128)(2,1)S(1)}, u32[]{:S(2)}, u32[]{:S(2)}) collective-permute-start(bf16[256,512]{1,0:T(8,128)(2,1)S(1)} %get-tuple-element.111), channel_id=1, source_target_pairs={{0,2},{1,3},{2,0},{3,1},{4,6},{5,7},{6,4},{7,5},{8,10},{9,11},{10,... | collective-permute-start | bytes 786440 | tf_op jit(solution)/shard_map/ppermute | solution.py:486
  51.8 23.4 %collective-permute-start.10 = (bf16[256,512]{1,0:T(8,128)(2,1)S(1)}, bf16[256,512]{1,0:T(8,128)(2,1)S(1)}, u32[]{:S(2)}, u32[]{:S(2)}) collective-permute-start(bf16[256,512]{1,0:T(8,128)(2,1)S(1)} %get-tuple-element.112), channel_id=1, source_target_pairs={{0,3},{1,2},{2,1},{3,0},{4,7},{5,6},{6,5},{7,4},{8,11},{9,10},{10,... | collective-permute-start | bytes 786440 | tf_op jit(solution)/shard_map/ppermute | solution.py:486
  87.2 9.3 %collective-permute-start.11 = (bf16[1984,256]{1,0:T(8,128)(2,1)S(1)}, bf16[1984,256]{1,0:T(8,128)(2,1)S(1)}, u32[]{:S(2)}, u32[]{:S(2)}) collective-permute-start(bf16[1984,256]{1,0:T(8,128)(2,1)S(1)} %hidden.1.refs_0_), channel_id=1, source_target_pairs={{0,1},{1,0},{2,3},{3,2},{4,5},{5,4},{6,7},{7,6},{8,9},{9,8},{10,11... | collective-permute-start | bytes 3047432 | tf_op jit(solution)/shard_map/ppermute | solution.py:486
  87.3 24.9 %collective-permute-start.12 = (bf16[1984,256]{1,0:T(8,128)(2,1)S(1)}, bf16[1984,256]{1,0:T(8,128)(2,1)S(1)}, u32[]{:S(2)}, u32[]{:S(2)}) collective-permute-start(bf16[1984,256]{1,0:T(8,128)(2,1)S(1)} %hidden.1.refs_0_), channel_id=1, source_target_pairs={{0,2},{1,3},{2,0},{3,1},{4,6},{5,7},{6,4},{7,5},{8,10},{9,11},{10,... | collective-permute-start | bytes 3047432 | tf_op jit(solution)/shard_map/ppermute | solution.py:486
  112.2 17.5 %collective-permute-start.14 = (bf16[512,256]{1,0:T(8,128)(2,1)}, bf16[512,256]{1,0:T(8,128)(2,1)S(1)}, u32[]{:S(2)}, u32[]{:S(2)}) collective-permute-start(bf16[512,256]{1,0:T(8,128)(2,1)} %get-tuple-element.119), channel_id=1, source_target_pairs={{0,2},{1,3},{2,0},{3,1},{4,6},{5,7},{6,4},{7,5},{8,10},{9,11},{10,... | collective-permute-start | bytes 786440 | tf_op jit(solution)/shard_map/ppermute | solution.py:486
  113.7 16.7 %collective-permute-start.15 = (bf16[512,256]{1,0:T(8,128)(2,1)S(1)}, bf16[512,256]{1,0:T(8,128)(2,1)S(1)}, u32[]{:S(2)}, u32[]{:S(2)}) collective-permute-start(bf16[512,256]{1,0:T(8,128)(2,1)S(1)} %get-tuple-element.120), channel_id=1, source_target_pairs={{0,3},{1,2},{2,1},{3,0},{4,7},{5,6},{6,5},{7,4},{8,11},{9,10},{10,... | collective-permute-start | bytes 786440 | tf_op jit(solution)/shard_map/ppermute | solution.py:486
  144.1 29.4 %collective-permute-start.19 = (bf16[1984,256]{1,0:T(8,128)(2,1)S(1)}, bf16[1984,256]{1,0:T(8,128)(2,1)S(1)}, u32[]{:S(2)}, u32[]{:S(2)}) collective-permute-start(bf16[1984,256]{1,0:T(8,128)(2,1)S(1)} %get-tuple-element.125), channel_id=1, source_target_pairs={{0,1},{1,0},{2,3},{3,2},{4,5},{5,4},{6,7},{7,6},{8,9},{9,8},{10,11... | collective-permute-start | bytes 3047432 | tf_op jit(solution)/shard_map/ppermute | solution.py:486
  146.2 27.4 %collective-permute-start.20 = (bf16[1984,256]{1,0:T(8,128)(2,1)S(1)}, bf16[1984,256]{1,0:T(8,128)(2,1)S(1)}, u32[]{:S(2)}, u32[]{:S(2)}) collective-permute-start(bf16[1984,256]{1,0:T(8,128)(2,1)S(1)} %merge.1), channel_id=1, source_target_pairs={{0,2},{1,3},{2,0},{3,1},{4,6},{5,7},{6,4},{7,5},{8,10},{9,11},{10,... | collective-permute-start | bytes 3047432 | tf_op jit(solution)/shard_map/ppermute | solution.py:486
  150.7 13.7 %collective-permute-start.17 = (bf16[4,128,512]{2,1,0:T(8,128)(2,1)S(1)}, bf16[4,128,512]{2,1,0:T(8,128)(2,1)S(1)}, u32[]{:S(2)}, u32[]{:S(2)}) collective-permute-start(bf16[4,128,512]{2,1,0:T(8,128)(2,1)S(1)} %send.6), channel_id=1, source_target_pairs={{0,4},{4,0},{8,12},{12,8},{16,20},{20,16},{24,28},{28,24},{1,5},{5... | collective-permute-start | bytes 1572872 | tf_op jit(solution)/shard_map/ppermute | solution.py:486
  165.1 7.3 %collective-permute-start.18 = (bf16[4,64,512]{2,1,0:T(8,128)(2,1)S(1)}, bf16[4,64,512]{2,1,0:T(8,128)(2,1)S(1)}, u32[]{:S(2)}, u32[]{:S(2)}) collective-permute-start(bf16[4,64,512]{2,1,0:T(8,128)(2,1)S(1)} %send.7), channel_id=1, source_target_pairs={{0,8},{4,12},{8,0},{12,4},{16,24},{20,28},{24,16},{28,20},{1,9},{5... | collective-permute-start | bytes 786440 | tf_op jit(solution)/shard_map/ppermute | solution.py:486
  173.0 16.7 %collective-permute-start.21 = (bf16[4,64,512]{2,1,0:T(8,128)(2,1)S(1)}, bf16[4,64,512]{2,1,0:T(8,128)(2,1)S(1)}, u32[]{:S(2)}, u32[]{:S(2)}) collective-permute-start(bf16[4,64,512]{2,1,0:T(8,128)(2,1)S(1)} %send.8.a), channel_id=1, source_target_pairs={{0,16},{4,20},{8,24},{12,28},{16,0},{20,4},{24,8},{28,12},{1,17},{... | collective-permute-start | bytes 786440 | tf_op jit(solution)/shard_map/ppermute | solution.py:486
  205.8 19.3 %collective-permute-start.23 = (bf16[1024,256]{1,0:T(8,128)(2,1)S(1)}, bf16[1024,256]{1,0:T(8,128)(2,1)S(1)}, u32[]{:S(2)}, u32[]{:S(2)}) collective-permute-start(bf16[1024,256]{1,0:T(8,128)(2,1)S(1)} %send.9), channel_id=1, source_target_pairs={{0,4},{4,0},{8,12},{12,8},{16,20},{20,16},{24,28},{28,24},{1,5},{5... | collective-permute-start | bytes 1572872 | tf_op jit(solution)/shard_map/ppermute | solution.py:486
  212.5 12.0 %collective-permute-start.27 = (bf16[64,2048]{1,0:T(8,128)(2,1)S(1)}, bf16[64,2048]{1,0:T(8,128)(2,1)S(1)}, u32[]{:S(2)}, u32[]{:S(2)}) collective-permute-start(bf16[64,2048]{1,0:T(8,128)(2,1)S(1)} %arrange.1.mine), channel_id=1, source_target_pairs={{0,8},{4,12},{8,0},{12,4},{16,24},{20,28},{24,16},{28,20},{1,9},{5... | collective-permute-start | bytes 786440 | tf_op jit(solution)/shard_map/ppermute | solution.py:486
  213.2 11.3 %collective-permute-start.28 = (bf16[288,256]{1,0:T(8,128)(2,1)S(1)}, bf16[288,256]{1,0:T(8,128)(2,1)S(1)}, u32[]{:S(2)}, u32[]{:S(2)}) collective-permute-start(bf16[288,256]{1,0:T(8,128)(2,1)S(1)} %group_grad.1.a), channel_id=1, source_target_pairs={{0,8},{4,12},{8,0},{12,4},{16,24},{20,28},{24,16},{28,20},{1,9},{5... | collective-permute-start | bytes 442376 | tf_op jit(solution)/shard_map/ppermute | solution.py:486
  225.8 9.4 %collective-permute-start.30 = (bf16[64,2048]{1,0:T(8,128)(2,1)S(1)}, bf16[64,2048]{1,0:T(8,128)(2,1)S(1)}, u32[]{:S(2)}, u32[]{:S(2)}) collective-permute-start(bf16[64,2048]{1,0:T(8,128)(2,1)S(1)} %slice.36), channel_id=1, source_target_pairs={{0,4},{4,0},{8,12},{12,8},{16,20},{20,16},{24,28},{28,24},{1,5},{5... | collective-permute-start | bytes 786440 | tf_op jit(solution)/shard_map/ppermute | solution.py:486
  227.3 7.8 %collective-permute-start.29 = (bf16[512,256]{1,0:T(8,128)(2,1)S(1)}, bf16[512,256]{1,0:T(8,128)(2,1)S(1)}, u32[]{:S(2)}, u32[]{:S(2)}) collective-permute-start(bf16[512,256]{1,0:T(8,128)(2,1)S(1)} %send.10), channel_id=1, source_target_pairs={{0,8},{4,12},{8,0},{12,4},{16,24},{20,28},{24,16},{28,20},{1,9},{5... | collective-permute-start | bytes 786440 | tf_op jit(solution)/shard_map/ppermute | solution.py:486
  227.8 7.3 %collective-permute-start.31 = (bf16[496,256]{1,0:T(8,128)(2,1)S(1)}, bf16[496,256]{1,0:T(8,128)(2,1)S(1)}, u32[]{:S(2)}, u32[]{:S(2)}) collective-permute-start(bf16[496,256]{1,0:T(8,128)(2,1)S(1)} %slice.37), channel_id=1, source_target_pairs={{0,2},{1,3},{2,0},{3,1},{4,6},{5,7},{6,4},{7,5},{8,10},{9,11},{10,... | collective-permute-start | bytes 761864 | tf_op jit(solution)/shard_map/ppermute | solution.py:486
  237.8 8.2 %collective-permute-start.36 = (bf16[496,256]{1,0:T(8,128)(2,1)S(1)}, bf16[496,256]{1,0:T(8,128)(2,1)S(1)}, u32[]{:S(2)}, u32[]{:S(2)}) collective-permute-start(bf16[496,256]{1,0:T(8,128)(2,1)S(1)} %get-tuple-element.176), channel_id=1, source_target_pairs={{0,2},{1,3},{2,0},{3,1},{4,6},{5,7},{6,4},{7,5},{8,10},{9,11},{10,... | collective-permute-start | bytes 761864 | tf_op jit(solution)/shard_map/ppermute | solution.py:486
  238.3 7.6 %collective-permute-start.34 = (bf16[64,2048]{1,0:T(8,128)(2,1)S(1)}, bf16[64,2048]{1,0:T(8,128)(2,1)S(1)}, u32[]{:S(2)}, u32[]{:S(2)}) collective-permute-start(bf16[64,2048]{1,0:T(8,128)(2,1)S(1)} %slice.38), channel_id=1, source_target_pairs={{0,4},{4,0},{8,12},{12,8},{16,20},{20,16},{24,28},{28,24},{1,5},{5... | collective-permute-start | bytes 786440 | tf_op jit(solution)/shard_map/ppermute | solution.py:486
  238.9 13.3 %collective-permute-start.32 = (bf16[512,256]{1,0:T(8,128)(2,1)S(1)}, bf16[512,256]{1,0:T(8,128)(2,1)S(1)}, u32[]{:S(2)}, u32[]{:S(2)}) collective-permute-start(bf16[512,256]{1,0:T(8,128)(2,1)S(1)} %send.11.a), channel_id=1, source_target_pairs={{0,16},{4,20},{8,24},{12,28},{16,0},{20,4},{24,8},{28,12},{1,17},{... | collective-permute-start | bytes 786440 | tf_op jit(solution)/shard_map/ppermute | solution.py:486
  239.5 12.7 %collective-permute-start.35 = (bf16[496,256]{1,0:T(8,128)(2,1)S(1)}, bf16[496,256]{1,0:T(8,128)(2,1)S(1)}, u32[]{:S(2)}, u32[]{:S(2)}) collective-permute-start(bf16[496,256]{1,0:T(8,128)(2,1)S(1)} %collective-permute-done.31.refs_0_), channel_id=1, source_target_pairs={{0,1},{1,0},{2,3},{3,2},{4,5},{5,4},{6,7},{7,6},{8,9},{9,8},{10,11... | collective-permute-start | bytes 761864 | tf_op jit(solution)/shard_map/ppermute | solution.py:486
  239.5 12.7 %collective-permute-start.38 = (bf16[496,256]{1,0:T(8,128)(2,1)S(1)}, bf16[496,256]{1,0:T(8,128)(2,1)S(1)}, u32[]{:S(2)}, u32[]{:S(2)}) collective-permute-start(bf16[496,256]{1,0:T(8,128)(2,1)S(1)} %get-tuple-element.175), channel_id=1, source_target_pairs={{0,2},{1,3},{2,0},{3,1},{4,6},{5,7},{6,4},{7,5},{8,10},{9,11},{10,... | collective-permute-start | bytes 761864 | tf_op jit(solution)/shard_map/ppermute | solution.py:486
  245.9 6.3 %collective-permute-start.37 = (bf16[496,256]{1,0:T(8,128)(2,1)S(1)}, bf16[496,256]{1,0:T(8,128)(2,1)S(1)}, u32[]{:S(2)}, u32[]{:S(2)}) collective-permute-start(bf16[496,256]{1,0:T(8,128)(2,1)S(1)} %collective-permute-done.36.refs_1_), channel_id=1, source_target_pairs={{0,1},{1,0},{2,3},{3,2},{4,5},{5,4},{6,7},{7,6},{8,9},{9,8},{10,11... | collective-permute-start | bytes 761864 | tf_op jit(solution)/shard_map/ppermute | solution.py:486
  252.4 10.2 %collective-permute-start.39 = (bf16[512,256]{1,0:T(8,128)(2,1)S(1)}, bf16[512,256]{1,0:T(8,128)(2,1)S(1)}, u32[]{:S(2)}, u32[]{:S(2)}) collective-permute-start(bf16[512,256]{1,0:T(8,128)(2,1)S(1)} %add.33.mine), channel_id=1, source_target_pairs={{0,8},{4,12},{8,0},{12,4},{16,24},{20,28},{24,16},{28,20},{1,9},{5... | collective-permute-start | bytes 786440 | tf_op jit(solution)/shard_map/ppermute | solution.py:486
  254.0 8.5 %collective-permute-start.41 = (bf16[496,256]{1,0:T(8,128)(2,1)S(1)}, bf16[496,256]{1,0:T(8,128)(2,1)S(1)}, u32[]{:S(2)}, u32[]{:S(2)}) collective-permute-start(bf16[496,256]{1,0:T(8,128)(2,1)S(1)} %slice.41), channel_id=1, source_target_pairs={{0,2},{1,3},{2,0},{3,1},{4,6},{5,7},{6,4},{7,5},{8,10},{9,11},{10,... | collective-permute-start | bytes 761864 | tf_op jit(solution)/shard_map/ppermute | solution.py:486
  263.1 15.4 %collective-permute-start.43 = (bf16[1024,256]{1,0:T(8,128)(2,1)S(1)}, bf16[1024,256]{1,0:T(8,128)(2,1)S(1)}, u32[]{:S(2)}, u32[]{:S(2)}) collective-permute-start(bf16[1024,256]{1,0:T(8,128)(2,1)S(1)} %double.6.mine), channel_id=1, source_target_pairs={{0,4},{4,0},{8,12},{12,8},{16,20},{20,16},{24,28},{28,24},{1,5},{5... | collective-permute-start | bytes 1572872 | tf_op jit(solution)/shard_map/ppermute | solution.py:486
  263.5 11.6 %collective-permute-start.42 = (bf16[496,256]{1,0:T(8,128)(2,1)S(1)}, bf16[496,256]{1,0:T(8,128)(2,1)S(1)}, u32[]{:S(2)}, u32[]{:S(2)}) collective-permute-start(bf16[496,256]{1,0:T(8,128)(2,1)S(1)} %collective-permute-done.41.refs_3_), channel_id=1, source_target_pairs={{0,1},{1,0},{2,3},{3,2},{4,5},{5,4},{6,7},{7,6},{8,9},{9,8},{10,11... | collective-permute-start | bytes 761864 | tf_op jit(solution)/shard_map/ppermute | solution.py:486
  264.0 10.3 %collective-permute-start.44 = (bf16[288,256]{1,0:T(8,128)(2,1)S(1)}, bf16[288,256]{1,0:T(8,128)(2,1)S(1)}, u32[]{:S(2)}, u32[]{:S(2)}) collective-permute-start(bf16[288,256]{1,0:T(8,128)(2,1)S(1)} %add.32.a), channel_id=1, source_target_pairs={{0,16},{4,20},{8,24},{12,28},{16,0},{20,4},{24,8},{28,12},{1,17},{... | collective-permute-start | bytes 442376 | tf_op jit(solution)/shard_map/ppermute | solution.py:486
  (45 other events, 394.6 us)

commit v2 on v1

--- a/solution.py
+++ b/solution.py
@@ -101,14 +101,27 @@
     out[...] = sum(dot(f[...], wk) for f, wk in zip(feats, ws))
 
 
-def far_kernel(dims, live, part, *refs):
-    *feats, w, out, spread, acc = refs
-    share = feats[0].shape[1]
-    me = dims[2]
+def part_far_kernel(dims, own, beside, *refs):
+    n = len(refs) // 4
+    ws, outs, rows, passed = (refs[i * n : (i + 1) * n] for i in range(4))
+    share = own.shape[1]
+    core = lax.bitwise_and(dims[2], 1)
+    mine = pl.ds(pl.multiple_of(core * share, share), share)
+    other = pl.ds(pl.multiple_of((1 - core) * share, share), share)
+    for w, out in zip(ws, outs):
+        out[...] = (dot(own[...], w[mine, :]) + dot(beside[...], w[other, :])).astype(BF16)
+
+    @pl.when(pl.program_id(0) == 0)
+    def _():
+        for w, row, pass_on in zip(ws, rows, passed):
+            row[...] = w[mine, :]
+            pass_on[...] = w[other, :]
+
+
+def far_kernel(live, part, *refs):
+    *got, out, spread, acc = refs
     start_sums(acc)
-    z = part[...]
-    for k, f in enumerate(feats, 2):
-        z += dot(f[...], w[pl.ds(pl.multiple_of((me ^ k) * share, share), share), :])
+    z = part[...] + sum(g[...].astype(F32) for g in got)
     m = widen(live[...], z.shape[1])
     z = jnp.where(m > 0.0, z, 0.0)
     out[...] = z
@@ -353,12 +366,27 @@
 
 
 def reduce_grad_kernel(dims, d_red, *refs):
+    *feats, out, rest = refs
+    share = feats[0].shape[1]
+    me = dims[2]
+    for k in range(2):
+        rows = pl.ds(pl.multiple_of((me ^ k) * share, share), share)
+        out[rows, :] = dot_tn(feats[k][...], d_red[...]).astype(BF16)
+    for k, f in enumerate(feats[2:]):
+        rest[k] = dot_tn(f[...], d_red[0 : f.shape[0]])
+
+
+def reduce_grad_rest_kernel(dims, d_red, near, rest, *refs):
     *feats, out = refs
     share = feats[0].shape[1]
     me = dims[2]
+    for k in range(2):
+        rows = pl.ds(pl.multiple_of((me ^ k) * share, share), share)
+        out[rows, :] = near[rows, :]
     for k, f in enumerate(feats):
-        rows = pl.ds(pl.multiple_of((me ^ k) * share, share), share)
-        out[rows, :] = dot_tn(f[...], d_red[0 : f.shape[0]]).astype(BF16)
+        rows = pl.ds(pl.multiple_of((me ^ (k + 2)) * share, share), share)
+        first = d_red.shape[0] - f.shape[0]
+        out[rows, :] = (rest[k] + dot_tn(f[...], d_red[first:])).astype(BF16)
 
 
 def features_grad_kernel(part, *refs):
@@ -369,8 +397,8 @@
 
 def pick_kernel(dims, w_expand, w_reduce, gain, shift, cot, *outs):
     me = dims[2]
-    n = (len(outs) - 3) // 2
-    cols, rows, rest = outs[:n], outs[n : 2 * n], outs[2 * n :]
+    n = len(outs) - 5
+    cols, rows, rest = outs[:n], outs[n : n + 2], outs[n + 2 :]
     share = rows[0].shape[0]
 
     @pl.when(pl.program_id(0) == 0)
@@ -378,7 +406,8 @@
         for k in range(n):
             at = pl.ds(pl.multiple_of((me ^ k) * share, share), share)
             cols[k][...] = w_expand[:, at]
-            rows[k][...] = w_reduce[at, :]
+            if k < 2:
+                rows[k][...] = w_reduce[at, :]
         at = pl.ds(pl.multiple_of(me * share, share), share)
         rest[0][...] = gain[:, at]
         rest[1][...] = shift[:, at]
@@ -558,7 +587,10 @@
 
     feats = features.transpose(1, 2, 0, 3).reshape(rows, share)
     ends = ((0, padded - rows), (0, 0))
-    first = gather_y(feats, n_chan)
+    even = [k for k in others[2:] if k % 2 == 0]
+    at = [lax.bitwise_and(me ^ k, n_chan - 2) * share for k in even]
+    w_far = [lax.dynamic_slice_in_dim(w_reduce, o, 2 * share, 0) for o in at]
+    w_far = [swap(w, "chan", n_chan, k) for k, w in zip(even, w_far)]
     own = jnp.pad(feats, ends)
     beside = swap(own, "chan", n_chan, 1)
 
@@ -577,31 +609,37 @@
         line_of, (gain_one, shift_one, gain_two, shift_two)
     )
 
+    got = call(
+        part_far_kernel,
+        [shape((padded, width), BF16)] * len(even) + [shape((share, width), BF16)] * 2 * len(even),
+        [dims, own, beside, *w_far],
+        flops=2 * len(even) * mm, name="part_far", steps=STEPS, smem=True,
+    )
+    parts, rows_far, passed = (got[i * len(even) : (i + 1) * len(even)] for i in range(3))
+    got = [swap(p, "chan", n_chan, k) for k, p in zip(even, parts)]
+
     *picked, gain_c, shift_c, cot = call(
         pick_kernel,
-        [shape((width, share), BF16)] * n_chan + [shape((share, width), BF16)] * n_chan
+        [shape((width, share), BF16)] * n_chan + [shape((share, width), BF16)] * 2
         + [shape((1, share), F32)] * 2 + [shape((padded, share), BF16)],
-        [dims, w_expand, w_reduce, line_of(gain_three), line_of(shift_three),
+        [dims, after(w_expand, *parts), w_reduce, line_of(gain_three), line_of(shift_three),
          cotangent.transpose(1, 2, 0, 3).reshape(rows, -1)],
         flops=mm, name="pick", smem=True, steps=STEPS,
     )
-
     part = call(
-        near_kernel, [shape((padded, width), F32)], [dims, own, beside, w_reduce],
+        near_kernel, [shape((padded, width), F32)], [dims, after(own, *parts), beside, w_reduce],
         flops=2 * mm, name="near", steps=STEPS, smem=True,
     )
     w_cols = [picked[0], swap(after(picked[1], part), "chan", n_chan, 1)]
     w_rows = [picked[n_chan], swap(after(picked[n_chan + 1], part), "chan", n_chan, 1)]
-    ready = (part, live, cot, taps, gain_c, shift_c, w_cols[1], w_rows[1], *picked)
-    first = {k: after(v, *ready) for k, v in first.items()}
-    w_cols += [swap(after(picked[k], *first.values()), "chan", n_chan, k) for k in others[2:]]
-    first = gather_core(first, n_chan)
-    far = [first[k] for k in others[2:]]
+    for row, pass_on in zip(rows_far, passed):
+        w_rows += [row, swap(after(pass_on, part), "chan", n_chan, 1)]
+    ready = (part, live, cot, taps, gain_c, shift_c, w_cols[1], *w_rows, *picked)
+    got = [after(v, *ready) for v in got]
+    w_cols += [swap(after(picked[k], *got), "chan", n_chan, k) for k in others[2:]]
     z, spread = call(
-        far_kernel,
-        [shape((padded, width), F32), shape((1, 3, width), F32)],
-        [dims, live, part, *far, w_reduce], [acc(3, width)],
-        flops=(n_chan - 2) * mm, name="far", steps=STEPS, smem=True,
+        far_kernel, [shape((padded, width), F32), shape((1, 3, width), F32)],
+        [live, part, *got], [acc(3, width)], flops=mm, name="far", steps=STEPS,
     )
     got_one = batch_sum_stepwise(spread, n_batch)
 
@@ -631,9 +669,8 @@
         flops=2 * mm, name="expand_near", steps=STEPS,
     )
     first = {k: after(v, part, slope_one, slope_two, *w_cols) for k, v in first.items()}
-    w_rows += [
-        swap(after(picked[n_chan + k], *first.values()), "chan", n_chan, k) for k in others[2:]
-    ]
+    half = padded * 42 // 64 // 16 * 16
+    far_halves = [gather_y(after(own, *first.values())[:half], n_chan)]
     first = gather_core(first, n_chan)
     hidden_all = [hidden_two, beside_two] + [first[k] for k in others if k > 1]
     expanded, spread = call(
@@ -647,7 +684,7 @@
         [live, expanded, got_one, got_three, gain_c, shift_c, own, cot], [acc(2, share)],
         flops=4 * mm, name="third", steps=STEPS,
     )
-    totals_three = batch_sum(after(spread, *w_rows))
+    totals_three = batch_sum(spread)
     top = n_chan - 1
     d_expanded, sent, sums_three = call(
         d_expanded_kernel,
@@ -657,9 +694,10 @@
         flops=2 * mm, name="d_expanded", steps=STEPS,
     )
     early = [0, 1]
+    far_halves[0] = {k: after(v, d_expanded) for k, v in far_halves[0].items()}
     d_zero, d_near = call(
         back_expand_kernel, [shape((padded, width), F32), shape((padded, width), BF16)],
-        [after(d_expanded, sent)] + [w_cols[k] for k in early], flops=2 * mm,
+        [after(d_expanded, sent, *far_halves[0].values())] + [w_cols[k] for k in early], flops=2 * mm,
         name="back_expand", steps=STEPS,
     )
 
@@ -690,22 +728,26 @@
         expand_grad_kernel, [shape((n_chan, width, share), BF16)],
         [after(d_expanded, far_sum), *hidden_all], flops=n_chan * mm, name="expand_grad",
     )
+    expand_terms = [expand_part]
+    bits = n_batch.bit_length() - 1
+    send = send_of(dims, expand_terms, 0)
+    got = swap(send, "batch", n_batch, 1)
     block_out = call(
         block_kernel, [shape((rows, share), BF16)],
-        [live, after(expanded, expand_part), got_one, got_three, gain_c, shift_c, own],
+        [live, after(expanded, send), got_one, got_three, gain_c, shift_c, own],
         flops=2 * mm, name="block", steps=STEPS,
     )
-    expand_terms = [expand_part]
-    bits = n_batch.bit_length() - 1
-    for s in range(2):
-        send = send_of(dims, expand_terms, s)
-        expand_terms.append(swap(send, "batch", n_batch, 1 << s))
+    expand_terms.append(after(got, block_out))
+    send = send_of(dims, expand_terms, 1)
+    expand_terms.append(swap(send, "batch", n_batch, 2))
     for t in range(2, bits - 1):
         expand_send = send_of(dims, expand_terms, t)
         expand_terms.append(swap(expand_send, "batch", n_batch, 1 << t))
     mine = send_of(dims, expand_terms, bits - 1, True)
     expand_other = swap(mine, "batch", n_batch, 1 << (bits - 1))
-    terms[0] = after(d_zero, mine, block_out)
+    far_halves[0] = gather_core({k: after(v, far_sum) for k, v in far_halves[0].items()}, n_chan)
+    terms[0] = after(d_zero, *far_halves[0].values())
+    far_halves.append(gather_y(after(own, terms[-1], mine)[half:], n_chan))
     d_two, spread = call(
         d_two_kernel, [shape((padded, width), F32), shape((n_batch, 2, width), F32)],
         [slope_two, grouped, got_one, got_two, *terms], [acc(2, width)], flops=mm, name="d_two", steps=STEPS,
@@ -721,15 +763,22 @@
         split_kernel, [shape(mine.shape[1:], BF16)] * n_chan,
         [mine, after(expand_other, d_one)], name="split",
     )
-    totals_one = batch_sum(after(spread, *parts))
+    far_halves[1] = {k: after(v, d_one) for k, v in far_halves[1].items()}
+    totals_one = batch_sum(after(spread, *parts, *far_halves[1].values()))
     d_reduced, sums_one = call(
         d_reduced_kernel, [shape((padded, width), BF16), shape((2, width), F32)],
         [live, d_one, z, got_one, totals_one, gain_one], flops=mm, name="d_reduced", steps=STEPS,
     )
+    far_halves[1] = gather_core(far_halves[1], n_chan)
+    firsts, lasts = ([far_halves[h][k] for k in others[2:]] for h in range(2))
+    tail, rest = call(
+        reduce_grad_kernel,
+        [shape((n_chan * share, width), BF16), shape((n_chan - 2, share, width), F32)],
+        [dims, d_reduced, own, beside, *firsts], flops=n_chan * mm, name="reduce_grad", smem=True,
+    )
     tail = call(
-        reduce_grad_kernel,
-        [shape((n_chan * share, width), BF16)], [dims, d_reduced, own, beside, *far],
-        flops=n_chan * mm, name="reduce_grad", smem=True,
+        reduce_grad_rest_kernel, [shape((n_chan * share, width), BF16)],
+        [dims, d_reduced, tail, rest, *lasts], flops=mm, name="reduce_grad_rest", smem=True,
     )
     d_beside = swap(d_reduced, "chan", n_chan, 1)
     tail_terms = [after(tail, d_beside)]
@@ -758,7 +807,6 @@
                 [shape((9 * group_width, width), BF16)], [hid, after(d_grouped, *parts)],
                 [tall], flops=mm, name="group_grad",
             )
-            group_other = swap(group_part, "batch", n_batch, 2)
             cols[1] = after(cols[1], group_part)
             cols = call(
                 arrange_kernel, [shape((mine.shape[1], n_chan * share), BF16)], [dims, *cols],
@@ -766,9 +814,6 @@
             )
             for t in reversed(range(1, top)):
                 other = swap(cols, "batch", n_batch, 1 << t)
-                if t == 1:
-                    group_part = add(group_part, after(group_other, cols))
-                    other = after(other, group_part)
                 cols = double(dims, cols, other, t)
             got = after(got, cols)
         elif s == 1:
@@ -778,33 +823,37 @@
         tail_terms.append(got)
     mine = send_of(dims, tail_terms, top, True)
     other = swap(mine, "batch", n_batch, 1 << top)
-    part = call(
-        features_grad_kernel, [shape((padded, share), F32)],
-        [d_pre, after(d_reduced, mine), d_beside, *w_rows[:2]], flops=2 * mm,
-        name="input_near", steps=STEPS,
-    )
-    others_cols.append(swap(after(cols, part)[split:], "batch", n_batch, 1))
-    moved = next_far(part)
-    others_cols[0] = after(others_cols[0], part)
+    others_cols.append(swap(after(cols, mine)[split:], "batch", n_batch, 1))
+    moved = next_far(mine)
     expand_grad = double(dims, cols, others_cols, 0, F32)
-    group_other = swap(after(group_part, part), "batch", n_batch, 1)
+    group_other = swap(after(group_part, mine), "batch", n_batch, 1)
     group_part = add(group_part, after(group_other, expand_grad))
-    moved = next_far(part)
+    moved = next_far(expand_grad)
     tail = add(mine, after(other, group_part, *moved))
     for s in reversed(range(top)):
         got = swap(tail, "batch", n_batch, 1 << s)
         before = next_far(tail)
+        if s == top - 1:
+            group_other = swap(after(group_part, tail), "batch", n_batch, 2)
+            part = call(
+                features_grad_kernel, [shape((padded, share), F32)],
+                [d_pre, after(d_reduced, tail), d_beside, *w_rows[:2]], flops=2 * mm,
+                name="input_near", steps=STEPS,
+            )
+            group_part = add(group_part, after(group_other, part))
+            before = (group_part, *before)
         if s == 0:
-            for t in range(2, bits):
-                group_part = after(group_part, tail)
-                group_other = swap(group_part, "batch", n_batch, 1 << t)
-                group_part = add(group_part, group_other, BF16 if t + 1 < bits else F32)
             features_grad = call(
                 input_far_kernel, [shape((rows, share), F32)],
                 [after(part, tail), *[d[k] for k in others[2:] for d in d_far], *w_rows[2:]],
                 flops=(n_chan - 2) * mm, name="input_far", steps=STEPS,
             )
-            before = (features_grad, group_part)
+            for t in range(2, bits):
+                group_part = after(group_part, tail)
+                group_other = swap(group_part, "batch", n_batch, 1 << t)
+                group_other = after(group_other, features_grad)
+                group_part = add(group_part, group_other, BF16 if t + 1 < bits else F32)
+            before = (group_part,)
         tail = double(dims, tail, after(got, *before), s, BF16 if s else F32)
     reduce_grad, group_grad = tail, group_part
 

time: 281 us -> 271 us (0.964)
  waiting for transfers between devices: 110 us -> 104 us
  local copies, waits for them, and re-layouts: 14.4 us -> 9.61 us
    unnamed x64 -> x72, local copies, waits for them, and re-layouts: 10.7 us -> 4.96 us
    ppermute x45 -> x48, waiting for transfers between devices: 110 us -> 104 us  [swap(): return lax.ppermute(v, axis, [(i, i ^ k) for i in range(size)])]
    pallas_call x41 -> x43, Pallas kernels: 69.2 us -> 69.6 us  [call(): pl.pallas_call(kernel, out_shape=list(outs), grid=(steps,) if steps else...]
    ppermute x45 -> x48, starting transfers between devices: 32.6 us -> 32.6 us  [swap(): return lax.ppermute(v, axis, [(i, i ^ k) for i in range(size)])]
  transfers between devices with their start and end apart: 45 -> 48, of which waited for: 19 -> 19; matrix products, arithmetic and copies ran while one was open for 2% -> 2% of each run, Pallas kernels for 20% -> 20%
where the time goes in v2:
time: 271 us
  waiting for transfers between devices  104 us (38%)
  Pallas kernels  69.6 us (26%)
  blocking collectives  49.6 us (18%)
  starting transfers between devices  32.6 us (12%)
  local copies, waits for them, and re-layouts  9.61 us (4%)
  between operations  2.8 us (1%)
    ppermute x48, waiting for transfers between devices, swap(): return lax.ppermute(v, axis, [(i, i ^ k) for i in range(size)])  104 us
    pallas_call x43, Pallas kernels, call(): pl.pallas_call(kernel, out_shape=list(outs), grid=(steps,) if steps else...  69.6 us
    all_to_all x5, blocking collectives, batch_sum(): return lax.all_to_all(spread, 'batch', 0, 0)  49.6 us
    ppermute x48, starting transfers between devices, swap(): return lax.ppermute(v, axis, [(i, i ^ k) for i in range(size)])  32.6 us
  transfers between devices with their start and end apart: 48, of which 19 were waited for; matrix products, arithmetic and copies ran while one was open for 2% of the time, Pallas kernels for 20%

profile of v2, /device:TPU:0, one launch (start us, length us, event | category | flops | bytes accessed | tf_op | source)
XLA Modules:
  0.0 271.0 jit_solution(4860383331914654354)
XLA Ops:
  3.8 2.5 collective-permute-start.1
  7.7 11.5 %collective-permute-done.1.refs_0_ = bf16[1024,256]{1,0:T(8,128)(2,1)} collective-permute-done((bf16[1024,256]{1,0:T(8,128)(2,1)}, bf16[1024,256]{1,0:T(8,128)(2,1)}, u32[]{:S(2)}, u32[]{:S(2)}) %collective-permute-start.1) | collective-permute-done | bytes 524320 | tf_op jit(solution)/shard_map/ppermute | solution.py:515
  19.2 4.1 %part_far.1 = (bf16[1984,256]{1,0:T(8,128)(2,1)S(1)}, bf16[512,256]{1,0:T(8,128)(2,1)S(1)}, bf16[512,256]{1,0:T(8,128)(2,1)S(1)}) custom-call(s32[5]{0:T(128)S(1)} %stack.11.dims, bf16[1984,512]{1,0:T(8,128)(2,1)S(1)} %pad.4.own.refs_0_.feats, bf16[1984,512]{1,0:T(8,128)(2,1)} %collective-permute-done.beside.refs_1_, ...), custom_call_target="tpu_custom_call" | custom-call | flops 1040187392 | bytes 6127636 | tf_op jit(solution)/shard_map/part_far/pallas_call | solution.py:496
  25.3 3.6 %near.1.part = f32[1984,256]{1,0:T(8,128)S(1)} custom-call(s32[5]{0:T(128)S(1)} %stack.11.dims, bf16[1984,512]{1,0:T(8,128)(2,1)S(1)} %pad.4.own.refs_0_.feats, bf16[1984,512]{1,0:T(8,128)(2,1)} %collective-permute-done.beside.refs_1_, bf16[2048,256]{1,0:T(8,128)(2,1)S(1)} %copy-done.5), custom_call_target="tpu_custom_call" | custom-call | flops 1040187392 | bytes 7143444 | tf_op jit(solution)/shard_map/near/pallas_call | solution.py:496
  30.8 2.5 fusion.5.live
  33.6 14.1 %collective-permute-done.2.refs_0_ = bf16[1984,256]{1,0:T(8,128)(2,1)S(1)} collective-permute-done((bf16[1984,256]{1,0:T(8,128)(2,1)S(1)}, bf16[1984,256]{1,0:T(8,128)(2,1)S(1)}, u32[]{:S(2)}, u32[]{:S(2)}) %collective-permute-start.2) | collective-permute-done | bytes 1015840 | tf_op jit(solution)/shard_map/ppermute | solution.py:515
  49.8 3.7 %collective-permute-start.8 = (f32[1,3,256]{2,1,0:T(4,128)S(1)}, f32[1,3,256]{2,1,0:T(4,128)S(1)}, u32[]{:S(2)}, u32[]{:S(2)}) collective-permute-start(f32[1,3,256]{2,1,0:T(4,128)S(1)} %get-tuple-element.121.refs_0_), channel_id=1, source_target_pairs={{0,24},{4,28},{8,16},{12,20},{16,8},{20,12},{24,0},{28,4},{1,25},{... | collective-permute-start | bytes 9224 | tf_op jit(solution)/shard_map/ppermute | solution.py:515
  55.3 2.7 collective-permute-done.7.refs_2_
  61.7 3.5 %conv.1 = (f32[1984,256]{1,0:T(8,128)S(1)}, f32[1984,256]{1,0:T(8,128)S(1)}, f32[8,2,256]{2,1,0:T(2,128)S(1)}) custom-call(f32[1984,128]{1,0:T(8,128)S(1)} %fusion.5.live, f32[1984,256]{1,0:T(8,128)S(1)} %get-tuple-element.120.z, f32[2,3,256]{2,1,0:T(4,128)S(1)} %pair.1.got.counts, f32[1,256]{1,0:T(1,128)S(1)} %bitcast.40, f32[1,256]{1,0:T(1,128)S(1)} %bitcast.43, ...), custom_call_target="tpu_custom_call" | custom-call | flops 2340421632 | bytes 8314880 | tf_op jit(solution)/shard_map/conv/pallas_call | solution.py:496
  66.6 10.5 %all_to_all.25.got.got_two = f32[8,2,256]{2,1,0:T(2,128)S(1)} all-to-all(f32[8,2,256]{2,1,0:T(2,128)S(1)} %get-tuple-element.126), channel_id=1, replica_groups=mesh['batch'=8,'chan'=4] {'batch'}, dimensions={0} | all-to-all | bytes 32768 | tf_op jit(solution)/shard_map/all_to_all | solution.py:519
  79.3 2.5 slope_one.1.slope
  83.2 2.5 slope_two.1.slope
  88.7 14.9 %collective-permute-done.13.refs_0_.refs_2_ = bf16[1984,256]{1,0:T(8,128)(2,1)S(1)} collective-permute-done((bf16[1984,256]{1,0:T(8,128)(2,1)S(1)}, bf16[1984,256]{1,0:T(8,128)(2,1)S(1)}, u32[]{:S(2)}, u32[]{:S(2)}) %collective-permute-start.13) | collective-permute-done | bytes 1015840 | tf_op jit(solution)/shard_map/ppermute | solution.py:515
  108.2 9.1 %all_to_all.26.got = f32[8,2,512]{2,1,0:T(2,128)S(1)} all-to-all(f32[8,2,512]{2,1,0:T(2,128)S(1)} %get-tuple-element.129), channel_id=1, replica_groups=mesh['batch'=8,'chan'=4] {'batch'}, dimensions={0} | all-to-all | bytes 65536 | tf_op jit(solution)/shard_map/all_to_all | solution.py:519
  117.3 3.9 %third.1 = (f32[1984,512]{1,0:T(8,128)S(1)}, f32[8,2,512]{2,1,0:T(2,128)S(1)}) custom-call(f32[1984,128]{1,0:T(8,128)S(1)} %fusion.5.live, f32[1984,512]{1,0:T(8,128)S(1)} %get-tuple-element.140.e, f32[2,3,256]{2,1,0:T(4,128)S(1)} %pair.1.got.counts, f32[8,2,512]{2,1,0:T(2,128)S(1)} %all_to_all.26.got, f32[1,512]{1,0:T(1,128)S(1)} %get-tuple-element.106.gain, ...), custom_call_target="tpu_custom_call" | custom-call | flops 2080374784 | bytes 13281280 | tf_op jit(solution)/shard_map/third/pallas_call | solution.py:496
  121.2 9.1 %all_to_all.27.totals = f32[8,2,512]{2,1,0:T(2,128)S(1)} all-to-all(f32[8,2,512]{2,1,0:T(2,128)S(1)} %get-tuple-element.131), channel_id=1, replica_groups=mesh['batch'=8,'chan'=4] {'batch'}, dimensions={0} | all-to-all | bytes 65536 | tf_op jit(solution)/shard_map/all_to_all | solution.py:519
  132.3 3.0 %collective-permute-done.15.refs_2_ = bf16[1296,512]{1,0:T(8,128)(2,1)S(1)} collective-permute-done((bf16[1296,512]{1,0:T(8,128)(2,1)S(1)}, bf16[1296,512]{1,0:T(8,128)(2,1)S(1)}, u32[]{:S(2)}, u32[]{:S(2)}) %collective-permute-start.15) | collective-permute-done | bytes 1327136 | tf_op jit(solution)/shard_map/ppermute | solution.py:515
  143.9 5.1 %block.1 = bf16[1944,512]{1,0:T(8,128)(2,1)} custom-call(f32[1984,128]{1,0:T(8,128)S(1)} %fusion.5.live, f32[1984,512]{1,0:T(8,128)S(1)} %get-tuple-element.140.e, f32[2,3,256]{2,1,0:T(4,128)S(1)} %pair.1.got.counts, f32[8,2,512]{2,1,0:T(2,128)S(1)} %all_to_all.26.got, f32[1,512]{1,0:T(1,128)S(1)} %get-tuple-element.106.gain, ...), custom_call_target="tpu_custom_call" | custom-call | flops 1040187392 | bytes 9144320 | tf_op jit(solution)/shard_map/block/pallas_call | solution.py:496
  149.0 8.5 %collective-permute-done.20.refs_1_ = bf16[4,128,512]{2,1,0:T(8,128)(2,1)S(1)} collective-permute-done((bf16[4,128,512]{2,1,0:T(8,128)(2,1)S(1)}, bf16[4,128,512]{2,1,0:T(8,128)(2,1)S(1)}, u32[]{:S(2)}, u32[]{:S(2)}) %collective-permute-start.20) | collective-permute-done | bytes 524320 | tf_op jit(solution)/shard_map/ppermute | solution.py:515
  158.6 7.5 %collective-permute-done.21.refs_2_ = bf16[4,64,512]{2,1,0:T(8,128)(2,1)S(1)} collective-permute-done((bf16[4,64,512]{2,1,0:T(8,128)(2,1)S(1)}, bf16[4,64,512]{2,1,0:T(8,128)(2,1)S(1)}, u32[]{:S(2)}, u32[]{:S(2)}) %collective-permute-start.21) | collective-permute-done | bytes 262176 | tf_op jit(solution)/shard_map/ppermute | solution.py:515
  170.2 11.7 %all_to_all.28.totals = f32[8,2,256]{2,1,0:T(2,128)S(1)} all-to-all(f32[8,2,256]{2,1,0:T(2,128)S(1)} %get-tuple-element.145), channel_id=1, replica_groups=mesh['batch'=8,'chan'=4] {'batch'}, dimensions={0} | all-to-all | bytes 32768 | tf_op jit(solution)/shard_map/all_to_all | solution.py:519
  181.9 3.5 %conv_back.1 = (f32[1984,256]{1,0:T(8,128)S(1)}, f32[1984,256]{1,0:T(8,128)S(1)}, f32[8,2,256]{2,1,0:T(2,128)S(1)}, f32[2,256]{1,0:T(2,128)S(1)}) custom-call(f32[1984,128]{1,0:T(8,128)S(1)} %fusion.5.live, f32[1984,256]{1,0:T(8,128)S(1)} %get-tuple-element.144.d_two, f32[1984,256]{1,0:T(8,128)S(1)} %get-tuple-element.122.z.grouped, ...), custom_call_target="tpu_custom_call" | custom-call | flops 2340421632 | bytes 14443520 | tf_op jit(solution)/shard_map/conv_back/pallas_call | solution.py:496
  185.6 9.2 %all_to_all.29.totals = f32[8,2,256]{2,1,0:T(2,128)S(1)} all-to-all(f32[8,2,256]{2,1,0:T(2,128)S(1)} %get-tuple-element.156), channel_id=1, replica_groups=mesh['batch'=8,'chan'=4] {'batch'}, dimensions={0} | all-to-all | bytes 32768 | tf_op jit(solution)/shard_map/all_to_all | solution.py:519
  196.6 3.7 %reduce_grad.1 = (bf16[2048,256]{1,0:T(8,128)(2,1)S(1)}, f32[2,512,256]{2,1,0:T(8,128)S(1)}) custom-call(s32[5]{0:T(128)S(1)} %stack.11.dims, bf16[1984,256]{1,0:T(8,128)(2,1)S(1)} %get-tuple-element.180.d_red.refs_0_, bf16[1984,512]{1,0:T(8,128)(2,1)S(1)} %pad.4.own.refs_0_.feats, bf16[1984,512]{1,0:T(8,128)(2,1)} %collective-permute-done.beside.refs_1_, ...), custom_call_target="tpu_custom_call" | custom-call | flops 2080374784 | bytes 9830420 | tf_op jit(solution)/shard_map/reduce_grad/pallas_call | solution.py:496
  204.6 2.9 %group_grad.1.a = bf16[288,256]{1,0:T(8,128)(2,1)S(1)} custom-call(f32[1984,256]{1,0:T(8,128)S(1)} %copy-done.7, f32[1984,256]{1,0:T(8,128)S(1)} %get-tuple-element.164.d_grouped), custom_call_target="tpu_custom_call" | custom-call | flops 520093696 | bytes 4210688 | tf_op jit(solution)/shard_map/group_grad/pallas_call | solution.py:496
  209.6 8.1 %collective-permute-done.30.refs_0_ = bf16[64,2048]{1,0:T(8,128)(2,1)S(1)} collective-permute-done((bf16[64,2048]{1,0:T(8,128)(2,1)S(1)}, bf16[64,2048]{1,0:T(8,128)(2,1)S(1)}, u32[]{:S(2)}, u32[]{:S(2)}) %collective-permute-start.30) | collective-permute-done | bytes 262176 | tf_op jit(solution)/shard_map/ppermute | solution.py:515
  221.5 6.7 %collective-permute-done.33.refs_0_ = bf16[496,256]{1,0:T(8,128)(2,1)S(1)} collective-permute-done((bf16[496,256]{1,0:T(8,128)(2,1)S(1)}, bf16[496,256]{1,0:T(8,128)(2,1)S(1)}, u32[]{:S(2)}, u32[]{:S(2)}) %collective-permute-start.33) | collective-permute-done | bytes 253984 | tf_op jit(solution)/shard_map/ppermute | solution.py:515
  230.8 4.8 %collective-permute-done.36.refs_1_ = bf16[64,2048]{1,0:T(8,128)(2,1)S(1)} collective-permute-done((bf16[64,2048]{1,0:T(8,128)(2,1)S(1)}, bf16[64,2048]{1,0:T(8,128)(2,1)S(1)}, u32[]{:S(2)}, u32[]{:S(2)}) %collective-permute-start.36) | collective-permute-done | bytes 262176 | tf_op jit(solution)/shard_map/ppermute | solution.py:515
  238.6 5.7 %collective-permute-done.35.b = bf16[288,256]{1,0:T(8,128)(2,1)S(1)} collective-permute-done((bf16[288,256]{1,0:T(8,128)(2,1)S(1)}, bf16[288,256]{1,0:T(8,128)(2,1)S(1)}, u32[]{:S(2)}, u32[]{:S(2)}) %collective-permute-start.35) | collective-permute-done | bytes 147488 | tf_op jit(solution)/shard_map/ppermute | solution.py:515
  250.8 4.8 %collective-permute-done.42.b = bf16[288,256]{1,0:T(8,128)(2,1)S(1)} collective-permute-done((bf16[288,256]{1,0:T(8,128)(2,1)S(1)}, bf16[288,256]{1,0:T(8,128)(2,1)S(1)}, u32[]{:S(2)}, u32[]{:S(2)}) %collective-permute-start.42) | collective-permute-done | bytes 147488 | tf_op jit(solution)/shard_map/ppermute | solution.py:515
  258.6 3.4 %input_far.1 = f32[1944,512]{1,0:T(8,128)} custom-call(f32[1984,512]{1,0:T(8,128)S(1)} %input_near.1.part, bf16[496,256]{1,0:T(8,128)(2,1)S(1)} %collective-permute-done.33.refs_0_, bf16[496,256]{1,0:T(8,128)(2,1)S(1)} %collective-permute-done.38.refs_1_, bf16[496,256]{1,0:T(8,128)(2,1)S(1)} %collective-permute-done.40.refs_2_, ...), custom_call_target="tpu_custom_call" | custom-call | flops 1040187392 | bytes 10600448 | tf_op jit(solution)/shard_map/input_far/pallas_call | solution.py:496
  262.0 5.8 %collective-permute-done.47.b = bf16[288,256]{1,0:T(8,128)(2,1)S(1)} collective-permute-done((bf16[288,256]{1,0:T(8,128)(2,1)S(1)}, bf16[288,256]{1,0:T(8,128)(2,1)S(1)}, u32[]{:S(2)}, u32[]{:S(2)}) %collective-permute-start.47) | collective-permute-done | bytes 147488 | tf_op jit(solution)/shard_map/ppermute | solution.py:515
  (204 shorter events, 73.1 us)
Async XLA Ops:
  2.4 16.8 %collective-permute-start = (bf16[1984,512]{1,0:T(8,128)(2,1)S(1)}, bf16[1984,512]{1,0:T(8,128)(2,1)}, u32[]{:S(2)}, u32[]{:S(2)}) collective-permute-start(bf16[1984,512]{1,0:T(8,128)(2,1)S(1)} %pad.4.own.refs_0_.feats), channel_id=1, source_target_pairs={{0,1},{1,0},{2,3},{3,2},{4,5},{5,4},{6,7},{7,6},{8,9},{9,8},{10,11... | collective-permute-start | bytes 6094856 | tf_op jit(solution)/shard_map/ppermute | solution.py:515
  3.8 15.4 %collective-permute-start.1 = (bf16[1024,256]{1,0:T(8,128)(2,1)}, bf16[1024,256]{1,0:T(8,128)(2,1)}, u32[]{:S(2)}, u32[]{:S(2)}) collective-permute-start(bf16[1024,256]{1,0:T(8,128)(2,1)} %constant_dynamic-slice_fusion), channel_id=1, source_target_pairs={{0,2},{1,3},{2,0},{3,1},{4,6},{5,7},{6,4},{7,5},{8,10},{9,11},{10,... | collective-permute-start | bytes 1572872 | tf_op jit(solution)/shard_map/ppermute | solution.py:515
  23.4 24.3 %collective-permute-start.2 = (bf16[1984,256]{1,0:T(8,128)(2,1)S(1)}, bf16[1984,256]{1,0:T(8,128)(2,1)S(1)}, u32[]{:S(2)}, u32[]{:S(2)}) collective-permute-start(bf16[1984,256]{1,0:T(8,128)(2,1)S(1)} %get-tuple-element.102), channel_id=1, source_target_pairs={{0,2},{1,3},{2,0},{3,1},{4,6},{5,7},{6,4},{7,5},{8,10},{9,11},{10,... | collective-permute-start | bytes 3047432 | tf_op jit(solution)/shard_map/ppermute | solution.py:515
  47.7 18.9 %collective-permute-start.10 = (bf16[256,512]{1,0:T(8,128)(2,1)S(1)}, bf16[256,512]{1,0:T(8,128)(2,1)S(1)}, u32[]{:S(2)}, u32[]{:S(2)}) collective-permute-start(bf16[256,512]{1,0:T(8,128)(2,1)S(1)} %get-tuple-element.124), channel_id=1, source_target_pairs={{0,2},{1,3},{2,0},{3,1},{4,6},{5,7},{6,4},{7,5},{8,10},{9,11},{10,... | collective-permute-start | bytes 786440 | tf_op jit(solution)/shard_map/ppermute | solution.py:515
  49.2 17.4 %collective-permute-start.11 = (bf16[256,512]{1,0:T(8,128)(2,1)S(1)}, bf16[256,512]{1,0:T(8,128)(2,1)S(1)}, u32[]{:S(2)}, u32[]{:S(2)}) collective-permute-start(bf16[256,512]{1,0:T(8,128)(2,1)S(1)} %get-tuple-element.125), channel_id=1, source_target_pairs={{0,3},{1,2},{2,1},{3,0},{4,7},{5,6},{6,5},{7,4},{8,11},{9,10},{10,... | collective-permute-start | bytes 786440 | tf_op jit(solution)/shard_map/ppermute | solution.py:515
  78.7 8.3 %collective-permute-start.12 = (bf16[1984,256]{1,0:T(8,128)(2,1)S(1)}, bf16[1984,256]{1,0:T(8,128)(2,1)S(1)}, u32[]{:S(2)}, u32[]{:S(2)}) collective-permute-start(bf16[1984,256]{1,0:T(8,128)(2,1)S(1)} %hidden.1.refs_0_), channel_id=1, source_target_pairs={{0,1},{1,0},{2,3},{3,2},{4,5},{5,4},{6,7},{7,6},{8,9},{9,8},{10,11... | collective-permute-start | bytes 3047432 | tf_op jit(solution)/shard_map/ppermute | solution.py:515
  78.7 24.9 %collective-permute-start.13 = (bf16[1984,256]{1,0:T(8,128)(2,1)S(1)}, bf16[1984,256]{1,0:T(8,128)(2,1)S(1)}, u32[]{:S(2)}, u32[]{:S(2)}) collective-permute-start(bf16[1984,256]{1,0:T(8,128)(2,1)S(1)} %hidden.1.refs_0_), channel_id=1, source_target_pairs={{0,2},{1,3},{2,0},{3,1},{4,6},{5,7},{6,4},{7,5},{8,10},{9,11},{10,... | collective-permute-start | bytes 3047432 | tf_op jit(solution)/shard_map/ppermute | solution.py:515
  103.7 31.6 %collective-permute-start.15 = (bf16[1296,512]{1,0:T(8,128)(2,1)S(1)}, bf16[1296,512]{1,0:T(8,128)(2,1)S(1)}, u32[]{:S(2)}, u32[]{:S(2)}) collective-permute-start(bf16[1296,512]{1,0:T(8,128)(2,1)S(1)} %slice.42), channel_id=1, source_target_pairs={{0,2},{1,3},{2,0},{3,1},{4,6},{5,7},{6,4},{7,5},{8,10},{9,11},{10,... | collective-permute-start | bytes 3981320 | tf_op jit(solution)/shard_map/ppermute | solution.py:515
  139.5 27.2 %collective-permute-start.19 = (bf16[1984,256]{1,0:T(8,128)(2,1)S(1)}, bf16[1984,256]{1,0:T(8,128)(2,1)S(1)}, u32[]{:S(2)}, u32[]{:S(2)}) collective-permute-start(bf16[1984,256]{1,0:T(8,128)(2,1)S(1)} %merge.1), channel_id=1, source_target_pairs={{0,2},{1,3},{2,0},{3,1},{4,6},{5,7},{6,4},{7,5},{8,10},{9,11},{10,... | collective-permute-start | bytes 3047432 | tf_op jit(solution)/shard_map/ppermute | solution.py:515
  140.1 28.9 %collective-permute-start.17 = (bf16[1296,512]{1,0:T(8,128)(2,1)S(1)}, bf16[1296,512]{1,0:T(8,128)(2,1)S(1)}, u32[]{:S(2)}, u32[]{:S(2)}) collective-permute-start(bf16[1296,512]{1,0:T(8,128)(2,1)S(1)} %collective-permute-done.15.refs_2_), channel_id=1, source_target_pairs={{0,1},{1,0},{2,3},{3,2},{4,5},{5,4},{6,7},{7,6},{8,9},{9,8},{10,11... | collective-permute-start | bytes 3981320 | tf_op jit(solution)/shard_map/ppermute | solution.py:515
  143.0 14.4 %collective-permute-start.20 = (bf16[4,128,512]{2,1,0:T(8,128)(2,1)S(1)}, bf16[4,128,512]{2,1,0:T(8,128)(2,1)S(1)}, u32[]{:S(2)}, u32[]{:S(2)}) collective-permute-start(bf16[4,128,512]{2,1,0:T(8,128)(2,1)S(1)} %send.6), channel_id=1, source_target_pairs={{0,4},{4,0},{8,12},{12,8},{16,20},{20,16},{24,28},{28,24},{1,5},{5... | collective-permute-start | bytes 1572872 | tf_op jit(solution)/shard_map/ppermute | solution.py:515
  143.6 25.3 %collective-permute-start.18 = (bf16[1984,256]{1,0:T(8,128)(2,1)S(1)}, bf16[1984,256]{1,0:T(8,128)(2,1)S(1)}, u32[]{:S(2)}, u32[]{:S(2)}) collective-permute-start(bf16[1984,256]{1,0:T(8,128)(2,1)S(1)} %copy-done.34), channel_id=1, source_target_pairs={{0,1},{1,0},{2,3},{3,2},{4,5},{5,4},{6,7},{7,6},{8,9},{9,8},{10,11... | collective-permute-start | bytes 3047432 | tf_op jit(solution)/shard_map/ppermute | solution.py:515
  158.1 8.0 %collective-permute-start.21 = (bf16[4,64,512]{2,1,0:T(8,128)(2,1)S(1)}, bf16[4,64,512]{2,1,0:T(8,128)(2,1)S(1)}, u32[]{:S(2)}, u32[]{:S(2)}) collective-permute-start(bf16[4,64,512]{2,1,0:T(8,128)(2,1)S(1)} %send.7), channel_id=1, source_target_pairs={{0,8},{4,12},{8,0},{12,4},{16,24},{20,28},{24,16},{28,20},{1,9},{5... | collective-permute-start | bytes 786440 | tf_op jit(solution)/shard_map/ppermute | solution.py:515
  166.8 18.8 %collective-permute-start.23 = (bf16[688,512]{1,0:T(8,128)(2,1)S(1)}, bf16[688,512]{1,0:T(8,128)(2,1)S(1)}, u32[]{:S(2)}, u32[]{:S(2)}) collective-permute-start(bf16[688,512]{1,0:T(8,128)(2,1)S(1)} %slice.43), channel_id=1, source_target_pairs={{0,2},{1,3},{2,0},{3,1},{4,6},{5,7},{6,4},{7,5},{8,10},{9,11},{10,... | collective-permute-start | bytes 2113544 | tf_op jit(solution)/shard_map/ppermute | solution.py:515
  168.4 17.1 %collective-permute-start.22 = (bf16[4,64,512]{2,1,0:T(8,128)(2,1)S(1)}, bf16[4,64,512]{2,1,0:T(8,128)(2,1)S(1)}, u32[]{:S(2)}, u32[]{:S(2)}) collective-permute-start(bf16[4,64,512]{2,1,0:T(8,128)(2,1)S(1)} %send.8.a), channel_id=1, source_target_pairs={{0,16},{4,20},{8,24},{12,28},{16,0},{20,4},{24,8},{28,12},{1,17},{... | collective-permute-start | bytes 786440 | tf_op jit(solution)/shard_map/ppermute | solution.py:515
  202.2 16.1 %collective-permute-start.26 = (bf16[1024,256]{1,0:T(8,128)(2,1)S(1)}, bf16[1024,256]{1,0:T(8,128)(2,1)S(1)}, u32[]{:S(2)}, u32[]{:S(2)}) collective-permute-start(bf16[1024,256]{1,0:T(8,128)(2,1)S(1)} %send.9), channel_id=1, source_target_pairs={{0,4},{4,0},{8,12},{12,8},{16,20},{20,16},{24,28},{28,24},{1,5},{5... | collective-permute-start | bytes 1572872 | tf_op jit(solution)/shard_map/ppermute | solution.py:515
  208.9 8.8 %collective-permute-start.30 = (bf16[64,2048]{1,0:T(8,128)(2,1)S(1)}, bf16[64,2048]{1,0:T(8,128)(2,1)S(1)}, u32[]{:S(2)}, u32[]{:S(2)}) collective-permute-start(bf16[64,2048]{1,0:T(8,128)(2,1)S(1)} %arrange.1.mine), channel_id=1, source_target_pairs={{0,8},{4,12},{8,0},{12,4},{16,24},{20,28},{24,16},{28,20},{1,9},{5... | collective-permute-start | bytes 786440 | tf_op jit(solution)/shard_map/ppermute | solution.py:515
  218.9 9.3 %collective-permute-start.32 = (bf16[64,2048]{1,0:T(8,128)(2,1)S(1)}, bf16[64,2048]{1,0:T(8,128)(2,1)S(1)}, u32[]{:S(2)}, u32[]{:S(2)}) collective-permute-start(bf16[64,2048]{1,0:T(8,128)(2,1)S(1)} %slice.44), channel_id=1, source_target_pairs={{0,4},{4,0},{8,12},{12,8},{16,20},{20,16},{24,28},{28,24},{1,5},{5... | collective-permute-start | bytes 786440 | tf_op jit(solution)/shard_map/ppermute | solution.py:515
  220.5 7.8 %collective-permute-start.31 = (bf16[512,256]{1,0:T(8,128)(2,1)S(1)}, bf16[512,256]{1,0:T(8,128)(2,1)S(1)}, u32[]{:S(2)}, u32[]{:S(2)}) collective-permute-start(bf16[512,256]{1,0:T(8,128)(2,1)S(1)} %send.10), channel_id=1, source_target_pairs={{0,8},{4,12},{8,0},{12,4},{16,24},{20,28},{24,16},{28,20},{1,9},{5... | collective-permute-start | bytes 786440 | tf_op jit(solution)/shard_map/ppermute | solution.py:515
  221.0 7.3 %collective-permute-start.33 = (bf16[496,256]{1,0:T(8,128)(2,1)S(1)}, bf16[496,256]{1,0:T(8,128)(2,1)S(1)}, u32[]{:S(2)}, u32[]{:S(2)}) collective-permute-start(bf16[496,256]{1,0:T(8,128)(2,1)S(1)} %slice.45), channel_id=1, source_target_pairs={{0,2},{1,3},{2,0},{3,1},{4,6},{5,7},{6,4},{7,5},{8,10},{9,11},{10,... | collective-permute-start | bytes 761864 | tf_op jit(solution)/shard_map/ppermute | solution.py:515
  228.9 6.7 %collective-permute-start.36 = (bf16[64,2048]{1,0:T(8,128)(2,1)S(1)}, bf16[64,2048]{1,0:T(8,128)(2,1)S(1)}, u32[]{:S(2)}, u32[]{:S(2)}) collective-permute-start(bf16[64,2048]{1,0:T(8,128)(2,1)S(1)} %slice.46), channel_id=1, source_target_pairs={{0,4},{4,0},{8,12},{12,8},{16,20},{20,16},{24,28},{28,24},{1,5},{5... | collective-permute-start | bytes 786440 | tf_op jit(solution)/shard_map/ppermute | solution.py:515
  229.7 7.9 %collective-permute-start.38 = (bf16[496,256]{1,0:T(8,128)(2,1)S(1)}, bf16[496,256]{1,0:T(8,128)(2,1)S(1)}, u32[]{:S(2)}, u32[]{:S(2)}) collective-permute-start(bf16[496,256]{1,0:T(8,128)(2,1)S(1)} %slice.47), channel_id=1, source_target_pairs={{0,2},{1,3},{2,0},{3,1},{4,6},{5,7},{6,4},{7,5},{8,10},{9,11},{10,... | collective-permute-start | bytes 761864 | tf_op jit(solution)/shard_map/ppermute | solution.py:515
  230.2 14.2 %collective-permute-start.34 = (bf16[512,256]{1,0:T(8,128)(2,1)S(1)}, bf16[512,256]{1,0:T(8,128)(2,1)S(1)}, u32[]{:S(2)}, u32[]{:S(2)}) collective-permute-start(bf16[512,256]{1,0:T(8,128)(2,1)S(1)} %send.11.a), channel_id=1, source_target_pairs={{0,16},{4,20},{8,24},{12,28},{16,0},{20,4},{24,8},{28,12},{1,17},{... | collective-permute-start | bytes 786440 | tf_op jit(solution)/shard_map/ppermute | solution.py:515
  230.8 13.6 %collective-permute-start.37 = (bf16[496,256]{1,0:T(8,128)(2,1)S(1)}, bf16[496,256]{1,0:T(8,128)(2,1)S(1)}, u32[]{:S(2)}, u32[]{:S(2)}) collective-permute-start(bf16[496,256]{1,0:T(8,128)(2,1)S(1)} %collective-permute-done.33.refs_0_), channel_id=1, source_target_pairs={{0,1},{1,0},{2,3},{3,2},{4,5},{5,4},{6,7},{7,6},{8,9},{9,8},{10,11... | collective-permute-start | bytes 761864 | tf_op jit(solution)/shard_map/ppermute | solution.py:515
  237.6 6.7 %collective-permute-start.40 = (bf16[496,256]{1,0:T(8,128)(2,1)S(1)}, bf16[496,256]{1,0:T(8,128)(2,1)S(1)}, u32[]{:S(2)}, u32[]{:S(2)}) collective-permute-start(bf16[496,256]{1,0:T(8,128)(2,1)S(1)} %slice.48), channel_id=1, source_target_pairs={{0,2},{1,3},{2,0},{3,1},{4,6},{5,7},{6,4},{7,5},{8,10},{9,11},{10,... | collective-permute-start | bytes 761864 | tf_op jit(solution)/shard_map/ppermute | solution.py:515
  238.0 6.3 %collective-permute-start.39 = (bf16[496,256]{1,0:T(8,128)(2,1)S(1)}, bf16[496,256]{1,0:T(8,128)(2,1)S(1)}, u32[]{:S(2)}, u32[]{:S(2)}) collective-permute-start(bf16[496,256]{1,0:T(8,128)(2,1)S(1)} %collective-permute-done.38.refs_1_), channel_id=1, source_target_pairs={{0,1},{1,0},{2,3},{3,2},{4,5},{5,4},{6,7},{7,6},{8,9},{9,8},{10,11... | collective-permute-start | bytes 761864 | tf_op jit(solution)/shard_map/ppermute | solution.py:515
  244.4 11.2 %collective-permute-start.41 = (bf16[512,256]{1,0:T(8,128)(2,1)S(1)}, bf16[512,256]{1,0:T(8,128)(2,1)S(1)}, u32[]{:S(2)}, u32[]{:S(2)}) collective-permute-start(bf16[512,256]{1,0:T(8,128)(2,1)S(1)} %add.36.mine), channel_id=1, source_target_pairs={{0,8},{4,12},{8,0},{12,4},{16,24},{20,28},{24,16},{28,20},{1,9},{5... | collective-permute-start | bytes 786440 | tf_op jit(solution)/shard_map/ppermute | solution.py:515
  245.9 9.7 %collective-permute-start.42 = (bf16[288,256]{1,0:T(8,128)(2,1)S(1)}, bf16[288,256]{1,0:T(8,128)(2,1)S(1)}, u32[]{:S(2)}, u32[]{:S(2)}) collective-permute-start(bf16[288,256]{1,0:T(8,128)(2,1)S(1)} %add.35.a), channel_id=1, source_target_pairs={{0,8},{4,12},{8,0},{12,4},{16,24},{20,28},{24,16},{28,20},{1,9},{5... | collective-permute-start | bytes 442376 | tf_op jit(solution)/shard_map/ppermute | solution.py:515
  246.6 9.0 %collective-permute-start.44 = (bf16[496,256]{1,0:T(8,128)(2,1)S(1)}, bf16[496,256]{1,0:T(8,128)(2,1)S(1)}, u32[]{:S(2)}, u32[]{:S(2)}) collective-permute-start(bf16[496,256]{1,0:T(8,128)(2,1)S(1)} %slice.49), channel_id=1, source_target_pairs={{0,2},{1,3},{2,0},{3,1},{4,6},{5,7},{6,4},{7,5},{8,10},{9,11},{10,... | collective-permute-start | bytes 761864 | tf_op jit(solution)/shard_map/ppermute | solution.py:515
  248.3 7.4 %collective-permute-start.43 = (bf16[496,256]{1,0:T(8,128)(2,1)S(1)}, bf16[496,256]{1,0:T(8,128)(2,1)S(1)}, u32[]{:S(2)}, u32[]{:S(2)}) collective-permute-start(bf16[496,256]{1,0:T(8,128)(2,1)S(1)} %collective-permute-done.40.refs_2_), channel_id=1, source_target_pairs={{0,1},{1,0},{2,3},{3,2},{4,5},{5,4},{6,7},{7,6},{8,9},{9,8},{10,11... | collective-permute-start | bytes 761864 | tf_op jit(solution)/shard_map/ppermute | solution.py:515
  256.3 12.7 %collective-permute-start.46 = (bf16[1024,256]{1,0:T(8,128)(2,1)S(1)}, bf16[1024,256]{1,0:T(8,128)(2,1)S(1)}, u32[]{:S(2)}, u32[]{:S(2)}) collective-permute-start(bf16[1024,256]{1,0:T(8,128)(2,1)S(1)} %double.6.mine), channel_id=1, source_target_pairs={{0,4},{4,0},{8,12},{12,8},{16,20},{20,16},{24,28},{28,24},{1,5},{5... | collective-permute-start | bytes 1572872 | tf_op jit(solution)/shard_map/ppermute | solution.py:515
  257.5 10.3 %collective-permute-start.47 = (bf16[288,256]{1,0:T(8,128)(2,1)S(1)}, bf16[288,256]{1,0:T(8,128)(2,1)S(1)}, u32[]{:S(2)}, u32[]{:S(2)}) collective-permute-start(bf16[288,256]{1,0:T(8,128)(2,1)S(1)} %add.37.a), channel_id=1, source_target_pairs={{0,16},{4,20},{8,24},{12,28},{16,0},{20,4},{24,8},{28,12},{1,17},{... | collective-permute-start | bytes 442376 | tf_op jit(solution)/shard_map/ppermute | solution.py:515
  (52 other events, 422.0 us)

commit v3 on v2

--- a/solution.py
+++ b/solution.py
@@ -16,6 +16,7 @@
 LANES = 128
 LINES = 3
 STEPS = 4
+PIECES = 2
 TN = (((0,), (0,)), ((), ()))
 NT = (((1,), (1,)), ((), ()))
 VM = pl.BlockSpec(memory_space=pltpu.VMEM)
@@ -102,20 +103,23 @@
 
 
 def part_far_kernel(dims, own, beside, *refs):
-    n = len(refs) // 4
-    ws, outs, rows, passed = (refs[i * n : (i + 1) * n] for i in range(4))
+    n = len(refs) // 2
     share = own.shape[1]
     core = lax.bitwise_and(dims[2], 1)
     mine = pl.ds(pl.multiple_of(core * share, share), share)
     other = pl.ds(pl.multiple_of((1 - core) * share, share), share)
-    for w, out in zip(ws, outs):
+    for w, out in zip(refs[:n], refs[n:]):
         out[...] = (dot(own[...], w[mine, :]) + dot(beside[...], w[other, :])).astype(BF16)
 
-    @pl.when(pl.program_id(0) == 0)
-    def _():
-        for w, row, pass_on in zip(ws, rows, passed):
-            row[...] = w[mine, :]
-            pass_on[...] = w[other, :]
+
+def rows_kernel(dims, *refs):
+    n = len(refs) // 3
+    ws, rows, passed = (refs[i * n : (i + 1) * n] for i in range(3))
+    share = rows[0].shape[0]
+    core = lax.bitwise_and(dims[2], 1)
+    for w, row, pass_on in zip(ws, rows, passed):
+        row[...] = w[pl.ds(pl.multiple_of(core * share, share), share), :]
+        pass_on[...] = w[pl.ds(pl.multiple_of((1 - core) * share, share), share), :]
 
 
 def far_kernel(live, part, *refs):
@@ -165,7 +169,7 @@
         out[t] = jnp.where(same, tiled, 0.0).astype(BF16)
 
 
-def conv_kernel(side, slots, live, z, got, gain, shift, taps, hid, out, spread, pad, acc):
+def conv_kernel(side, slots, live, z, got, gain, shift, taps, out, spread, pad, acc):
     line, wide = side * slots, (side + 2) * slots
     rows, width = z.shape
     mu, r, _ = norm_of(got, got)
@@ -177,9 +181,7 @@
     def fill(i, carry):
         here = pl.ds(pl.multiple_of(i * line, 8), line)
         h = widen(live[here, :], width) * act(z[here, :] * a + b)
-        h = h.astype(BF16).astype(F32)
-        hid[here, :] = h
-        pad_line(pad, i, h, line, wide, slots)
+        pad_line(pad, i, h.astype(BF16).astype(F32), line, wide, slots)
         return carry
 
     lax.fori_loop(0, side, fill, 0)
@@ -194,7 +196,6 @@
         acc[1] += fold(m * total)
     used = side * line
     out[used:rows] = jnp.zeros((rows - used, width), F32)
-    hid[used:rows] = jnp.zeros((rows - used, width), F32)
     send_sums(spread, acc)
 
 
@@ -342,14 +343,18 @@
     out[...] = (m * (r * gain[...]) * (d_one[...] - t[0:1] - zhat * t[1:2])).astype(BF16)
 
 
-def group_grad_kernel(side, slots, group_width, hid, d_grouped, out, pad):
+def group_grad_kernel(side, slots, group_width, live, z, got, gain, shift, d_grouped, out, pad):
     line, wide = side * slots, (side + 2) * slots
-    width = hid.shape[1]
+    width = z.shape[1]
+    mu, r, _ = norm_of(got, got)
+    scale = r * gain[...]
+    offset = shift[...] - mu * scale
     pad_edges(pad, side, line, wide, slots)
 
     def fill(i, carry):
         here = pl.ds(pl.multiple_of(i * line, 8), line)
-        pad_line(pad, i, hid[here, :], line, wide, slots)
+        h = widen(live[here, :], width) * act(z[here, :] * scale + offset)
+        pad_line(pad, i, h.astype(BF16).astype(F32), line, wide, slots)
         return carry
 
     lax.fori_loop(0, side, fill, 0)
@@ -422,19 +427,57 @@
     return lax.bitwise_and(lax.shift_right_logical(v, bit), 1)
 
 
-def send_kernel(step, last, dims, *refs):
-    *terms, out = refs
+def add_terms(b, terms, order, step, last, base):
     total = None
-    for first, term in enumerate(terms):
-        rows, at = term.shape[-2], 0
+    for first, (term, size) in enumerate(terms):
+        rows, at = size, base if first == 0 else 0
         for t in range(first, step + (not last)):
             rows //= 2
-            side = bit_of(dims[3], t)
+            side = bit_of(b, order[t])
             at += rows * (side if t < step else 1 - side)
         here = pl.ds(at if isinstance(at, int) else pl.multiple_of(at, 16), rows)
         v = term[:, here, :] if len(term.shape) == 3 else term[here, :]
         total = v.astype(F32) if total is None else total + v.astype(F32)
-    out[...] = total.astype(BF16)
+    return total.astype(BF16)
+
+
+def send_kernel(step, last, dims, *refs):
+    *terms, out = refs
+    sized = [(t, t.shape[-2]) for t in terms]
+    out[...] = add_terms(dims[3], sized, range(step + 1), step, last, 0)
+
+
+def send_both_kernel(step, last, orders, dims, whole, *refs):
+    half = whole.shape[0] // 2
+    n = step
+    outs = refs[2 * n :]
+    for i, order in enumerate(orders):
+        terms = [(whole, half)] + [(r, r.shape[0]) for r in refs[i * n : (i + 1) * n]]
+        total = add_terms(dims[3], terms, order, step, last, i * half)
+        if last:
+            outs[0][i * total.shape[0] : (i + 1) * total.shape[0]] = total
+        else:
+            outs[i][...] = total
+
+
+def double_pair_kernel(bits, dims, sums, *refs):
+    *ins, a, b = refs
+    n = ins[0].shape[0]
+    for i, (bit, out) in enumerate(zip(bits, (a, b))):
+        mine = sums[i * n : (i + 1) * n] if len(ins) == 2 else (sums, ins[0])[i][...]
+        other = ins[i] if len(ins) == 2 else ins[i + 1]
+        upper = bit_of(dims[3], bit)
+        out[pl.ds(pl.multiple_of(upper * n, 16), n), :] = mine
+        out[pl.ds(pl.multiple_of((1 - upper) * n, 16), n), :] = other[...]
+
+
+def finish_kernel(bits, dims, a, b, other_a, other_b, out):
+    n = a.shape[0]
+    for i, (bit, mine, other) in enumerate(zip(bits, (a, b), (other_a, other_b))):
+        upper = bit_of(dims[3], bit)
+        at = 2 * i * n
+        out[pl.ds(pl.multiple_of(at + upper * n, 16), n), :] = mine[...].astype(F32)
+        out[pl.ds(pl.multiple_of(at + (1 - upper) * n, 16), n), :] = other[...].astype(F32)
 
 
 def arrange_kernel(dims, *refs):
@@ -466,27 +509,26 @@
 
 def input_far_kernel(part, *refs):
     *ins, out = refs
-    n = len(ins) // (STEPS + 1)
-    ds, ws = ins[: n * STEPS], ins[n * STEPS :]
-    for step in range(STEPS):
+    n = len(ins) // (PIECES + 1)
+    ds, ws = ins[: n * PIECES], ins[n * PIECES :]
+    for step in range(PIECES):
 
         @pl.when(pl.program_id(0) == step)
         def _(step=step):
-            got = sum(dot_nt(ds[k * STEPS + step][...], w[...]) for k, w in enumerate(ws))
+            got = sum(dot_nt(ds[k * PIECES + step][...], w[...]) for k, w in enumerate(ws))
             out[...] = part[...] + got
 
 
-def call(kernel, outs, ins, scratch=(), flops=0, name=None, smem=False, steps=0):
+def call(kernel, outs, ins, scratch=(), flops=0, name=None, smem=False, steps=0, size=0):
     moved = sum(x.size * x.dtype.itemsize for x in ins)
     moved += sum(int(o.size) * o.dtype.itemsize for o in outs)
-    block = -(-max(o.shape[0] for o in outs) // (16 * steps)) * 16 if steps else 0
-
-    most = max(o.shape[0] for o in outs)
+    size = size or max(o.shape[0] for o in outs)
+    block = -(-size // (16 * steps)) * 16 if steps else 0
 
     def spec(x):
         if not steps:
             return VM
-        if len(x.shape) == 2 and most - block < x.shape[0] <= steps * block:
+        if len(x.shape) == 2 and steps * block - 64 < x.shape[0] <= steps * block:
             return pl.BlockSpec((block, x.shape[1]), lambda s: (s, 0))
         return pl.BlockSpec(x.shape, lambda s: (0,) * len(x.shape))
 
@@ -500,7 +542,7 @@
         in_specs=specs,
         out_specs=[spec(o) for o in outs],
         scratch_shapes=list(scratch),
-        compiler_params=pltpu.CompilerParams(vmem_limit_bytes=32 << 20),
+        compiler_params=pltpu.CompilerParams(vmem_limit_bytes=16 << 20),
         cost_estimate=pl.CostEstimate(flops=flops, bytes_accessed=moved, transcendentals=0),
         name=name,
     )(*ins)
@@ -590,8 +632,8 @@
     even = [k for k in others[2:] if k % 2 == 0]
     at = [lax.bitwise_and(me ^ k, n_chan - 2) * share for k in even]
     w_far = [lax.dynamic_slice_in_dim(w_reduce, o, 2 * share, 0) for o in at]
+    own = jnp.pad(after(feats, *w_far), ends)
     w_far = [swap(w, "chan", n_chan, k) for k, w in zip(even, w_far)]
-    own = jnp.pad(feats, ends)
     beside = swap(own, "chan", n_chan, 1)
 
     dims = jnp.stack(
@@ -609,13 +651,16 @@
         line_of, (gain_one, shift_one, gain_two, shift_two)
     )
 
+    parts = call(
+        part_far_kernel, [shape((padded, width), BF16)] * len(even), [dims, own, beside, *w_far],
+        flops=2 * len(even) * mm, name="part_far", steps=2, smem=True,
+    )
+    parts = parts if len(even) > 1 else [parts]
     got = call(
-        part_far_kernel,
-        [shape((padded, width), BF16)] * len(even) + [shape((share, width), BF16)] * 2 * len(even),
-        [dims, own, beside, *w_far],
-        flops=2 * len(even) * mm, name="part_far", steps=STEPS, smem=True,
-    )
-    parts, rows_far, passed = (got[i * len(even) : (i + 1) * len(even)] for i in range(3))
+        rows_kernel, [shape((share, width), BF16)] * 2 * len(even),
+        [dims, *[after(w, *parts) for w in w_far]], name="rows", smem=True,
+    )
+    rows_far, passed = got[: len(even)], got[len(even) :]
     got = [swap(p, "chan", n_chan, k) for k, p in zip(even, parts)]
 
     *picked, gain_c, shift_c, cot = call(
@@ -643,9 +688,9 @@
     )
     got_one = batch_sum_stepwise(spread, n_batch)
 
-    hid, grouped, spread = call(
+    grouped, spread = call(
         functools.partial(conv_kernel, side, slots),
-        [shape((padded, width), F32)] * 2 + [shape((n_batch, 2, width), F32)],
+        [shape((padded, width), F32), shape((n_batch, 2, width), F32)],
         [live, z, got_one, gain_one, shift_one, taps], [tall, acc(2, width)],
         flops=18 * padded * width * width, name="conv",
     )
@@ -654,6 +699,8 @@
         hidden_kernel, [shape((padded, width), BF16)],
         [live, grouped, got_one, got_two, gain_two, shift_two], flops=mm, name="hidden", steps=STEPS,
     )
+    half = padded * 42 // 64 // 16 * 16
+    own_first = after(own, hidden_two)[:half]
     first = gather_y(hidden_two, n_chan)
     beside_two = swap(hidden_two, "chan", n_chan, 1)
     slope_two = call(
@@ -666,11 +713,10 @@
     )
     part = call(
         expand_near_kernel, [shape((padded, share), F32)], [hidden_two, beside_two, *w_cols[:2]],
-        flops=2 * mm, name="expand_near", steps=STEPS,
-    )
-    first = {k: after(v, part, slope_one, slope_two, *w_cols) for k, v in first.items()}
-    half = padded * 42 // 64 // 16 * 16
-    far_halves = [gather_y(after(own, *first.values())[:half], n_chan)]
+        flops=2 * mm, name="expand_near", steps=2,
+    )
+    first = {k: after(v, part, slope_one, slope_two, own_first, *w_cols) for k, v in first.items()}
+    far_halves = [gather_y(after(own_first, *first.values()), n_chan)]
     first = gather_core(first, n_chan)
     hidden_all = [hidden_two, beside_two] + [first[k] for k in others if k > 1]
     expanded, spread = call(
@@ -698,7 +744,7 @@
     d_zero, d_near = call(
         back_expand_kernel, [shape((padded, width), F32), shape((padded, width), BF16)],
         [after(d_expanded, sent, *far_halves[0].values())] + [w_cols[k] for k in early], flops=2 * mm,
-        name="back_expand", steps=STEPS,
+        name="back_expand", steps=2,
     )
 
     def part_sum(k, below):
@@ -714,7 +760,7 @@
             return [d_zero, *got]
         return call(
             merge_kernel, [shape((padded, width), BF16)],
-            [after(d_expanded, d_near), w_cols[k], *got], flops=mm, name="merge", steps=STEPS,
+            [after(d_expanded, d_near), w_cols[k], *got], flops=mm, name="merge", steps=2,
         )
 
     far_sum = part_sum(n_chan // 2, n_chan // 2)
@@ -781,80 +827,104 @@
         [dims, d_reduced, tail, rest, *lasts], flops=mm, name="reduce_grad_rest", smem=True,
     )
     d_beside = swap(d_reduced, "chan", n_chan, 1)
-    tail_terms = [after(tail, d_beside)]
-    quarter = padded // STEPS
+    tail = after(tail, d_beside)
+    piece_rows = padded // PIECES
     d_far = []
 
-    def next_far(*ready):
-        at = len(d_far) * quarter
-        if d_far and len(d_far[-1]) < n_chan - 2:
-            last = {k: after(v, *ready) for k, v in d_far[-1].items()}
-            d_far[-1] = gather_core(last, n_chan)
-        if at < padded:
-            piece = after(d_reduced, *ready)[at : at + quarter]
-            d_far.append(gather_y(piece, n_chan))
-        return [v for d in d_far for v in d.values()]
+    def far_rows(at, *ready):
+        piece = after(d_reduced, *ready)[at * piece_rows : (at + 1) * piece_rows]
+        d_far.append(gather_y(piece, n_chan))
+        return list(d_far[at].values())
+
+    def pass_on(at, *ready):
+        d_far[at] = gather_core({k: after(v, *ready) for k, v in d_far[at].items()}, n_chan)
+        return list(d_far[at].values())
 
     top = bits - 1
+    orders = [list(range(top)), [1, 0, *range(2, top)]]
+    got = [[], []]
     for s in range(top):
-        send = send_of(dims, tail_terms, s)
-        got = swap(send, "batch", n_batch, 1 << s)
+        rows_here = n_chan * share >> (s + 2)
+        send = call(
+            functools.partial(send_both_kernel, s, False, orders),
+            [shape((rows_here, width), BF16)] * 2, [dims, tail, *got[0], *got[1]],
+            name="send_both", smem=True,
+        )
+        new = [swap(send[i], "batch", n_batch, 1 << orders[i][s]) for i in range(2)]
+        ties = []
         if s == 0:
             cols = [parts[0]]
-            cols += [swap(after(parts[k], send), "chan", n_chan, k) for k in others if k]
-            group_part = call(
-                functools.partial(group_grad_kernel, side, slots, group_width),
-                [shape((9 * group_width, width), BF16)], [hid, after(d_grouped, *parts)],
-                [tall], flops=mm, name="group_grad",
-            )
-            cols[1] = after(cols[1], group_part)
+            cols += [swap(after(parts[k], send[0]), "chan", n_chan, k) for k in others if k]
             cols = call(
                 arrange_kernel, [shape((mine.shape[1], n_chan * share), BF16)], [dims, *cols],
                 name="arrange", smem=True,
             )
+            group_part = call(
+                functools.partial(group_grad_kernel, side, slots, group_width),
+                [shape((9 * group_width, width), BF16)],
+                [live, z, got_one, gain_one, shift_one, after(d_grouped, cols)],
+                [tall], flops=mm, name="group_grad",
+            )
+            far_rows(0, cols)
+            ties = [group_part]
+        elif s == 1:
+            group_other = swap(after(group_part, send[0]), "batch", n_batch, 1)
             for t in reversed(range(1, top)):
-                other = swap(cols, "batch", n_batch, 1 << t)
+                other = swap(after(cols, send[0]), "batch", n_batch, 1 << t)
                 cols = double(dims, cols, other, t)
-            got = after(got, cols)
-        elif s == 1:
-            split = cols.shape[0] // 2
-            others_cols = [swap(after(cols, send)[:split], "batch", n_batch, 1)]
-            got = after(got, *others_cols, *next_far(send))
-        tail_terms.append(got)
-    mine = send_of(dims, tail_terms, top, True)
-    other = swap(mine, "batch", n_batch, 1 << top)
-    others_cols.append(swap(after(cols, mine)[split:], "batch", n_batch, 1))
-    moved = next_far(mine)
-    expand_grad = double(dims, cols, others_cols, 0, F32)
-    group_other = swap(after(group_part, mine), "batch", n_batch, 1)
-    group_part = add(group_part, after(group_other, expand_grad))
-    moved = next_far(expand_grad)
-    tail = add(mine, after(other, group_part, *moved))
+            group_part = add(group_part, after(group_other, cols))
+            ties += [group_part, *d_far[0].values()]
+            ties.append(cols)
+        new = [after(v, *ties) for v in new]
+        got = [got[i] + [new[i]] for i in range(2)]
+    sums = call(
+        functools.partial(send_both_kernel, top, True, orders),
+        [shape((n_chan * share >> top, width), BF16)], [dims, tail, *got[0], *got[1]],
+        name="send_both", smem=True,
+    )
+    other = swap(sums, "batch", n_batch, 1 << top)
+    cols_other = swap(after(cols, sums), "batch", n_batch, 1)
+    moved = [*far_rows(1, sums), *pass_on(0, sums)]
+    part = call(
+        features_grad_kernel, [shape((padded, share), F32)],
+        [d_pre, after(d_reduced, sums), d_beside, *w_rows[:2]], flops=2 * mm,
+        name="input_near", steps=STEPS,
+    )
+    expand_grad = double(dims, cols, after(cols_other, part), 0, F32)
+    sums = add(sums, after(other, expand_grad, *moved))
+    pair = [sums]
     for s in reversed(range(top)):
-        got = swap(tail, "batch", n_batch, 1 << s)
-        before = next_far(tail)
+        n = pair[0].shape[0] // (2 if len(pair) == 1 else 1)
+        cut = [sums[:n], sums[n:]] if len(pair) == 1 else pair
+        new = [swap(cut[i], "batch", n_batch, 1 << orders[i][s]) for i in range(2)]
         if s == top - 1:
-            group_other = swap(after(group_part, tail), "batch", n_batch, 2)
-            part = call(
-                features_grad_kernel, [shape((padded, share), F32)],
-                [d_pre, after(d_reduced, tail), d_beside, *w_rows[:2]], flops=2 * mm,
-                name="input_near", steps=STEPS,
-            )
-            group_part = add(group_part, after(group_other, part))
-            before = (group_part, *before)
+            group_other = swap(after(group_part, sums), "batch", n_batch, 2)
+            group_part = add(group_part, group_other)
+            before = (group_part, *pass_on(1, sums))
         if s == 0:
-            features_grad = call(
-                input_far_kernel, [shape((rows, share), F32)],
-                [after(part, tail), *[d[k] for k in others[2:] for d in d_far], *w_rows[2:]],
-                flops=(n_chan - 2) * mm, name="input_far", steps=STEPS,
-            )
             for t in range(2, bits):
-                group_part = after(group_part, tail)
+                group_part = after(group_part, cut[0])
                 group_other = swap(group_part, "batch", n_batch, 1 << t)
-                group_other = after(group_other, features_grad)
+                if t == 2:
+                    features_grad = call(
+                        input_far_kernel, [shape((rows, share), F32)],
+                        [after(part, cut[0]), *[d[k] for k in others[2:] for d in d_far], *w_rows[2:]],
+                        flops=(n_chan - 2) * mm, name="input_far", steps=PIECES, size=padded,
+                    )
+                    group_other = after(group_other, features_grad)
                 group_part = add(group_part, group_other, BF16 if t + 1 < bits else F32)
             before = (group_part,)
-        tail = double(dims, tail, after(got, *before), s, BF16 if s else F32)
+        new = [after(v, *before) for v in new]
+        if s:
+            pair = call(
+                functools.partial(double_pair_kernel, [o[s] for o in orders]),
+                [shape((2 * n, width), BF16)] * 2, [dims, *pair, *new], name="double_pair",
+                smem=True,
+            )
+    tail = call(
+        functools.partial(finish_kernel, [o[0] for o in orders]),
+        [shape((n_chan * share, width), F32)], [dims, *pair, *new], name="finish", smem=True,
+    )
     reduce_grad, group_grad = tail, group_part
 
     shaped = lambda v: v.reshape(side, side, slots, share).transpose(2, 0, 1, 3)

time: 271 us -> 263 us (0.970)
  waiting for transfers between devices: 104 us -> 95.9 us
  starting transfers between devices: 32.6 us -> 36 us
    ppermute x48 -> x47, waiting for transfers between devices: 104 us -> 95.9 us  [swap(): return lax.ppermute(v, axis, [(i, i ^ k) for i in range(size)])]
    ppermute x48 -> x47, starting transfers between devices: 32.6 us -> 36 us  [swap(): return lax.ppermute(v, axis, [(i, i ^ k) for i in range(size)])]
    pallas_call x43 -> x44, Pallas kernels: 69.6 us -> 67.5 us  [call(): pl.pallas_call(kernel, out_shape=list(outs), grid=(steps,) if steps else...]
  transfers between devices with their start and end apart: 48 -> 47, of which waited for: 19 -> 21; matrix products, arithmetic and copies ran while one was open for 2% -> 2% of each run, Pallas kernels for 20% -> 21%
where the time goes in v3:
time: 263 us; the launch traced here: 262 us
  waiting for transfers between devices  95.9 us (36%)
  Pallas kernels  67.5 us (26%)
  blocking collectives  49.6 us (19%)
  starting transfers between devices  36 us (14%)
  local copies, waits for them, and re-layouts  8.1 us (3%)
    ppermute x47, waiting for transfers between devices, swap(): return lax.ppermute(v, axis, [(i, i ^ k) for i in range(size)])  95.9 us
    pallas_call x44, Pallas kernels, call(): pl.pallas_call(kernel, out_shape=list(outs), grid=(steps,) if steps else...  67.5 us
    all_to_all x5, blocking collectives, batch_sum(): return lax.all_to_all(spread, 'batch', 0, 0)  49.6 us
    ppermute x47, starting transfers between devices, swap(): return lax.ppermute(v, axis, [(i, i ^ k) for i in range(size)])  36 us
  transfers between devices with their start and end apart: 47, of which 21 were waited for; matrix products, arithmetic and copies ran while one was open for 2% of the time, Pallas kernels for 21%

profile of v3, /device:TPU:0, one launch (start us, length us, event | category | flops | bytes accessed | tf_op | source)
XLA Modules:
  0.0 262.3 jit_solution(13551720584859139680)
XLA Ops:
  3.9 2.6 collective-permute-start.1
  7.9 11.1 %collective-permute-done.1.refs_0_ = bf16[1024,256]{1,0:T(8,128)(2,1)S(1)} collective-permute-done((bf16[1024,256]{1,0:T(8,128)(2,1)S(1)}, bf16[1024,256]{1,0:T(8,128)(2,1)S(1)}, u32[]{:S(2)}, u32[]{:S(2)}) %collective-permute-start.1) | collective-permute-done | bytes 524320 | tf_op jit(solution)/shard_map/ppermute | solution.py:557
  19.1 2.7 %part_far.1 = bf16[1984,256]{1,0:T(8,128)(2,1)S(1)} custom-call(s32[5]{0:T(128)S(1)} %stack.11.dims, bf16[1984,512]{1,0:T(8,128)(2,1)S(1)} %pad.4.own.refs_0_.feats, bf16[1984,512]{1,0:T(8,128)(2,1)} %collective-permute-done.beside.refs_1_, bf16[1024,256]{1,0:T(8,128)(2,1)S(1)} %collective-permute-done.1.refs_0_), custom_call_target="tpu_custom_call" | custom-call | flops 1040187392 | bytes 5603348 | tf_op jit(solution)/shard_map/part_far/pallas_call | solution.py:538
  24.2 3.6 %near.1.part = f32[1984,256]{1,0:T(8,128)S(1)} custom-call(s32[5]{0:T(128)S(1)} %stack.11.dims, bf16[1984,512]{1,0:T(8,128)(2,1)S(1)} %pad.4.own.refs_0_.feats, bf16[1984,512]{1,0:T(8,128)(2,1)} %collective-permute-done.beside.refs_1_, bf16[2048,256]{1,0:T(8,128)(2,1)S(1)} %copy-done.1), custom_call_target="tpu_custom_call" | custom-call | flops 1040187392 | bytes 7143444 | tf_op jit(solution)/shard_map/near/pallas_call | solution.py:538
  27.9 3.3 %copy-done = bf16[24,9,9,2048]{3,0,2,1:T(8,128)(2,1)S(1)} copy-done((bf16[24,9,9,2048]{3,0,2,1:T(8,128)(2,1)S(1)}, bf16[24,9,9,2048]{3,0,2,1:T(8,128)(2,1)}, u32[]{:S(2)}) %copy-start) | copy-done | bytes 7962648
  33.0 2.5 fusion.5.live
  35.8 10.2 %collective-permute-done.2.refs_0_ = bf16[1984,256]{1,0:T(8,128)(2,1)S(1)} collective-permute-done((bf16[1984,256]{1,0:T(8,128)(2,1)S(1)}, bf16[1984,256]{1,0:T(8,128)(2,1)S(1)}, u32[]{:S(2)}, u32[]{:S(2)}) %collective-permute-start.2) | collective-permute-done | bytes 1015840 | tf_op jit(solution)/shard_map/ppermute | solution.py:557
  48.1 3.7 %collective-permute-start.8 = (f32[1,3,256]{2,1,0:T(4,128)S(1)}, f32[1,3,256]{2,1,0:T(4,128)S(1)}, u32[]{:S(2)}, u32[]{:S(2)}) collective-permute-start(f32[1,3,256]{2,1,0:T(4,128)S(1)} %get-tuple-element.128.refs_0_), channel_id=1, source_target_pairs={{0,24},{4,28},{8,16},{12,20},{16,8},{20,12},{24,0},{28,4},{1,25},{... | collective-permute-start | bytes 9224 | tf_op jit(solution)/shard_map/ppermute | solution.py:557
  53.6 2.7 %collective-permute-done.7.refs_2_ = f32[1,3,256]{2,1,0:T(4,128)S(1)} collective-permute-done((f32[1,3,256]{2,1,0:T(4,128)S(1)}, f32[1,3,256]{2,1,0:T(4,128)S(1)}, u32[]{:S(2)}, u32[]{:S(2)}) %collective-permute-start.7) | collective-permute-done | bytes 3104 | tf_op jit(solution)/shard_map/ppermute | solution.py:557
  60.0 3.5 %conv.1 = (f32[1984,256]{1,0:T(8,128)S(1)}, f32[8,2,256]{2,1,0:T(2,128)S(1)}) custom-call(f32[1984,128]{1,0:T(8,128)S(1)} %fusion.5.live, f32[1984,256]{1,0:T(8,128)S(1)} %get-tuple-element.127.z, f32[2,3,256]{2,1,0:T(4,128)S(1)} %pair.1.got.counts, f32[1,256]{1,0:T(1,128)S(1)} %bitcast.36, f32[1,256]{1,0:T(1,128)S(1)} %bitcast.44, bf16[9,256,256]{2,1,0:T(8,128)(2,1)S(1)} %taps.1), custom_call_target="tpu_custom_call" | custom-call | flops 2340421632 | bytes 6283264 | tf_op jit(solution)/shard_map/conv/pallas_call | solution.py:538
  63.6 10.5 %all_to_all.25.got.got_two = f32[8,2,256]{2,1,0:T(2,128)S(1)} all-to-all(f32[8,2,256]{2,1,0:T(2,128)S(1)} %get-tuple-element.133), channel_id=1, replica_groups=mesh['batch'=8,'chan'=4] {'batch'}, dimensions={0} | all-to-all | bytes 32768 | tf_op jit(solution)/shard_map/all_to_all | solution.py:561
  76.3 2.5 slope_one.1.slope
  79.0 2.5 slope_two.1.slope
  82.9 17.7 %collective-permute-done.13.refs_0_.refs_2_ = bf16[1984,256]{1,0:T(8,128)(2,1)S(1)} collective-permute-done((bf16[1984,256]{1,0:T(8,128)(2,1)S(1)}, bf16[1984,256]{1,0:T(8,128)(2,1)S(1)}, u32[]{:S(2)}, u32[]{:S(2)}) %collective-permute-start.13) | collective-permute-done | bytes 1015840 | tf_op jit(solution)/shard_map/ppermute | solution.py:557
  105.2 9.1 %all_to_all.26.got = f32[8,2,512]{2,1,0:T(2,128)S(1)} all-to-all(f32[8,2,512]{2,1,0:T(2,128)S(1)} %get-tuple-element.137), channel_id=1, replica_groups=mesh['batch'=8,'chan'=4] {'batch'}, dimensions={0} | all-to-all | bytes 65536 | tf_op jit(solution)/shard_map/all_to_all | solution.py:561
  114.3 3.8 %third.1 = (f32[1984,512]{1,0:T(8,128)S(1)}, f32[8,2,512]{2,1,0:T(2,128)S(1)}) custom-call(f32[1984,128]{1,0:T(8,128)S(1)} %fusion.5.live, f32[1984,512]{1,0:T(8,128)S(1)} %get-tuple-element.148.e, f32[2,3,256]{2,1,0:T(4,128)S(1)} %pair.1.got.counts, f32[8,2,512]{2,1,0:T(2,128)S(1)} %all_to_all.26.got, f32[1,512]{1,0:T(1,128)S(1)} %get-tuple-element.112.gain, ...), custom_call_target="tpu_custom_call" | custom-call | flops 2080374784 | bytes 13281280 | tf_op jit(solution)/shard_map/third/pallas_call | solution.py:538
  118.2 9.1 %all_to_all.27.totals = f32[8,2,512]{2,1,0:T(2,128)S(1)} all-to-all(f32[8,2,512]{2,1,0:T(2,128)S(1)} %get-tuple-element.139), channel_id=1, replica_groups=mesh['batch'=8,'chan'=4] {'batch'}, dimensions={0} | all-to-all | bytes 65536 | tf_op jit(solution)/shard_map/all_to_all | solution.py:561
  129.3 2.9 %collective-permute-done.15.refs_2_ = bf16[1296,512]{1,0:T(8,128)(2,1)S(1)} collective-permute-done((bf16[1296,512]{1,0:T(8,128)(2,1)S(1)}, bf16[1296,512]{1,0:T(8,128)(2,1)S(1)}, u32[]{:S(2)}, u32[]{:S(2)}) %collective-permute-start.15) | collective-permute-done | bytes 1327136 | tf_op jit(solution)/shard_map/ppermute | solution.py:557
  135.2 2.4 expand_grad.1.refs_0_
  139.0 5.1 %block.1 = bf16[1944,512]{1,0:T(8,128)(2,1)} custom-call(f32[1984,128]{1,0:T(8,128)S(1)} %fusion.5.live, f32[1984,512]{1,0:T(8,128)S(1)} %get-tuple-element.148.e, f32[2,3,256]{2,1,0:T(4,128)S(1)} %pair.1.got.counts, f32[8,2,512]{2,1,0:T(2,128)S(1)} %all_to_all.26.got, f32[1,512]{1,0:T(1,128)S(1)} %get-tuple-element.112.gain, ...), custom_call_target="tpu_custom_call" | custom-call | flops 1040187392 | bytes 9144320 | tf_op jit(solution)/shard_map/block/pallas_call | solution.py:538
  144.1 8.5 %collective-permute-done.20.refs_1_ = bf16[4,128,512]{2,1,0:T(8,128)(2,1)S(1)} collective-permute-done((bf16[4,128,512]{2,1,0:T(8,128)(2,1)S(1)}, bf16[4,128,512]{2,1,0:T(8,128)(2,1)S(1)}, u32[]{:S(2)}, u32[]{:S(2)}) %collective-permute-start.20) | collective-permute-done | bytes 524320 | tf_op jit(solution)/shard_map/ppermute | solution.py:557
  153.7 7.5 %collective-permute-done.21.refs_2_ = bf16[4,64,512]{2,1,0:T(8,128)(2,1)S(1)} collective-permute-done((bf16[4,64,512]{2,1,0:T(8,128)(2,1)S(1)}, bf16[4,64,512]{2,1,0:T(8,128)(2,1)S(1)}, u32[]{:S(2)}, u32[]{:S(2)}) %collective-permute-start.21) | collective-permute-done | bytes 262176 | tf_op jit(solution)/shard_map/ppermute | solution.py:557
  165.2 11.8 %all_to_all.28.totals = f32[8,2,256]{2,1,0:T(2,128)S(1)} all-to-all(f32[8,2,256]{2,1,0:T(2,128)S(1)} %get-tuple-element.153), channel_id=1, replica_groups=mesh['batch'=8,'chan'=4] {'batch'}, dimensions={0} | all-to-all | bytes 32768 | tf_op jit(solution)/shard_map/all_to_all | solution.py:561
  177.0 3.5 %conv_back.1 = (f32[1984,256]{1,0:T(8,128)S(1)}, f32[1984,256]{1,0:T(8,128)S(1)}, f32[8,2,256]{2,1,0:T(2,128)S(1)}, f32[2,256]{1,0:T(2,128)S(1)}) custom-call(f32[1984,128]{1,0:T(8,128)S(1)} %fusion.5.live, f32[1984,256]{1,0:T(8,128)S(1)} %get-tuple-element.152.d_two, f32[1984,256]{1,0:T(8,128)S(1)} %get-tuple-element.129.z.grouped, ...), custom_call_target="tpu_custom_call" | custom-call | flops 2340421632 | bytes 14443520 | tf_op jit(solution)/shard_map/conv_back/pallas_call | solution.py:538
  180.6 9.2 %all_to_all.29.totals = f32[8,2,256]{2,1,0:T(2,128)S(1)} all-to-all(f32[8,2,256]{2,1,0:T(2,128)S(1)} %get-tuple-element.164), channel_id=1, replica_groups=mesh['batch'=8,'chan'=4] {'batch'}, dimensions={0} | all-to-all | bytes 32768 | tf_op jit(solution)/shard_map/all_to_all | solution.py:561
  191.6 3.7 %reduce_grad.1 = (bf16[2048,256]{1,0:T(8,128)(2,1)S(1)}, f32[2,512,256]{2,1,0:T(8,128)S(1)}) custom-call(s32[5]{0:T(128)S(1)} %stack.11.dims, bf16[1984,256]{1,0:T(8,128)(2,1)S(1)} %get-tuple-element.186.d_red.refs_0_, bf16[1984,512]{1,0:T(8,128)(2,1)S(1)} %pad.4.own.refs_0_.feats, bf16[1984,512]{1,0:T(8,128)(2,1)} %collective-permute-done.beside.refs_1_, ...), custom_call_target="tpu_custom_call" | custom-call | flops 2080374784 | bytes 9830420 | tf_op jit(solution)/shard_map/reduce_grad/pallas_call | solution.py:538
  204.1 3.7 %group_grad.1.a = bf16[288,256]{1,0:T(8,128)(2,1)S(1)} custom-call(f32[1984,128]{1,0:T(8,128)S(1)} %fusion.5.live, f32[1984,256]{1,0:T(8,128)S(1)} %get-tuple-element.127.z, f32[2,3,256]{2,1,0:T(4,128)S(1)} %pair.1.got.counts, f32[1,256]{1,0:T(1,128)S(1)} %bitcast.39, f32[1,256]{1,0:T(1,128)S(1)} %bitcast.46, f32[1984,256]{1,0:T(8,128)S(1)} %get-tuple-element.174.d_grouped), custom_call_target="tpu_custom_call" | custom-call | flops 520093696 | bytes 5234688 | tf_op jit(solution)/shard_map/group_grad/pallas_call | solution.py:538
  212.6 5.1 %collective-permute-done.33.refs_0_ = bf16[64,2048]{1,0:T(8,128)(2,1)S(1)} collective-permute-done((bf16[64,2048]{1,0:T(8,128)(2,1)S(1)}, bf16[64,2048]{1,0:T(8,128)(2,1)S(1)}, u32[]{:S(2)}, u32[]{:S(2)}) %collective-permute-start.33) | collective-permute-done | bytes 262176 | tf_op jit(solution)/shard_map/ppermute | solution.py:557
  224.9 8.6 %collective-permute-done.37.refs_0_ = bf16[128,2048]{1,0:T(8,128)(2,1)S(1)} collective-permute-done((bf16[128,2048]{1,0:T(8,128)(2,1)S(1)}, bf16[128,2048]{1,0:T(8,128)(2,1)S(1)}, u32[]{:S(2)}, u32[]{:S(2)}) %collective-permute-start.37) | collective-permute-done | bytes 524320 | tf_op jit(solution)/shard_map/ppermute | solution.py:557
  242.6 2.5 collective-permute-done.41.b
  251.3 2.7 %input_far.1 = f32[1944,512]{1,0:T(8,128)} custom-call(f32[1984,512]{1,0:T(8,128)S(1)} %input_near.1.part, bf16[992,256]{1,0:T(8,128)(2,1)S(1)} %collective-permute-done.34.refs_0_, bf16[992,256]{1,0:T(8,128)(2,1)S(1)} %collective-permute-done.38.refs_1_, bf16[992,256]{1,0:T(8,128)(2,1)S(1)} %collective-permute-done.39.refs_2_, ...), custom_call_target="tpu_custom_call" | custom-call | flops 1040187392 | bytes 10600448 | tf_op jit(solution)/shard_map/input_far/pallas_call | solution.py:538
  254.1 4.7 %collective-permute-done.45.b = bf16[288,256]{1,0:T(8,128)(2,1)S(1)} collective-permute-done((bf16[288,256]{1,0:T(8,128)(2,1)S(1)}, bf16[288,256]{1,0:T(8,128)(2,1)S(1)}, u32[]{:S(2)}, u32[]{:S(2)}) %collective-permute-start.45) | collective-permute-done | bytes 147488 | tf_op jit(solution)/shard_map/ppermute | solution.py:557
  (148 shorter events, 76.8 us)
Async XLA Ops:
  3.4 15.6 %collective-permute-start = (bf16[1984,512]{1,0:T(8,128)(2,1)S(1)}, bf16[1984,512]{1,0:T(8,128)(2,1)}, u32[]{:S(2)}, u32[]{:S(2)}) collective-permute-start(bf16[1984,512]{1,0:T(8,128)(2,1)S(1)} %pad.4.own.refs_0_.feats), channel_id=1, source_target_pairs={{0,1},{1,0},{2,3},{3,2},{4,5},{5,4},{6,7},{7,6},{8,9},{9,8},{10,11... | collective-permute-start | bytes 6094856 | tf_op jit(solution)/shard_map/ppermute | solution.py:557
  3.9 15.1 %collective-permute-start.1 = (bf16[1024,256]{1,0:T(8,128)(2,1)S(1)}, bf16[1024,256]{1,0:T(8,128)(2,1)S(1)}, u32[]{:S(2)}, u32[]{:S(2)}) collective-permute-start(bf16[1024,256]{1,0:T(8,128)(2,1)S(1)} %constant_dynamic-slice_fusion), channel_id=1, source_target_pairs={{0,2},{1,3},{2,0},{3,1},{4,6},{5,7},{6,4},{7,5},{8,10},{9,11},{10,... | collective-permute-start | bytes 1572872 | tf_op jit(solution)/shard_map/ppermute | solution.py:557
  21.7 24.3 %collective-permute-start.2 = (bf16[1984,256]{1,0:T(8,128)(2,1)S(1)}, bf16[1984,256]{1,0:T(8,128)(2,1)S(1)}, u32[]{:S(2)}, u32[]{:S(2)}) collective-permute-start(bf16[1984,256]{1,0:T(8,128)(2,1)S(1)} %part_far.1), channel_id=1, source_target_pairs={{0,2},{1,3},{2,0},{3,1},{4,6},{5,7},{6,4},{7,5},{8,10},{9,11},{10,... | collective-permute-start | bytes 3047432 | tf_op jit(solution)/shard_map/ppermute | solution.py:557
  27.8 7.9 %collective-permute-start.5 = (bf16[512,256]{1,0:T(8,128)(2,1)S(1)}, bf16[512,256]{1,0:T(8,128)(2,1)S(1)}, u32[]{:S(2)}, u32[]{:S(2)}) collective-permute-start(bf16[512,256]{1,0:T(8,128)(2,1)S(1)} %get-tuple-element.122), channel_id=1, source_target_pairs={{0,1},{1,0},{2,3},{3,2},{4,5},{5,4},{6,7},{7,6},{8,9},{9,8},{10,11... | collective-permute-start | bytes 786440 | tf_op jit(solution)/shard_map/ppermute | solution.py:557
  46.0 17.6 %collective-permute-start.10 = (bf16[256,512]{1,0:T(8,128)(2,1)S(1)}, bf16[256,512]{1,0:T(8,128)(2,1)S(1)}, u32[]{:S(2)}, u32[]{:S(2)}) collective-permute-start(bf16[256,512]{1,0:T(8,128)(2,1)S(1)} %get-tuple-element.131), channel_id=1, source_target_pairs={{0,2},{1,3},{2,0},{3,1},{4,6},{5,7},{6,4},{7,5},{8,10},{9,11},{10,... | collective-permute-start | bytes 786440 | tf_op jit(solution)/shard_map/ppermute | solution.py:557
  47.6 16.0 %collective-permute-start.11 = (bf16[256,512]{1,0:T(8,128)(2,1)S(1)}, bf16[256,512]{1,0:T(8,128)(2,1)S(1)}, u32[]{:S(2)}, u32[]{:S(2)}) collective-permute-start(bf16[256,512]{1,0:T(8,128)(2,1)S(1)} %get-tuple-element.132), channel_id=1, source_target_pairs={{0,3},{1,2},{2,1},{3,0},{4,7},{5,6},{6,5},{7,4},{8,11},{9,10},{10,... | collective-permute-start | bytes 786440 | tf_op jit(solution)/shard_map/ppermute | solution.py:557
  75.8 24.9 %collective-permute-start.13 = (bf16[1984,256]{1,0:T(8,128)(2,1)S(1)}, bf16[1984,256]{1,0:T(8,128)(2,1)S(1)}, u32[]{:S(2)}, u32[]{:S(2)}) collective-permute-start(bf16[1984,256]{1,0:T(8,128)(2,1)S(1)} %hidden.1.refs_0_), channel_id=1, source_target_pairs={{0,2},{1,3},{2,0},{3,1},{4,6},{5,7},{6,4},{7,5},{8,10},{9,11},{10,... | collective-permute-start | bytes 3047432 | tf_op jit(solution)/shard_map/ppermute | solution.py:557
  100.6 31.5 %collective-permute-start.15 = (bf16[1296,512]{1,0:T(8,128)(2,1)S(1)}, bf16[1296,512]{1,0:T(8,128)(2,1)S(1)}, u32[]{:S(2)}, u32[]{:S(2)}) collective-permute-start(bf16[1296,512]{1,0:T(8,128)(2,1)S(1)} %slice.36), channel_id=1, source_target_pairs={{0,2},{1,3},{2,0},{3,1},{4,6},{5,7},{6,4},{7,5},{8,10},{9,11},{10,... | collective-permute-start | bytes 3981320 | tf_op jit(solution)/shard_map/ppermute | solution.py:557
  134.6 27.2 %collective-permute-start.19 = (bf16[1984,256]{1,0:T(8,128)(2,1)S(1)}, bf16[1984,256]{1,0:T(8,128)(2,1)S(1)}, u32[]{:S(2)}, u32[]{:S(2)}) collective-permute-start(bf16[1984,256]{1,0:T(8,128)(2,1)S(1)} %merge.1), channel_id=1, source_target_pairs={{0,2},{1,3},{2,0},{3,1},{4,6},{5,7},{6,4},{7,5},{8,10},{9,11},{10,... | collective-permute-start | bytes 3047432 | tf_op jit(solution)/shard_map/ppermute | solution.py:557
  135.2 28.8 %collective-permute-start.17 = (bf16[1296,512]{1,0:T(8,128)(2,1)S(1)}, bf16[1296,512]{1,0:T(8,128)(2,1)S(1)}, u32[]{:S(2)}, u32[]{:S(2)}) collective-permute-start(bf16[1296,512]{1,0:T(8,128)(2,1)S(1)} %collective-permute-done.15.refs_2_), channel_id=1, source_target_pairs={{0,1},{1,0},{2,3},{3,2},{4,5},{5,4},{6,7},{7,6},{8,9},{9,8},{10,11... | collective-permute-start | bytes 3981320 | tf_op jit(solution)/shard_map/ppermute | solution.py:557
  138.1 14.4 %collective-permute-start.20 = (bf16[4,128,512]{2,1,0:T(8,128)(2,1)S(1)}, bf16[4,128,512]{2,1,0:T(8,128)(2,1)S(1)}, u32[]{:S(2)}, u32[]{:S(2)}) collective-permute-start(bf16[4,128,512]{2,1,0:T(8,128)(2,1)S(1)} %send.3), channel_id=1, source_target_pairs={{0,4},{4,0},{8,12},{12,8},{16,20},{20,16},{24,28},{28,24},{1,5},{5... | collective-permute-start | bytes 1572872 | tf_op jit(solution)/shard_map/ppermute | solution.py:557
  138.7 25.3 %collective-permute-start.18 = (bf16[1984,256]{1,0:T(8,128)(2,1)S(1)}, bf16[1984,256]{1,0:T(8,128)(2,1)S(1)}, u32[]{:S(2)}, u32[]{:S(2)}) collective-permute-start(bf16[1984,256]{1,0:T(8,128)(2,1)S(1)} %get-tuple-element.145), channel_id=1, source_target_pairs={{0,1},{1,0},{2,3},{3,2},{4,5},{5,4},{6,7},{7,6},{8,9},{9,8},{10,11... | collective-permute-start | bytes 3047432 | tf_op jit(solution)/shard_map/ppermute | solution.py:557
  153.2 8.0 %collective-permute-start.21 = (bf16[4,64,512]{2,1,0:T(8,128)(2,1)S(1)}, bf16[4,64,512]{2,1,0:T(8,128)(2,1)S(1)}, u32[]{:S(2)}, u32[]{:S(2)}) collective-permute-start(bf16[4,64,512]{2,1,0:T(8,128)(2,1)S(1)} %send.4), channel_id=1, source_target_pairs={{0,8},{4,12},{8,0},{12,4},{16,24},{20,28},{24,16},{28,20},{1,9},{5... | collective-permute-start | bytes 786440 | tf_op jit(solution)/shard_map/ppermute | solution.py:557
  161.9 18.7 %collective-permute-start.23 = (bf16[688,512]{1,0:T(8,128)(2,1)S(1)}, bf16[688,512]{1,0:T(8,128)(2,1)S(1)}, u32[]{:S(2)}, u32[]{:S(2)}) collective-permute-start(bf16[688,512]{1,0:T(8,128)(2,1)S(1)} %slice.37), channel_id=1, source_target_pairs={{0,2},{1,3},{2,0},{3,1},{4,6},{5,7},{6,4},{7,5},{8,10},{9,11},{10,... | collective-permute-start | bytes 2113544 | tf_op jit(solution)/shard_map/ppermute | solution.py:557
  163.5 17.0 %collective-permute-start.22 = (bf16[4,64,512]{2,1,0:T(8,128)(2,1)S(1)}, bf16[4,64,512]{2,1,0:T(8,128)(2,1)S(1)}, u32[]{:S(2)}, u32[]{:S(2)}) collective-permute-start(bf16[4,64,512]{2,1,0:T(8,128)(2,1)S(1)} %send.5.a), channel_id=1, source_target_pairs={{0,16},{4,20},{8,24},{12,28},{16,0},{20,4},{24,8},{28,12},{1,17},{... | collective-permute-start | bytes 786440 | tf_op jit(solution)/shard_map/ppermute | solution.py:557
  199.1 8.7 %collective-permute-start.30 = (bf16[512,256]{1,0:T(8,128)(2,1)S(1)}, bf16[512,256]{1,0:T(8,128)(2,1)S(1)}, u32[]{:S(2)}, u32[]{:S(2)}) collective-permute-start(bf16[512,256]{1,0:T(8,128)(2,1)S(1)} %get-tuple-element.176), channel_id=1, source_target_pairs={{0,8},{4,12},{8,0},{12,4},{16,24},{20,28},{24,16},{28,20},{1,9},{5... | collective-permute-start | bytes 786440 | tf_op jit(solution)/shard_map/ppermute | solution.py:557
  199.6 8.3 %collective-permute-start.26 = (bf16[512,256]{1,0:T(8,128)(2,1)S(1)}, bf16[512,256]{1,0:T(8,128)(2,1)S(1)}, u32[]{:S(2)}, u32[]{:S(2)}) collective-permute-start(bf16[512,256]{1,0:T(8,128)(2,1)S(1)} %get-tuple-element.169), channel_id=1, source_target_pairs={{0,4},{4,0},{8,12},{12,8},{16,20},{20,16},{24,28},{28,24},{1,5},{5... | collective-permute-start | bytes 786440 | tf_op jit(solution)/shard_map/ppermute | solution.py:557
  203.3 15.1 %collective-permute-start.34 = (bf16[992,256]{1,0:T(8,128)(2,1)S(1)}, bf16[992,256]{1,0:T(8,128)(2,1)S(1)}, u32[]{:S(2)}, u32[]{:S(2)}) collective-permute-start(bf16[992,256]{1,0:T(8,128)(2,1)S(1)} %slice.38), channel_id=1, source_target_pairs={{0,2},{1,3},{2,0},{3,1},{4,6},{5,7},{6,4},{7,5},{8,10},{9,11},{10,... | collective-permute-start | bytes 1523720 | tf_op jit(solution)/shard_map/ppermute | solution.py:557
  208.5 9.2 %collective-permute-start.33 = (bf16[64,2048]{1,0:T(8,128)(2,1)S(1)}, bf16[64,2048]{1,0:T(8,128)(2,1)S(1)}, u32[]{:S(2)}, u32[]{:S(2)}) collective-permute-start(bf16[64,2048]{1,0:T(8,128)(2,1)S(1)} %arrange.1.mine), channel_id=1, source_target_pairs={{0,8},{4,12},{8,0},{12,4},{16,24},{20,28},{24,16},{28,20},{1,9},{5... | collective-permute-start | bytes 786440 | tf_op jit(solution)/shard_map/ppermute | solution.py:557
  210.1 8.2 %collective-permute-start.32 = (bf16[288,256]{1,0:T(8,128)(2,1)S(1)}, bf16[288,256]{1,0:T(8,128)(2,1)S(1)}, u32[]{:S(2)}, u32[]{:S(2)}) collective-permute-start(bf16[288,256]{1,0:T(8,128)(2,1)S(1)} %group_grad.1.a), channel_id=1, source_target_pairs={{0,4},{4,0},{8,12},{12,8},{16,20},{20,16},{24,28},{28,24},{1,5},{5... | collective-permute-start | bytes 442376 | tf_op jit(solution)/shard_map/ppermute | solution.py:557
  210.6 7.7 %collective-permute-start.35 = (bf16[256,256]{1,0:T(8,128)(2,1)S(1)}, bf16[256,256]{1,0:T(8,128)(2,1)S(1)}, u32[]{:S(2)}, u32[]{:S(2)}) collective-permute-start(bf16[256,256]{1,0:T(8,128)(2,1)S(1)} %get-tuple-element.184), channel_id=1, source_target_pairs={{0,4},{4,0},{8,12},{12,8},{16,20},{20,16},{24,28},{28,24},{1,5},{5... | collective-permute-start | bytes 393224 | tf_op jit(solution)/shard_map/ppermute | solution.py:557
  212.1 7.5 %collective-permute-start.31 = (bf16[256,256]{1,0:T(8,128)(2,1)S(1)}, bf16[256,256]{1,0:T(8,128)(2,1)S(1)}, u32[]{:S(2)}, u32[]{:S(2)}) collective-permute-start(bf16[256,256]{1,0:T(8,128)(2,1)S(1)} %get-tuple-element.178), channel_id=1, source_target_pairs={{0,8},{4,12},{8,0},{12,4},{16,24},{20,28},{24,16},{28,20},{1,9},{5... | collective-permute-start | bytes 393224 | tf_op jit(solution)/shard_map/ppermute | solution.py:557
  220.3 13.2 %collective-permute-start.37 = (bf16[128,2048]{1,0:T(8,128)(2,1)S(1)}, bf16[128,2048]{1,0:T(8,128)(2,1)S(1)}, u32[]{:S(2)}, u32[]{:S(2)}) collective-permute-start(bf16[128,2048]{1,0:T(8,128)(2,1)S(1)} %double.2.mine), channel_id=1, source_target_pairs={{0,4},{4,0},{8,12},{12,8},{16,20},{20,16},{24,28},{28,24},{1,5},{5... | collective-permute-start | bytes 1572872 | tf_op jit(solution)/shard_map/ppermute | solution.py:557
  220.9 16.8 %collective-permute-start.38 = (bf16[992,256]{1,0:T(8,128)(2,1)S(1)}, bf16[992,256]{1,0:T(8,128)(2,1)S(1)}, u32[]{:S(2)}, u32[]{:S(2)}) collective-permute-start(bf16[992,256]{1,0:T(8,128)(2,1)S(1)} %slice.39), channel_id=1, source_target_pairs={{0,2},{1,3},{2,0},{3,1},{4,6},{5,7},{6,4},{7,5},{8,10},{9,11},{10,... | collective-permute-start | bytes 1523720 | tf_op jit(solution)/shard_map/ppermute | solution.py:557
  222.4 15.2 %collective-permute-start.39 = (bf16[992,256]{1,0:T(8,128)(2,1)S(1)}, bf16[992,256]{1,0:T(8,128)(2,1)S(1)}, u32[]{:S(2)}, u32[]{:S(2)}) collective-permute-start(bf16[992,256]{1,0:T(8,128)(2,1)S(1)} %collective-permute-done.34.refs_0_), channel_id=1, source_target_pairs={{0,1},{1,0},{2,3},{3,2},{4,5},{5,4},{6,7},{7,6},{8,9},{9,8},{10,11... | collective-permute-start | bytes 1523720 | tf_op jit(solution)/shard_map/ppermute | solution.py:557
  222.4 15.2 %collective-permute-start.36 = (bf16[512,256]{1,0:T(8,128)(2,1)S(1)}, bf16[512,256]{1,0:T(8,128)(2,1)S(1)}, u32[]{:S(2)}, u32[]{:S(2)}) collective-permute-start(bf16[512,256]{1,0:T(8,128)(2,1)S(1)} %send_both.5.a), channel_id=1, source_target_pairs={{0,16},{4,20},{8,24},{12,28},{16,0},{20,4},{24,8},{28,12},{1,17},{... | collective-permute-start | bytes 786440 | tf_op jit(solution)/shard_map/ppermute | solution.py:557
  237.8 7.4 %collective-permute-start.42 = (bf16[992,256]{1,0:T(8,128)(2,1)S(1)}, bf16[992,256]{1,0:T(8,128)(2,1)S(1)}, u32[]{:S(2)}, u32[]{:S(2)}) collective-permute-start(bf16[992,256]{1,0:T(8,128)(2,1)S(1)} %collective-permute-done.38.refs_1_), channel_id=1, source_target_pairs={{0,1},{1,0},{2,3},{3,2},{4,5},{5,4},{6,7},{7,6},{8,9},{9,8},{10,11... | collective-permute-start | bytes 1523720 | tf_op jit(solution)/shard_map/ppermute | solution.py:557
  238.4 6.7 %collective-permute-start.43 = (bf16[256,256]{1,0:T(8,128)(2,1)S(1)}, bf16[256,256]{1,0:T(8,128)(2,1)S(1)}, u32[]{:S(2)}, u32[]{:S(2)}) collective-permute-start(bf16[256,256]{1,0:T(8,128)(2,1)S(1)} %get-tuple-element.205), channel_id=1, source_target_pairs={{0,4},{4,0},{8,12},{12,8},{16,20},{20,16},{24,28},{28,24},{1,5},{5... | collective-permute-start | bytes 393224 | tf_op jit(solution)/shard_map/ppermute | solution.py:557
  240.0 7.5 %collective-permute-start.40 = (bf16[256,256]{1,0:T(8,128)(2,1)S(1)}, bf16[256,256]{1,0:T(8,128)(2,1)S(1)}, u32[]{:S(2)}, u32[]{:S(2)}) collective-permute-start(bf16[256,256]{1,0:T(8,128)(2,1)S(1)} %get-tuple-element.206), channel_id=1, source_target_pairs={{0,8},{4,12},{8,0},{12,4},{16,24},{20,28},{24,16},{28,20},{1,9},{5... | collective-permute-start | bytes 393224 | tf_op jit(solution)/shard_map/ppermute | solution.py:557
  248.1 12.2 %collective-permute-start.44 = (bf16[512,256]{1,0:T(8,128)(2,1)S(1)}, bf16[512,256]{1,0:T(8,128)(2,1)S(1)}, u32[]{:S(2)}, u32[]{:S(2)}) collective-permute-start(bf16[512,256]{1,0:T(8,128)(2,1)S(1)} %get-tuple-element.195.a), channel_id=1, source_target_pairs={{0,4},{4,0},{8,12},{12,8},{16,20},{20,16},{24,28},{28,24},{1,5},{5... | collective-permute-start | bytes 786440 | tf_op jit(solution)/shard_map/ppermute | solution.py:557
  249.6 9.2 %collective-permute-start.45 = (bf16[288,256]{1,0:T(8,128)(2,1)S(1)}, bf16[288,256]{1,0:T(8,128)(2,1)S(1)}, u32[]{:S(2)}, u32[]{:S(2)}) collective-permute-start(bf16[288,256]{1,0:T(8,128)(2,1)S(1)} %add.37.a), channel_id=1, source_target_pairs={{0,16},{4,20},{8,24},{12,28},{16,0},{20,4},{24,8},{28,12},{1,17},{... | collective-permute-start | bytes 442376 | tf_op jit(solution)/shard_map/ppermute | solution.py:557
  249.6 10.7 %collective-permute-start.46 = (bf16[512,256]{1,0:T(8,128)(2,1)S(1)}, bf16[512,256]{1,0:T(8,128)(2,1)S(1)}, u32[]{:S(2)}, u32[]{:S(2)}) collective-permute-start(bf16[512,256]{1,0:T(8,128)(2,1)S(1)} %get-tuple-element.197.b), channel_id=1, source_target_pairs={{0,8},{4,12},{8,0},{12,4},{16,24},{20,28},{24,16},{28,20},{1,9},{5... | collective-permute-start | bytes 786440 | tf_op jit(solution)/shard_map/ppermute | solution.py:557
  (25 other events, 157.7 us)

commit v4 on v3

--- a/solution.py
+++ b/solution.py
@@ -435,27 +435,24 @@
             rows //= 2
             side = bit_of(b, order[t])
             at += rows * (side if t < step else 1 - side)
-        here = pl.ds(at if isinstance(at, int) else pl.multiple_of(at, 16), rows)
+        here = pl.ds(at if isinstance(at, int) else pl.multiple_of(at, min(rows, 16)), rows)
         v = term[:, here, :] if len(term.shape) == 3 else term[here, :]
         total = v.astype(F32) if total is None else total + v.astype(F32)
     return total.astype(BF16)
 
 
-def send_kernel(step, last, dims, *refs):
-    *terms, out = refs
-    sized = [(t, t.shape[-2]) for t in terms]
-    out[...] = add_terms(dims[3], sized, range(step + 1), step, last, 0)
-
-
 def send_both_kernel(step, last, orders, dims, whole, *refs):
-    half = whole.shape[0] // 2
+    half = whole.shape[-2] // 2
     n = step
     outs = refs[2 * n :]
     for i, order in enumerate(orders):
-        terms = [(whole, half)] + [(r, r.shape[0]) for r in refs[i * n : (i + 1) * n]]
+        terms = [(whole, half)] + [(r, r.shape[-2]) for r in refs[i * n : (i + 1) * n]]
         total = add_terms(dims[3], terms, order, step, last, i * half)
-        if last:
-            outs[0][i * total.shape[0] : (i + 1) * total.shape[0]] = total
+        rows = total.shape[-2]
+        if last and len(whole.shape) == 3:
+            outs[0][:, i * rows : (i + 1) * rows, :] = total
+        elif last:
+            outs[0][i * rows : (i + 1) * rows] = total
         else:
             outs[i][...] = total
 
@@ -467,8 +464,8 @@
         mine = sums[i * n : (i + 1) * n] if len(ins) == 2 else (sums, ins[0])[i][...]
         other = ins[i] if len(ins) == 2 else ins[i + 1]
         upper = bit_of(dims[3], bit)
-        out[pl.ds(pl.multiple_of(upper * n, 16), n), :] = mine
-        out[pl.ds(pl.multiple_of((1 - upper) * n, 16), n), :] = other[...]
+        out[pl.ds(pl.multiple_of(upper * n, min(n, 16)), n), :] = mine
+        out[pl.ds(pl.multiple_of((1 - upper) * n, min(n, 16)), n), :] = other[...]
 
 
 def finish_kernel(bits, dims, a, b, other_a, other_b, out):
@@ -476,26 +473,17 @@
     for i, (bit, mine, other) in enumerate(zip(bits, (a, b), (other_a, other_b))):
         upper = bit_of(dims[3], bit)
         at = 2 * i * n
-        out[pl.ds(pl.multiple_of(at + upper * n, 16), n), :] = mine[...].astype(F32)
-        out[pl.ds(pl.multiple_of(at + (1 - upper) * n, 16), n), :] = other[...].astype(F32)
+        out[pl.ds(pl.multiple_of(at + upper * n, min(n, 16)), n), :] = mine[...].astype(F32)
+        out[pl.ds(pl.multiple_of(at + (1 - upper) * n, min(n, 16)), n), :] = other[...].astype(F32)
 
 
 def arrange_kernel(dims, *refs):
-    *cols, out = refs
-    share = cols[0].shape[1]
+    *cols, a, b = refs
+    n, share = a.shape[0], cols[0].shape[1]
     for k, c in enumerate(cols):
-        out[:, pl.ds(pl.multiple_of((dims[2] ^ k) * share, share), share)] = c[...]
-
-
-def double_kernel(bit, dims, mine, *refs):
-    *other, out = refs
-    n = mine.shape[0]
-    upper = bit_of(dims[3], bit)
-    out[pl.ds(pl.multiple_of(upper * n, 16), n), :] = mine[...].astype(out.dtype)
-    at = (1 - upper) * n
-    for v in other:
-        out[pl.ds(pl.multiple_of(at, 16), v.shape[0]), :] = v[...].astype(out.dtype)
-        at += v.shape[0]
+        at = pl.ds(pl.multiple_of((dims[2] ^ k) * share, share), share)
+        a[:, at] = c[0:n]
+        b[:, at] = c[n:]
 
 
 def split_kernel(a, b, *outs):
@@ -588,21 +576,30 @@
     return [held[k] for k in range(size)]
 
 
-def send_of(dims, terms, step, last=False):
-    shape = list(terms[0].shape)
-    shape[-2] >>= step + (not last)
+def send_both(dims, whole, got, orders, step, last=False):
+    shape = list(whole.shape)
+    shape[-2] >>= step if last else step + 2
     return call(
-        functools.partial(send_kernel, step, last), [jax.ShapeDtypeStruct(tuple(shape), BF16)],
-        [dims, *terms], name="send", smem=True,
-    )
-
-
-def double(dims, mine, other, bit, dtype=BF16):
-    other = other if isinstance(other, list) else [other]
-    shape = (2 * mine.shape[0], mine.shape[1])
+        functools.partial(send_both_kernel, step, last, orders),
+        [jax.ShapeDtypeStruct(tuple(shape), BF16)] * (1 if last else 2),
+        [dims, whole, *got[0], *got[1]], name="send_both", smem=True,
+    )
+
+
+def double_pair(dims, pair, new, bits):
+    n, columns = new[0].shape
     return call(
-        functools.partial(double_kernel, bit), [jax.ShapeDtypeStruct(shape, dtype)],
-        [dims, mine, *other], name="double", smem=True,
+        functools.partial(double_pair_kernel, bits),
+        [jax.ShapeDtypeStruct((2 * n, columns), BF16)] * 2, [dims, *pair, *new],
+        name="double_pair", smem=True,
+    )
+
+
+def finish(dims, pair, new, bits):
+    n, columns = new[0].shape
+    return call(
+        functools.partial(finish_kernel, bits), [jax.ShapeDtypeStruct((4 * n, columns), F32)],
+        [dims, *pair, *new], name="finish", smem=True,
     )
 
 
@@ -774,22 +771,23 @@
         expand_grad_kernel, [shape((n_chan, width, share), BF16)],
         [after(d_expanded, far_sum), *hidden_all], flops=n_chan * mm, name="expand_grad",
     )
-    expand_terms = [expand_part]
     bits = n_batch.bit_length() - 1
-    send = send_of(dims, expand_terms, 0)
-    got = swap(send, "batch", n_batch, 1)
-    block_out = call(
-        block_kernel, [shape((rows, share), BF16)],
-        [live, after(expanded, send), got_one, got_three, gain_c, shift_c, own],
-        flops=2 * mm, name="block", steps=STEPS,
-    )
-    expand_terms.append(after(got, block_out))
-    send = send_of(dims, expand_terms, 1)
-    expand_terms.append(swap(send, "batch", n_batch, 2))
-    for t in range(2, bits - 1):
-        expand_send = send_of(dims, expand_terms, t)
-        expand_terms.append(swap(expand_send, "batch", n_batch, 1 << t))
-    mine = send_of(dims, expand_terms, bits - 1, True)
+    top = bits - 1
+    orders = [list(range(top)), [1, 0, *range(2, top)]]
+    halves = [0, 1]
+    got = [[], []]
+    for s in range(top):
+        send = send_both(dims, expand_part, got, orders, s)
+        new = [swap(send[h], "batch", n_batch, 1 << orders[h][s]) for h in halves]
+        if s == 0:
+            block_out = call(
+                block_kernel, [shape((rows, share), BF16)],
+                [live, after(expanded, send[0]), got_one, got_three, gain_c, shift_c, own],
+                flops=2 * mm, name="block", steps=STEPS,
+            )
+            new = [after(v, block_out) for v in new]
+        got = [got[h] + [new[h]] for h in halves]
+    mine = send_both(dims, expand_part, got, orders, top, True)
     expand_other = swap(mine, "batch", n_batch, 1 << (bits - 1))
     far_halves[0] = gather_core({k: after(v, far_sum) for k, v in far_halves[0].items()}, n_chan)
     terms[0] = after(d_zero, *far_halves[0].values())
@@ -840,57 +838,52 @@
         d_far[at] = gather_core({k: after(v, *ready) for k, v in d_far[at].items()}, n_chan)
         return list(d_far[at].values())
 
-    top = bits - 1
-    orders = [list(range(top)), [1, 0, *range(2, top)]]
     got = [[], []]
     for s in range(top):
-        rows_here = n_chan * share >> (s + 2)
-        send = call(
-            functools.partial(send_both_kernel, s, False, orders),
-            [shape((rows_here, width), BF16)] * 2, [dims, tail, *got[0], *got[1]],
-            name="send_both", smem=True,
-        )
-        new = [swap(send[i], "batch", n_batch, 1 << orders[i][s]) for i in range(2)]
+        send = send_both(dims, tail, got, orders, s)
+        new = [swap(send[h], "batch", n_batch, 1 << orders[h][s]) for h in halves]
         ties = []
         if s == 0:
             cols = [parts[0]]
             cols += [swap(after(parts[k], send[0]), "chan", n_chan, k) for k in others if k]
             cols = call(
-                arrange_kernel, [shape((mine.shape[1], n_chan * share), BF16)], [dims, *cols],
+                arrange_kernel, [shape((mine.shape[1] // 2, n_chan * share), BF16)] * 2, [dims, *cols],
                 name="arrange", smem=True,
             )
             group_part = call(
                 functools.partial(group_grad_kernel, side, slots, group_width),
                 [shape((9 * group_width, width), BF16)],
-                [live, z, got_one, gain_one, shift_one, after(d_grouped, cols)],
+                [live, z, got_one, gain_one, shift_one, after(d_grouped, *cols)],
                 [tall], flops=mm, name="group_grad",
             )
-            far_rows(0, cols)
+            far_rows(0, *cols)
             ties = [group_part]
         elif s == 1:
             group_other = swap(after(group_part, send[0]), "batch", n_batch, 1)
             for t in reversed(range(1, top)):
-                other = swap(after(cols, send[0]), "batch", n_batch, 1 << t)
-                cols = double(dims, cols, other, t)
-            group_part = add(group_part, after(group_other, cols))
+                others_cols = [
+                    swap(after(cols[h], send[0]), "batch", n_batch, 1 << orders[h][t])
+                    for h in halves
+                ]
+                cols = double_pair(dims, cols, others_cols, [o[t] for o in orders])
+            group_part = add(group_part, after(group_other, *cols))
             ties += [group_part, *d_far[0].values()]
             ties.append(cols)
         new = [after(v, *ties) for v in new]
         got = [got[i] + [new[i]] for i in range(2)]
-    sums = call(
-        functools.partial(send_both_kernel, top, True, orders),
-        [shape((n_chan * share >> top, width), BF16)], [dims, tail, *got[0], *got[1]],
-        name="send_both", smem=True,
-    )
+    sums = send_both(dims, tail, got, orders, top, True)
     other = swap(sums, "batch", n_batch, 1 << top)
-    cols_other = swap(after(cols, sums), "batch", n_batch, 1)
+    others_cols = [
+        swap(after(cols[h], sums), "batch", n_batch, 1 << orders[h][0]) for h in halves
+    ]
     moved = [*far_rows(1, sums), *pass_on(0, sums)]
     part = call(
         features_grad_kernel, [shape((padded, share), F32)],
         [d_pre, after(d_reduced, sums), d_beside, *w_rows[:2]], flops=2 * mm,
         name="input_near", steps=STEPS,
     )
-    expand_grad = double(dims, cols, after(cols_other, part), 0, F32)
+    others_cols[0] = after(others_cols[0], part)
+    expand_grad = finish(dims, cols, others_cols, [o[0] for o in orders])
     sums = add(sums, after(other, expand_grad, *moved))
     pair = [sums]
     for s in reversed(range(top)):
@@ -916,15 +909,8 @@
             before = (group_part,)
         new = [after(v, *before) for v in new]
         if s:
-            pair = call(
-                functools.partial(double_pair_kernel, [o[s] for o in orders]),
-                [shape((2 * n, width), BF16)] * 2, [dims, *pair, *new], name="double_pair",
-                smem=True,
-            )
-    tail = call(
-        functools.partial(finish_kernel, [o[0] for o in orders]),
-        [shape((n_chan * share, width), F32)], [dims, *pair, *new], name="finish", smem=True,
-    )
+            pair = double_pair(dims, pair, new, [o[s] for o in orders])
+    tail = finish(dims, pair, new, [o[0] for o in orders])
     reduce_grad, group_grad = tail, group_part
 
     shaped = lambda v: v.reshape(side, side, slots, share).transpose(2, 0, 1, 3)

time: 263 us -> 261 us (level)
  waiting for transfers between devices: 95.9 us -> 90.3 us
  starting transfers between devices: 36 us -> 39.3 us
    ppermute x47 -> x51, waiting for transfers between devices: 95.9 us -> 90.3 us  [swap(): return lax.ppermute(v, axis, [(i, i ^ k) for i in range(size)])]
    ppermute x47 -> x51, starting transfers between devices: 36 us -> 39.3 us  [swap(): return lax.ppermute(v, axis, [(i, i ^ k) for i in range(size)])]
  transfers between devices with their start and end apart: 47 -> 51, of which waited for: 21 -> 25; matrix products, arithmetic and copies ran while one was open for 2% -> 2% of each run, Pallas kernels for 21% -> 22%
where the time goes in v4:
time: 261 us; the launch traced here: 260 us
  waiting for transfers between devices  90.3 us (35%)
  Pallas kernels  67.5 us (26%)
  blocking collectives  49.6 us (19%)
  starting transfers between devices  39.3 us (15%)
  local copies, waits for them, and re-layouts  8.1 us (3%)
    ppermute x51, waiting for transfers between devices, swap(): return lax.ppermute(v, axis, [(i, i ^ k) for i in range(size)])  90.3 us
    pallas_call x44, Pallas kernels, call(): pl.pallas_call(kernel, out_shape=list(outs), grid=(steps,) if steps else...  67.5 us
    all_to_all x5, blocking collectives, batch_sum(): return lax.all_to_all(spread, 'batch', 0, 0)  49.6 us
    ppermute x51, starting transfers between devices, swap(): return lax.ppermute(v, axis, [(i, i ^ k) for i in range(size)])  39.3 us
  transfers between devices with their start and end apart: 51, of which 25 were waited for; matrix products, arithmetic and copies ran while one was open for 2% of the time, Pallas kernels for 22%

profile of v4, /device:TPU:0, one launch (start us, length us, event | category | flops | bytes accessed | tf_op | source)
XLA Modules:
  0.0 260.0 jit_solution(944536521421451088)
XLA Ops:
  3.9 2.6 collective-permute-start.1
  7.9 11.1 %collective-permute-done.1.refs_0_ = bf16[1024,256]{1,0:T(8,128)(2,1)S(1)} collective-permute-done((bf16[1024,256]{1,0:T(8,128)(2,1)S(1)}, bf16[1024,256]{1,0:T(8,128)(2,1)S(1)}, u32[]{:S(2)}, u32[]{:S(2)}) %collective-permute-start.1) | collective-permute-done | bytes 524320 | tf_op jit(solution)/shard_map/ppermute | solution.py:545
  19.1 2.7 %part_far.1 = bf16[1984,256]{1,0:T(8,128)(2,1)S(1)} custom-call(s32[5]{0:T(128)S(1)} %stack.11.dims, bf16[1984,512]{1,0:T(8,128)(2,1)S(1)} %pad.4.own.refs_0_.feats, bf16[1984,512]{1,0:T(8,128)(2,1)} %collective-permute-done.beside.refs_1_, bf16[1024,256]{1,0:T(8,128)(2,1)S(1)} %collective-permute-done.1.refs_0_), custom_call_target="tpu_custom_call" | custom-call | flops 1040187392 | bytes 5603348 | tf_op jit(solution)/shard_map/part_far/pallas_call | solution.py:526
  24.2 3.6 %near.1.part = f32[1984,256]{1,0:T(8,128)S(1)} custom-call(s32[5]{0:T(128)S(1)} %stack.11.dims, bf16[1984,512]{1,0:T(8,128)(2,1)S(1)} %pad.4.own.refs_0_.feats, bf16[1984,512]{1,0:T(8,128)(2,1)} %collective-permute-done.beside.refs_1_, bf16[2048,256]{1,0:T(8,128)(2,1)S(1)} %copy-done.1), custom_call_target="tpu_custom_call" | custom-call | flops 1040187392 | bytes 7143444 | tf_op jit(solution)/shard_map/near/pallas_call | solution.py:526
  27.9 3.3 %copy-done = bf16[24,9,9,2048]{3,0,2,1:T(8,128)(2,1)S(1)} copy-done((bf16[24,9,9,2048]{3,0,2,1:T(8,128)(2,1)S(1)}, bf16[24,9,9,2048]{3,0,2,1:T(8,128)(2,1)}, u32[]{:S(2)}) %copy-start) | copy-done | bytes 7962648
  33.0 2.5 fusion.5.live
  35.8 10.2 %collective-permute-done.2.refs_0_ = bf16[1984,256]{1,0:T(8,128)(2,1)S(1)} collective-permute-done((bf16[1984,256]{1,0:T(8,128)(2,1)S(1)}, bf16[1984,256]{1,0:T(8,128)(2,1)S(1)}, u32[]{:S(2)}, u32[]{:S(2)}) %collective-permute-start.2) | collective-permute-done | bytes 1015840 | tf_op jit(solution)/shard_map/ppermute | solution.py:545
  48.1 3.7 %collective-permute-start.8 = (f32[1,3,256]{2,1,0:T(4,128)S(1)}, f32[1,3,256]{2,1,0:T(4,128)S(1)}, u32[]{:S(2)}, u32[]{:S(2)}) collective-permute-start(f32[1,3,256]{2,1,0:T(4,128)S(1)} %get-tuple-element.139.refs_0_), channel_id=1, source_target_pairs={{0,24},{4,28},{8,16},{12,20},{16,8},{20,12},{24,0},{28,4},{1,25},{... | collective-permute-start | bytes 9224 | tf_op jit(solution)/shard_map/ppermute | solution.py:545
  53.6 2.7 %collective-permute-done.7.refs_2_ = f32[1,3,256]{2,1,0:T(4,128)S(1)} collective-permute-done((f32[1,3,256]{2,1,0:T(4,128)S(1)}, f32[1,3,256]{2,1,0:T(4,128)S(1)}, u32[]{:S(2)}, u32[]{:S(2)}) %collective-permute-start.7) | collective-permute-done | bytes 3104 | tf_op jit(solution)/shard_map/ppermute | solution.py:545
  60.0 3.5 %conv.1 = (f32[1984,256]{1,0:T(8,128)S(1)}, f32[8,2,256]{2,1,0:T(2,128)S(1)}) custom-call(f32[1984,128]{1,0:T(8,128)S(1)} %fusion.5.live, f32[1984,256]{1,0:T(8,128)S(1)} %get-tuple-element.138.z, f32[2,3,256]{2,1,0:T(4,128)S(1)} %pair.1.got.counts, f32[1,256]{1,0:T(1,128)S(1)} %bitcast.36, f32[1,256]{1,0:T(1,128)S(1)} %bitcast.44, bf16[9,256,256]{2,1,0:T(8,128)(2,1)S(1)} %taps.1), custom_call_target="tpu_custom_call" | custom-call | flops 2340421632 | bytes 6283264 | tf_op jit(solution)/shard_map/conv/pallas_call | solution.py:526
  63.6 10.5 %all_to_all.25.got.got_two = f32[8,2,256]{2,1,0:T(2,128)S(1)} all-to-all(f32[8,2,256]{2,1,0:T(2,128)S(1)} %get-tuple-element.144), channel_id=1, replica_groups=mesh['batch'=8,'chan'=4] {'batch'}, dimensions={0} | all-to-all | bytes 32768 | tf_op jit(solution)/shard_map/all_to_all | solution.py:549
  76.3 2.5 slope_one.1.slope
  79.0 2.5 slope_two.1.slope
  82.9 17.7 %collective-permute-done.13.refs_0_.refs_2_ = bf16[1984,256]{1,0:T(8,128)(2,1)S(1)} collective-permute-done((bf16[1984,256]{1,0:T(8,128)(2,1)S(1)}, bf16[1984,256]{1,0:T(8,128)(2,1)S(1)}, u32[]{:S(2)}, u32[]{:S(2)}) %collective-permute-start.13) | collective-permute-done | bytes 1015840 | tf_op jit(solution)/shard_map/ppermute | solution.py:545
  105.2 9.1 %all_to_all.26.got = f32[8,2,512]{2,1,0:T(2,128)S(1)} all-to-all(f32[8,2,512]{2,1,0:T(2,128)S(1)} %get-tuple-element.148), channel_id=1, replica_groups=mesh['batch'=8,'chan'=4] {'batch'}, dimensions={0} | all-to-all | bytes 65536 | tf_op jit(solution)/shard_map/all_to_all | solution.py:549
  114.3 3.9 %third.1 = (f32[1984,512]{1,0:T(8,128)S(1)}, f32[8,2,512]{2,1,0:T(2,128)S(1)}) custom-call(f32[1984,128]{1,0:T(8,128)S(1)} %fusion.5.live, f32[1984,512]{1,0:T(8,128)S(1)} %get-tuple-element.160.e, f32[2,3,256]{2,1,0:T(4,128)S(1)} %pair.1.got.counts, f32[8,2,512]{2,1,0:T(2,128)S(1)} %all_to_all.26.got, f32[1,512]{1,0:T(1,128)S(1)} %get-tuple-element.123.gain, ...), custom_call_target="tpu_custom_call" | custom-call | flops 2080374784 | bytes 13281280 | tf_op jit(solution)/shard_map/third/pallas_call | solution.py:526
  118.2 9.1 %all_to_all.27.totals = f32[8,2,512]{2,1,0:T(2,128)S(1)} all-to-all(f32[8,2,512]{2,1,0:T(2,128)S(1)} %get-tuple-element.150), channel_id=1, replica_groups=mesh['batch'=8,'chan'=4] {'batch'}, dimensions={0} | all-to-all | bytes 65536 | tf_op jit(solution)/shard_map/all_to_all | solution.py:549
  129.3 2.9 %collective-permute-done.15.refs_2_ = bf16[1296,512]{1,0:T(8,128)(2,1)S(1)} collective-permute-done((bf16[1296,512]{1,0:T(8,128)(2,1)S(1)}, bf16[1296,512]{1,0:T(8,128)(2,1)S(1)}, u32[]{:S(2)}, u32[]{:S(2)}) %collective-permute-start.15) | collective-permute-done | bytes 1327136 | tf_op jit(solution)/shard_map/ppermute | solution.py:545
  139.9 5.1 %block.1 = bf16[1944,512]{1,0:T(8,128)(2,1)} custom-call(f32[1984,128]{1,0:T(8,128)S(1)} %fusion.5.live, f32[1984,512]{1,0:T(8,128)S(1)} %get-tuple-element.160.e, f32[2,3,256]{2,1,0:T(4,128)S(1)} %pair.1.got.counts, f32[8,2,512]{2,1,0:T(2,128)S(1)} %all_to_all.26.got, f32[1,512]{1,0:T(1,128)S(1)} %get-tuple-element.123.gain, ...), custom_call_target="tpu_custom_call" | custom-call | flops 1040187392 | bytes 9144320 | tf_op jit(solution)/shard_map/block/pallas_call | solution.py:526
  149.9 2.9 %collective-permute-done.22.refs_1_ = bf16[4,32,512]{2,1,0:T(8,128)(2,1)S(1)} collective-permute-done((bf16[4,32,512]{2,1,0:T(8,128)(2,1)S(1)}, bf16[4,32,512]{2,1,0:T(8,128)(2,1)S(1)}, u32[]{:S(2)}, u32[]{:S(2)}) %collective-permute-start.22) | collective-permute-done | bytes 131104 | tf_op jit(solution)/shard_map/ppermute | solution.py:545
  155.0 3.8 %collective-permute-done.19.refs_2_ = bf16[1984,256]{1,0:T(8,128)(2,1)S(1)} collective-permute-done((bf16[1984,256]{1,0:T(8,128)(2,1)S(1)}, bf16[1984,256]{1,0:T(8,128)(2,1)S(1)}, u32[]{:S(2)}, u32[]{:S(2)}) %collective-permute-start.19) | collective-permute-done | bytes 1015840 | tf_op jit(solution)/shard_map/ppermute | solution.py:545
  161.2 11.8 %all_to_all.28.totals = f32[8,2,256]{2,1,0:T(2,128)S(1)} all-to-all(f32[8,2,256]{2,1,0:T(2,128)S(1)} %get-tuple-element.165), channel_id=1, replica_groups=mesh['batch'=8,'chan'=4] {'batch'}, dimensions={0} | all-to-all | bytes 32768 | tf_op jit(solution)/shard_map/all_to_all | solution.py:549
  172.9 3.5 %conv_back.1 = (f32[1984,256]{1,0:T(8,128)S(1)}, f32[1984,256]{1,0:T(8,128)S(1)}, f32[8,2,256]{2,1,0:T(2,128)S(1)}, f32[2,256]{1,0:T(2,128)S(1)}) custom-call(f32[1984,128]{1,0:T(8,128)S(1)} %fusion.5.live, f32[1984,256]{1,0:T(8,128)S(1)} %get-tuple-element.164.d_two, f32[1984,256]{1,0:T(8,128)S(1)} %get-tuple-element.140.z.grouped, ...), custom_call_target="tpu_custom_call" | custom-call | flops 2340421632 | bytes 14443520 | tf_op jit(solution)/shard_map/conv_back/pallas_call | solution.py:526
  176.5 9.2 %all_to_all.29.totals = f32[8,2,256]{2,1,0:T(2,128)S(1)} all-to-all(f32[8,2,256]{2,1,0:T(2,128)S(1)} %get-tuple-element.180), channel_id=1, replica_groups=mesh['batch'=8,'chan'=4] {'batch'}, dimensions={0} | all-to-all | bytes 32768 | tf_op jit(solution)/shard_map/all_to_all | solution.py:549
  187.5 3.7 %reduce_grad.1 = (bf16[2048,256]{1,0:T(8,128)(2,1)S(1)}, f32[2,512,256]{2,1,0:T(8,128)S(1)}) custom-call(s32[5]{0:T(128)S(1)} %stack.11.dims, bf16[1984,256]{1,0:T(8,128)(2,1)S(1)} %get-tuple-element.207.d_red.refs_0_, bf16[1984,512]{1,0:T(8,128)(2,1)S(1)} %pad.4.own.refs_0_.feats, bf16[1984,512]{1,0:T(8,128)(2,1)} %collective-permute-done.beside.refs_1_, ...), custom_call_target="tpu_custom_call" | custom-call | flops 2080374784 | bytes 9830420 | tf_op jit(solution)/shard_map/reduce_grad/pallas_call | solution.py:526
  200.8 3.7 %group_grad.1.a = bf16[288,256]{1,0:T(8,128)(2,1)S(1)} custom-call(f32[1984,128]{1,0:T(8,128)S(1)} %fusion.5.live, f32[1984,256]{1,0:T(8,128)S(1)} %get-tuple-element.138.z, f32[2,3,256]{2,1,0:T(4,128)S(1)} %pair.1.got.counts, f32[1,256]{1,0:T(1,128)S(1)} %bitcast.39, f32[1,256]{1,0:T(1,128)S(1)} %bitcast.46, f32[1984,256]{1,0:T(8,128)S(1)} %get-tuple-element.192.d_grouped), custom_call_target="tpu_custom_call" | custom-call | flops 520093696 | bytes 5234688 | tf_op jit(solution)/shard_map/group_grad/pallas_call | solution.py:526
  211.4 4.2 %collective-permute-done.36.refs_2_ = bf16[32,2048]{1,0:T(8,128)(2,1)S(1)} collective-permute-done((bf16[32,2048]{1,0:T(8,128)(2,1)S(1)}, bf16[32,2048]{1,0:T(8,128)(2,1)S(1)}, u32[]{:S(2)}, u32[]{:S(2)}) %collective-permute-start.36) | collective-permute-done | bytes 131104 | tf_op jit(solution)/shard_map/ppermute | solution.py:545
  222.9 4.4 %collective-permute-done.40.other_a = bf16[64,2048]{1,0:T(8,128)(2,1)S(1)} collective-permute-done((bf16[64,2048]{1,0:T(8,128)(2,1)S(1)}, bf16[64,2048]{1,0:T(8,128)(2,1)S(1)}, u32[]{:S(2)}, u32[]{:S(2)}) %collective-permute-start.40) | collective-permute-done | bytes 262176 | tf_op jit(solution)/shard_map/ppermute | solution.py:545
  227.3 3.9 %collective-permute-done.41.other_b = bf16[64,2048]{1,0:T(8,128)(2,1)S(1)} collective-permute-done((bf16[64,2048]{1,0:T(8,128)(2,1)S(1)}, bf16[64,2048]{1,0:T(8,128)(2,1)S(1)}, u32[]{:S(2)}, u32[]{:S(2)}) %collective-permute-start.41) | collective-permute-done | bytes 262176 | tf_op jit(solution)/shard_map/ppermute | solution.py:545
  240.1 2.5 collective-permute-done.45.b
  249.6 2.7 %input_far.1 = f32[1944,512]{1,0:T(8,128)} custom-call(f32[1984,512]{1,0:T(8,128)S(1)} %input_near.1.part, bf16[992,256]{1,0:T(8,128)(2,1)S(1)} %collective-permute-done.37.refs_0_, bf16[992,256]{1,0:T(8,128)(2,1)S(1)} %collective-permute-done.42.refs_1_, bf16[992,256]{1,0:T(8,128)(2,1)S(1)} %collective-permute-done.43.refs_2_, ...), custom_call_target="tpu_custom_call" | custom-call | flops 1040187392 | bytes 10600448 | tf_op jit(solution)/shard_map/input_far/pallas_call | solution.py:526
  252.3 4.1 %collective-permute-done.49.b = bf16[288,256]{1,0:T(8,128)(2,1)S(1)} collective-permute-done((bf16[288,256]{1,0:T(8,128)(2,1)S(1)}, bf16[288,256]{1,0:T(8,128)(2,1)S(1)}, u32[]{:S(2)}, u32[]{:S(2)}) %collective-permute-start.49) | collective-permute-done | bytes 147488 | tf_op jit(solution)/shard_map/ppermute | solution.py:545
  (156 shorter events, 87.9 us)
Async XLA Ops:
  3.4 15.6 %collective-permute-start = (bf16[1984,512]{1,0:T(8,128)(2,1)S(1)}, bf16[1984,512]{1,0:T(8,128)(2,1)}, u32[]{:S(2)}, u32[]{:S(2)}) collective-permute-start(bf16[1984,512]{1,0:T(8,128)(2,1)S(1)} %pad.4.own.refs_0_.feats), channel_id=1, source_target_pairs={{0,1},{1,0},{2,3},{3,2},{4,5},{5,4},{6,7},{7,6},{8,9},{9,8},{10,11... | collective-permute-start | bytes 6094856 | tf_op jit(solution)/shard_map/ppermute | solution.py:545
  3.9 15.1 %collective-permute-start.1 = (bf16[1024,256]{1,0:T(8,128)(2,1)S(1)}, bf16[1024,256]{1,0:T(8,128)(2,1)S(1)}, u32[]{:S(2)}, u32[]{:S(2)}) collective-permute-start(bf16[1024,256]{1,0:T(8,128)(2,1)S(1)} %constant_dynamic-slice_fusion), channel_id=1, source_target_pairs={{0,2},{1,3},{2,0},{3,1},{4,6},{5,7},{6,4},{7,5},{8,10},{9,11},{10,... | collective-permute-start | bytes 1572872 | tf_op jit(solution)/shard_map/ppermute | solution.py:545
  21.7 24.3 %collective-permute-start.2 = (bf16[1984,256]{1,0:T(8,128)(2,1)S(1)}, bf16[1984,256]{1,0:T(8,128)(2,1)S(1)}, u32[]{:S(2)}, u32[]{:S(2)}) collective-permute-start(bf16[1984,256]{1,0:T(8,128)(2,1)S(1)} %part_far.1), channel_id=1, source_target_pairs={{0,2},{1,3},{2,0},{3,1},{4,6},{5,7},{6,4},{7,5},{8,10},{9,11},{10,... | collective-permute-start | bytes 3047432 | tf_op jit(solution)/shard_map/ppermute | solution.py:545
  27.8 7.9 %collective-permute-start.5 = (bf16[512,256]{1,0:T(8,128)(2,1)S(1)}, bf16[512,256]{1,0:T(8,128)(2,1)S(1)}, u32[]{:S(2)}, u32[]{:S(2)}) collective-permute-start(bf16[512,256]{1,0:T(8,128)(2,1)S(1)} %get-tuple-element.133), channel_id=1, source_target_pairs={{0,1},{1,0},{2,3},{3,2},{4,5},{5,4},{6,7},{7,6},{8,9},{9,8},{10,11... | collective-permute-start | bytes 786440 | tf_op jit(solution)/shard_map/ppermute | solution.py:545
  46.0 17.6 %collective-permute-start.10 = (bf16[256,512]{1,0:T(8,128)(2,1)S(1)}, bf16[256,512]{1,0:T(8,128)(2,1)S(1)}, u32[]{:S(2)}, u32[]{:S(2)}) collective-permute-start(bf16[256,512]{1,0:T(8,128)(2,1)S(1)} %get-tuple-element.142), channel_id=1, source_target_pairs={{0,2},{1,3},{2,0},{3,1},{4,6},{5,7},{6,4},{7,5},{8,10},{9,11},{10,... | collective-permute-start | bytes 786440 | tf_op jit(solution)/shard_map/ppermute | solution.py:545
  47.6 16.0 %collective-permute-start.11 = (bf16[256,512]{1,0:T(8,128)(2,1)S(1)}, bf16[256,512]{1,0:T(8,128)(2,1)S(1)}, u32[]{:S(2)}, u32[]{:S(2)}) collective-permute-start(bf16[256,512]{1,0:T(8,128)(2,1)S(1)} %get-tuple-element.143), channel_id=1, source_target_pairs={{0,3},{1,2},{2,1},{3,0},{4,7},{5,6},{6,5},{7,4},{8,11},{9,10},{10,... | collective-permute-start | bytes 786440 | tf_op jit(solution)/shard_map/ppermute | solution.py:545
  75.8 24.9 %collective-permute-start.13 = (bf16[1984,256]{1,0:T(8,128)(2,1)S(1)}, bf16[1984,256]{1,0:T(8,128)(2,1)S(1)}, u32[]{:S(2)}, u32[]{:S(2)}) collective-permute-start(bf16[1984,256]{1,0:T(8,128)(2,1)S(1)} %hidden.1.refs_0_), channel_id=1, source_target_pairs={{0,2},{1,3},{2,0},{3,1},{4,6},{5,7},{6,4},{7,5},{8,10},{9,11},{10,... | collective-permute-start | bytes 3047432 | tf_op jit(solution)/shard_map/ppermute | solution.py:545
  100.6 31.5 %collective-permute-start.15 = (bf16[1296,512]{1,0:T(8,128)(2,1)S(1)}, bf16[1296,512]{1,0:T(8,128)(2,1)S(1)}, u32[]{:S(2)}, u32[]{:S(2)}) collective-permute-start(bf16[1296,512]{1,0:T(8,128)(2,1)S(1)} %slice.36), channel_id=1, source_target_pairs={{0,2},{1,3},{2,0},{3,1},{4,6},{5,7},{6,4},{7,5},{8,10},{9,11},{10,... | collective-permute-start | bytes 3981320 | tf_op jit(solution)/shard_map/ppermute | solution.py:545
  134.6 24.2 %collective-permute-start.19 = (bf16[1984,256]{1,0:T(8,128)(2,1)S(1)}, bf16[1984,256]{1,0:T(8,128)(2,1)S(1)}, u32[]{:S(2)}, u32[]{:S(2)}) collective-permute-start(bf16[1984,256]{1,0:T(8,128)(2,1)S(1)} %merge.1), channel_id=1, source_target_pairs={{0,2},{1,3},{2,0},{3,1},{4,6},{5,7},{6,4},{7,5},{8,10},{9,11},{10,... | collective-permute-start | bytes 3047432 | tf_op jit(solution)/shard_map/ppermute | solution.py:545
  135.2 24.7 %collective-permute-start.17 = (bf16[1296,512]{1,0:T(8,128)(2,1)S(1)}, bf16[1296,512]{1,0:T(8,128)(2,1)S(1)}, u32[]{:S(2)}, u32[]{:S(2)}) collective-permute-start(bf16[1296,512]{1,0:T(8,128)(2,1)S(1)} %collective-permute-done.15.refs_2_), channel_id=1, source_target_pairs={{0,1},{1,0},{2,3},{3,2},{4,5},{5,4},{6,7},{7,6},{8,9},{9,8},{10,11... | collective-permute-start | bytes 3981320 | tf_op jit(solution)/shard_map/ppermute | solution.py:545
  135.2 24.7 %collective-permute-start.18 = (bf16[1984,256]{1,0:T(8,128)(2,1)S(1)}, bf16[1984,256]{1,0:T(8,128)(2,1)S(1)}, u32[]{:S(2)}, u32[]{:S(2)}) collective-permute-start(bf16[1984,256]{1,0:T(8,128)(2,1)S(1)} %get-tuple-element.156), channel_id=1, source_target_pairs={{0,1},{1,0},{2,3},{3,2},{4,5},{5,4},{6,7},{7,6},{8,9},{9,8},{10,11... | collective-permute-start | bytes 3047432 | tf_op jit(solution)/shard_map/ppermute | solution.py:545
  138.7 8.3 %collective-permute-start.21 = (bf16[4,64,512]{2,1,0:T(8,128)(2,1)S(1)}, bf16[4,64,512]{2,1,0:T(8,128)(2,1)S(1)}, u32[]{:S(2)}, u32[]{:S(2)}) collective-permute-start(bf16[4,64,512]{2,1,0:T(8,128)(2,1)S(1)} %get-tuple-element.169), channel_id=1, source_target_pairs={{0,8},{4,12},{8,0},{12,4},{16,24},{20,28},{24,16},{28,20},{1,9},{5... | collective-permute-start | bytes 786440 | tf_op jit(solution)/shard_map/ppermute | solution.py:545
  139.2 7.9 %collective-permute-start.20 = (bf16[4,64,512]{2,1,0:T(8,128)(2,1)S(1)}, bf16[4,64,512]{2,1,0:T(8,128)(2,1)S(1)}, u32[]{:S(2)}, u32[]{:S(2)}) collective-permute-start(bf16[4,64,512]{2,1,0:T(8,128)(2,1)S(1)} %get-tuple-element.159), channel_id=1, source_target_pairs={{0,4},{4,0},{8,12},{12,8},{16,20},{20,16},{24,28},{28,24},{1,5},{5... | collective-permute-start | bytes 786440 | tf_op jit(solution)/shard_map/ppermute | solution.py:545
  158.8 17.7 %collective-permute-start.25 = (bf16[688,512]{1,0:T(8,128)(2,1)S(1)}, bf16[688,512]{1,0:T(8,128)(2,1)S(1)}, u32[]{:S(2)}, u32[]{:S(2)}) collective-permute-start(bf16[688,512]{1,0:T(8,128)(2,1)S(1)} %slice.37), channel_id=1, source_target_pairs={{0,2},{1,3},{2,0},{3,1},{4,6},{5,7},{6,4},{7,5},{8,10},{9,11},{10,... | collective-permute-start | bytes 2113544 | tf_op jit(solution)/shard_map/ppermute | solution.py:545
  159.4 17.0 %collective-permute-start.24 = (bf16[4,64,512]{2,1,0:T(8,128)(2,1)S(1)}, bf16[4,64,512]{2,1,0:T(8,128)(2,1)S(1)}, u32[]{:S(2)}, u32[]{:S(2)}) collective-permute-start(bf16[4,64,512]{2,1,0:T(8,128)(2,1)S(1)} %send_both.8.a), channel_id=1, source_target_pairs={{0,16},{4,20},{8,24},{12,28},{16,0},{20,4},{24,8},{28,12},{1,17},{... | collective-permute-start | bytes 786440 | tf_op jit(solution)/shard_map/ppermute | solution.py:545
  195.0 9.5 %collective-permute-start.32 = (bf16[512,256]{1,0:T(8,128)(2,1)S(1)}, bf16[512,256]{1,0:T(8,128)(2,1)S(1)}, u32[]{:S(2)}, u32[]{:S(2)}) collective-permute-start(bf16[512,256]{1,0:T(8,128)(2,1)S(1)} %get-tuple-element.194), channel_id=1, source_target_pairs={{0,8},{4,12},{8,0},{12,4},{16,24},{20,28},{24,16},{28,20},{1,9},{5... | collective-permute-start | bytes 786440 | tf_op jit(solution)/shard_map/ppermute | solution.py:545
  195.5 9.0 %collective-permute-start.28 = (bf16[512,256]{1,0:T(8,128)(2,1)S(1)}, bf16[512,256]{1,0:T(8,128)(2,1)S(1)}, u32[]{:S(2)}, u32[]{:S(2)}) collective-permute-start(bf16[512,256]{1,0:T(8,128)(2,1)S(1)} %get-tuple-element.185), channel_id=1, source_target_pairs={{0,4},{4,0},{8,12},{12,8},{16,20},{20,16},{24,28},{28,24},{1,5},{5... | collective-permute-start | bytes 786440 | tf_op jit(solution)/shard_map/ppermute | solution.py:545
  199.4 17.7 %collective-permute-start.37 = (bf16[992,256]{1,0:T(8,128)(2,1)S(1)}, bf16[992,256]{1,0:T(8,128)(2,1)S(1)}, u32[]{:S(2)}, u32[]{:S(2)}) collective-permute-start(bf16[992,256]{1,0:T(8,128)(2,1)S(1)} %slice.38), channel_id=1, source_target_pairs={{0,2},{1,3},{2,0},{3,1},{4,6},{5,7},{6,4},{7,5},{8,10},{9,11},{10,... | collective-permute-start | bytes 1523720 | tf_op jit(solution)/shard_map/ppermute | solution.py:545
  206.0 10.2 %collective-permute-start.34 = (bf16[288,256]{1,0:T(8,128)(2,1)S(1)}, bf16[288,256]{1,0:T(8,128)(2,1)S(1)}, u32[]{:S(2)}, u32[]{:S(2)}) collective-permute-start(bf16[288,256]{1,0:T(8,128)(2,1)S(1)} %group_grad.1.a), channel_id=1, source_target_pairs={{0,4},{4,0},{8,12},{12,8},{16,20},{20,16},{24,28},{28,24},{1,5},{5... | collective-permute-start | bytes 442376 | tf_op jit(solution)/shard_map/ppermute | solution.py:545
  206.5 9.0 %collective-permute-start.36 = (bf16[32,2048]{1,0:T(8,128)(2,1)S(1)}, bf16[32,2048]{1,0:T(8,128)(2,1)S(1)}, u32[]{:S(2)}, u32[]{:S(2)}) collective-permute-start(bf16[32,2048]{1,0:T(8,128)(2,1)S(1)} %get-tuple-element.199.refs_0_), channel_id=1, source_target_pairs={{0,4},{4,0},{8,12},{12,8},{16,20},{20,16},{24,28},{28,24},{1,5},{5... | collective-permute-start | bytes 393224 | tf_op jit(solution)/shard_map/ppermute | solution.py:545
  208.0 9.0 %collective-permute-start.38 = (bf16[256,256]{1,0:T(8,128)(2,1)S(1)}, bf16[256,256]{1,0:T(8,128)(2,1)S(1)}, u32[]{:S(2)}, u32[]{:S(2)}) collective-permute-start(bf16[256,256]{1,0:T(8,128)(2,1)S(1)} %get-tuple-element.205), channel_id=1, source_target_pairs={{0,4},{4,0},{8,12},{12,8},{16,20},{20,16},{24,28},{28,24},{1,5},{5... | collective-permute-start | bytes 393224 | tf_op jit(solution)/shard_map/ppermute | solution.py:545
  217.8 17.4 %collective-permute-start.42 = (bf16[992,256]{1,0:T(8,128)(2,1)S(1)}, bf16[992,256]{1,0:T(8,128)(2,1)S(1)}, u32[]{:S(2)}, u32[]{:S(2)}) collective-permute-start(bf16[992,256]{1,0:T(8,128)(2,1)S(1)} %slice.39), channel_id=1, source_target_pairs={{0,2},{1,3},{2,0},{3,1},{4,6},{5,7},{6,4},{7,5},{8,10},{9,11},{10,... | collective-permute-start | bytes 1523720 | tf_op jit(solution)/shard_map/ppermute | solution.py:545
  218.6 16.6 %collective-permute-start.43 = (bf16[992,256]{1,0:T(8,128)(2,1)S(1)}, bf16[992,256]{1,0:T(8,128)(2,1)S(1)}, u32[]{:S(2)}, u32[]{:S(2)}) collective-permute-start(bf16[992,256]{1,0:T(8,128)(2,1)S(1)} %collective-permute-done.37.refs_0_), channel_id=1, source_target_pairs={{0,1},{1,0},{2,3},{3,2},{4,5},{5,4},{6,7},{7,6},{8,9},{9,8},{10,11... | collective-permute-start | bytes 1523720 | tf_op jit(solution)/shard_map/ppermute | solution.py:545
  218.6 8.7 %collective-permute-start.40 = (bf16[64,2048]{1,0:T(8,128)(2,1)S(1)}, bf16[64,2048]{1,0:T(8,128)(2,1)S(1)}, u32[]{:S(2)}, u32[]{:S(2)}) collective-permute-start(bf16[64,2048]{1,0:T(8,128)(2,1)S(1)} %get-tuple-element.208.a), channel_id=1, source_target_pairs={{0,4},{4,0},{8,12},{12,8},{16,20},{20,16},{24,28},{28,24},{1,5},{5... | collective-permute-start | bytes 786440 | tf_op jit(solution)/shard_map/ppermute | solution.py:545
  219.1 12.1 %collective-permute-start.41 = (bf16[64,2048]{1,0:T(8,128)(2,1)S(1)}, bf16[64,2048]{1,0:T(8,128)(2,1)S(1)}, u32[]{:S(2)}, u32[]{:S(2)}) collective-permute-start(bf16[64,2048]{1,0:T(8,128)(2,1)S(1)} %get-tuple-element.210.b), channel_id=1, source_target_pairs={{0,8},{4,12},{8,0},{12,4},{16,24},{20,28},{24,16},{28,20},{1,9},{5... | collective-permute-start | bytes 786440 | tf_op jit(solution)/shard_map/ppermute | solution.py:545
  220.5 14.7 %collective-permute-start.39 = (bf16[512,256]{1,0:T(8,128)(2,1)S(1)}, bf16[512,256]{1,0:T(8,128)(2,1)S(1)}, u32[]{:S(2)}, u32[]{:S(2)}) collective-permute-start(bf16[512,256]{1,0:T(8,128)(2,1)S(1)} %send_both.11.a), channel_id=1, source_target_pairs={{0,16},{4,20},{8,24},{12,28},{16,0},{20,4},{24,8},{28,12},{1,17},{... | collective-permute-start | bytes 786440 | tf_op jit(solution)/shard_map/ppermute | solution.py:545
  235.3 7.4 %collective-permute-start.46 = (bf16[992,256]{1,0:T(8,128)(2,1)S(1)}, bf16[992,256]{1,0:T(8,128)(2,1)S(1)}, u32[]{:S(2)}, u32[]{:S(2)}) collective-permute-start(bf16[992,256]{1,0:T(8,128)(2,1)S(1)} %collective-permute-done.42.refs_1_), channel_id=1, source_target_pairs={{0,1},{1,0},{2,3},{3,2},{4,5},{5,4},{6,7},{7,6},{8,9},{9,8},{10,11... | collective-permute-start | bytes 1523720 | tf_op jit(solution)/shard_map/ppermute | solution.py:545
  236.0 6.7 %collective-permute-start.47 = (bf16[256,256]{1,0:T(8,128)(2,1)S(1)}, bf16[256,256]{1,0:T(8,128)(2,1)S(1)}, u32[]{:S(2)}, u32[]{:S(2)}) collective-permute-start(bf16[256,256]{1,0:T(8,128)(2,1)S(1)} %get-tuple-element.227), channel_id=1, source_target_pairs={{0,4},{4,0},{8,12},{12,8},{16,20},{20,16},{24,28},{28,24},{1,5},{5... | collective-permute-start | bytes 393224 | tf_op jit(solution)/shard_map/ppermute | solution.py:545
  237.5 7.5 %collective-permute-start.44 = (bf16[256,256]{1,0:T(8,128)(2,1)S(1)}, bf16[256,256]{1,0:T(8,128)(2,1)S(1)}, u32[]{:S(2)}, u32[]{:S(2)}) collective-permute-start(bf16[256,256]{1,0:T(8,128)(2,1)S(1)} %get-tuple-element.228), channel_id=1, source_target_pairs={{0,8},{4,12},{8,0},{12,4},{16,24},{20,28},{24,16},{28,20},{1,9},{5... | collective-permute-start | bytes 393224 | tf_op jit(solution)/shard_map/ppermute | solution.py:545
  245.6 12.4 %collective-permute-start.48 = (bf16[512,256]{1,0:T(8,128)(2,1)S(1)}, bf16[512,256]{1,0:T(8,128)(2,1)S(1)}, u32[]{:S(2)}, u32[]{:S(2)}) collective-permute-start(bf16[512,256]{1,0:T(8,128)(2,1)S(1)} %get-tuple-element.217.a), channel_id=1, source_target_pairs={{0,4},{4,0},{8,12},{12,8},{16,20},{20,16},{24,28},{28,24},{1,5},{5... | collective-permute-start | bytes 786440 | tf_op jit(solution)/shard_map/ppermute | solution.py:545
  247.1 9.3 %collective-permute-start.49 = (bf16[288,256]{1,0:T(8,128)(2,1)S(1)}, bf16[288,256]{1,0:T(8,128)(2,1)S(1)}, u32[]{:S(2)}, u32[]{:S(2)}) collective-permute-start(bf16[288,256]{1,0:T(8,128)(2,1)S(1)} %add.37.a), channel_id=1, source_target_pairs={{0,16},{4,20},{8,24},{12,28},{16,0},{20,4},{24,8},{28,12},{1,17},{... | collective-permute-start | bytes 442376 | tf_op jit(solution)/shard_map/ppermute | solution.py:545
  247.4 10.6 %collective-permute-start.50 = (bf16[512,256]{1,0:T(8,128)(2,1)S(1)}, bf16[512,256]{1,0:T(8,128)(2,1)S(1)}, u32[]{:S(2)}, u32[]{:S(2)}) collective-permute-start(bf16[512,256]{1,0:T(8,128)(2,1)S(1)} %get-tuple-element.219.b), channel_id=1, source_target_pairs={{0,8},{4,12},{8,0},{12,4},{16,24},{20,28},{24,16},{28,20},{1,9},{5... | collective-permute-start | bytes 786440 | tf_op jit(solution)/shard_map/ppermute | solution.py:545
  (29 other events, 178.4 us)

commit v5 on v4

--- a/solution.py
+++ b/solution.py
@@ -860,31 +860,33 @@
             ties = [group_part]
         elif s == 1:
             group_other = swap(after(group_part, send[0]), "batch", n_batch, 1)
-            for t in reversed(range(1, top)):
-                others_cols = [
-                    swap(after(cols[h], send[0]), "batch", n_batch, 1 << orders[h][t])
-                    for h in halves
-                ]
-                cols = double_pair(dims, cols, others_cols, [o[t] for o in orders])
-            group_part = add(group_part, after(group_other, *cols))
-            ties += [group_part, *d_far[0].values()]
-            ties.append(cols)
+            others_cols = [
+                swap(after(cols[h], send[0]), "batch", n_batch, 1 << orders[h][top - 1])
+                for h in halves
+            ]
         new = [after(v, *ties) for v in new]
         got = [got[i] + [new[i]] for i in range(2)]
     sums = send_both(dims, tail, got, orders, top, True)
     other = swap(sums, "batch", n_batch, 1 << top)
+    others_cols = [after(v, sums) for v in others_cols]
+    cols = double_pair(dims, cols, others_cols, [o[top - 1] for o in orders])
+    for t in reversed(range(1, top - 1)):
+        others_cols = [swap(cols[h], "batch", n_batch, 1 << orders[h][t]) for h in halves]
+        cols = double_pair(dims, cols, others_cols, [o[t] for o in orders])
+    group_part = add(group_part, after(group_other, *cols))
     others_cols = [
         swap(after(cols[h], sums), "batch", n_batch, 1 << orders[h][0]) for h in halves
     ]
     moved = [*far_rows(1, sums), *pass_on(0, sums)]
     part = call(
         features_grad_kernel, [shape((padded, share), F32)],
-        [d_pre, after(d_reduced, sums), d_beside, *w_rows[:2]], flops=2 * mm,
+        [d_pre, after(d_reduced, group_part), d_beside, *w_rows[:2]], flops=2 * mm,
         name="input_near", steps=STEPS,
     )
-    others_cols[0] = after(others_cols[0], part)
+    sums = add(sums, after(other, part))
+    others_cols = [after(v, sums) for v in others_cols]
+    moved = [after(v, sums) for v in moved]
     expand_grad = finish(dims, cols, others_cols, [o[0] for o in orders])
-    sums = add(sums, after(other, expand_grad, *moved))
     pair = [sums]
     for s in reversed(range(top)):
         n = pair[0].shape[0] // (2 if len(pair) == 1 else 1)
@@ -892,9 +894,10 @@
         new = [swap(cut[i], "batch", n_batch, 1 << orders[i][s]) for i in range(2)]
         if s == top - 1:
             group_other = swap(after(group_part, sums), "batch", n_batch, 2)
-            group_part = add(group_part, group_other)
-            before = (group_part, *pass_on(1, sums))
+            group_part = add(group_part, after(group_other, expand_grad))
+            before = (group_part,)
         if s == 0:
+            pass_on(1, cut[0])
             for t in range(2, bits):
                 group_part = after(group_part, cut[0])
                 group_other = swap(group_part, "batch", n_batch, 1 << t)

time: 261 us -> 255 us (0.977)
  waiting for transfers between devices: 90.3 us -> 83.6 us
    ppermute x51, waiting for transfers between devices: 90.3 us -> 83.6 us  [swap(): return lax.ppermute(v, axis, [(i, i ^ k) for i in range(size)])]
  transfers between devices with their start and end apart: 51 -> 51, of which waited for: 25 -> 23; matrix products, arithmetic and copies ran while one was open for 2% -> 2% of each run, Pallas kernels for 22% -> 23%
where the time goes in v5:
time: 255 us
  waiting for transfers between devices  83.6 us (33%)
  Pallas kernels  67.6 us (27%)
  blocking collectives  49.6 us (19%)
  starting transfers between devices  40.7 us (16%)
  local copies, waits for them, and re-layouts  8.1 us (3%)
  other arithmetic  2.58 us (1%)
  between operations  2.58 us (1%)
    ppermute x51, waiting for transfers between devices, swap(): return lax.ppermute(v, axis, [(i, i ^ k) for i in range(size)])  83.6 us
    pallas_call x44, Pallas kernels, call(): pl.pallas_call(kernel, out_shape=list(outs), grid=(steps,) if steps else...  67.6 us
    all_to_all x5, blocking collectives, batch_sum(): return lax.all_to_all(spread, 'batch', 0, 0)  49.6 us
    ppermute x51, starting transfers between devices, swap(): return lax.ppermute(v, axis, [(i, i ^ k) for i in range(size)])  40.7 us
  transfers between devices with their start and end apart: 51, of which 23 were waited for; matrix products, arithmetic and copies ran while one was open for 2% of the time, Pallas kernels for 23%

profile of v5, /device:TPU:0, one launch (start us, length us, event | category | flops | bytes accessed | tf_op | source)
XLA Modules:
  0.0 254.8 jit_solution(17497217906032384445)
XLA Ops:
  3.9 2.6 %collective-permute-start.1 = (bf16[1024,256]{1,0:T(8,128)(2,1)S(1)}, bf16[1024,256]{1,0:T(8,128)(2,1)S(1)}, u32[]{:S(2)}, u32[]{:S(2)}) collective-permute-start(bf16[1024,256]{1,0:T(8,128)(2,1)S(1)} %constant_dynamic-slice_fusion), channel_id=1, source_target_pairs={{0,2},{1,3},{2,0},{3,1},{4,6},{5,7},{6,4},{7,5},{8,10},{9,11},{10,... | collective-permute-start | bytes 1572872 | tf_op jit(solution)/shard_map/ppermute | solution.py:545
  7.9 11.1 %collective-permute-done.1.refs_0_ = bf16[1024,256]{1,0:T(8,128)(2,1)S(1)} collective-permute-done((bf16[1024,256]{1,0:T(8,128)(2,1)S(1)}, bf16[1024,256]{1,0:T(8,128)(2,1)S(1)}, u32[]{:S(2)}, u32[]{:S(2)}) %collective-permute-start.1) | collective-permute-done | bytes 524320 | tf_op jit(solution)/shard_map/ppermute | solution.py:545
  19.1 2.7 %part_far.1 = bf16[1984,256]{1,0:T(8,128)(2,1)S(1)} custom-call(s32[5]{0:T(128)S(1)} %stack.11.dims, bf16[1984,512]{1,0:T(8,128)(2,1)S(1)} %pad.4.own.refs_0_.feats, bf16[1984,512]{1,0:T(8,128)(2,1)} %collective-permute-done.beside.refs_1_, bf16[1024,256]{1,0:T(8,128)(2,1)S(1)} %collective-permute-done.1.refs_0_), custom_call_target="tpu_custom_call" | custom-call | flops 1040187392 | bytes 5603348 | tf_op jit(solution)/shard_map/part_far/pallas_call | solution.py:526
  24.2 3.6 %near.1.part = f32[1984,256]{1,0:T(8,128)S(1)} custom-call(s32[5]{0:T(128)S(1)} %stack.11.dims, bf16[1984,512]{1,0:T(8,128)(2,1)S(1)} %pad.4.own.refs_0_.feats, bf16[1984,512]{1,0:T(8,128)(2,1)} %collective-permute-done.beside.refs_1_, bf16[2048,256]{1,0:T(8,128)(2,1)S(1)} %copy-done.1), custom_call_target="tpu_custom_call" | custom-call | flops 1040187392 | bytes 7143444 | tf_op jit(solution)/shard_map/near/pallas_call | solution.py:526
  27.9 3.3 %copy-done = bf16[24,9,9,2048]{3,0,2,1:T(8,128)(2,1)S(1)} copy-done((bf16[24,9,9,2048]{3,0,2,1:T(8,128)(2,1)S(1)}, bf16[24,9,9,2048]{3,0,2,1:T(8,128)(2,1)}, u32[]{:S(2)}) %copy-start) | copy-done | bytes 7962648
  33.0 2.5 fusion.5.live
  35.8 10.2 %collective-permute-done.2.refs_0_ = bf16[1984,256]{1,0:T(8,128)(2,1)S(1)} collective-permute-done((bf16[1984,256]{1,0:T(8,128)(2,1)S(1)}, bf16[1984,256]{1,0:T(8,128)(2,1)S(1)}, u32[]{:S(2)}, u32[]{:S(2)}) %collective-permute-start.2) | collective-permute-done | bytes 1015840 | tf_op jit(solution)/shard_map/ppermute | solution.py:545
  48.1 3.7 %collective-permute-start.8 = (f32[1,3,256]{2,1,0:T(4,128)S(1)}, f32[1,3,256]{2,1,0:T(4,128)S(1)}, u32[]{:S(2)}, u32[]{:S(2)}) collective-permute-start(f32[1,3,256]{2,1,0:T(4,128)S(1)} %get-tuple-element.142.refs_0_), channel_id=1, source_target_pairs={{0,24},{4,28},{8,16},{12,20},{16,8},{20,12},{24,0},{28,4},{1,25},{... | collective-permute-start | bytes 9224 | tf_op jit(solution)/shard_map/ppermute | solution.py:545
  53.6 2.7 %collective-permute-done.7.refs_2_ = f32[1,3,256]{2,1,0:T(4,128)S(1)} collective-permute-done((f32[1,3,256]{2,1,0:T(4,128)S(1)}, f32[1,3,256]{2,1,0:T(4,128)S(1)}, u32[]{:S(2)}, u32[]{:S(2)}) %collective-permute-start.7) | collective-permute-done | bytes 3104 | tf_op jit(solution)/shard_map/ppermute | solution.py:545
  60.0 3.5 %conv.1 = (f32[1984,256]{1,0:T(8,128)S(1)}, f32[8,2,256]{2,1,0:T(2,128)S(1)}) custom-call(f32[1984,128]{1,0:T(8,128)S(1)} %fusion.5.live, f32[1984,256]{1,0:T(8,128)S(1)} %get-tuple-element.141.z, f32[2,3,256]{2,1,0:T(4,128)S(1)} %pair.1.got.counts, f32[1,256]{1,0:T(1,128)S(1)} %bitcast.36, f32[1,256]{1,0:T(1,128)S(1)} %bitcast.44, bf16[9,256,256]{2,1,0:T(8,128)(2,1)S(1)} %taps.1), custom_call_target="tpu_custom_call" | custom-call | flops 2340421632 | bytes 6283264 | tf_op jit(solution)/shard_map/conv/pallas_call | solution.py:526
  63.6 10.5 %all_to_all.25.got.got_two = f32[8,2,256]{2,1,0:T(2,128)S(1)} all-to-all(f32[8,2,256]{2,1,0:T(2,128)S(1)} %get-tuple-element.147), channel_id=1, replica_groups=mesh['batch'=8,'chan'=4] {'batch'}, dimensions={0} | all-to-all | bytes 32768 | tf_op jit(solution)/shard_map/all_to_all | solution.py:549
  79.0 2.5 slope_two.1.slope
  82.9 17.7 %collective-permute-done.13.refs_0_.refs_2_ = bf16[1984,256]{1,0:T(8,128)(2,1)S(1)} collective-permute-done((bf16[1984,256]{1,0:T(8,128)(2,1)S(1)}, bf16[1984,256]{1,0:T(8,128)(2,1)S(1)}, u32[]{:S(2)}, u32[]{:S(2)}) %collective-permute-start.13) | collective-permute-done | bytes 1015840 | tf_op jit(solution)/shard_map/ppermute | solution.py:545
  105.2 9.1 %all_to_all.26.got = f32[8,2,512]{2,1,0:T(2,128)S(1)} all-to-all(f32[8,2,512]{2,1,0:T(2,128)S(1)} %get-tuple-element.151), channel_id=1, replica_groups=mesh['batch'=8,'chan'=4] {'batch'}, dimensions={0} | all-to-all | bytes 65536 | tf_op jit(solution)/shard_map/all_to_all | solution.py:549
  114.3 3.9 %third.1 = (f32[1984,512]{1,0:T(8,128)S(1)}, f32[8,2,512]{2,1,0:T(2,128)S(1)}) custom-call(f32[1984,128]{1,0:T(8,128)S(1)} %fusion.5.live, f32[1984,512]{1,0:T(8,128)S(1)} %get-tuple-element.163.e, f32[2,3,256]{2,1,0:T(4,128)S(1)} %pair.1.got.counts, f32[8,2,512]{2,1,0:T(2,128)S(1)} %all_to_all.26.got, f32[1,512]{1,0:T(1,128)S(1)} %get-tuple-element.126.gain, ...), custom_call_target="tpu_custom_call" | custom-call | flops 2080374784 | bytes 13281280 | tf_op jit(solution)/shard_map/third/pallas_call | solution.py:526
  118.2 9.1 %all_to_all.27.totals = f32[8,2,512]{2,1,0:T(2,128)S(1)} all-to-all(f32[8,2,512]{2,1,0:T(2,128)S(1)} %get-tuple-element.153), channel_id=1, replica_groups=mesh['batch'=8,'chan'=4] {'batch'}, dimensions={0} | all-to-all | bytes 65536 | tf_op jit(solution)/shard_map/all_to_all | solution.py:549
  129.3 2.9 %collective-permute-done.15.refs_2_ = bf16[1296,512]{1,0:T(8,128)(2,1)S(1)} collective-permute-done((bf16[1296,512]{1,0:T(8,128)(2,1)S(1)}, bf16[1296,512]{1,0:T(8,128)(2,1)S(1)}, u32[]{:S(2)}, u32[]{:S(2)}) %collective-permute-start.15) | collective-permute-done | bytes 1327136 | tf_op jit(solution)/shard_map/ppermute | solution.py:545
  139.9 5.1 %block.1 = bf16[1944,512]{1,0:T(8,128)(2,1)} custom-call(f32[1984,128]{1,0:T(8,128)S(1)} %fusion.5.live, f32[1984,512]{1,0:T(8,128)S(1)} %get-tuple-element.163.e, f32[2,3,256]{2,1,0:T(4,128)S(1)} %pair.1.got.counts, f32[8,2,512]{2,1,0:T(2,128)S(1)} %all_to_all.26.got, f32[1,512]{1,0:T(1,128)S(1)} %get-tuple-element.126.gain, ...), custom_call_target="tpu_custom_call" | custom-call | flops 1040187392 | bytes 9144320 | tf_op jit(solution)/shard_map/block/pallas_call | solution.py:526
  149.9 2.9 %collective-permute-done.22.refs_1_ = bf16[4,32,512]{2,1,0:T(8,128)(2,1)S(1)} collective-permute-done((bf16[4,32,512]{2,1,0:T(8,128)(2,1)S(1)}, bf16[4,32,512]{2,1,0:T(8,128)(2,1)S(1)}, u32[]{:S(2)}, u32[]{:S(2)}) %collective-permute-start.22) | collective-permute-done | bytes 131104 | tf_op jit(solution)/shard_map/ppermute | solution.py:545
  155.0 3.8 %collective-permute-done.19.refs_2_ = bf16[1984,256]{1,0:T(8,128)(2,1)S(1)} collective-permute-done((bf16[1984,256]{1,0:T(8,128)(2,1)S(1)}, bf16[1984,256]{1,0:T(8,128)(2,1)S(1)}, u32[]{:S(2)}, u32[]{:S(2)}) %collective-permute-start.19) | collective-permute-done | bytes 1015840 | tf_op jit(solution)/shard_map/ppermute | solution.py:545
  161.2 11.8 %all_to_all.28.totals = f32[8,2,256]{2,1,0:T(2,128)S(1)} all-to-all(f32[8,2,256]{2,1,0:T(2,128)S(1)} %get-tuple-element.168), channel_id=1, replica_groups=mesh['batch'=8,'chan'=4] {'batch'}, dimensions={0} | all-to-all | bytes 32768 | tf_op jit(solution)/shard_map/all_to_all | solution.py:549
  172.9 3.5 %conv_back.1 = (f32[1984,256]{1,0:T(8,128)S(1)}, f32[1984,256]{1,0:T(8,128)S(1)}, f32[8,2,256]{2,1,0:T(2,128)S(1)}, f32[2,256]{1,0:T(2,128)S(1)}) custom-call(f32[1984,128]{1,0:T(8,128)S(1)} %fusion.5.live, f32[1984,256]{1,0:T(8,128)S(1)} %get-tuple-element.167.d_two, f32[1984,256]{1,0:T(8,128)S(1)} %get-tuple-element.143.z.grouped, ...), custom_call_target="tpu_custom_call" | custom-call | flops 2340421632 | bytes 14443520 | tf_op jit(solution)/shard_map/conv_back/pallas_call | solution.py:526
  176.5 9.2 %all_to_all.29.totals = f32[8,2,256]{2,1,0:T(2,128)S(1)} all-to-all(f32[8,2,256]{2,1,0:T(2,128)S(1)} %get-tuple-element.183), channel_id=1, replica_groups=mesh['batch'=8,'chan'=4] {'batch'}, dimensions={0} | all-to-all | bytes 32768 | tf_op jit(solution)/shard_map/all_to_all | solution.py:549
  187.5 3.7 %reduce_grad.1 = (bf16[2048,256]{1,0:T(8,128)(2,1)S(1)}, f32[2,512,256]{2,1,0:T(8,128)S(1)}) custom-call(s32[5]{0:T(128)S(1)} %stack.11.dims, bf16[1984,256]{1,0:T(8,128)(2,1)S(1)} %get-tuple-element.223.d_red.refs_0_, bf16[1984,512]{1,0:T(8,128)(2,1)S(1)} %pad.4.own.refs_0_.feats, bf16[1984,512]{1,0:T(8,128)(2,1)} %collective-permute-done.beside.refs_1_, ...), custom_call_target="tpu_custom_call" | custom-call | flops 2080374784 | bytes 9830420 | tf_op jit(solution)/shard_map/reduce_grad/pallas_call | solution.py:526
  196.1 2.6 %collective-permute-done.29.refs_2_ = bf16[64,512]{1,0:T(8,128)(2,1)S(1)} collective-permute-done((bf16[64,512]{1,0:T(8,128)(2,1)S(1)}, bf16[64,512]{1,0:T(8,128)(2,1)S(1)}, u32[]{:S(2)}, u32[]{:S(2)}) %collective-permute-start.29) | collective-permute-done | bytes 65568 | tf_op jit(solution)/shard_map/ppermute | solution.py:545
  200.4 3.7 %group_grad.1.a = bf16[288,256]{1,0:T(8,128)(2,1)S(1)} custom-call(f32[1984,128]{1,0:T(8,128)S(1)} %fusion.5.live, f32[1984,256]{1,0:T(8,128)S(1)} %get-tuple-element.141.z, f32[2,3,256]{2,1,0:T(4,128)S(1)} %pair.1.got.counts, f32[1,256]{1,0:T(1,128)S(1)} %bitcast.39, f32[1,256]{1,0:T(1,128)S(1)} %bitcast.46, f32[1984,256]{1,0:T(8,128)S(1)} %get-tuple-element.195.d_grouped), custom_call_target="tpu_custom_call" | custom-call | flops 520093696 | bytes 5234688 | tf_op jit(solution)/shard_map/group_grad/pallas_call | solution.py:526
  216.9 4.2 %collective-permute-done.34.refs_1_ = bf16[32,2048]{1,0:T(8,128)(2,1)S(1)} collective-permute-done((bf16[32,2048]{1,0:T(8,128)(2,1)S(1)}, bf16[32,2048]{1,0:T(8,128)(2,1)S(1)}, u32[]{:S(2)}, u32[]{:S(2)}) %collective-permute-start.34) | collective-permute-done | bytes 131104 | tf_op jit(solution)/shard_map/ppermute | solution.py:545
  221.6 2.5 collective-permute-start.42
  228.5 3.8 %collective-permute-done.42.other_b = bf16[64,2048]{1,0:T(8,128)(2,1)S(1)} collective-permute-done((bf16[64,2048]{1,0:T(8,128)(2,1)S(1)}, bf16[64,2048]{1,0:T(8,128)(2,1)S(1)}, u32[]{:S(2)}, u32[]{:S(2)}) %collective-permute-start.42) | collective-permute-done | bytes 262176 | tf_op jit(solution)/shard_map/ppermute | solution.py:545
  235.5 2.7 %collective-permute-done.39.refs_0_ = bf16[256,256]{1,0:T(8,128)(2,1)S(1)} collective-permute-done((bf16[256,256]{1,0:T(8,128)(2,1)S(1)}, bf16[256,256]{1,0:T(8,128)(2,1)S(1)}, u32[]{:S(2)}, u32[]{:S(2)}) %collective-permute-start.39) | collective-permute-done | bytes 131104 | tf_op jit(solution)/shard_map/ppermute | solution.py:545
  243.2 2.8 %input_far.1 = f32[1944,512]{1,0:T(8,128)} custom-call(f32[1984,512]{1,0:T(8,128)S(1)} %input_near.1.part, bf16[992,256]{1,0:T(8,128)(2,1)S(1)} %collective-permute-done.44.refs_0_, bf16[992,256]{1,0:T(8,128)(2,1)S(1)} %collective-permute-done.45.refs_1_, bf16[992,256]{1,0:T(8,128)(2,1)S(1)} %collective-permute-done.46.refs_2_, ...), custom_call_target="tpu_custom_call" | custom-call | flops 1040187392 | bytes 10600448 | tf_op jit(solution)/shard_map/input_far/pallas_call | solution.py:526
  246.0 3.9 %collective-permute-done.49.b = bf16[288,256]{1,0:T(8,128)(2,1)S(1)} collective-permute-done((bf16[288,256]{1,0:T(8,128)(2,1)S(1)}, bf16[288,256]{1,0:T(8,128)(2,1)S(1)}, u32[]{:S(2)}, u32[]{:S(2)}) %collective-permute-start.49) | collective-permute-done | bytes 147488 | tf_op jit(solution)/shard_map/ppermute | solution.py:545
  (156 shorter events, 84.6 us)
Async XLA Ops:
  3.4 15.6 %collective-permute-start = (bf16[1984,512]{1,0:T(8,128)(2,1)S(1)}, bf16[1984,512]{1,0:T(8,128)(2,1)}, u32[]{:S(2)}, u32[]{:S(2)}) collective-permute-start(bf16[1984,512]{1,0:T(8,128)(2,1)S(1)} %pad.4.own.refs_0_.feats), channel_id=1, source_target_pairs={{0,1},{1,0},{2,3},{3,2},{4,5},{5,4},{6,7},{7,6},{8,9},{9,8},{10,11... | collective-permute-start | bytes 6094856 | tf_op jit(solution)/shard_map/ppermute | solution.py:545
  3.9 15.1 %collective-permute-start.1 = (bf16[1024,256]{1,0:T(8,128)(2,1)S(1)}, bf16[1024,256]{1,0:T(8,128)(2,1)S(1)}, u32[]{:S(2)}, u32[]{:S(2)}) collective-permute-start(bf16[1024,256]{1,0:T(8,128)(2,1)S(1)} %constant_dynamic-slice_fusion), channel_id=1, source_target_pairs={{0,2},{1,3},{2,0},{3,1},{4,6},{5,7},{6,4},{7,5},{8,10},{9,11},{10,... | collective-permute-start | bytes 1572872 | tf_op jit(solution)/shard_map/ppermute | solution.py:545
  21.7 24.3 %collective-permute-start.2 = (bf16[1984,256]{1,0:T(8,128)(2,1)S(1)}, bf16[1984,256]{1,0:T(8,128)(2,1)S(1)}, u32[]{:S(2)}, u32[]{:S(2)}) collective-permute-start(bf16[1984,256]{1,0:T(8,128)(2,1)S(1)} %part_far.1), channel_id=1, source_target_pairs={{0,2},{1,3},{2,0},{3,1},{4,6},{5,7},{6,4},{7,5},{8,10},{9,11},{10,... | collective-permute-start | bytes 3047432 | tf_op jit(solution)/shard_map/ppermute | solution.py:545
  27.8 7.9 %collective-permute-start.5 = (bf16[512,256]{1,0:T(8,128)(2,1)S(1)}, bf16[512,256]{1,0:T(8,128)(2,1)S(1)}, u32[]{:S(2)}, u32[]{:S(2)}) collective-permute-start(bf16[512,256]{1,0:T(8,128)(2,1)S(1)} %get-tuple-element.136), channel_id=1, source_target_pairs={{0,1},{1,0},{2,3},{3,2},{4,5},{5,4},{6,7},{7,6},{8,9},{9,8},{10,11... | collective-permute-start | bytes 786440 | tf_op jit(solution)/shard_map/ppermute | solution.py:545
  46.0 17.6 %collective-permute-start.10 = (bf16[256,512]{1,0:T(8,128)(2,1)S(1)}, bf16[256,512]{1,0:T(8,128)(2,1)S(1)}, u32[]{:S(2)}, u32[]{:S(2)}) collective-permute-start(bf16[256,512]{1,0:T(8,128)(2,1)S(1)} %get-tuple-element.145), channel_id=1, source_target_pairs={{0,2},{1,3},{2,0},{3,1},{4,6},{5,7},{6,4},{7,5},{8,10},{9,11},{10,... | collective-permute-start | bytes 786440 | tf_op jit(solution)/shard_map/ppermute | solution.py:545
  47.6 16.0 %collective-permute-start.11 = (bf16[256,512]{1,0:T(8,128)(2,1)S(1)}, bf16[256,512]{1,0:T(8,128)(2,1)S(1)}, u32[]{:S(2)}, u32[]{:S(2)}) collective-permute-start(bf16[256,512]{1,0:T(8,128)(2,1)S(1)} %get-tuple-element.146), channel_id=1, source_target_pairs={{0,3},{1,2},{2,1},{3,0},{4,7},{5,6},{6,5},{7,4},{8,11},{9,10},{10,... | collective-permute-start | bytes 786440 | tf_op jit(solution)/shard_map/ppermute | solution.py:545
  75.8 24.9 %collective-permute-start.13 = (bf16[1984,256]{1,0:T(8,128)(2,1)S(1)}, bf16[1984,256]{1,0:T(8,128)(2,1)S(1)}, u32[]{:S(2)}, u32[]{:S(2)}) collective-permute-start(bf16[1984,256]{1,0:T(8,128)(2,1)S(1)} %hidden.1.refs_0_), channel_id=1, source_target_pairs={{0,2},{1,3},{2,0},{3,1},{4,6},{5,7},{6,4},{7,5},{8,10},{9,11},{10,... | collective-permute-start | bytes 3047432 | tf_op jit(solution)/shard_map/ppermute | solution.py:545
  100.6 31.5 %collective-permute-start.15 = (bf16[1296,512]{1,0:T(8,128)(2,1)S(1)}, bf16[1296,512]{1,0:T(8,128)(2,1)S(1)}, u32[]{:S(2)}, u32[]{:S(2)}) collective-permute-start(bf16[1296,512]{1,0:T(8,128)(2,1)S(1)} %slice.36), channel_id=1, source_target_pairs={{0,2},{1,3},{2,0},{3,1},{4,6},{5,7},{6,4},{7,5},{8,10},{9,11},{10,... | collective-permute-start | bytes 3981320 | tf_op jit(solution)/shard_map/ppermute | solution.py:545
  134.6 24.2 %collective-permute-start.19 = (bf16[1984,256]{1,0:T(8,128)(2,1)S(1)}, bf16[1984,256]{1,0:T(8,128)(2,1)S(1)}, u32[]{:S(2)}, u32[]{:S(2)}) collective-permute-start(bf16[1984,256]{1,0:T(8,128)(2,1)S(1)} %merge.1), channel_id=1, source_target_pairs={{0,2},{1,3},{2,0},{3,1},{4,6},{5,7},{6,4},{7,5},{8,10},{9,11},{10,... | collective-permute-start | bytes 3047432 | tf_op jit(solution)/shard_map/ppermute | solution.py:545
  135.2 24.7 %collective-permute-start.17 = (bf16[1296,512]{1,0:T(8,128)(2,1)S(1)}, bf16[1296,512]{1,0:T(8,128)(2,1)S(1)}, u32[]{:S(2)}, u32[]{:S(2)}) collective-permute-start(bf16[1296,512]{1,0:T(8,128)(2,1)S(1)} %collective-permute-done.15.refs_2_), channel_id=1, source_target_pairs={{0,1},{1,0},{2,3},{3,2},{4,5},{5,4},{6,7},{7,6},{8,9},{9,8},{10,11... | collective-permute-start | bytes 3981320 | tf_op jit(solution)/shard_map/ppermute | solution.py:545
  135.2 24.7 %collective-permute-start.18 = (bf16[1984,256]{1,0:T(8,128)(2,1)S(1)}, bf16[1984,256]{1,0:T(8,128)(2,1)S(1)}, u32[]{:S(2)}, u32[]{:S(2)}) collective-permute-start(bf16[1984,256]{1,0:T(8,128)(2,1)S(1)} %get-tuple-element.159), channel_id=1, source_target_pairs={{0,1},{1,0},{2,3},{3,2},{4,5},{5,4},{6,7},{7,6},{8,9},{9,8},{10,11... | collective-permute-start | bytes 3047432 | tf_op jit(solution)/shard_map/ppermute | solution.py:545
  138.7 8.3 %collective-permute-start.21 = (bf16[4,64,512]{2,1,0:T(8,128)(2,1)S(1)}, bf16[4,64,512]{2,1,0:T(8,128)(2,1)S(1)}, u32[]{:S(2)}, u32[]{:S(2)}) collective-permute-start(bf16[4,64,512]{2,1,0:T(8,128)(2,1)S(1)} %get-tuple-element.172), channel_id=1, source_target_pairs={{0,8},{4,12},{8,0},{12,4},{16,24},{20,28},{24,16},{28,20},{1,9},{5... | collective-permute-start | bytes 786440 | tf_op jit(solution)/shard_map/ppermute | solution.py:545
  139.2 7.9 %collective-permute-start.20 = (bf16[4,64,512]{2,1,0:T(8,128)(2,1)S(1)}, bf16[4,64,512]{2,1,0:T(8,128)(2,1)S(1)}, u32[]{:S(2)}, u32[]{:S(2)}) collective-permute-start(bf16[4,64,512]{2,1,0:T(8,128)(2,1)S(1)} %get-tuple-element.162), channel_id=1, source_target_pairs={{0,4},{4,0},{8,12},{12,8},{16,20},{20,16},{24,28},{28,24},{1,5},{5... | collective-permute-start | bytes 786440 | tf_op jit(solution)/shard_map/ppermute | solution.py:545
  158.8 17.7 %collective-permute-start.25 = (bf16[688,512]{1,0:T(8,128)(2,1)S(1)}, bf16[688,512]{1,0:T(8,128)(2,1)S(1)}, u32[]{:S(2)}, u32[]{:S(2)}) collective-permute-start(bf16[688,512]{1,0:T(8,128)(2,1)S(1)} %slice.37), channel_id=1, source_target_pairs={{0,2},{1,3},{2,0},{3,1},{4,6},{5,7},{6,4},{7,5},{8,10},{9,11},{10,... | collective-permute-start | bytes 2113544 | tf_op jit(solution)/shard_map/ppermute | solution.py:545
  159.4 17.0 %collective-permute-start.24 = (bf16[4,64,512]{2,1,0:T(8,128)(2,1)S(1)}, bf16[4,64,512]{2,1,0:T(8,128)(2,1)S(1)}, u32[]{:S(2)}, u32[]{:S(2)}) collective-permute-start(bf16[4,64,512]{2,1,0:T(8,128)(2,1)S(1)} %send_both.8.a), channel_id=1, source_target_pairs={{0,16},{4,20},{8,24},{12,28},{16,0},{20,4},{24,8},{28,12},{1,17},{... | collective-permute-start | bytes 786440 | tf_op jit(solution)/shard_map/ppermute | solution.py:545
  193.1 11.1 %collective-permute-start.32 = (bf16[512,256]{1,0:T(8,128)(2,1)S(1)}, bf16[512,256]{1,0:T(8,128)(2,1)S(1)}, u32[]{:S(2)}, u32[]{:S(2)}) collective-permute-start(bf16[512,256]{1,0:T(8,128)(2,1)S(1)} %get-tuple-element.197), channel_id=1, source_target_pairs={{0,8},{4,12},{8,0},{12,4},{16,24},{20,28},{24,16},{28,20},{1,9},{5... | collective-permute-start | bytes 786440 | tf_op jit(solution)/shard_map/ppermute | solution.py:545
  193.6 10.6 %collective-permute-start.31 = (bf16[512,256]{1,0:T(8,128)(2,1)S(1)}, bf16[512,256]{1,0:T(8,128)(2,1)S(1)}, u32[]{:S(2)}, u32[]{:S(2)}) collective-permute-start(bf16[512,256]{1,0:T(8,128)(2,1)S(1)} %get-tuple-element.189), channel_id=1, source_target_pairs={{0,4},{4,0},{8,12},{12,8},{16,20},{20,16},{24,28},{28,24},{1,5},{5... | collective-permute-start | bytes 786440 | tf_op jit(solution)/shard_map/ppermute | solution.py:545
  204.8 5.9 %collective-permute-start.36 = (bf16[256,256]{1,0:T(8,128)(2,1)S(1)}, bf16[256,256]{1,0:T(8,128)(2,1)S(1)}, u32[]{:S(2)}, u32[]{:S(2)}) collective-permute-start(bf16[256,256]{1,0:T(8,128)(2,1)S(1)} %get-tuple-element.202), channel_id=1, source_target_pairs={{0,4},{4,0},{8,12},{12,8},{16,20},{20,16},{24,28},{28,24},{1,5},{5... | collective-permute-start | bytes 393224 | tf_op jit(solution)/shard_map/ppermute | solution.py:545
  207.8 19.2 %collective-permute-start.44 = (bf16[992,256]{1,0:T(8,128)(2,1)S(1)}, bf16[992,256]{1,0:T(8,128)(2,1)S(1)}, u32[]{:S(2)}, u32[]{:S(2)}) collective-permute-start(bf16[992,256]{1,0:T(8,128)(2,1)S(1)} %slice.40), channel_id=1, source_target_pairs={{0,2},{1,3},{2,0},{3,1},{4,6},{5,7},{6,4},{7,5},{8,10},{9,11},{10,... | collective-permute-start | bytes 1523720 | tf_op jit(solution)/shard_map/ppermute | solution.py:545
  209.3 6.1 %collective-permute-start.37 = (bf16[32,2048]{1,0:T(8,128)(2,1)S(1)}, bf16[32,2048]{1,0:T(8,128)(2,1)S(1)}, u32[]{:S(2)}, u32[]{:S(2)}) collective-permute-start(bf16[32,2048]{1,0:T(8,128)(2,1)S(1)} %get-tuple-element.204.refs_0_), channel_id=1, source_target_pairs={{0,4},{4,0},{8,12},{12,8},{16,20},{20,16},{24,28},{28,24},{1,5},{5... | collective-permute-start | bytes 393224 | tf_op jit(solution)/shard_map/ppermute | solution.py:545
  212.4 14.3 %collective-permute-start.38 = (bf16[512,256]{1,0:T(8,128)(2,1)S(1)}, bf16[512,256]{1,0:T(8,128)(2,1)S(1)}, u32[]{:S(2)}, u32[]{:S(2)}) collective-permute-start(bf16[512,256]{1,0:T(8,128)(2,1)S(1)} %send_both.11.a), channel_id=1, source_target_pairs={{0,16},{4,20},{8,24},{12,28},{16,0},{20,4},{24,8},{28,12},{1,17},{... | collective-permute-start | bytes 786440 | tf_op jit(solution)/shard_map/ppermute | solution.py:545
  213.1 11.1 %collective-permute-start.33 = (bf16[288,256]{1,0:T(8,128)(2,1)S(1)}, bf16[288,256]{1,0:T(8,128)(2,1)S(1)}, u32[]{:S(2)}, u32[]{:S(2)}) collective-permute-start(bf16[288,256]{1,0:T(8,128)(2,1)S(1)} %group_grad.1.a), channel_id=1, source_target_pairs={{0,4},{4,0},{8,12},{12,8},{16,20},{20,16},{24,28},{28,24},{1,5},{5... | collective-permute-start | bytes 442376 | tf_op jit(solution)/shard_map/ppermute | solution.py:545
  213.8 7.3 %collective-permute-start.34 = (bf16[32,2048]{1,0:T(8,128)(2,1)S(1)}, bf16[32,2048]{1,0:T(8,128)(2,1)S(1)}, u32[]{:S(2)}, u32[]{:S(2)}) collective-permute-start(bf16[32,2048]{1,0:T(8,128)(2,1)S(1)} %get-tuple-element.201.sums), channel_id=1, source_target_pairs={{0,8},{4,12},{8,0},{12,4},{16,24},{20,28},{24,16},{28,20},{1,9},{5... | collective-permute-start | bytes 393224 | tf_op jit(solution)/shard_map/ppermute | solution.py:545
  215.4 23.4 %collective-permute-start.45 = (bf16[992,256]{1,0:T(8,128)(2,1)S(1)}, bf16[992,256]{1,0:T(8,128)(2,1)S(1)}, u32[]{:S(2)}, u32[]{:S(2)}) collective-permute-start(bf16[992,256]{1,0:T(8,128)(2,1)S(1)} %slice.41), channel_id=1, source_target_pairs={{0,2},{1,3},{2,0},{3,1},{4,6},{5,7},{6,4},{7,5},{8,10},{9,11},{10,... | collective-permute-start | bytes 1523720 | tf_op jit(solution)/shard_map/ppermute | solution.py:545
  221.6 10.6 %collective-permute-start.42 = (bf16[64,2048]{1,0:T(8,128)(2,1)S(1)}, bf16[64,2048]{1,0:T(8,128)(2,1)S(1)}, u32[]{:S(2)}, u32[]{:S(2)}) collective-permute-start(bf16[64,2048]{1,0:T(8,128)(2,1)S(1)} %get-tuple-element.214.b), channel_id=1, source_target_pairs={{0,8},{4,12},{8,0},{12,4},{16,24},{20,28},{24,16},{28,20},{1,9},{5... | collective-permute-start | bytes 786440 | tf_op jit(solution)/shard_map/ppermute | solution.py:545
  224.2 8.2 %collective-permute-start.41 = (bf16[64,2048]{1,0:T(8,128)(2,1)S(1)}, bf16[64,2048]{1,0:T(8,128)(2,1)S(1)}, u32[]{:S(2)}, u32[]{:S(2)}) collective-permute-start(bf16[64,2048]{1,0:T(8,128)(2,1)S(1)} %get-tuple-element.212.a), channel_id=1, source_target_pairs={{0,4},{4,0},{8,12},{12,8},{16,20},{20,16},{24,28},{28,24},{1,5},{5... | collective-permute-start | bytes 786440 | tf_op jit(solution)/shard_map/ppermute | solution.py:545
  226.8 8.6 %collective-permute-start.40 = (bf16[288,256]{1,0:T(8,128)(2,1)S(1)}, bf16[288,256]{1,0:T(8,128)(2,1)S(1)}, u32[]{:S(2)}, u32[]{:S(2)}) collective-permute-start(bf16[288,256]{1,0:T(8,128)(2,1)S(1)} %add.35.a), channel_id=1, source_target_pairs={{0,8},{4,12},{8,0},{12,4},{16,24},{20,28},{24,16},{28,20},{1,9},{5... | collective-permute-start | bytes 442376 | tf_op jit(solution)/shard_map/ppermute | solution.py:545
  227.0 8.5 %collective-permute-start.43 = (bf16[256,256]{1,0:T(8,128)(2,1)S(1)}, bf16[256,256]{1,0:T(8,128)(2,1)S(1)}, u32[]{:S(2)}, u32[]{:S(2)}) collective-permute-start(bf16[256,256]{1,0:T(8,128)(2,1)S(1)} %get-tuple-element.233), channel_id=1, source_target_pairs={{0,4},{4,0},{8,12},{12,8},{16,20},{20,16},{24,28},{28,24},{1,5},{5... | collective-permute-start | bytes 393224 | tf_op jit(solution)/shard_map/ppermute | solution.py:545
  232.4 10.8 %collective-permute-start.46 = (bf16[992,256]{1,0:T(8,128)(2,1)S(1)}, bf16[992,256]{1,0:T(8,128)(2,1)S(1)}, u32[]{:S(2)}, u32[]{:S(2)}) collective-permute-start(bf16[992,256]{1,0:T(8,128)(2,1)S(1)} %collective-permute-done.44.refs_0_), channel_id=1, source_target_pairs={{0,1},{1,0},{2,3},{3,2},{4,5},{5,4},{6,7},{7,6},{8,9},{9,8},{10,11... | collective-permute-start | bytes 1523720 | tf_op jit(solution)/shard_map/ppermute | solution.py:545
  240.0 12.8 %collective-permute-start.48 = (bf16[512,256]{1,0:T(8,128)(2,1)S(1)}, bf16[512,256]{1,0:T(8,128)(2,1)S(1)}, u32[]{:S(2)}, u32[]{:S(2)}) collective-permute-start(bf16[512,256]{1,0:T(8,128)(2,1)S(1)} %get-tuple-element.219.a), channel_id=1, source_target_pairs={{0,4},{4,0},{8,12},{12,8},{16,20},{20,16},{24,28},{28,24},{1,5},{5... | collective-permute-start | bytes 786440 | tf_op jit(solution)/shard_map/ppermute | solution.py:545
  240.6 9.3 %collective-permute-start.49 = (bf16[288,256]{1,0:T(8,128)(2,1)S(1)}, bf16[288,256]{1,0:T(8,128)(2,1)S(1)}, u32[]{:S(2)}, u32[]{:S(2)}) collective-permute-start(bf16[288,256]{1,0:T(8,128)(2,1)S(1)} %add.37.a), channel_id=1, source_target_pairs={{0,16},{4,20},{8,24},{12,28},{16,0},{20,4},{24,8},{28,12},{1,17},{... | collective-permute-start | bytes 442376 | tf_op jit(solution)/shard_map/ppermute | solution.py:545
  241.5 11.3 %collective-permute-start.50 = (bf16[512,256]{1,0:T(8,128)(2,1)S(1)}, bf16[512,256]{1,0:T(8,128)(2,1)S(1)}, u32[]{:S(2)}, u32[]{:S(2)}) collective-permute-start(bf16[512,256]{1,0:T(8,128)(2,1)S(1)} %get-tuple-element.225.b), channel_id=1, source_target_pairs={{0,8},{4,12},{8,0},{12,4},{16,24},{20,28},{24,16},{28,20},{1,9},{5... | collective-permute-start | bytes 786440 | tf_op jit(solution)/shard_map/ppermute | solution.py:545
  (29 other events, 174.6 us)

commit v6 on v5

--- a/solution.py
+++ b/solution.py
@@ -850,16 +850,17 @@
                 arrange_kernel, [shape((mine.shape[1] // 2, n_chan * share), BF16)] * 2, [dims, *cols],
                 name="arrange", smem=True,
             )
+            far_rows(0, *cols)
+            ties = cols
+        elif s == 1:
             group_part = call(
                 functools.partial(group_grad_kernel, side, slots, group_width),
                 [shape((9 * group_width, width), BF16)],
-                [live, z, got_one, gain_one, shift_one, after(d_grouped, *cols)],
+                [live, z, got_one, gain_one, shift_one, after(d_grouped, send[0])],
                 [tall], flops=mm, name="group_grad",
             )
-            far_rows(0, *cols)
+            group_other = swap(group_part, "batch", n_batch, 1)
             ties = [group_part]
-        elif s == 1:
-            group_other = swap(after(group_part, send[0]), "batch", n_batch, 1)
             others_cols = [
                 swap(after(cols[h], send[0]), "batch", n_batch, 1 << orders[h][top - 1])
                 for h in halves

time: 255 us -> 254 us (level)
  no operation moved by 1% of the time
where the time goes in v6:
time: 254 us; the launch traced here: 253 us
  waiting for transfers between devices  83.8 us (33%)
  Pallas kernels  67.6 us (27%)
  blocking collectives  49.6 us (20%)
  starting transfers between devices  38.9 us (15%)
  local copies, waits for them, and re-layouts  8.1 us (3%)
  between operations  2.59 us (1%)
  other arithmetic  2.58 us (1%)
    ppermute x51, waiting for transfers between devices, swap(): return lax.ppermute(v, axis, [(i, i ^ k) for i in range(size)])  83.8 us
    pallas_call x44, Pallas kernels, call(): pl.pallas_call(kernel, out_shape=list(outs), grid=(steps,) if steps else...  67.6 us
    all_to_all x5, blocking collectives, batch_sum(): return lax.all_to_all(spread, 'batch', 0, 0)  49.6 us
    ppermute x51, starting transfers between devices, swap(): return lax.ppermute(v, axis, [(i, i ^ k) for i in range(size)])  38.9 us
  transfers between devices with their start and end apart: 51, of which 23 were waited for; matrix products, arithmetic and copies ran while one was open for 2% of the time, Pallas kernels for 23%

profile of v6, /device:TPU:0, one launch (start us, length us, event | category | flops | bytes accessed | tf_op | source)
XLA Modules:
  0.0 253.1 jit_solution(15835405308428823079)
XLA Ops:
  3.9 2.6 %collective-permute-start.1 = (bf16[1024,256]{1,0:T(8,128)(2,1)S(1)}, bf16[1024,256]{1,0:T(8,128)(2,1)S(1)}, u32[]{:S(2)}, u32[]{:S(2)}) collective-permute-start(bf16[1024,256]{1,0:T(8,128)(2,1)S(1)} %constant_dynamic-slice_fusion), channel_id=1, source_target_pairs={{0,2},{1,3},{2,0},{3,1},{4,6},{5,7},{6,4},{7,5},{8,10},{9,11},{10,... | collective-permute-start | bytes 1572872 | tf_op jit(solution)/shard_map/ppermute | solution.py:545
  7.9 11.1 %collective-permute-done.1.refs_0_ = bf16[1024,256]{1,0:T(8,128)(2,1)S(1)} collective-permute-done((bf16[1024,256]{1,0:T(8,128)(2,1)S(1)}, bf16[1024,256]{1,0:T(8,128)(2,1)S(1)}, u32[]{:S(2)}, u32[]{:S(2)}) %collective-permute-start.1) | collective-permute-done | bytes 524320 | tf_op jit(solution)/shard_map/ppermute | solution.py:545
  19.1 2.7 %part_far.1 = bf16[1984,256]{1,0:T(8,128)(2,1)S(1)} custom-call(s32[5]{0:T(128)S(1)} %stack.11.dims, bf16[1984,512]{1,0:T(8,128)(2,1)S(1)} %pad.4.own.refs_0_.feats, bf16[1984,512]{1,0:T(8,128)(2,1)} %collective-permute-done.beside.refs_1_, bf16[1024,256]{1,0:T(8,128)(2,1)S(1)} %collective-permute-done.1.refs_0_), custom_call_target="tpu_custom_call" | custom-call | flops 1040187392 | bytes 5603348 | tf_op jit(solution)/shard_map/part_far/pallas_call | solution.py:526
  24.2 3.6 %near.1.part = f32[1984,256]{1,0:T(8,128)S(1)} custom-call(s32[5]{0:T(128)S(1)} %stack.11.dims, bf16[1984,512]{1,0:T(8,128)(2,1)S(1)} %pad.4.own.refs_0_.feats, bf16[1984,512]{1,0:T(8,128)(2,1)} %collective-permute-done.beside.refs_1_, bf16[2048,256]{1,0:T(8,128)(2,1)S(1)} %copy-done.1), custom_call_target="tpu_custom_call" | custom-call | flops 1040187392 | bytes 7143444 | tf_op jit(solution)/shard_map/near/pallas_call | solution.py:526
  27.9 3.3 %copy-done = bf16[24,9,9,2048]{3,0,2,1:T(8,128)(2,1)S(1)} copy-done((bf16[24,9,9,2048]{3,0,2,1:T(8,128)(2,1)S(1)}, bf16[24,9,9,2048]{3,0,2,1:T(8,128)(2,1)}, u32[]{:S(2)}) %copy-start) | copy-done | bytes 7962648
  33.0 2.5 %fusion.5.live = f32[1984,128]{1,0:T(8,128)S(1)} fusion(s32[1984]{0:T(1024)S(1)} %get-tuple-element.244, s32[1984]{0:T(1024)S(1)} %get-tuple-element.249, s32[]{:T(128)} %bitcast.30, s32[1984]{0:T(1024)S(1)} %get-tuple-element.243, s32[1984]{0:T(1024)S(1)} %get-tuple-element.250, s32[]{:T(128)} %bitcast.31, s32[1984]{0:T(1024)S(1)} %get-tuple-element.247, ...), kind=kLoop, calls=%fused_computation.9 | loop fusion | flops 3809280 | bytes 1069384 | tf_op jit(solution)/shard_map/convert_element_type | solution.py:641
  35.8 10.2 %collective-permute-done.2.refs_0_ = bf16[1984,256]{1,0:T(8,128)(2,1)S(1)} collective-permute-done((bf16[1984,256]{1,0:T(8,128)(2,1)S(1)}, bf16[1984,256]{1,0:T(8,128)(2,1)S(1)}, u32[]{:S(2)}, u32[]{:S(2)}) %collective-permute-start.2) | collective-permute-done | bytes 1015840 | tf_op jit(solution)/shard_map/ppermute | solution.py:545
  48.1 3.7 %collective-permute-start.8 = (f32[1,3,256]{2,1,0:T(4,128)S(1)}, f32[1,3,256]{2,1,0:T(4,128)S(1)}, u32[]{:S(2)}, u32[]{:S(2)}) collective-permute-start(f32[1,3,256]{2,1,0:T(4,128)S(1)} %get-tuple-element.143.refs_0_), channel_id=1, source_target_pairs={{0,24},{4,28},{8,16},{12,20},{16,8},{20,12},{24,0},{28,4},{1,25},{... | collective-permute-start | bytes 9224 | tf_op jit(solution)/shard_map/ppermute | solution.py:545
  53.6 2.7 %collective-permute-done.7.refs_2_ = f32[1,3,256]{2,1,0:T(4,128)S(1)} collective-permute-done((f32[1,3,256]{2,1,0:T(4,128)S(1)}, f32[1,3,256]{2,1,0:T(4,128)S(1)}, u32[]{:S(2)}, u32[]{:S(2)}) %collective-permute-start.7) | collective-permute-done | bytes 3104 | tf_op jit(solution)/shard_map/ppermute | solution.py:545
  60.0 3.5 %conv.1 = (f32[1984,256]{1,0:T(8,128)S(1)}, f32[8,2,256]{2,1,0:T(2,128)S(1)}) custom-call(f32[1984,128]{1,0:T(8,128)S(1)} %fusion.5.live, f32[1984,256]{1,0:T(8,128)S(1)} %get-tuple-element.142.z, f32[2,3,256]{2,1,0:T(4,128)S(1)} %pair.1.got.counts, f32[1,256]{1,0:T(1,128)S(1)} %bitcast.36, f32[1,256]{1,0:T(1,128)S(1)} %bitcast.44, bf16[9,256,256]{2,1,0:T(8,128)(2,1)S(1)} %taps.1), custom_call_target="tpu_custom_call" | custom-call | flops 2340421632 | bytes 6283264 | tf_op jit(solution)/shard_map/conv/pallas_call | solution.py:526
  63.6 10.5 %all_to_all.25.got.got_two = f32[8,2,256]{2,1,0:T(2,128)S(1)} all-to-all(f32[8,2,256]{2,1,0:T(2,128)S(1)} %get-tuple-element.148), channel_id=1, replica_groups=mesh['batch'=8,'chan'=4] {'batch'}, dimensions={0} | all-to-all | bytes 32768 | tf_op jit(solution)/shard_map/all_to_all | solution.py:549
  76.3 2.5 slope_one.1.slope
  79.0 2.5 %slope_two.1.slope = f32[1984,256]{1,0:T(8,128)S(1)} custom-call(f32[1984,128]{1,0:T(8,128)S(1)} %fusion.5.live, f32[1984,256]{1,0:T(8,128)S(1)} %get-tuple-element.144.z.grouped, f32[2,3,256]{2,1,0:T(4,128)S(1)} %pair.1.got.counts, f32[8,2,256]{2,1,0:T(2,128)S(1)} %all_to_all.25.got.got_two, f32[1,256]{1,0:T(1,128)S(1)} %bitcast.34, f32[1,256]{1,0:T(1,128)S(1)} %bitcast.43), custom_call_target="tpu_custom_call" | custom-call | flops 520093696 | bytes 5103616 | tf_op jit(solution)/shard_map/slope_two/pallas_call | solution.py:526
  82.9 17.7 %collective-permute-done.13.refs_0_.refs_2_ = bf16[1984,256]{1,0:T(8,128)(2,1)S(1)} collective-permute-done((bf16[1984,256]{1,0:T(8,128)(2,1)S(1)}, bf16[1984,256]{1,0:T(8,128)(2,1)S(1)}, u32[]{:S(2)}, u32[]{:S(2)}) %collective-permute-start.13) | collective-permute-done | bytes 1015840 | tf_op jit(solution)/shard_map/ppermute | solution.py:545
  105.2 9.1 %all_to_all.26.got = f32[8,2,512]{2,1,0:T(2,128)S(1)} all-to-all(f32[8,2,512]{2,1,0:T(2,128)S(1)} %get-tuple-element.152), channel_id=1, replica_groups=mesh['batch'=8,'chan'=4] {'batch'}, dimensions={0} | all-to-all | bytes 65536 | tf_op jit(solution)/shard_map/all_to_all | solution.py:549
  114.3 3.9 %third.1 = (f32[1984,512]{1,0:T(8,128)S(1)}, f32[8,2,512]{2,1,0:T(2,128)S(1)}) custom-call(f32[1984,128]{1,0:T(8,128)S(1)} %fusion.5.live, f32[1984,512]{1,0:T(8,128)S(1)} %get-tuple-element.164.e, f32[2,3,256]{2,1,0:T(4,128)S(1)} %pair.1.got.counts, f32[8,2,512]{2,1,0:T(2,128)S(1)} %all_to_all.26.got, f32[1,512]{1,0:T(1,128)S(1)} %get-tuple-element.127.gain, ...), custom_call_target="tpu_custom_call" | custom-call | flops 2080374784 | bytes 13281280 | tf_op jit(solution)/shard_map/third/pallas_call | solution.py:526
  118.2 9.1 %all_to_all.27.totals = f32[8,2,512]{2,1,0:T(2,128)S(1)} all-to-all(f32[8,2,512]{2,1,0:T(2,128)S(1)} %get-tuple-element.154), channel_id=1, replica_groups=mesh['batch'=8,'chan'=4] {'batch'}, dimensions={0} | all-to-all | bytes 65536 | tf_op jit(solution)/shard_map/all_to_all | solution.py:549
  129.3 2.9 %collective-permute-done.15.refs_2_ = bf16[1296,512]{1,0:T(8,128)(2,1)S(1)} collective-permute-done((bf16[1296,512]{1,0:T(8,128)(2,1)S(1)}, bf16[1296,512]{1,0:T(8,128)(2,1)S(1)}, u32[]{:S(2)}, u32[]{:S(2)}) %collective-permute-start.15) | collective-permute-done | bytes 1327136 | tf_op jit(solution)/shard_map/ppermute | solution.py:545
  139.9 5.1 %block.1 = bf16[1944,512]{1,0:T(8,128)(2,1)} custom-call(f32[1984,128]{1,0:T(8,128)S(1)} %fusion.5.live, f32[1984,512]{1,0:T(8,128)S(1)} %get-tuple-element.164.e, f32[2,3,256]{2,1,0:T(4,128)S(1)} %pair.1.got.counts, f32[8,2,512]{2,1,0:T(2,128)S(1)} %all_to_all.26.got, f32[1,512]{1,0:T(1,128)S(1)} %get-tuple-element.127.gain, ...), custom_call_target="tpu_custom_call" | custom-call | flops 1040187392 | bytes 9144320 | tf_op jit(solution)/shard_map/block/pallas_call | solution.py:526
  149.9 2.9 %collective-permute-done.22.refs_1_ = bf16[4,32,512]{2,1,0:T(8,128)(2,1)S(1)} collective-permute-done((bf16[4,32,512]{2,1,0:T(8,128)(2,1)S(1)}, bf16[4,32,512]{2,1,0:T(8,128)(2,1)S(1)}, u32[]{:S(2)}, u32[]{:S(2)}) %collective-permute-start.22) | collective-permute-done | bytes 131104 | tf_op jit(solution)/shard_map/ppermute | solution.py:545
  155.0 3.8 %collective-permute-done.19.refs_2_ = bf16[1984,256]{1,0:T(8,128)(2,1)S(1)} collective-permute-done((bf16[1984,256]{1,0:T(8,128)(2,1)S(1)}, bf16[1984,256]{1,0:T(8,128)(2,1)S(1)}, u32[]{:S(2)}, u32[]{:S(2)}) %collective-permute-start.19) | collective-permute-done | bytes 1015840 | tf_op jit(solution)/shard_map/ppermute | solution.py:545
  161.2 11.8 %all_to_all.28.totals = f32[8,2,256]{2,1,0:T(2,128)S(1)} all-to-all(f32[8,2,256]{2,1,0:T(2,128)S(1)} %get-tuple-element.169), channel_id=1, replica_groups=mesh['batch'=8,'chan'=4] {'batch'}, dimensions={0} | all-to-all | bytes 32768 | tf_op jit(solution)/shard_map/all_to_all | solution.py:549
  172.9 3.5 %conv_back.1 = (f32[1984,256]{1,0:T(8,128)S(1)}, f32[1984,256]{1,0:T(8,128)S(1)}, f32[8,2,256]{2,1,0:T(2,128)S(1)}, f32[2,256]{1,0:T(2,128)S(1)}) custom-call(f32[1984,128]{1,0:T(8,128)S(1)} %fusion.5.live, f32[1984,256]{1,0:T(8,128)S(1)} %get-tuple-element.168.d_two, f32[1984,256]{1,0:T(8,128)S(1)} %get-tuple-element.144.z.grouped, ...), custom_call_target="tpu_custom_call" | custom-call | flops 2340421632 | bytes 14443520 | tf_op jit(solution)/shard_map/conv_back/pallas_call | solution.py:526
  176.5 9.2 %all_to_all.29.totals = f32[8,2,256]{2,1,0:T(2,128)S(1)} all-to-all(f32[8,2,256]{2,1,0:T(2,128)S(1)} %get-tuple-element.184), channel_id=1, replica_groups=mesh['batch'=8,'chan'=4] {'batch'}, dimensions={0} | all-to-all | bytes 32768 | tf_op jit(solution)/shard_map/all_to_all | solution.py:549
  187.5 3.7 %reduce_grad.1 = (bf16[2048,256]{1,0:T(8,128)(2,1)S(1)}, f32[2,512,256]{2,1,0:T(8,128)S(1)}) custom-call(s32[5]{0:T(128)S(1)} %stack.11.dims, bf16[1984,256]{1,0:T(8,128)(2,1)S(1)} %get-tuple-element.225.d_red.refs_0_, bf16[1984,512]{1,0:T(8,128)(2,1)S(1)} %pad.4.own.refs_0_.feats, bf16[1984,512]{1,0:T(8,128)(2,1)} %collective-permute-done.beside.refs_1_, ...), custom_call_target="tpu_custom_call" | custom-call | flops 2080374784 | bytes 9830420 | tf_op jit(solution)/shard_map/reduce_grad/pallas_call | solution.py:526
  196.1 2.6 %collective-permute-done.30.refs_2_ = bf16[64,512]{1,0:T(8,128)(2,1)S(1)} collective-permute-done((bf16[64,512]{1,0:T(8,128)(2,1)S(1)}, bf16[64,512]{1,0:T(8,128)(2,1)S(1)}, u32[]{:S(2)}, u32[]{:S(2)}) %collective-permute-start.30) | collective-permute-done | bytes 65568 | tf_op jit(solution)/shard_map/ppermute | solution.py:545
  207.5 3.7 %group_grad.1.a = bf16[288,256]{1,0:T(8,128)(2,1)S(1)} custom-call(f32[1984,128]{1,0:T(8,128)S(1)} %fusion.5.live, f32[1984,256]{1,0:T(8,128)S(1)} %get-tuple-element.142.z, f32[2,3,256]{2,1,0:T(4,128)S(1)} %pair.1.got.counts, f32[1,256]{1,0:T(1,128)S(1)} %bitcast.39, f32[1,256]{1,0:T(1,128)S(1)} %bitcast.46, f32[1984,256]{1,0:T(8,128)S(1)} %get-tuple-element.200.d_grouped), custom_call_target="tpu_custom_call" | custom-call | flops 520093696 | bytes 5234688 | tf_op jit(solution)/shard_map/group_grad/pallas_call | solution.py:526
  214.3 5.0 %collective-permute-done.34.refs_1_ = bf16[32,2048]{1,0:T(8,128)(2,1)S(1)} collective-permute-done((bf16[32,2048]{1,0:T(8,128)(2,1)S(1)}, bf16[32,2048]{1,0:T(8,128)(2,1)S(1)}, u32[]{:S(2)}, u32[]{:S(2)}) %collective-permute-start.34) | collective-permute-done | bytes 131104 | tf_op jit(solution)/shard_map/ppermute | solution.py:545
  219.9 2.4 collective-permute-start.42
  226.5 4.0 %collective-permute-done.42.other_b = bf16[64,2048]{1,0:T(8,128)(2,1)S(1)} collective-permute-done((bf16[64,2048]{1,0:T(8,128)(2,1)S(1)}, bf16[64,2048]{1,0:T(8,128)(2,1)S(1)}, u32[]{:S(2)}, u32[]{:S(2)}) %collective-permute-start.42) | collective-permute-done | bytes 262176 | tf_op jit(solution)/shard_map/ppermute | solution.py:545
  241.3 2.8 %input_far.1 = f32[1944,512]{1,0:T(8,128)} custom-call(f32[1984,512]{1,0:T(8,128)S(1)} %input_near.1.part, bf16[992,256]{1,0:T(8,128)(2,1)S(1)} %collective-permute-done.44.refs_0_, bf16[992,256]{1,0:T(8,128)(2,1)S(1)} %collective-permute-done.45.refs_1_, bf16[992,256]{1,0:T(8,128)(2,1)S(1)} %collective-permute-done.46.refs_2_, ...), custom_call_target="tpu_custom_call" | custom-call | flops 1040187392 | bytes 10600448 | tf_op jit(solution)/shard_map/input_far/pallas_call | solution.py:526
  244.1 4.7 %collective-permute-done.49.b = bf16[288,256]{1,0:T(8,128)(2,1)S(1)} collective-permute-done((bf16[288,256]{1,0:T(8,128)(2,1)S(1)}, bf16[288,256]{1,0:T(8,128)(2,1)S(1)}, u32[]{:S(2)}, u32[]{:S(2)}) %collective-permute-start.49) | collective-permute-done | bytes 147488 | tf_op jit(solution)/shard_map/ppermute | solution.py:545
  (156 shorter events, 81.5 us)
Async XLA Ops:
  3.4 15.6 %collective-permute-start = (bf16[1984,512]{1,0:T(8,128)(2,1)S(1)}, bf16[1984,512]{1,0:T(8,128)(2,1)}, u32[]{:S(2)}, u32[]{:S(2)}) collective-permute-start(bf16[1984,512]{1,0:T(8,128)(2,1)S(1)} %pad.4.own.refs_0_.feats), channel_id=1, source_target_pairs={{0,1},{1,0},{2,3},{3,2},{4,5},{5,4},{6,7},{7,6},{8,9},{9,8},{10,11... | collective-permute-start | bytes 6094856 | tf_op jit(solution)/shard_map/ppermute | solution.py:545
  3.9 15.1 %collective-permute-start.1 = (bf16[1024,256]{1,0:T(8,128)(2,1)S(1)}, bf16[1024,256]{1,0:T(8,128)(2,1)S(1)}, u32[]{:S(2)}, u32[]{:S(2)}) collective-permute-start(bf16[1024,256]{1,0:T(8,128)(2,1)S(1)} %constant_dynamic-slice_fusion), channel_id=1, source_target_pairs={{0,2},{1,3},{2,0},{3,1},{4,6},{5,7},{6,4},{7,5},{8,10},{9,11},{10,... | collective-permute-start | bytes 1572872 | tf_op jit(solution)/shard_map/ppermute | solution.py:545
  21.7 24.3 %collective-permute-start.2 = (bf16[1984,256]{1,0:T(8,128)(2,1)S(1)}, bf16[1984,256]{1,0:T(8,128)(2,1)S(1)}, u32[]{:S(2)}, u32[]{:S(2)}) collective-permute-start(bf16[1984,256]{1,0:T(8,128)(2,1)S(1)} %part_far.1), channel_id=1, source_target_pairs={{0,2},{1,3},{2,0},{3,1},{4,6},{5,7},{6,4},{7,5},{8,10},{9,11},{10,... | collective-permute-start | bytes 3047432 | tf_op jit(solution)/shard_map/ppermute | solution.py:545
  27.8 7.9 %collective-permute-start.5 = (bf16[512,256]{1,0:T(8,128)(2,1)S(1)}, bf16[512,256]{1,0:T(8,128)(2,1)S(1)}, u32[]{:S(2)}, u32[]{:S(2)}) collective-permute-start(bf16[512,256]{1,0:T(8,128)(2,1)S(1)} %get-tuple-element.137), channel_id=1, source_target_pairs={{0,1},{1,0},{2,3},{3,2},{4,5},{5,4},{6,7},{7,6},{8,9},{9,8},{10,11... | collective-permute-start | bytes 786440 | tf_op jit(solution)/shard_map/ppermute | solution.py:545
  46.0 17.6 %collective-permute-start.10 = (bf16[256,512]{1,0:T(8,128)(2,1)S(1)}, bf16[256,512]{1,0:T(8,128)(2,1)S(1)}, u32[]{:S(2)}, u32[]{:S(2)}) collective-permute-start(bf16[256,512]{1,0:T(8,128)(2,1)S(1)} %get-tuple-element.146), channel_id=1, source_target_pairs={{0,2},{1,3},{2,0},{3,1},{4,6},{5,7},{6,4},{7,5},{8,10},{9,11},{10,... | collective-permute-start | bytes 786440 | tf_op jit(solution)/shard_map/ppermute | solution.py:545
  47.6 16.0 %collective-permute-start.11 = (bf16[256,512]{1,0:T(8,128)(2,1)S(1)}, bf16[256,512]{1,0:T(8,128)(2,1)S(1)}, u32[]{:S(2)}, u32[]{:S(2)}) collective-permute-start(bf16[256,512]{1,0:T(8,128)(2,1)S(1)} %get-tuple-element.147), channel_id=1, source_target_pairs={{0,3},{1,2},{2,1},{3,0},{4,7},{5,6},{6,5},{7,4},{8,11},{9,10},{10,... | collective-permute-start | bytes 786440 | tf_op jit(solution)/shard_map/ppermute | solution.py:545
  75.8 24.9 %collective-permute-start.13 = (bf16[1984,256]{1,0:T(8,128)(2,1)S(1)}, bf16[1984,256]{1,0:T(8,128)(2,1)S(1)}, u32[]{:S(2)}, u32[]{:S(2)}) collective-permute-start(bf16[1984,256]{1,0:T(8,128)(2,1)S(1)} %hidden.1.refs_0_), channel_id=1, source_target_pairs={{0,2},{1,3},{2,0},{3,1},{4,6},{5,7},{6,4},{7,5},{8,10},{9,11},{10,... | collective-permute-start | bytes 3047432 | tf_op jit(solution)/shard_map/ppermute | solution.py:545
  100.6 31.5 %collective-permute-start.15 = (bf16[1296,512]{1,0:T(8,128)(2,1)S(1)}, bf16[1296,512]{1,0:T(8,128)(2,1)S(1)}, u32[]{:S(2)}, u32[]{:S(2)}) collective-permute-start(bf16[1296,512]{1,0:T(8,128)(2,1)S(1)} %slice.36), channel_id=1, source_target_pairs={{0,2},{1,3},{2,0},{3,1},{4,6},{5,7},{6,4},{7,5},{8,10},{9,11},{10,... | collective-permute-start | bytes 3981320 | tf_op jit(solution)/shard_map/ppermute | solution.py:545
  134.6 24.2 %collective-permute-start.19 = (bf16[1984,256]{1,0:T(8,128)(2,1)S(1)}, bf16[1984,256]{1,0:T(8,128)(2,1)S(1)}, u32[]{:S(2)}, u32[]{:S(2)}) collective-permute-start(bf16[1984,256]{1,0:T(8,128)(2,1)S(1)} %merge.1), channel_id=1, source_target_pairs={{0,2},{1,3},{2,0},{3,1},{4,6},{5,7},{6,4},{7,5},{8,10},{9,11},{10,... | collective-permute-start | bytes 3047432 | tf_op jit(solution)/shard_map/ppermute | solution.py:545
  135.2 24.7 %collective-permute-start.17 = (bf16[1296,512]{1,0:T(8,128)(2,1)S(1)}, bf16[1296,512]{1,0:T(8,128)(2,1)S(1)}, u32[]{:S(2)}, u32[]{:S(2)}) collective-permute-start(bf16[1296,512]{1,0:T(8,128)(2,1)S(1)} %collective-permute-done.15.refs_2_), channel_id=1, source_target_pairs={{0,1},{1,0},{2,3},{3,2},{4,5},{5,4},{6,7},{7,6},{8,9},{9,8},{10,11... | collective-permute-start | bytes 3981320 | tf_op jit(solution)/shard_map/ppermute | solution.py:545
  135.2 24.7 %collective-permute-start.18 = (bf16[1984,256]{1,0:T(8,128)(2,1)S(1)}, bf16[1984,256]{1,0:T(8,128)(2,1)S(1)}, u32[]{:S(2)}, u32[]{:S(2)}) collective-permute-start(bf16[1984,256]{1,0:T(8,128)(2,1)S(1)} %get-tuple-element.160), channel_id=1, source_target_pairs={{0,1},{1,0},{2,3},{3,2},{4,5},{5,4},{6,7},{7,6},{8,9},{9,8},{10,11... | collective-permute-start | bytes 3047432 | tf_op jit(solution)/shard_map/ppermute | solution.py:545
  138.7 8.3 %collective-permute-start.21 = (bf16[4,64,512]{2,1,0:T(8,128)(2,1)S(1)}, bf16[4,64,512]{2,1,0:T(8,128)(2,1)S(1)}, u32[]{:S(2)}, u32[]{:S(2)}) collective-permute-start(bf16[4,64,512]{2,1,0:T(8,128)(2,1)S(1)} %get-tuple-element.173), channel_id=1, source_target_pairs={{0,8},{4,12},{8,0},{12,4},{16,24},{20,28},{24,16},{28,20},{1,9},{5... | collective-permute-start | bytes 786440 | tf_op jit(solution)/shard_map/ppermute | solution.py:545
  139.2 7.9 %collective-permute-start.20 = (bf16[4,64,512]{2,1,0:T(8,128)(2,1)S(1)}, bf16[4,64,512]{2,1,0:T(8,128)(2,1)S(1)}, u32[]{:S(2)}, u32[]{:S(2)}) collective-permute-start(bf16[4,64,512]{2,1,0:T(8,128)(2,1)S(1)} %get-tuple-element.163), channel_id=1, source_target_pairs={{0,4},{4,0},{8,12},{12,8},{16,20},{20,16},{24,28},{28,24},{1,5},{5... | collective-permute-start | bytes 786440 | tf_op jit(solution)/shard_map/ppermute | solution.py:545
  158.8 17.7 %collective-permute-start.25 = (bf16[688,512]{1,0:T(8,128)(2,1)S(1)}, bf16[688,512]{1,0:T(8,128)(2,1)S(1)}, u32[]{:S(2)}, u32[]{:S(2)}) collective-permute-start(bf16[688,512]{1,0:T(8,128)(2,1)S(1)} %slice.37), channel_id=1, source_target_pairs={{0,2},{1,3},{2,0},{3,1},{4,6},{5,7},{6,4},{7,5},{8,10},{9,11},{10,... | collective-permute-start | bytes 2113544 | tf_op jit(solution)/shard_map/ppermute | solution.py:545
  159.4 17.0 %collective-permute-start.24 = (bf16[4,64,512]{2,1,0:T(8,128)(2,1)S(1)}, bf16[4,64,512]{2,1,0:T(8,128)(2,1)S(1)}, u32[]{:S(2)}, u32[]{:S(2)}) collective-permute-start(bf16[4,64,512]{2,1,0:T(8,128)(2,1)S(1)} %send_both.8.a), channel_id=1, source_target_pairs={{0,16},{4,20},{8,24},{12,28},{16,0},{20,4},{24,8},{28,12},{1,17},{... | collective-permute-start | bytes 786440 | tf_op jit(solution)/shard_map/ppermute | solution.py:545
  193.1 8.4 %collective-permute-start.32 = (bf16[512,256]{1,0:T(8,128)(2,1)S(1)}, bf16[512,256]{1,0:T(8,128)(2,1)S(1)}, u32[]{:S(2)}, u32[]{:S(2)}) collective-permute-start(bf16[512,256]{1,0:T(8,128)(2,1)S(1)} %get-tuple-element.197), channel_id=1, source_target_pairs={{0,8},{4,12},{8,0},{12,4},{16,24},{20,28},{24,16},{28,20},{1,9},{5... | collective-permute-start | bytes 786440 | tf_op jit(solution)/shard_map/ppermute | solution.py:545
  193.6 8.0 %collective-permute-start.28 = (bf16[512,256]{1,0:T(8,128)(2,1)S(1)}, bf16[512,256]{1,0:T(8,128)(2,1)S(1)}, u32[]{:S(2)}, u32[]{:S(2)}) collective-permute-start(bf16[512,256]{1,0:T(8,128)(2,1)S(1)} %get-tuple-element.190), channel_id=1, source_target_pairs={{0,4},{4,0},{8,12},{12,8},{16,20},{20,16},{24,28},{28,24},{1,5},{5... | collective-permute-start | bytes 786440 | tf_op jit(solution)/shard_map/ppermute | solution.py:545
  202.2 9.0 %collective-permute-start.36 = (bf16[256,256]{1,0:T(8,128)(2,1)S(1)}, bf16[256,256]{1,0:T(8,128)(2,1)S(1)}, u32[]{:S(2)}, u32[]{:S(2)}) collective-permute-start(bf16[256,256]{1,0:T(8,128)(2,1)S(1)} %get-tuple-element.203), channel_id=1, source_target_pairs={{0,4},{4,0},{8,12},{12,8},{16,20},{20,16},{24,28},{28,24},{1,5},{5... | collective-permute-start | bytes 393224 | tf_op jit(solution)/shard_map/ppermute | solution.py:545
  203.0 8.2 %collective-permute-start.35 = (bf16[256,256]{1,0:T(8,128)(2,1)S(1)}, bf16[256,256]{1,0:T(8,128)(2,1)S(1)}, u32[]{:S(2)}, u32[]{:S(2)}) collective-permute-start(bf16[256,256]{1,0:T(8,128)(2,1)S(1)} %get-tuple-element.199), channel_id=1, source_target_pairs={{0,8},{4,12},{8,0},{12,4},{16,24},{20,28},{24,16},{28,20},{1,9},{5... | collective-permute-start | bytes 393224 | tf_op jit(solution)/shard_map/ppermute | solution.py:545
  204.4 21.5 %collective-permute-start.44 = (bf16[992,256]{1,0:T(8,128)(2,1)S(1)}, bf16[992,256]{1,0:T(8,128)(2,1)S(1)}, u32[]{:S(2)}, u32[]{:S(2)}) collective-permute-start(bf16[992,256]{1,0:T(8,128)(2,1)S(1)} %slice.40), channel_id=1, source_target_pairs={{0,2},{1,3},{2,0},{3,1},{4,6},{5,7},{6,4},{7,5},{8,10},{9,11},{10,... | collective-permute-start | bytes 1523720 | tf_op jit(solution)/shard_map/ppermute | solution.py:545
  206.0 7.7 %collective-permute-start.37 = (bf16[32,2048]{1,0:T(8,128)(2,1)S(1)}, bf16[32,2048]{1,0:T(8,128)(2,1)S(1)}, u32[]{:S(2)}, u32[]{:S(2)}) collective-permute-start(bf16[32,2048]{1,0:T(8,128)(2,1)S(1)} %get-tuple-element.206.refs_0_), channel_id=1, source_target_pairs={{0,4},{4,0},{8,12},{12,8},{16,20},{20,16},{24,28},{28,24},{1,5},{5... | collective-permute-start | bytes 393224 | tf_op jit(solution)/shard_map/ppermute | solution.py:545
  211.9 13.8 %collective-permute-start.38 = (bf16[512,256]{1,0:T(8,128)(2,1)S(1)}, bf16[512,256]{1,0:T(8,128)(2,1)S(1)}, u32[]{:S(2)}, u32[]{:S(2)}) collective-permute-start(bf16[512,256]{1,0:T(8,128)(2,1)S(1)} %send_both.11.a), channel_id=1, source_target_pairs={{0,16},{4,20},{8,24},{12,28},{16,0},{20,4},{24,8},{28,12},{1,17},{... | collective-permute-start | bytes 786440 | tf_op jit(solution)/shard_map/ppermute | solution.py:545
  212.5 9.7 %collective-permute-start.33 = (bf16[288,256]{1,0:T(8,128)(2,1)S(1)}, bf16[288,256]{1,0:T(8,128)(2,1)S(1)}, u32[]{:S(2)}, u32[]{:S(2)}) collective-permute-start(bf16[288,256]{1,0:T(8,128)(2,1)S(1)} %group_grad.1.a), channel_id=1, source_target_pairs={{0,4},{4,0},{8,12},{12,8},{16,20},{20,16},{24,28},{28,24},{1,5},{5... | collective-permute-start | bytes 442376 | tf_op jit(solution)/shard_map/ppermute | solution.py:545
  213.7 22.7 %collective-permute-start.45 = (bf16[992,256]{1,0:T(8,128)(2,1)S(1)}, bf16[992,256]{1,0:T(8,128)(2,1)S(1)}, u32[]{:S(2)}, u32[]{:S(2)}) collective-permute-start(bf16[992,256]{1,0:T(8,128)(2,1)S(1)} %slice.41), channel_id=1, source_target_pairs={{0,2},{1,3},{2,0},{3,1},{4,6},{5,7},{6,4},{7,5},{8,10},{9,11},{10,... | collective-permute-start | bytes 1523720 | tf_op jit(solution)/shard_map/ppermute | solution.py:545
  219.9 10.6 %collective-permute-start.42 = (bf16[64,2048]{1,0:T(8,128)(2,1)S(1)}, bf16[64,2048]{1,0:T(8,128)(2,1)S(1)}, u32[]{:S(2)}, u32[]{:S(2)}) collective-permute-start(bf16[64,2048]{1,0:T(8,128)(2,1)S(1)} %get-tuple-element.216.b), channel_id=1, source_target_pairs={{0,8},{4,12},{8,0},{12,4},{16,24},{20,28},{24,16},{28,20},{1,9},{5... | collective-permute-start | bytes 786440 | tf_op jit(solution)/shard_map/ppermute | solution.py:545
  222.2 8.2 %collective-permute-start.41 = (bf16[64,2048]{1,0:T(8,128)(2,1)S(1)}, bf16[64,2048]{1,0:T(8,128)(2,1)S(1)}, u32[]{:S(2)}, u32[]{:S(2)}) collective-permute-start(bf16[64,2048]{1,0:T(8,128)(2,1)S(1)} %get-tuple-element.214.a), channel_id=1, source_target_pairs={{0,4},{4,0},{8,12},{12,8},{16,20},{20,16},{24,28},{28,24},{1,5},{5... | collective-permute-start | bytes 786440 | tf_op jit(solution)/shard_map/ppermute | solution.py:545
  225.7 7.9 %collective-permute-start.40 = (bf16[288,256]{1,0:T(8,128)(2,1)S(1)}, bf16[288,256]{1,0:T(8,128)(2,1)S(1)}, u32[]{:S(2)}, u32[]{:S(2)}) collective-permute-start(bf16[288,256]{1,0:T(8,128)(2,1)S(1)} %add.35.a), channel_id=1, source_target_pairs={{0,8},{4,12},{8,0},{12,4},{16,24},{20,28},{24,16},{28,20},{1,9},{5... | collective-permute-start | bytes 442376 | tf_op jit(solution)/shard_map/ppermute | solution.py:545
  225.9 7.7 %collective-permute-start.43 = (bf16[256,256]{1,0:T(8,128)(2,1)S(1)}, bf16[256,256]{1,0:T(8,128)(2,1)S(1)}, u32[]{:S(2)}, u32[]{:S(2)}) collective-permute-start(bf16[256,256]{1,0:T(8,128)(2,1)S(1)} %get-tuple-element.235), channel_id=1, source_target_pairs={{0,4},{4,0},{8,12},{12,8},{16,20},{20,16},{24,28},{28,24},{1,5},{5... | collective-permute-start | bytes 393224 | tf_op jit(solution)/shard_map/ppermute | solution.py:545
  230.5 10.8 %collective-permute-start.46 = (bf16[992,256]{1,0:T(8,128)(2,1)S(1)}, bf16[992,256]{1,0:T(8,128)(2,1)S(1)}, u32[]{:S(2)}, u32[]{:S(2)}) collective-permute-start(bf16[992,256]{1,0:T(8,128)(2,1)S(1)} %collective-permute-done.44.refs_0_), channel_id=1, source_target_pairs={{0,1},{1,0},{2,3},{3,2},{4,5},{5,4},{6,7},{7,6},{8,9},{9,8},{10,11... | collective-permute-start | bytes 1523720 | tf_op jit(solution)/shard_map/ppermute | solution.py:545
  237.7 13.4 %collective-permute-start.48 = (bf16[512,256]{1,0:T(8,128)(2,1)S(1)}, bf16[512,256]{1,0:T(8,128)(2,1)S(1)}, u32[]{:S(2)}, u32[]{:S(2)}) collective-permute-start(bf16[512,256]{1,0:T(8,128)(2,1)S(1)} %get-tuple-element.221.a), channel_id=1, source_target_pairs={{0,4},{4,0},{8,12},{12,8},{16,20},{20,16},{24,28},{28,24},{1,5},{5... | collective-permute-start | bytes 786440 | tf_op jit(solution)/shard_map/ppermute | solution.py:545
  239.5 9.3 %collective-permute-start.49 = (bf16[288,256]{1,0:T(8,128)(2,1)S(1)}, bf16[288,256]{1,0:T(8,128)(2,1)S(1)}, u32[]{:S(2)}, u32[]{:S(2)}) collective-permute-start(bf16[288,256]{1,0:T(8,128)(2,1)S(1)} %add.37.a), channel_id=1, source_target_pairs={{0,16},{4,20},{8,24},{12,28},{16,0},{20,4},{24,8},{28,12},{1,17},{... | collective-permute-start | bytes 442376 | tf_op jit(solution)/shard_map/ppermute | solution.py:545
  239.5 11.6 %collective-permute-start.50 = (bf16[512,256]{1,0:T(8,128)(2,1)S(1)}, bf16[512,256]{1,0:T(8,128)(2,1)S(1)}, u32[]{:S(2)}, u32[]{:S(2)}) collective-permute-start(bf16[512,256]{1,0:T(8,128)(2,1)S(1)} %get-tuple-element.227.b), channel_id=1, source_target_pairs={{0,8},{4,12},{8,0},{12,4},{16,24},{20,28},{24,16},{28,20},{1,9},{5... | collective-permute-start | bytes 786440 | tf_op jit(solution)/shard_map/ppermute | solution.py:545
  (29 other events, 175.1 us)

commit v7 on v6

--- a/solution.py
+++ b/solution.py
@@ -853,14 +853,6 @@
             far_rows(0, *cols)
             ties = cols
         elif s == 1:
-            group_part = call(
-                functools.partial(group_grad_kernel, side, slots, group_width),
-                [shape((9 * group_width, width), BF16)],
-                [live, z, got_one, gain_one, shift_one, after(d_grouped, send[0])],
-                [tall], flops=mm, name="group_grad",
-            )
-            group_other = swap(group_part, "batch", n_batch, 1)
-            ties = [group_part]
             others_cols = [
                 swap(after(cols[h], send[0]), "batch", n_batch, 1 << orders[h][top - 1])
                 for h in halves
@@ -874,7 +866,13 @@
     for t in reversed(range(1, top - 1)):
         others_cols = [swap(cols[h], "batch", n_batch, 1 << orders[h][t]) for h in halves]
         cols = double_pair(dims, cols, others_cols, [o[t] for o in orders])
-    group_part = add(group_part, after(group_other, *cols))
+    group_part = call(
+        functools.partial(group_grad_kernel, side, slots, group_width),
+        [shape((9 * group_width, width), BF16)],
+        [live, z, got_one, gain_one, shift_one, after(d_grouped, *cols)],
+        [tall], flops=mm, name="group_grad",
+    )
+    group_other = swap(group_part, "batch", n_batch, 1)
     others_cols = [
         swap(after(cols[h], sums), "batch", n_batch, 1 << orders[h][0]) for h in halves
     ]
@@ -885,6 +883,7 @@
         name="input_near", steps=STEPS,
     )
     sums = add(sums, after(other, part))
+    group_part = add(group_part, after(group_other, sums))
     others_cols = [after(v, sums) for v in others_cols]
     moved = [after(v, sums) for v in moved]
     expand_grad = finish(dims, cols, others_cols, [o[0] for o in orders])

time: 254 us -> 251 us (0.988)
  waiting for transfers between devices: 83.8 us -> 78.8 us
    ppermute x51, waiting for transfers between devices: 83.8 us -> 78.8 us  [swap(): return lax.ppermute(v, axis, [(i, i ^ k) for i in range(size)])]
  transfers between devices with their start and end apart: 51 -> 51, of which waited for: 23 -> 26; matrix products, arithmetic and copies ran while one was open for 2% -> 2% of each run, Pallas kernels for 23% -> 23%
where the time goes in v7:
time: 251 us; the launch traced here: 250 us
  waiting for transfers between devices  78.8 us (31%)
  Pallas kernels  67.6 us (27%)
  blocking collectives  49.6 us (20%)
  starting transfers between devices  40.9 us (16%)
  local copies, waits for them, and re-layouts  8.1 us (3%)
  other arithmetic  2.58 us (1%)
  between operations  2.57 us (1%)
    ppermute x51, waiting for transfers between devices, swap(): return lax.ppermute(v, axis, [(i, i ^ k) for i in range(size)])  78.8 us
    pallas_call x44, Pallas kernels, call(): pl.pallas_call(kernel, out_shape=list(outs), grid=(steps,) if steps else...  67.6 us
    all_to_all x5, blocking collectives, batch_sum(): return lax.all_to_all(spread, 'batch', 0, 0)  49.6 us
    ppermute x51, starting transfers between devices, swap(): return lax.ppermute(v, axis, [(i, i ^ k) for i in range(size)])  40.9 us
  transfers between devices with their start and end apart: 51, of which 26 were waited for; matrix products, arithmetic and copies ran while one was open for 2% of the time, Pallas kernels for 23%

profile of v7, /device:TPU:0, one launch (start us, length us, event | category | flops | bytes accessed | tf_op | source)
XLA Modules:
  0.0 250.1 jit_solution(1719023961373523576)
XLA Ops:
  3.9 2.6 %collective-permute-start.1 = (bf16[1024,256]{1,0:T(8,128)(2,1)S(1)}, bf16[1024,256]{1,0:T(8,128)(2,1)S(1)}, u32[]{:S(2)}, u32[]{:S(2)}) collective-permute-start(bf16[1024,256]{1,0:T(8,128)(2,1)S(1)} %constant_dynamic-slice_fusion), channel_id=1, source_target_pairs={{0,2},{1,3},{2,0},{3,1},{4,6},{5,7},{6,4},{7,5},{8,10},{9,11},{10,... | collective-permute-start | bytes 1572872 | tf_op jit(solution)/shard_map/ppermute | solution.py:545
  7.9 11.1 %collective-permute-done.1.refs_0_ = bf16[1024,256]{1,0:T(8,128)(2,1)S(1)} collective-permute-done((bf16[1024,256]{1,0:T(8,128)(2,1)S(1)}, bf16[1024,256]{1,0:T(8,128)(2,1)S(1)}, u32[]{:S(2)}, u32[]{:S(2)}) %collective-permute-start.1) | collective-permute-done | bytes 524320 | tf_op jit(solution)/shard_map/ppermute | solution.py:545
  19.1 2.7 %part_far.1 = bf16[1984,256]{1,0:T(8,128)(2,1)S(1)} custom-call(s32[5]{0:T(128)S(1)} %stack.11.dims, bf16[1984,512]{1,0:T(8,128)(2,1)S(1)} %pad.4.own.refs_0_.feats, bf16[1984,512]{1,0:T(8,128)(2,1)} %collective-permute-done.beside.refs_1_, bf16[1024,256]{1,0:T(8,128)(2,1)S(1)} %collective-permute-done.1.refs_0_), custom_call_target="tpu_custom_call" | custom-call | flops 1040187392 | bytes 5603348 | tf_op jit(solution)/shard_map/part_far/pallas_call | solution.py:526
  24.2 3.6 %near.1.part = f32[1984,256]{1,0:T(8,128)S(1)} custom-call(s32[5]{0:T(128)S(1)} %stack.11.dims, bf16[1984,512]{1,0:T(8,128)(2,1)S(1)} %pad.4.own.refs_0_.feats, bf16[1984,512]{1,0:T(8,128)(2,1)} %collective-permute-done.beside.refs_1_, bf16[2048,256]{1,0:T(8,128)(2,1)S(1)} %copy-done.1), custom_call_target="tpu_custom_call" | custom-call | flops 1040187392 | bytes 7143444 | tf_op jit(solution)/shard_map/near/pallas_call | solution.py:526
  27.9 3.3 %copy-done = bf16[24,9,9,2048]{3,0,2,1:T(8,128)(2,1)S(1)} copy-done((bf16[24,9,9,2048]{3,0,2,1:T(8,128)(2,1)S(1)}, bf16[24,9,9,2048]{3,0,2,1:T(8,128)(2,1)}, u32[]{:S(2)}) %copy-start) | copy-done | bytes 7962648
  33.0 2.5 %fusion.5.live = f32[1984,128]{1,0:T(8,128)S(1)} fusion(s32[1984]{0:T(1024)S(1)} %get-tuple-element.240, s32[1984]{0:T(1024)S(1)} %get-tuple-element.245, s32[]{:T(128)} %bitcast.30, s32[1984]{0:T(1024)S(1)} %get-tuple-element.239, s32[1984]{0:T(1024)S(1)} %get-tuple-element.246, s32[]{:T(128)} %bitcast.31, s32[1984]{0:T(1024)S(1)} %get-tuple-element.243, ...), kind=kLoop, calls=%fused_computation.9 | loop fusion | flops 3809280 | bytes 1069384 | tf_op jit(solution)/shard_map/convert_element_type | solution.py:641
  35.8 10.2 %collective-permute-done.2.refs_0_ = bf16[1984,256]{1,0:T(8,128)(2,1)S(1)} collective-permute-done((bf16[1984,256]{1,0:T(8,128)(2,1)S(1)}, bf16[1984,256]{1,0:T(8,128)(2,1)S(1)}, u32[]{:S(2)}, u32[]{:S(2)}) %collective-permute-start.2) | collective-permute-done | bytes 1015840 | tf_op jit(solution)/shard_map/ppermute | solution.py:545
  48.1 3.7 %collective-permute-start.8 = (f32[1,3,256]{2,1,0:T(4,128)S(1)}, f32[1,3,256]{2,1,0:T(4,128)S(1)}, u32[]{:S(2)}, u32[]{:S(2)}) collective-permute-start(f32[1,3,256]{2,1,0:T(4,128)S(1)} %get-tuple-element.141.refs_0_), channel_id=1, source_target_pairs={{0,24},{4,28},{8,16},{12,20},{16,8},{20,12},{24,0},{28,4},{1,25},{... | collective-permute-start | bytes 9224 | tf_op jit(solution)/shard_map/ppermute | solution.py:545
  53.6 2.7 %collective-permute-done.7.refs_2_ = f32[1,3,256]{2,1,0:T(4,128)S(1)} collective-permute-done((f32[1,3,256]{2,1,0:T(4,128)S(1)}, f32[1,3,256]{2,1,0:T(4,128)S(1)}, u32[]{:S(2)}, u32[]{:S(2)}) %collective-permute-start.7) | collective-permute-done | bytes 3104 | tf_op jit(solution)/shard_map/ppermute | solution.py:545
  60.0 3.5 %conv.1 = (f32[1984,256]{1,0:T(8,128)S(1)}, f32[8,2,256]{2,1,0:T(2,128)S(1)}) custom-call(f32[1984,128]{1,0:T(8,128)S(1)} %fusion.5.live, f32[1984,256]{1,0:T(8,128)S(1)} %get-tuple-element.140.z, f32[2,3,256]{2,1,0:T(4,128)S(1)} %pair.1.got.counts, f32[1,256]{1,0:T(1,128)S(1)} %bitcast.36, f32[1,256]{1,0:T(1,128)S(1)} %bitcast.44, bf16[9,256,256]{2,1,0:T(8,128)(2,1)S(1)} %taps.1), custom_call_target="tpu_custom_call" | custom-call | flops 2340421632 | bytes 6283264 | tf_op jit(solution)/shard_map/conv/pallas_call | solution.py:526
  63.6 10.5 %all_to_all.25.got.got_two = f32[8,2,256]{2,1,0:T(2,128)S(1)} all-to-all(f32[8,2,256]{2,1,0:T(2,128)S(1)} %get-tuple-element.146), channel_id=1, replica_groups=mesh['batch'=8,'chan'=4] {'batch'}, dimensions={0} | all-to-all | bytes 32768 | tf_op jit(solution)/shard_map/all_to_all | solution.py:549
  76.3 2.5 %slope_one.1.slope = f32[1984,256]{1,0:T(8,128)S(1)} custom-call(f32[1984,128]{1,0:T(8,128)S(1)} %fusion.5.live, f32[1984,256]{1,0:T(8,128)S(1)} %get-tuple-element.140.z, f32[2,3,256]{2,1,0:T(4,128)S(1)} %pair.1.got.counts, f32[2,3,256]{2,1,0:T(4,128)S(1)} %pair.1.got.counts, f32[1,256]{1,0:T(1,128)S(1)} %bitcast.37, f32[1,256]{1,0:T(1,128)S(1)} %bitcast.45), custom_call_target="tpu_custom_call" | custom-call | flops 520093696 | bytes 5093376 | tf_op jit(solution)/shard_map/slope_one/pallas_call | solution.py:526
  79.0 2.5 %slope_two.1.slope = f32[1984,256]{1,0:T(8,128)S(1)} custom-call(f32[1984,128]{1,0:T(8,128)S(1)} %fusion.5.live, f32[1984,256]{1,0:T(8,128)S(1)} %get-tuple-element.142.z.grouped, f32[2,3,256]{2,1,0:T(4,128)S(1)} %pair.1.got.counts, f32[8,2,256]{2,1,0:T(2,128)S(1)} %all_to_all.25.got.got_two, f32[1,256]{1,0:T(1,128)S(1)} %bitcast.34, f32[1,256]{1,0:T(1,128)S(1)} %bitcast.43), custom_call_target="tpu_custom_call" | custom-call | flops 520093696 | bytes 5103616 | tf_op jit(solution)/shard_map/slope_two/pallas_call | solution.py:526
  82.9 17.7 %collective-permute-done.13.refs_0_.refs_2_ = bf16[1984,256]{1,0:T(8,128)(2,1)S(1)} collective-permute-done((bf16[1984,256]{1,0:T(8,128)(2,1)S(1)}, bf16[1984,256]{1,0:T(8,128)(2,1)S(1)}, u32[]{:S(2)}, u32[]{:S(2)}) %collective-permute-start.13) | collective-permute-done | bytes 1015840 | tf_op jit(solution)/shard_map/ppermute | solution.py:545
  105.2 9.1 %all_to_all.26.got = f32[8,2,512]{2,1,0:T(2,128)S(1)} all-to-all(f32[8,2,512]{2,1,0:T(2,128)S(1)} %get-tuple-element.150), channel_id=1, replica_groups=mesh['batch'=8,'chan'=4] {'batch'}, dimensions={0} | all-to-all | bytes 65536 | tf_op jit(solution)/shard_map/all_to_all | solution.py:549
  114.3 3.9 %third.1 = (f32[1984,512]{1,0:T(8,128)S(1)}, f32[8,2,512]{2,1,0:T(2,128)S(1)}) custom-call(f32[1984,128]{1,0:T(8,128)S(1)} %fusion.5.live, f32[1984,512]{1,0:T(8,128)S(1)} %get-tuple-element.162.e, f32[2,3,256]{2,1,0:T(4,128)S(1)} %pair.1.got.counts, f32[8,2,512]{2,1,0:T(2,128)S(1)} %all_to_all.26.got, f32[1,512]{1,0:T(1,128)S(1)} %get-tuple-element.125.gain, ...), custom_call_target="tpu_custom_call" | custom-call | flops 2080374784 | bytes 13281280 | tf_op jit(solution)/shard_map/third/pallas_call | solution.py:526
  118.2 9.1 %all_to_all.27.totals = f32[8,2,512]{2,1,0:T(2,128)S(1)} all-to-all(f32[8,2,512]{2,1,0:T(2,128)S(1)} %get-tuple-element.152), channel_id=1, replica_groups=mesh['batch'=8,'chan'=4] {'batch'}, dimensions={0} | all-to-all | bytes 65536 | tf_op jit(solution)/shard_map/all_to_all | solution.py:549
  129.3 2.9 %collective-permute-done.15.refs_2_ = bf16[1296,512]{1,0:T(8,128)(2,1)S(1)} collective-permute-done((bf16[1296,512]{1,0:T(8,128)(2,1)S(1)}, bf16[1296,512]{1,0:T(8,128)(2,1)S(1)}, u32[]{:S(2)}, u32[]{:S(2)}) %collective-permute-start.15) | collective-permute-done | bytes 1327136 | tf_op jit(solution)/shard_map/ppermute | solution.py:545
  135.7 2.4 expand_grad.1.whole
  139.9 5.1 %block.1 = bf16[1944,512]{1,0:T(8,128)(2,1)} custom-call(f32[1984,128]{1,0:T(8,128)S(1)} %fusion.5.live, f32[1984,512]{1,0:T(8,128)S(1)} %get-tuple-element.162.e, f32[2,3,256]{2,1,0:T(4,128)S(1)} %pair.1.got.counts, f32[8,2,512]{2,1,0:T(2,128)S(1)} %all_to_all.26.got, f32[1,512]{1,0:T(1,128)S(1)} %get-tuple-element.125.gain, ...), custom_call_target="tpu_custom_call" | custom-call | flops 1040187392 | bytes 9144320 | tf_op jit(solution)/shard_map/block/pallas_call | solution.py:526
  149.9 2.9 %collective-permute-done.22.refs_1_ = bf16[4,32,512]{2,1,0:T(8,128)(2,1)S(1)} collective-permute-done((bf16[4,32,512]{2,1,0:T(8,128)(2,1)S(1)}, bf16[4,32,512]{2,1,0:T(8,128)(2,1)S(1)}, u32[]{:S(2)}, u32[]{:S(2)}) %collective-permute-start.22) | collective-permute-done | bytes 131104 | tf_op jit(solution)/shard_map/ppermute | solution.py:545
  155.0 3.8 %collective-permute-done.19.refs_2_ = bf16[1984,256]{1,0:T(8,128)(2,1)S(1)} collective-permute-done((bf16[1984,256]{1,0:T(8,128)(2,1)S(1)}, bf16[1984,256]{1,0:T(8,128)(2,1)S(1)}, u32[]{:S(2)}, u32[]{:S(2)}) %collective-permute-start.19) | collective-permute-done | bytes 1015840 | tf_op jit(solution)/shard_map/ppermute | solution.py:545
  161.2 11.8 %all_to_all.28.totals = f32[8,2,256]{2,1,0:T(2,128)S(1)} all-to-all(f32[8,2,256]{2,1,0:T(2,128)S(1)} %get-tuple-element.167), channel_id=1, replica_groups=mesh['batch'=8,'chan'=4] {'batch'}, dimensions={0} | all-to-all | bytes 32768 | tf_op jit(solution)/shard_map/all_to_all | solution.py:549
  172.9 3.5 %conv_back.1 = (f32[1984,256]{1,0:T(8,128)S(1)}, f32[1984,256]{1,0:T(8,128)S(1)}, f32[8,2,256]{2,1,0:T(2,128)S(1)}, f32[2,256]{1,0:T(2,128)S(1)}) custom-call(f32[1984,128]{1,0:T(8,128)S(1)} %fusion.5.live, f32[1984,256]{1,0:T(8,128)S(1)} %get-tuple-element.166.d_two, f32[1984,256]{1,0:T(8,128)S(1)} %get-tuple-element.142.z.grouped, ...), custom_call_target="tpu_custom_call" | custom-call | flops 2340421632 | bytes 14443520 | tf_op jit(solution)/shard_map/conv_back/pallas_call | solution.py:526
  176.5 9.2 %all_to_all.29.totals = f32[8,2,256]{2,1,0:T(2,128)S(1)} all-to-all(f32[8,2,256]{2,1,0:T(2,128)S(1)} %get-tuple-element.182), channel_id=1, replica_groups=mesh['batch'=8,'chan'=4] {'batch'}, dimensions={0} | all-to-all | bytes 32768 | tf_op jit(solution)/shard_map/all_to_all | solution.py:549
  187.5 3.7 %reduce_grad.1 = (bf16[2048,256]{1,0:T(8,128)(2,1)S(1)}, f32[2,512,256]{2,1,0:T(8,128)S(1)}) custom-call(s32[5]{0:T(128)S(1)} %stack.11.dims, bf16[1984,256]{1,0:T(8,128)(2,1)S(1)} %get-tuple-element.221.d_red.refs_0_, bf16[1984,512]{1,0:T(8,128)(2,1)S(1)} %pad.4.own.refs_0_.feats, bf16[1984,512]{1,0:T(8,128)(2,1)} %collective-permute-done.beside.refs_1_, ...), custom_call_target="tpu_custom_call" | custom-call | flops 2080374784 | bytes 9830420 | tf_op jit(solution)/shard_map/reduce_grad/pallas_call | solution.py:526
  196.1 2.6 %collective-permute-done.29.refs_2_ = bf16[64,512]{1,0:T(8,128)(2,1)S(1)} collective-permute-done((bf16[64,512]{1,0:T(8,128)(2,1)S(1)}, bf16[64,512]{1,0:T(8,128)(2,1)S(1)}, u32[]{:S(2)}, u32[]{:S(2)}) %collective-permute-start.29) | collective-permute-done | bytes 65568 | tf_op jit(solution)/shard_map/ppermute | solution.py:545
  211.7 3.7 %group_grad.1.a = bf16[288,256]{1,0:T(8,128)(2,1)S(1)} custom-call(f32[1984,128]{1,0:T(8,128)S(1)} %fusion.5.live, f32[1984,256]{1,0:T(8,128)S(1)} %get-tuple-element.140.z, f32[2,3,256]{2,1,0:T(4,128)S(1)} %pair.1.got.counts, f32[1,256]{1,0:T(1,128)S(1)} %bitcast.39, f32[1,256]{1,0:T(1,128)S(1)} %bitcast.46, f32[1984,256]{1,0:T(8,128)S(1)} %get-tuple-element.205.d_grouped), custom_call_target="tpu_custom_call" | custom-call | flops 520093696 | bytes 5234688 | tf_op jit(solution)/shard_map/group_grad/pallas_call | solution.py:526
  215.4 2.3 collective-permute-start.39
  225.6 2.9 %collective-permute-done.42.other_b = bf16[64,2048]{1,0:T(8,128)(2,1)S(1)} collective-permute-done((bf16[64,2048]{1,0:T(8,128)(2,1)S(1)}, bf16[64,2048]{1,0:T(8,128)(2,1)S(1)}, u32[]{:S(2)}, u32[]{:S(2)}) %collective-permute-start.42) | collective-permute-done | bytes 262176 | tf_op jit(solution)/shard_map/ppermute | solution.py:545
  239.1 2.8 %input_far.1 = f32[1944,512]{1,0:T(8,128)} custom-call(f32[1984,512]{1,0:T(8,128)S(1)} %input_near.1.part, bf16[992,256]{1,0:T(8,128)(2,1)S(1)} %collective-permute-done.44.refs_0_, bf16[992,256]{1,0:T(8,128)(2,1)S(1)} %collective-permute-done.45.refs_1_, bf16[992,256]{1,0:T(8,128)(2,1)S(1)} %collective-permute-done.46.refs_2_, ...), custom_call_target="tpu_custom_call" | custom-call | flops 1040187392 | bytes 10600448 | tf_op jit(solution)/shard_map/input_far/pallas_call | solution.py:526
  241.9 4.0 %collective-permute-done.49.b = bf16[288,256]{1,0:T(8,128)(2,1)S(1)} collective-permute-done((bf16[288,256]{1,0:T(8,128)(2,1)S(1)}, bf16[288,256]{1,0:T(8,128)(2,1)S(1)}, u32[]{:S(2)}, u32[]{:S(2)}) %collective-permute-start.49) | collective-permute-done | bytes 147488 | tf_op jit(solution)/shard_map/ppermute | solution.py:545
  (156 shorter events, 82.9 us)
Async XLA Ops:
  3.4 15.6 %collective-permute-start = (bf16[1984,512]{1,0:T(8,128)(2,1)S(1)}, bf16[1984,512]{1,0:T(8,128)(2,1)}, u32[]{:S(2)}, u32[]{:S(2)}) collective-permute-start(bf16[1984,512]{1,0:T(8,128)(2,1)S(1)} %pad.4.own.refs_0_.feats), channel_id=1, source_target_pairs={{0,1},{1,0},{2,3},{3,2},{4,5},{5,4},{6,7},{7,6},{8,9},{9,8},{10,11... | collective-permute-start | bytes 6094856 | tf_op jit(solution)/shard_map/ppermute | solution.py:545
  3.9 15.1 %collective-permute-start.1 = (bf16[1024,256]{1,0:T(8,128)(2,1)S(1)}, bf16[1024,256]{1,0:T(8,128)(2,1)S(1)}, u32[]{:S(2)}, u32[]{:S(2)}) collective-permute-start(bf16[1024,256]{1,0:T(8,128)(2,1)S(1)} %constant_dynamic-slice_fusion), channel_id=1, source_target_pairs={{0,2},{1,3},{2,0},{3,1},{4,6},{5,7},{6,4},{7,5},{8,10},{9,11},{10,... | collective-permute-start | bytes 1572872 | tf_op jit(solution)/shard_map/ppermute | solution.py:545
  21.7 24.3 %collective-permute-start.2 = (bf16[1984,256]{1,0:T(8,128)(2,1)S(1)}, bf16[1984,256]{1,0:T(8,128)(2,1)S(1)}, u32[]{:S(2)}, u32[]{:S(2)}) collective-permute-start(bf16[1984,256]{1,0:T(8,128)(2,1)S(1)} %part_far.1), channel_id=1, source_target_pairs={{0,2},{1,3},{2,0},{3,1},{4,6},{5,7},{6,4},{7,5},{8,10},{9,11},{10,... | collective-permute-start | bytes 3047432 | tf_op jit(solution)/shard_map/ppermute | solution.py:545
  27.8 7.9 %collective-permute-start.5 = (bf16[512,256]{1,0:T(8,128)(2,1)S(1)}, bf16[512,256]{1,0:T(8,128)(2,1)S(1)}, u32[]{:S(2)}, u32[]{:S(2)}) collective-permute-start(bf16[512,256]{1,0:T(8,128)(2,1)S(1)} %get-tuple-element.135), channel_id=1, source_target_pairs={{0,1},{1,0},{2,3},{3,2},{4,5},{5,4},{6,7},{7,6},{8,9},{9,8},{10,11... | collective-permute-start | bytes 786440 | tf_op jit(solution)/shard_map/ppermute | solution.py:545
  46.0 17.6 %collective-permute-start.10 = (bf16[256,512]{1,0:T(8,128)(2,1)S(1)}, bf16[256,512]{1,0:T(8,128)(2,1)S(1)}, u32[]{:S(2)}, u32[]{:S(2)}) collective-permute-start(bf16[256,512]{1,0:T(8,128)(2,1)S(1)} %get-tuple-element.144), channel_id=1, source_target_pairs={{0,2},{1,3},{2,0},{3,1},{4,6},{5,7},{6,4},{7,5},{8,10},{9,11},{10,... | collective-permute-start | bytes 786440 | tf_op jit(solution)/shard_map/ppermute | solution.py:545
  47.6 16.0 %collective-permute-start.11 = (bf16[256,512]{1,0:T(8,128)(2,1)S(1)}, bf16[256,512]{1,0:T(8,128)(2,1)S(1)}, u32[]{:S(2)}, u32[]{:S(2)}) collective-permute-start(bf16[256,512]{1,0:T(8,128)(2,1)S(1)} %get-tuple-element.145), channel_id=1, source_target_pairs={{0,3},{1,2},{2,1},{3,0},{4,7},{5,6},{6,5},{7,4},{8,11},{9,10},{10,... | collective-permute-start | bytes 786440 | tf_op jit(solution)/shard_map/ppermute | solution.py:545
  75.7 5.8 %collective-permute-start.12 = (bf16[1984,256]{1,0:T(8,128)(2,1)S(1)}, bf16[1984,256]{1,0:T(8,128)(2,1)S(1)}, u32[]{:S(2)}, u32[]{:S(2)}) collective-permute-start(bf16[1984,256]{1,0:T(8,128)(2,1)S(1)} %hidden.1.refs_0_), channel_id=1, source_target_pairs={{0,1},{1,0},{2,3},{3,2},{4,5},{5,4},{6,7},{7,6},{8,9},{9,8},{10,11... | collective-permute-start | bytes 3047432 | tf_op jit(solution)/shard_map/ppermute | solution.py:545
  75.8 24.9 %collective-permute-start.13 = (bf16[1984,256]{1,0:T(8,128)(2,1)S(1)}, bf16[1984,256]{1,0:T(8,128)(2,1)S(1)}, u32[]{:S(2)}, u32[]{:S(2)}) collective-permute-start(bf16[1984,256]{1,0:T(8,128)(2,1)S(1)} %hidden.1.refs_0_), channel_id=1, source_target_pairs={{0,2},{1,3},{2,0},{3,1},{4,6},{5,7},{6,4},{7,5},{8,10},{9,11},{10,... | collective-permute-start | bytes 3047432 | tf_op jit(solution)/shard_map/ppermute | solution.py:545
  100.6 31.5 %collective-permute-start.15 = (bf16[1296,512]{1,0:T(8,128)(2,1)S(1)}, bf16[1296,512]{1,0:T(8,128)(2,1)S(1)}, u32[]{:S(2)}, u32[]{:S(2)}) collective-permute-start(bf16[1296,512]{1,0:T(8,128)(2,1)S(1)} %slice.36), channel_id=1, source_target_pairs={{0,2},{1,3},{2,0},{3,1},{4,6},{5,7},{6,4},{7,5},{8,10},{9,11},{10,... | collective-permute-start | bytes 3981320 | tf_op jit(solution)/shard_map/ppermute | solution.py:545
  134.6 24.2 %collective-permute-start.19 = (bf16[1984,256]{1,0:T(8,128)(2,1)S(1)}, bf16[1984,256]{1,0:T(8,128)(2,1)S(1)}, u32[]{:S(2)}, u32[]{:S(2)}) collective-permute-start(bf16[1984,256]{1,0:T(8,128)(2,1)S(1)} %merge.1), channel_id=1, source_target_pairs={{0,2},{1,3},{2,0},{3,1},{4,6},{5,7},{6,4},{7,5},{8,10},{9,11},{10,... | collective-permute-start | bytes 3047432 | tf_op jit(solution)/shard_map/ppermute | solution.py:545
  135.2 24.7 %collective-permute-start.17 = (bf16[1296,512]{1,0:T(8,128)(2,1)S(1)}, bf16[1296,512]{1,0:T(8,128)(2,1)S(1)}, u32[]{:S(2)}, u32[]{:S(2)}) collective-permute-start(bf16[1296,512]{1,0:T(8,128)(2,1)S(1)} %collective-permute-done.15.refs_2_), channel_id=1, source_target_pairs={{0,1},{1,0},{2,3},{3,2},{4,5},{5,4},{6,7},{7,6},{8,9},{9,8},{10,11... | collective-permute-start | bytes 3981320 | tf_op jit(solution)/shard_map/ppermute | solution.py:545
  135.2 24.7 %collective-permute-start.18 = (bf16[1984,256]{1,0:T(8,128)(2,1)S(1)}, bf16[1984,256]{1,0:T(8,128)(2,1)S(1)}, u32[]{:S(2)}, u32[]{:S(2)}) collective-permute-start(bf16[1984,256]{1,0:T(8,128)(2,1)S(1)} %get-tuple-element.158), channel_id=1, source_target_pairs={{0,1},{1,0},{2,3},{3,2},{4,5},{5,4},{6,7},{7,6},{8,9},{9,8},{10,11... | collective-permute-start | bytes 3047432 | tf_op jit(solution)/shard_map/ppermute | solution.py:545
  138.7 8.3 %collective-permute-start.21 = (bf16[4,64,512]{2,1,0:T(8,128)(2,1)S(1)}, bf16[4,64,512]{2,1,0:T(8,128)(2,1)S(1)}, u32[]{:S(2)}, u32[]{:S(2)}) collective-permute-start(bf16[4,64,512]{2,1,0:T(8,128)(2,1)S(1)} %get-tuple-element.171), channel_id=1, source_target_pairs={{0,8},{4,12},{8,0},{12,4},{16,24},{20,28},{24,16},{28,20},{1,9},{5... | collective-permute-start | bytes 786440 | tf_op jit(solution)/shard_map/ppermute | solution.py:545
  139.2 7.9 %collective-permute-start.20 = (bf16[4,64,512]{2,1,0:T(8,128)(2,1)S(1)}, bf16[4,64,512]{2,1,0:T(8,128)(2,1)S(1)}, u32[]{:S(2)}, u32[]{:S(2)}) collective-permute-start(bf16[4,64,512]{2,1,0:T(8,128)(2,1)S(1)} %get-tuple-element.161), channel_id=1, source_target_pairs={{0,4},{4,0},{8,12},{12,8},{16,20},{20,16},{24,28},{28,24},{1,5},{5... | collective-permute-start | bytes 786440 | tf_op jit(solution)/shard_map/ppermute | solution.py:545
  158.8 17.7 %collective-permute-start.25 = (bf16[688,512]{1,0:T(8,128)(2,1)S(1)}, bf16[688,512]{1,0:T(8,128)(2,1)S(1)}, u32[]{:S(2)}, u32[]{:S(2)}) collective-permute-start(bf16[688,512]{1,0:T(8,128)(2,1)S(1)} %slice.37), channel_id=1, source_target_pairs={{0,2},{1,3},{2,0},{3,1},{4,6},{5,7},{6,4},{7,5},{8,10},{9,11},{10,... | collective-permute-start | bytes 2113544 | tf_op jit(solution)/shard_map/ppermute | solution.py:545
  159.4 17.0 %collective-permute-start.24 = (bf16[4,64,512]{2,1,0:T(8,128)(2,1)S(1)}, bf16[4,64,512]{2,1,0:T(8,128)(2,1)S(1)}, u32[]{:S(2)}, u32[]{:S(2)}) collective-permute-start(bf16[4,64,512]{2,1,0:T(8,128)(2,1)S(1)} %send_both.8.a), channel_id=1, source_target_pairs={{0,16},{4,20},{8,24},{12,28},{16,0},{20,4},{24,8},{28,12},{1,17},{... | collective-permute-start | bytes 786440 | tf_op jit(solution)/shard_map/ppermute | solution.py:545
  193.1 8.4 %collective-permute-start.32 = (bf16[512,256]{1,0:T(8,128)(2,1)S(1)}, bf16[512,256]{1,0:T(8,128)(2,1)S(1)}, u32[]{:S(2)}, u32[]{:S(2)}) collective-permute-start(bf16[512,256]{1,0:T(8,128)(2,1)S(1)} %get-tuple-element.195), channel_id=1, source_target_pairs={{0,8},{4,12},{8,0},{12,4},{16,24},{20,28},{24,16},{28,20},{1,9},{5... | collective-permute-start | bytes 786440 | tf_op jit(solution)/shard_map/ppermute | solution.py:545
  193.6 8.0 %collective-permute-start.31 = (bf16[512,256]{1,0:T(8,128)(2,1)S(1)}, bf16[512,256]{1,0:T(8,128)(2,1)S(1)}, u32[]{:S(2)}, u32[]{:S(2)}) collective-permute-start(bf16[512,256]{1,0:T(8,128)(2,1)S(1)} %get-tuple-element.188), channel_id=1, source_target_pairs={{0,4},{4,0},{8,12},{12,8},{16,20},{20,16},{24,28},{28,24},{1,5},{5... | collective-permute-start | bytes 786440 | tf_op jit(solution)/shard_map/ppermute | solution.py:545
  203.0 6.4 %collective-permute-start.34 = (bf16[256,256]{1,0:T(8,128)(2,1)S(1)}, bf16[256,256]{1,0:T(8,128)(2,1)S(1)}, u32[]{:S(2)}, u32[]{:S(2)}) collective-permute-start(bf16[256,256]{1,0:T(8,128)(2,1)S(1)} %get-tuple-element.197), channel_id=1, source_target_pairs={{0,8},{4,12},{8,0},{12,4},{16,24},{20,28},{24,16},{28,20},{1,9},{5... | collective-permute-start | bytes 393224 | tf_op jit(solution)/shard_map/ppermute | solution.py:545
  204.4 6.3 %collective-permute-start.36 = (bf16[32,2048]{1,0:T(8,128)(2,1)S(1)}, bf16[32,2048]{1,0:T(8,128)(2,1)S(1)}, u32[]{:S(2)}, u32[]{:S(2)}) collective-permute-start(bf16[32,2048]{1,0:T(8,128)(2,1)S(1)} %get-tuple-element.201.refs_0_), channel_id=1, source_target_pairs={{0,4},{4,0},{8,12},{12,8},{16,20},{20,16},{24,28},{28,24},{1,5},{5... | collective-permute-start | bytes 393224 | tf_op jit(solution)/shard_map/ppermute | solution.py:545
  206.4 17.4 %collective-permute-start.44 = (bf16[992,256]{1,0:T(8,128)(2,1)S(1)}, bf16[992,256]{1,0:T(8,128)(2,1)S(1)}, u32[]{:S(2)}, u32[]{:S(2)}) collective-permute-start(bf16[992,256]{1,0:T(8,128)(2,1)S(1)} %slice.40), channel_id=1, source_target_pairs={{0,2},{1,3},{2,0},{3,1},{4,6},{5,7},{6,4},{7,5},{8,10},{9,11},{10,... | collective-permute-start | bytes 1523720 | tf_op jit(solution)/shard_map/ppermute | solution.py:545
  210.0 12.4 %collective-permute-start.37 = (bf16[512,256]{1,0:T(8,128)(2,1)S(1)}, bf16[512,256]{1,0:T(8,128)(2,1)S(1)}, u32[]{:S(2)}, u32[]{:S(2)}) collective-permute-start(bf16[512,256]{1,0:T(8,128)(2,1)S(1)} %send_both.11.a), channel_id=1, source_target_pairs={{0,16},{4,20},{8,24},{12,28},{16,0},{20,4},{24,8},{28,12},{1,17},{... | collective-permute-start | bytes 786440 | tf_op jit(solution)/shard_map/ppermute | solution.py:545
  215.4 8.2 %collective-permute-start.39 = (bf16[288,256]{1,0:T(8,128)(2,1)S(1)}, bf16[288,256]{1,0:T(8,128)(2,1)S(1)}, u32[]{:S(2)}, u32[]{:S(2)}) collective-permute-start(bf16[288,256]{1,0:T(8,128)(2,1)S(1)} %group_grad.1.a), channel_id=1, source_target_pairs={{0,4},{4,0},{8,12},{12,8},{16,20},{20,16},{24,28},{28,24},{1,5},{5... | collective-permute-start | bytes 442376 | tf_op jit(solution)/shard_map/ppermute | solution.py:545
  217.7 16.8 %collective-permute-start.45 = (bf16[992,256]{1,0:T(8,128)(2,1)S(1)}, bf16[992,256]{1,0:T(8,128)(2,1)S(1)}, u32[]{:S(2)}, u32[]{:S(2)}) collective-permute-start(bf16[992,256]{1,0:T(8,128)(2,1)S(1)} %slice.41), channel_id=1, source_target_pairs={{0,2},{1,3},{2,0},{3,1},{4,6},{5,7},{6,4},{7,5},{8,10},{9,11},{10,... | collective-permute-start | bytes 1523720 | tf_op jit(solution)/shard_map/ppermute | solution.py:545
  219.3 9.2 %collective-permute-start.42 = (bf16[64,2048]{1,0:T(8,128)(2,1)S(1)}, bf16[64,2048]{1,0:T(8,128)(2,1)S(1)}, u32[]{:S(2)}, u32[]{:S(2)}) collective-permute-start(bf16[64,2048]{1,0:T(8,128)(2,1)S(1)} %get-tuple-element.212.b), channel_id=1, source_target_pairs={{0,8},{4,12},{8,0},{12,4},{16,24},{20,28},{24,16},{28,20},{1,9},{5... | collective-permute-start | bytes 786440 | tf_op jit(solution)/shard_map/ppermute | solution.py:545
  222.4 8.3 %collective-permute-start.41 = (bf16[64,2048]{1,0:T(8,128)(2,1)S(1)}, bf16[64,2048]{1,0:T(8,128)(2,1)S(1)}, u32[]{:S(2)}, u32[]{:S(2)}) collective-permute-start(bf16[64,2048]{1,0:T(8,128)(2,1)S(1)} %get-tuple-element.210.a), channel_id=1, source_target_pairs={{0,4},{4,0},{8,12},{12,8},{16,20},{20,16},{24,28},{28,24},{1,5},{5... | collective-permute-start | bytes 786440 | tf_op jit(solution)/shard_map/ppermute | solution.py:545
  223.6 9.1 %collective-permute-start.40 = (bf16[288,256]{1,0:T(8,128)(2,1)S(1)}, bf16[288,256]{1,0:T(8,128)(2,1)S(1)}, u32[]{:S(2)}, u32[]{:S(2)}) collective-permute-start(bf16[288,256]{1,0:T(8,128)(2,1)S(1)} %add.36.a), channel_id=1, source_target_pairs={{0,8},{4,12},{8,0},{12,4},{16,24},{20,28},{24,16},{28,20},{1,9},{5... | collective-permute-start | bytes 442376 | tf_op jit(solution)/shard_map/ppermute | solution.py:545
  223.8 9.0 %collective-permute-start.43 = (bf16[256,256]{1,0:T(8,128)(2,1)S(1)}, bf16[256,256]{1,0:T(8,128)(2,1)S(1)}, u32[]{:S(2)}, u32[]{:S(2)}) collective-permute-start(bf16[256,256]{1,0:T(8,128)(2,1)S(1)} %get-tuple-element.231), channel_id=1, source_target_pairs={{0,4},{4,0},{8,12},{12,8},{16,20},{20,16},{24,28},{28,24},{1,5},{5... | collective-permute-start | bytes 393224 | tf_op jit(solution)/shard_map/ppermute | solution.py:545
  230.8 8.4 %collective-permute-start.46 = (bf16[992,256]{1,0:T(8,128)(2,1)S(1)}, bf16[992,256]{1,0:T(8,128)(2,1)S(1)}, u32[]{:S(2)}, u32[]{:S(2)}) collective-permute-start(bf16[992,256]{1,0:T(8,128)(2,1)S(1)} %collective-permute-done.44.refs_0_), channel_id=1, source_target_pairs={{0,1},{1,0},{2,3},{3,2},{4,5},{5,4},{6,7},{7,6},{8,9},{9,8},{10,11... | collective-permute-start | bytes 1523720 | tf_op jit(solution)/shard_map/ppermute | solution.py:545
  235.7 12.4 %collective-permute-start.48 = (bf16[512,256]{1,0:T(8,128)(2,1)S(1)}, bf16[512,256]{1,0:T(8,128)(2,1)S(1)}, u32[]{:S(2)}, u32[]{:S(2)}) collective-permute-start(bf16[512,256]{1,0:T(8,128)(2,1)S(1)} %get-tuple-element.217.a), channel_id=1, source_target_pairs={{0,4},{4,0},{8,12},{12,8},{16,20},{20,16},{24,28},{28,24},{1,5},{5... | collective-permute-start | bytes 786440 | tf_op jit(solution)/shard_map/ppermute | solution.py:545
  236.4 9.5 %collective-permute-start.49 = (bf16[288,256]{1,0:T(8,128)(2,1)S(1)}, bf16[288,256]{1,0:T(8,128)(2,1)S(1)}, u32[]{:S(2)}, u32[]{:S(2)}) collective-permute-start(bf16[288,256]{1,0:T(8,128)(2,1)S(1)} %add.37.a), channel_id=1, source_target_pairs={{0,16},{4,20},{8,24},{12,28},{16,0},{20,4},{24,8},{28,12},{1,17},{... | collective-permute-start | bytes 442376 | tf_op jit(solution)/shard_map/ppermute | solution.py:545
  236.4 11.7 %collective-permute-start.50 = (bf16[512,256]{1,0:T(8,128)(2,1)S(1)}, bf16[512,256]{1,0:T(8,128)(2,1)S(1)}, u32[]{:S(2)}, u32[]{:S(2)}) collective-permute-start(bf16[512,256]{1,0:T(8,128)(2,1)S(1)} %get-tuple-element.223.b), channel_id=1, source_target_pairs={{0,8},{4,12},{8,0},{12,4},{16,24},{20,28},{24,16},{28,20},{1,9},{5... | collective-permute-start | bytes 786440 | tf_op jit(solution)/shard_map/ppermute | solution.py:545
  (29 other events, 173.8 us)

commit v8 on v7

--- a/solution.py
+++ b/solution.py
@@ -381,8 +381,8 @@
         rest[k] = dot_tn(f[...], d_red[0 : f.shape[0]])
 
 
-def reduce_grad_rest_kernel(dims, d_red, near, rest, *refs):
-    *feats, out = refs
+def reduce_grad_rest_kernel(firsts, dims, d_red, near, rest, *refs):
+    *feats, out, send_a, send_b = refs
     share = feats[0].shape[1]
     me = dims[2]
     for k in range(2):
@@ -392,6 +392,10 @@
         rows = pl.ds(pl.multiple_of((me ^ (k + 2)) * share, share), share)
         first = d_red.shape[0] - f.shape[0]
         out[rows, :] = (rest[k] + dot_tn(f[...], d_red[first:])).astype(BF16)
+    n = send_a.shape[0]
+    for h, send in enumerate((send_a, send_b)):
+        at = 2 * h * n + (1 - bit_of(dims[3], firsts[h])) * n
+        send[...] = out[pl.ds(pl.multiple_of(at, 16), n), :]
 
 
 def features_grad_kernel(part, *refs):
@@ -820,12 +824,13 @@
         [shape((n_chan * share, width), BF16), shape((n_chan - 2, share, width), F32)],
         [dims, d_reduced, own, beside, *firsts], flops=n_chan * mm, name="reduce_grad", smem=True,
     )
-    tail = call(
-        reduce_grad_rest_kernel, [shape((n_chan * share, width), BF16)],
+    tail, *sends = call(
+        functools.partial(reduce_grad_rest_kernel, [o[0] for o in orders]),
+        [shape((n_chan * share, width), BF16)] + [shape((n_chan * share // 4, width), BF16)] * 2,
         [dims, d_reduced, tail, rest, *lasts], flops=mm, name="reduce_grad_rest", smem=True,
     )
     d_beside = swap(d_reduced, "chan", n_chan, 1)
-    tail = after(tail, d_beside)
+    sends = [after(v, d_beside) for v in sends]
     piece_rows = padded // PIECES
     d_far = []
 
@@ -840,7 +845,7 @@
 
     got = [[], []]
     for s in range(top):
-        send = send_both(dims, tail, got, orders, s)
+        send = send_both(dims, tail, got, orders, s) if s else sends
         new = [swap(send[h], "batch", n_batch, 1 << orders[h][s]) for h in halves]
         ties = []
         if s == 0:

time: 251 us -> 250 us (level)
    pallas_call x44 -> x43, Pallas kernels: 67.6 us -> 67 us  [call(): pl.pallas_call(kernel, out_shape=list(outs), grid=(steps,) if steps else...]
where the time goes in v8:
time: 250 us
  waiting for transfers between devices  78.5 us (31%)
  Pallas kernels  67 us (27%)
  blocking collectives  49.6 us (20%)
  starting transfers between devices  41.3 us (17%)
  local copies, waits for them, and re-layouts  8.1 us (3%)
  other arithmetic  2.58 us (1%)
  between operations  2.56 us (1%)
    ppermute x51, waiting for transfers between devices, swap(): return lax.ppermute(v, axis, [(i, i ^ k) for i in range(size)])  78.5 us
    pallas_call x43, Pallas kernels, call(): pl.pallas_call(kernel, out_shape=list(outs), grid=(steps,) if steps else...  67 us
    all_to_all x5, blocking collectives, batch_sum(): return lax.all_to_all(spread, 'batch', 0, 0)  49.6 us
    ppermute x51, starting transfers between devices, swap(): return lax.ppermute(v, axis, [(i, i ^ k) for i in range(size)])  41.3 us
  transfers between devices with their start and end apart: 51, of which 26 were waited for; matrix products, arithmetic and copies ran while one was open for 2% of the time, Pallas kernels for 23%

profile of v8, /device:TPU:0, one launch (start us, length us, event | category | flops | bytes accessed | tf_op | source)
XLA Modules:
  0.0 249.5 jit_solution(16752724808080534583)
XLA Ops:
  3.9 2.6 %collective-permute-start.1 = (bf16[1024,256]{1,0:T(8,128)(2,1)S(1)}, bf16[1024,256]{1,0:T(8,128)(2,1)S(1)}, u32[]{:S(2)}, u32[]{:S(2)}) collective-permute-start(bf16[1024,256]{1,0:T(8,128)(2,1)S(1)} %constant_dynamic-slice_fusion), channel_id=1, source_target_pairs={{0,2},{1,3},{2,0},{3,1},{4,6},{5,7},{6,4},{7,5},{8,10},{9,11},{10,... | collective-permute-start | bytes 1572872 | tf_op jit(solution)/shard_map/ppermute | solution.py:549
  7.9 11.1 %collective-permute-done.1.refs_0_ = bf16[1024,256]{1,0:T(8,128)(2,1)S(1)} collective-permute-done((bf16[1024,256]{1,0:T(8,128)(2,1)S(1)}, bf16[1024,256]{1,0:T(8,128)(2,1)S(1)}, u32[]{:S(2)}, u32[]{:S(2)}) %collective-permute-start.1) | collective-permute-done | bytes 524320 | tf_op jit(solution)/shard_map/ppermute | solution.py:549
  19.1 2.7 %part_far.1 = bf16[1984,256]{1,0:T(8,128)(2,1)S(1)} custom-call(s32[5]{0:T(128)S(1)} %stack.11.dims, bf16[1984,512]{1,0:T(8,128)(2,1)S(1)} %pad.4.own.refs_0_.feats, bf16[1984,512]{1,0:T(8,128)(2,1)} %collective-permute-done.beside.refs_1_, bf16[1024,256]{1,0:T(8,128)(2,1)S(1)} %collective-permute-done.1.refs_0_), custom_call_target="tpu_custom_call" | custom-call | flops 1040187392 | bytes 5603348 | tf_op jit(solution)/shard_map/part_far/pallas_call | solution.py:530
  24.2 3.6 %near.1.part = f32[1984,256]{1,0:T(8,128)S(1)} custom-call(s32[5]{0:T(128)S(1)} %stack.11.dims, bf16[1984,512]{1,0:T(8,128)(2,1)S(1)} %pad.4.own.refs_0_.feats, bf16[1984,512]{1,0:T(8,128)(2,1)} %collective-permute-done.beside.refs_1_, bf16[2048,256]{1,0:T(8,128)(2,1)S(1)} %copy-done.1), custom_call_target="tpu_custom_call" | custom-call | flops 1040187392 | bytes 7143444 | tf_op jit(solution)/shard_map/near/pallas_call | solution.py:530
  27.9 3.3 %copy-done = bf16[24,9,9,2048]{3,0,2,1:T(8,128)(2,1)S(1)} copy-done((bf16[24,9,9,2048]{3,0,2,1:T(8,128)(2,1)S(1)}, bf16[24,9,9,2048]{3,0,2,1:T(8,128)(2,1)}, u32[]{:S(2)}) %copy-start) | copy-done | bytes 7962648
  33.0 2.5 %fusion.5.live = f32[1984,128]{1,0:T(8,128)S(1)} fusion(s32[1984]{0:T(1024)S(1)} %get-tuple-element.244, s32[1984]{0:T(1024)S(1)} %get-tuple-element.249, s32[]{:T(128)} %bitcast.30, s32[1984]{0:T(1024)S(1)} %get-tuple-element.243, s32[1984]{0:T(1024)S(1)} %get-tuple-element.250, s32[]{:T(128)} %bitcast.31, s32[1984]{0:T(1024)S(1)} %get-tuple-element.247, ...), kind=kLoop, calls=%fused_computation.9 | loop fusion | flops 3809280 | bytes 1069384 | tf_op jit(solution)/shard_map/convert_element_type | solution.py:645
  35.8 10.2 %collective-permute-done.2.refs_0_ = bf16[1984,256]{1,0:T(8,128)(2,1)S(1)} collective-permute-done((bf16[1984,256]{1,0:T(8,128)(2,1)S(1)}, bf16[1984,256]{1,0:T(8,128)(2,1)S(1)}, u32[]{:S(2)}, u32[]{:S(2)}) %collective-permute-start.2) | collective-permute-done | bytes 1015840 | tf_op jit(solution)/shard_map/ppermute | solution.py:549
  48.1 3.7 %collective-permute-start.8 = (f32[1,3,256]{2,1,0:T(4,128)S(1)}, f32[1,3,256]{2,1,0:T(4,128)S(1)}, u32[]{:S(2)}, u32[]{:S(2)}) collective-permute-start(f32[1,3,256]{2,1,0:T(4,128)S(1)} %get-tuple-element.143.refs_0_), channel_id=1, source_target_pairs={{0,24},{4,28},{8,16},{12,20},{16,8},{20,12},{24,0},{28,4},{1,25},{... | collective-permute-start | bytes 9224 | tf_op jit(solution)/shard_map/ppermute | solution.py:549
  53.6 2.7 %collective-permute-done.7.refs_2_ = f32[1,3,256]{2,1,0:T(4,128)S(1)} collective-permute-done((f32[1,3,256]{2,1,0:T(4,128)S(1)}, f32[1,3,256]{2,1,0:T(4,128)S(1)}, u32[]{:S(2)}, u32[]{:S(2)}) %collective-permute-start.7) | collective-permute-done | bytes 3104 | tf_op jit(solution)/shard_map/ppermute | solution.py:549
  60.0 3.5 %conv.1 = (f32[1984,256]{1,0:T(8,128)S(1)}, f32[8,2,256]{2,1,0:T(2,128)S(1)}) custom-call(f32[1984,128]{1,0:T(8,128)S(1)} %fusion.5.live, f32[1984,256]{1,0:T(8,128)S(1)} %get-tuple-element.142.z, f32[2,3,256]{2,1,0:T(4,128)S(1)} %pair.1.got.counts, f32[1,256]{1,0:T(1,128)S(1)} %bitcast.36, f32[1,256]{1,0:T(1,128)S(1)} %bitcast.44, bf16[9,256,256]{2,1,0:T(8,128)(2,1)S(1)} %taps.1), custom_call_target="tpu_custom_call" | custom-call | flops 2340421632 | bytes 6283264 | tf_op jit(solution)/shard_map/conv/pallas_call | solution.py:530
  63.6 10.5 %all_to_all.25.got.got_two = f32[8,2,256]{2,1,0:T(2,128)S(1)} all-to-all(f32[8,2,256]{2,1,0:T(2,128)S(1)} %get-tuple-element.148), channel_id=1, replica_groups=mesh['batch'=8,'chan'=4] {'batch'}, dimensions={0} | all-to-all | bytes 32768 | tf_op jit(solution)/shard_map/all_to_all | solution.py:553
  76.3 2.5 %slope_one.1.slope = f32[1984,256]{1,0:T(8,128)S(1)} custom-call(f32[1984,128]{1,0:T(8,128)S(1)} %fusion.5.live, f32[1984,256]{1,0:T(8,128)S(1)} %get-tuple-element.142.z, f32[2,3,256]{2,1,0:T(4,128)S(1)} %pair.1.got.counts, f32[2,3,256]{2,1,0:T(4,128)S(1)} %pair.1.got.counts, f32[1,256]{1,0:T(1,128)S(1)} %bitcast.37, f32[1,256]{1,0:T(1,128)S(1)} %bitcast.45), custom_call_target="tpu_custom_call" | custom-call | flops 520093696 | bytes 5093376 | tf_op jit(solution)/shard_map/slope_one/pallas_call | solution.py:530
  79.0 2.5 %slope_two.1.slope = f32[1984,256]{1,0:T(8,128)S(1)} custom-call(f32[1984,128]{1,0:T(8,128)S(1)} %fusion.5.live, f32[1984,256]{1,0:T(8,128)S(1)} %get-tuple-element.144.z.grouped, f32[2,3,256]{2,1,0:T(4,128)S(1)} %pair.1.got.counts, f32[8,2,256]{2,1,0:T(2,128)S(1)} %all_to_all.25.got.got_two, f32[1,256]{1,0:T(1,128)S(1)} %bitcast.34, f32[1,256]{1,0:T(1,128)S(1)} %bitcast.43), custom_call_target="tpu_custom_call" | custom-call | flops 520093696 | bytes 5103616 | tf_op jit(solution)/shard_map/slope_two/pallas_call | solution.py:530
  82.9 17.7 %collective-permute-done.13.refs_0_.refs_2_ = bf16[1984,256]{1,0:T(8,128)(2,1)S(1)} collective-permute-done((bf16[1984,256]{1,0:T(8,128)(2,1)S(1)}, bf16[1984,256]{1,0:T(8,128)(2,1)S(1)}, u32[]{:S(2)}, u32[]{:S(2)}) %collective-permute-start.13) | collective-permute-done | bytes 1015840 | tf_op jit(solution)/shard_map/ppermute | solution.py:549
  105.2 9.1 %all_to_all.26.got = f32[8,2,512]{2,1,0:T(2,128)S(1)} all-to-all(f32[8,2,512]{2,1,0:T(2,128)S(1)} %get-tuple-element.152), channel_id=1, replica_groups=mesh['batch'=8,'chan'=4] {'batch'}, dimensions={0} | all-to-all | bytes 65536 | tf_op jit(solution)/shard_map/all_to_all | solution.py:553
  114.3 3.9 %third.1 = (f32[1984,512]{1,0:T(8,128)S(1)}, f32[8,2,512]{2,1,0:T(2,128)S(1)}) custom-call(f32[1984,128]{1,0:T(8,128)S(1)} %fusion.5.live, f32[1984,512]{1,0:T(8,128)S(1)} %get-tuple-element.164.e, f32[2,3,256]{2,1,0:T(4,128)S(1)} %pair.1.got.counts, f32[8,2,512]{2,1,0:T(2,128)S(1)} %all_to_all.26.got, f32[1,512]{1,0:T(1,128)S(1)} %get-tuple-element.127.gain, ...), custom_call_target="tpu_custom_call" | custom-call | flops 2080374784 | bytes 13281280 | tf_op jit(solution)/shard_map/third/pallas_call | solution.py:530
  118.2 9.1 %all_to_all.27.totals = f32[8,2,512]{2,1,0:T(2,128)S(1)} all-to-all(f32[8,2,512]{2,1,0:T(2,128)S(1)} %get-tuple-element.154), channel_id=1, replica_groups=mesh['batch'=8,'chan'=4] {'batch'}, dimensions={0} | all-to-all | bytes 65536 | tf_op jit(solution)/shard_map/all_to_all | solution.py:553
  129.3 2.9 %collective-permute-done.15.refs_2_ = bf16[1296,512]{1,0:T(8,128)(2,1)S(1)} collective-permute-done((bf16[1296,512]{1,0:T(8,128)(2,1)S(1)}, bf16[1296,512]{1,0:T(8,128)(2,1)S(1)}, u32[]{:S(2)}, u32[]{:S(2)}) %collective-permute-start.15) | collective-permute-done | bytes 1327136 | tf_op jit(solution)/shard_map/ppermute | solution.py:549
  135.7 2.4 expand_grad.1.whole
  139.9 5.1 %block.1 = bf16[1944,512]{1,0:T(8,128)(2,1)} custom-call(f32[1984,128]{1,0:T(8,128)S(1)} %fusion.5.live, f32[1984,512]{1,0:T(8,128)S(1)} %get-tuple-element.164.e, f32[2,3,256]{2,1,0:T(4,128)S(1)} %pair.1.got.counts, f32[8,2,512]{2,1,0:T(2,128)S(1)} %all_to_all.26.got, f32[1,512]{1,0:T(1,128)S(1)} %get-tuple-element.127.gain, ...), custom_call_target="tpu_custom_call" | custom-call | flops 1040187392 | bytes 9144320 | tf_op jit(solution)/shard_map/block/pallas_call | solution.py:530
  149.9 2.9 %collective-permute-done.22.refs_1_ = bf16[4,32,512]{2,1,0:T(8,128)(2,1)S(1)} collective-permute-done((bf16[4,32,512]{2,1,0:T(8,128)(2,1)S(1)}, bf16[4,32,512]{2,1,0:T(8,128)(2,1)S(1)}, u32[]{:S(2)}, u32[]{:S(2)}) %collective-permute-start.22) | collective-permute-done | bytes 131104 | tf_op jit(solution)/shard_map/ppermute | solution.py:549
  155.0 3.8 %collective-permute-done.19.refs_2_ = bf16[1984,256]{1,0:T(8,128)(2,1)S(1)} collective-permute-done((bf16[1984,256]{1,0:T(8,128)(2,1)S(1)}, bf16[1984,256]{1,0:T(8,128)(2,1)S(1)}, u32[]{:S(2)}, u32[]{:S(2)}) %collective-permute-start.19) | collective-permute-done | bytes 1015840 | tf_op jit(solution)/shard_map/ppermute | solution.py:549
  161.1 11.8 %all_to_all.28.totals = f32[8,2,256]{2,1,0:T(2,128)S(1)} all-to-all(f32[8,2,256]{2,1,0:T(2,128)S(1)} %get-tuple-element.169), channel_id=1, replica_groups=mesh['batch'=8,'chan'=4] {'batch'}, dimensions={0} | all-to-all | bytes 32768 | tf_op jit(solution)/shard_map/all_to_all | solution.py:553
  172.9 3.5 %conv_back.1 = (f32[1984,256]{1,0:T(8,128)S(1)}, f32[1984,256]{1,0:T(8,128)S(1)}, f32[8,2,256]{2,1,0:T(2,128)S(1)}, f32[2,256]{1,0:T(2,128)S(1)}) custom-call(f32[1984,128]{1,0:T(8,128)S(1)} %fusion.5.live, f32[1984,256]{1,0:T(8,128)S(1)} %get-tuple-element.168.d_two, f32[1984,256]{1,0:T(8,128)S(1)} %get-tuple-element.144.z.grouped, ...), custom_call_target="tpu_custom_call" | custom-call | flops 2340421632 | bytes 14443520 | tf_op jit(solution)/shard_map/conv_back/pallas_call | solution.py:530
  176.5 9.2 %all_to_all.29.totals = f32[8,2,256]{2,1,0:T(2,128)S(1)} all-to-all(f32[8,2,256]{2,1,0:T(2,128)S(1)} %get-tuple-element.184), channel_id=1, replica_groups=mesh['batch'=8,'chan'=4] {'batch'}, dimensions={0} | all-to-all | bytes 32768 | tf_op jit(solution)/shard_map/all_to_all | solution.py:553
  187.5 3.7 %reduce_grad.1 = (bf16[2048,256]{1,0:T(8,128)(2,1)S(1)}, f32[2,512,256]{2,1,0:T(8,128)S(1)}) custom-call(s32[5]{0:T(128)S(1)} %stack.11.dims, bf16[1984,256]{1,0:T(8,128)(2,1)S(1)} %get-tuple-element.225.d_red.refs_0_, bf16[1984,512]{1,0:T(8,128)(2,1)S(1)} %pad.4.own.refs_0_.feats, bf16[1984,512]{1,0:T(8,128)(2,1)} %collective-permute-done.beside.refs_1_, ...), custom_call_target="tpu_custom_call" | custom-call | flops 2080374784 | bytes 9830420 | tf_op jit(solution)/shard_map/reduce_grad/pallas_call | solution.py:530
  195.6 2.6 %collective-permute-done.29.refs_2_ = bf16[64,512]{1,0:T(8,128)(2,1)S(1)} collective-permute-done((bf16[64,512]{1,0:T(8,128)(2,1)S(1)}, bf16[64,512]{1,0:T(8,128)(2,1)S(1)}, u32[]{:S(2)}, u32[]{:S(2)}) %collective-permute-start.29) | collective-permute-done | bytes 65568 | tf_op jit(solution)/shard_map/ppermute | solution.py:549
  211.1 3.7 %group_grad.1.a = bf16[288,256]{1,0:T(8,128)(2,1)S(1)} custom-call(f32[1984,128]{1,0:T(8,128)S(1)} %fusion.5.live, f32[1984,256]{1,0:T(8,128)S(1)} %get-tuple-element.142.z, f32[2,3,256]{2,1,0:T(4,128)S(1)} %pair.1.got.counts, f32[1,256]{1,0:T(1,128)S(1)} %bitcast.39, f32[1,256]{1,0:T(1,128)S(1)} %bitcast.46, f32[1984,256]{1,0:T(8,128)S(1)} %get-tuple-element.209.d_grouped), custom_call_target="tpu_custom_call" | custom-call | flops 520093696 | bytes 5234688 | tf_op jit(solution)/shard_map/group_grad/pallas_call | solution.py:530
  214.8 2.7 %collective-permute-start.39 = (bf16[288,256]{1,0:T(8,128)(2,1)S(1)}, bf16[288,256]{1,0:T(8,128)(2,1)S(1)}, u32[]{:S(2)}, u32[]{:S(2)}) collective-permute-start(bf16[288,256]{1,0:T(8,128)(2,1)S(1)} %group_grad.1.a), channel_id=1, source_target_pairs={{0,4},{4,0},{8,12},{12,8},{16,20},{20,16},{24,28},{28,24},{1,5},{5... | collective-permute-start | bytes 442376 | tf_op jit(solution)/shard_map/ppermute | solution.py:549
  225.4 3.0 %collective-permute-done.42.other_b = bf16[64,2048]{1,0:T(8,128)(2,1)S(1)} collective-permute-done((bf16[64,2048]{1,0:T(8,128)(2,1)S(1)}, bf16[64,2048]{1,0:T(8,128)(2,1)S(1)}, u32[]{:S(2)}, u32[]{:S(2)}) %collective-permute-start.42) | collective-permute-done | bytes 262176 | tf_op jit(solution)/shard_map/ppermute | solution.py:549
  238.5 2.8 %input_far.1 = f32[1944,512]{1,0:T(8,128)} custom-call(f32[1984,512]{1,0:T(8,128)S(1)} %input_near.1.part, bf16[992,256]{1,0:T(8,128)(2,1)S(1)} %collective-permute-done.44.refs_0_, bf16[992,256]{1,0:T(8,128)(2,1)S(1)} %collective-permute-done.45.refs_1_, bf16[992,256]{1,0:T(8,128)(2,1)S(1)} %collective-permute-done.46.refs_2_, ...), custom_call_target="tpu_custom_call" | custom-call | flops 1040187392 | bytes 10600448 | tf_op jit(solution)/shard_map/input_far/pallas_call | solution.py:530
  241.3 4.0 %collective-permute-done.49.b = bf16[288,256]{1,0:T(8,128)(2,1)S(1)} collective-permute-done((bf16[288,256]{1,0:T(8,128)(2,1)S(1)}, bf16[288,256]{1,0:T(8,128)(2,1)S(1)}, u32[]{:S(2)}, u32[]{:S(2)}) %collective-permute-start.49) | collective-permute-done | bytes 147488 | tf_op jit(solution)/shard_map/ppermute | solution.py:549
  (155 shorter events, 81.9 us)
Async XLA Ops:
  3.4 15.6 %collective-permute-start = (bf16[1984,512]{1,0:T(8,128)(2,1)S(1)}, bf16[1984,512]{1,0:T(8,128)(2,1)}, u32[]{:S(2)}, u32[]{:S(2)}) collective-permute-start(bf16[1984,512]{1,0:T(8,128)(2,1)S(1)} %pad.4.own.refs_0_.feats), channel_id=1, source_target_pairs={{0,1},{1,0},{2,3},{3,2},{4,5},{5,4},{6,7},{7,6},{8,9},{9,8},{10,11... | collective-permute-start | bytes 6094856 | tf_op jit(solution)/shard_map/ppermute | solution.py:549
  3.9 15.1 %collective-permute-start.1 = (bf16[1024,256]{1,0:T(8,128)(2,1)S(1)}, bf16[1024,256]{1,0:T(8,128)(2,1)S(1)}, u32[]{:S(2)}, u32[]{:S(2)}) collective-permute-start(bf16[1024,256]{1,0:T(8,128)(2,1)S(1)} %constant_dynamic-slice_fusion), channel_id=1, source_target_pairs={{0,2},{1,3},{2,0},{3,1},{4,6},{5,7},{6,4},{7,5},{8,10},{9,11},{10,... | collective-permute-start | bytes 1572872 | tf_op jit(solution)/shard_map/ppermute | solution.py:549
  21.7 24.3 %collective-permute-start.2 = (bf16[1984,256]{1,0:T(8,128)(2,1)S(1)}, bf16[1984,256]{1,0:T(8,128)(2,1)S(1)}, u32[]{:S(2)}, u32[]{:S(2)}) collective-permute-start(bf16[1984,256]{1,0:T(8,128)(2,1)S(1)} %part_far.1), channel_id=1, source_target_pairs={{0,2},{1,3},{2,0},{3,1},{4,6},{5,7},{6,4},{7,5},{8,10},{9,11},{10,... | collective-permute-start | bytes 3047432 | tf_op jit(solution)/shard_map/ppermute | solution.py:549
  27.8 7.9 %collective-permute-start.5 = (bf16[512,256]{1,0:T(8,128)(2,1)S(1)}, bf16[512,256]{1,0:T(8,128)(2,1)S(1)}, u32[]{:S(2)}, u32[]{:S(2)}) collective-permute-start(bf16[512,256]{1,0:T(8,128)(2,1)S(1)} %get-tuple-element.137), channel_id=1, source_target_pairs={{0,1},{1,0},{2,3},{3,2},{4,5},{5,4},{6,7},{7,6},{8,9},{9,8},{10,11... | collective-permute-start | bytes 786440 | tf_op jit(solution)/shard_map/ppermute | solution.py:549
  46.0 17.6 %collective-permute-start.10 = (bf16[256,512]{1,0:T(8,128)(2,1)S(1)}, bf16[256,512]{1,0:T(8,128)(2,1)S(1)}, u32[]{:S(2)}, u32[]{:S(2)}) collective-permute-start(bf16[256,512]{1,0:T(8,128)(2,1)S(1)} %get-tuple-element.146), channel_id=1, source_target_pairs={{0,2},{1,3},{2,0},{3,1},{4,6},{5,7},{6,4},{7,5},{8,10},{9,11},{10,... | collective-permute-start | bytes 786440 | tf_op jit(solution)/shard_map/ppermute | solution.py:549
  47.6 16.0 %collective-permute-start.11 = (bf16[256,512]{1,0:T(8,128)(2,1)S(1)}, bf16[256,512]{1,0:T(8,128)(2,1)S(1)}, u32[]{:S(2)}, u32[]{:S(2)}) collective-permute-start(bf16[256,512]{1,0:T(8,128)(2,1)S(1)} %get-tuple-element.147), channel_id=1, source_target_pairs={{0,3},{1,2},{2,1},{3,0},{4,7},{5,6},{6,5},{7,4},{8,11},{9,10},{10,... | collective-permute-start | bytes 786440 | tf_op jit(solution)/shard_map/ppermute | solution.py:549
  75.8 24.9 %collective-permute-start.13 = (bf16[1984,256]{1,0:T(8,128)(2,1)S(1)}, bf16[1984,256]{1,0:T(8,128)(2,1)S(1)}, u32[]{:S(2)}, u32[]{:S(2)}) collective-permute-start(bf16[1984,256]{1,0:T(8,128)(2,1)S(1)} %hidden.1.refs_0_), channel_id=1, source_target_pairs={{0,2},{1,3},{2,0},{3,1},{4,6},{5,7},{6,4},{7,5},{8,10},{9,11},{10,... | collective-permute-start | bytes 3047432 | tf_op jit(solution)/shard_map/ppermute | solution.py:549
  100.6 31.5 %collective-permute-start.15 = (bf16[1296,512]{1,0:T(8,128)(2,1)S(1)}, bf16[1296,512]{1,0:T(8,128)(2,1)S(1)}, u32[]{:S(2)}, u32[]{:S(2)}) collective-permute-start(bf16[1296,512]{1,0:T(8,128)(2,1)S(1)} %slice.36), channel_id=1, source_target_pairs={{0,2},{1,3},{2,0},{3,1},{4,6},{5,7},{6,4},{7,5},{8,10},{9,11},{10,... | collective-permute-start | bytes 3981320 | tf_op jit(solution)/shard_map/ppermute | solution.py:549
  134.6 24.1 %collective-permute-start.19 = (bf16[1984,256]{1,0:T(8,128)(2,1)S(1)}, bf16[1984,256]{1,0:T(8,128)(2,1)S(1)}, u32[]{:S(2)}, u32[]{:S(2)}) collective-permute-start(bf16[1984,256]{1,0:T(8,128)(2,1)S(1)} %merge.1), channel_id=1, source_target_pairs={{0,2},{1,3},{2,0},{3,1},{4,6},{5,7},{6,4},{7,5},{8,10},{9,11},{10,... | collective-permute-start | bytes 3047432 | tf_op jit(solution)/shard_map/ppermute | solution.py:549
  135.2 24.7 %collective-permute-start.17 = (bf16[1296,512]{1,0:T(8,128)(2,1)S(1)}, bf16[1296,512]{1,0:T(8,128)(2,1)S(1)}, u32[]{:S(2)}, u32[]{:S(2)}) collective-permute-start(bf16[1296,512]{1,0:T(8,128)(2,1)S(1)} %collective-permute-done.15.refs_2_), channel_id=1, source_target_pairs={{0,1},{1,0},{2,3},{3,2},{4,5},{5,4},{6,7},{7,6},{8,9},{9,8},{10,11... | collective-permute-start | bytes 3981320 | tf_op jit(solution)/shard_map/ppermute | solution.py:549
  135.2 24.7 %collective-permute-start.18 = (bf16[1984,256]{1,0:T(8,128)(2,1)S(1)}, bf16[1984,256]{1,0:T(8,128)(2,1)S(1)}, u32[]{:S(2)}, u32[]{:S(2)}) collective-permute-start(bf16[1984,256]{1,0:T(8,128)(2,1)S(1)} %get-tuple-element.160), channel_id=1, source_target_pairs={{0,1},{1,0},{2,3},{3,2},{4,5},{5,4},{6,7},{7,6},{8,9},{9,8},{10,11... | collective-permute-start | bytes 3047432 | tf_op jit(solution)/shard_map/ppermute | solution.py:549
  138.6 8.3 %collective-permute-start.21 = (bf16[4,64,512]{2,1,0:T(8,128)(2,1)S(1)}, bf16[4,64,512]{2,1,0:T(8,128)(2,1)S(1)}, u32[]{:S(2)}, u32[]{:S(2)}) collective-permute-start(bf16[4,64,512]{2,1,0:T(8,128)(2,1)S(1)} %get-tuple-element.173), channel_id=1, source_target_pairs={{0,8},{4,12},{8,0},{12,4},{16,24},{20,28},{24,16},{28,20},{1,9},{5... | collective-permute-start | bytes 786440 | tf_op jit(solution)/shard_map/ppermute | solution.py:549
  139.2 7.9 %collective-permute-start.20 = (bf16[4,64,512]{2,1,0:T(8,128)(2,1)S(1)}, bf16[4,64,512]{2,1,0:T(8,128)(2,1)S(1)}, u32[]{:S(2)}, u32[]{:S(2)}) collective-permute-start(bf16[4,64,512]{2,1,0:T(8,128)(2,1)S(1)} %get-tuple-element.163), channel_id=1, source_target_pairs={{0,4},{4,0},{8,12},{12,8},{16,20},{20,16},{24,28},{28,24},{1,5},{5... | collective-permute-start | bytes 786440 | tf_op jit(solution)/shard_map/ppermute | solution.py:549
  158.8 17.7 %collective-permute-start.25 = (bf16[688,512]{1,0:T(8,128)(2,1)S(1)}, bf16[688,512]{1,0:T(8,128)(2,1)S(1)}, u32[]{:S(2)}, u32[]{:S(2)}) collective-permute-start(bf16[688,512]{1,0:T(8,128)(2,1)S(1)} %slice.37), channel_id=1, source_target_pairs={{0,2},{1,3},{2,0},{3,1},{4,6},{5,7},{6,4},{7,5},{8,10},{9,11},{10,... | collective-permute-start | bytes 2113544 | tf_op jit(solution)/shard_map/ppermute | solution.py:549
  159.4 17.0 %collective-permute-start.24 = (bf16[4,64,512]{2,1,0:T(8,128)(2,1)S(1)}, bf16[4,64,512]{2,1,0:T(8,128)(2,1)S(1)}, u32[]{:S(2)}, u32[]{:S(2)}) collective-permute-start(bf16[4,64,512]{2,1,0:T(8,128)(2,1)S(1)} %send_both.7.a), channel_id=1, source_target_pairs={{0,16},{4,20},{8,24},{12,28},{16,0},{20,4},{24,8},{28,12},{1,17},{... | collective-permute-start | bytes 786440 | tf_op jit(solution)/shard_map/ppermute | solution.py:549
  192.5 8.4 %collective-permute-start.31 = (bf16[512,256]{1,0:T(8,128)(2,1)S(1)}, bf16[512,256]{1,0:T(8,128)(2,1)S(1)}, u32[]{:S(2)}, u32[]{:S(2)}) collective-permute-start(bf16[512,256]{1,0:T(8,128)(2,1)S(1)} %get-tuple-element.190), channel_id=1, source_target_pairs={{0,4},{4,0},{8,12},{12,8},{16,20},{20,16},{24,28},{28,24},{1,5},{5... | collective-permute-start | bytes 786440 | tf_op jit(solution)/shard_map/ppermute | solution.py:549
  193.1 8.0 %collective-permute-start.32 = (bf16[512,256]{1,0:T(8,128)(2,1)S(1)}, bf16[512,256]{1,0:T(8,128)(2,1)S(1)}, u32[]{:S(2)}, u32[]{:S(2)}) collective-permute-start(bf16[512,256]{1,0:T(8,128)(2,1)S(1)} %get-tuple-element.199), channel_id=1, source_target_pairs={{0,8},{4,12},{8,0},{12,4},{16,24},{20,28},{24,16},{28,20},{1,9},{5... | collective-permute-start | bytes 786440 | tf_op jit(solution)/shard_map/ppermute | solution.py:549
  201.7 5.9 %collective-permute-start.35 = (bf16[256,256]{1,0:T(8,128)(2,1)S(1)}, bf16[256,256]{1,0:T(8,128)(2,1)S(1)}, u32[]{:S(2)}, u32[]{:S(2)}) collective-permute-start(bf16[256,256]{1,0:T(8,128)(2,1)S(1)} %get-tuple-element.203), channel_id=1, source_target_pairs={{0,4},{4,0},{8,12},{12,8},{16,20},{20,16},{24,28},{28,24},{1,5},{5... | collective-permute-start | bytes 393224 | tf_op jit(solution)/shard_map/ppermute | solution.py:549
  203.8 6.5 %collective-permute-start.36 = (bf16[32,2048]{1,0:T(8,128)(2,1)S(1)}, bf16[32,2048]{1,0:T(8,128)(2,1)S(1)}, u32[]{:S(2)}, u32[]{:S(2)}) collective-permute-start(bf16[32,2048]{1,0:T(8,128)(2,1)S(1)} %get-tuple-element.205.refs_0_), channel_id=1, source_target_pairs={{0,4},{4,0},{8,12},{12,8},{16,20},{20,16},{24,28},{28,24},{1,5},{5... | collective-permute-start | bytes 393224 | tf_op jit(solution)/shard_map/ppermute | solution.py:549
  204.4 6.0 %collective-permute-start.33 = (bf16[32,2048]{1,0:T(8,128)(2,1)S(1)}, bf16[32,2048]{1,0:T(8,128)(2,1)S(1)}, u32[]{:S(2)}, u32[]{:S(2)}) collective-permute-start(bf16[32,2048]{1,0:T(8,128)(2,1)S(1)} %get-tuple-element.202.sums), channel_id=1, source_target_pairs={{0,8},{4,12},{8,0},{12,4},{16,24},{20,28},{24,16},{28,20},{1,9},{5... | collective-permute-start | bytes 393224 | tf_op jit(solution)/shard_map/ppermute | solution.py:549
  205.9 17.5 %collective-permute-start.44 = (bf16[992,256]{1,0:T(8,128)(2,1)S(1)}, bf16[992,256]{1,0:T(8,128)(2,1)S(1)}, u32[]{:S(2)}, u32[]{:S(2)}) collective-permute-start(bf16[992,256]{1,0:T(8,128)(2,1)S(1)} %slice.40), channel_id=1, source_target_pairs={{0,2},{1,3},{2,0},{3,1},{4,6},{5,7},{6,4},{7,5},{8,10},{9,11},{10,... | collective-permute-start | bytes 1523720 | tf_op jit(solution)/shard_map/ppermute | solution.py:549
  209.7 12.1 %collective-permute-start.37 = (bf16[512,256]{1,0:T(8,128)(2,1)S(1)}, bf16[512,256]{1,0:T(8,128)(2,1)S(1)}, u32[]{:S(2)}, u32[]{:S(2)}) collective-permute-start(bf16[512,256]{1,0:T(8,128)(2,1)S(1)} %send_both.9.a), channel_id=1, source_target_pairs={{0,16},{4,20},{8,24},{12,28},{16,0},{20,4},{24,8},{28,12},{1,17},{... | collective-permute-start | bytes 786440 | tf_op jit(solution)/shard_map/ppermute | solution.py:549
  214.8 8.2 %collective-permute-start.39 = (bf16[288,256]{1,0:T(8,128)(2,1)S(1)}, bf16[288,256]{1,0:T(8,128)(2,1)S(1)}, u32[]{:S(2)}, u32[]{:S(2)}) collective-permute-start(bf16[288,256]{1,0:T(8,128)(2,1)S(1)} %group_grad.1.a), channel_id=1, source_target_pairs={{0,4},{4,0},{8,12},{12,8},{16,20},{20,16},{24,28},{28,24},{1,5},{5... | collective-permute-start | bytes 442376 | tf_op jit(solution)/shard_map/ppermute | solution.py:549
  217.5 16.5 %collective-permute-start.45 = (bf16[992,256]{1,0:T(8,128)(2,1)S(1)}, bf16[992,256]{1,0:T(8,128)(2,1)S(1)}, u32[]{:S(2)}, u32[]{:S(2)}) collective-permute-start(bf16[992,256]{1,0:T(8,128)(2,1)S(1)} %slice.41), channel_id=1, source_target_pairs={{0,2},{1,3},{2,0},{3,1},{4,6},{5,7},{6,4},{7,5},{8,10},{9,11},{10,... | collective-permute-start | bytes 1523720 | tf_op jit(solution)/shard_map/ppermute | solution.py:549
  219.1 9.2 %collective-permute-start.42 = (bf16[64,2048]{1,0:T(8,128)(2,1)S(1)}, bf16[64,2048]{1,0:T(8,128)(2,1)S(1)}, u32[]{:S(2)}, u32[]{:S(2)}) collective-permute-start(bf16[64,2048]{1,0:T(8,128)(2,1)S(1)} %get-tuple-element.216.b), channel_id=1, source_target_pairs={{0,8},{4,12},{8,0},{12,4},{16,24},{20,28},{24,16},{28,20},{1,9},{5... | collective-permute-start | bytes 786440 | tf_op jit(solution)/shard_map/ppermute | solution.py:549
  221.8 8.2 %collective-permute-start.41 = (bf16[64,2048]{1,0:T(8,128)(2,1)S(1)}, bf16[64,2048]{1,0:T(8,128)(2,1)S(1)}, u32[]{:S(2)}, u32[]{:S(2)}) collective-permute-start(bf16[64,2048]{1,0:T(8,128)(2,1)S(1)} %get-tuple-element.214.a), channel_id=1, source_target_pairs={{0,4},{4,0},{8,12},{12,8},{16,20},{20,16},{24,28},{28,24},{1,5},{5... | collective-permute-start | bytes 786440 | tf_op jit(solution)/shard_map/ppermute | solution.py:549
  223.0 8.9 %collective-permute-start.40 = (bf16[288,256]{1,0:T(8,128)(2,1)S(1)}, bf16[288,256]{1,0:T(8,128)(2,1)S(1)}, u32[]{:S(2)}, u32[]{:S(2)}) collective-permute-start(bf16[288,256]{1,0:T(8,128)(2,1)S(1)} %add.36.a), channel_id=1, source_target_pairs={{0,8},{4,12},{8,0},{12,4},{16,24},{20,28},{24,16},{28,20},{1,9},{5... | collective-permute-start | bytes 442376 | tf_op jit(solution)/shard_map/ppermute | solution.py:549
  223.3 8.6 %collective-permute-start.43 = (bf16[256,256]{1,0:T(8,128)(2,1)S(1)}, bf16[256,256]{1,0:T(8,128)(2,1)S(1)}, u32[]{:S(2)}, u32[]{:S(2)}) collective-permute-start(bf16[256,256]{1,0:T(8,128)(2,1)S(1)} %get-tuple-element.235), channel_id=1, source_target_pairs={{0,4},{4,0},{8,12},{12,8},{16,20},{20,16},{24,28},{28,24},{1,5},{5... | collective-permute-start | bytes 393224 | tf_op jit(solution)/shard_map/ppermute | solution.py:549
  229.9 8.6 %collective-permute-start.46 = (bf16[992,256]{1,0:T(8,128)(2,1)S(1)}, bf16[992,256]{1,0:T(8,128)(2,1)S(1)}, u32[]{:S(2)}, u32[]{:S(2)}) collective-permute-start(bf16[992,256]{1,0:T(8,128)(2,1)S(1)} %collective-permute-done.44.refs_0_), channel_id=1, source_target_pairs={{0,1},{1,0},{2,3},{3,2},{4,5},{5,4},{6,7},{7,6},{8,9},{9,8},{10,11... | collective-permute-start | bytes 1523720 | tf_op jit(solution)/shard_map/ppermute | solution.py:549
  235.2 12.4 %collective-permute-start.48 = (bf16[512,256]{1,0:T(8,128)(2,1)S(1)}, bf16[512,256]{1,0:T(8,128)(2,1)S(1)}, u32[]{:S(2)}, u32[]{:S(2)}) collective-permute-start(bf16[512,256]{1,0:T(8,128)(2,1)S(1)} %get-tuple-element.221.a), channel_id=1, source_target_pairs={{0,4},{4,0},{8,12},{12,8},{16,20},{20,16},{24,28},{28,24},{1,5},{5... | collective-permute-start | bytes 786440 | tf_op jit(solution)/shard_map/ppermute | solution.py:549
  235.6 9.7 %collective-permute-start.49 = (bf16[288,256]{1,0:T(8,128)(2,1)S(1)}, bf16[288,256]{1,0:T(8,128)(2,1)S(1)}, u32[]{:S(2)}, u32[]{:S(2)}) collective-permute-start(bf16[288,256]{1,0:T(8,128)(2,1)S(1)} %add.37.a), channel_id=1, source_target_pairs={{0,16},{4,20},{8,24},{12,28},{16,0},{20,4},{24,8},{28,12},{1,17},{... | collective-permute-start | bytes 442376 | tf_op jit(solution)/shard_map/ppermute | solution.py:549
  235.8 11.7 %collective-permute-start.50 = (bf16[512,256]{1,0:T(8,128)(2,1)S(1)}, bf16[512,256]{1,0:T(8,128)(2,1)S(1)}, u32[]{:S(2)}, u32[]{:S(2)}) collective-permute-start(bf16[512,256]{1,0:T(8,128)(2,1)S(1)} %get-tuple-element.227.b), channel_id=1, source_target_pairs={{0,8},{4,12},{8,0},{12,4},{16,24},{20,28},{24,16},{28,20},{1,9},{5... | collective-permute-start | bytes 786440 | tf_op jit(solution)/shard_map/ppermute | solution.py:549
  (29 other events, 174.0 us)
